TPU v7x, 32 devices: a whole 2x2x4 slice. The times are simulated.
32 devices in a mesh: section: 2 (over core), dp: 4 (over y, x), expert: 4 (over z).
Axes of the slice: x: 2, y: 2, z: 4, core: 2. Of those that a mesh axis runs over, the one named last changes fastest.
Arguments:
- tokens: bfloat16 [3072, 1536], P(('dp', 'expert')), may hold values from -6 to 6
- cotangent: bfloat16 [3072, 1536], P(('dp', 'expert')), may hold values from -6 to 6
- segments: int32 [32, 96], P(('dp', 'expert')), may hold values from 0 to 3, never falling along the last dimension, each value on 1 to 48 neighbouring positions
- routes: int32 [2, 3072, 8], P('section', ('dp', 'expert')), may hold values from 0 to 15, as said below
- gain_attn: bfloat16 [2, 1536], P('section'), may hold values from 0.5 to 1.5
- w_query: bfloat16 [2, 1536, 1536], P('section'), may hold values from -0.15625 to 0.15625
- w_key: bfloat16 [2, 1536, 512], P('section'), may hold values from -0.15625 to 0.15625
- w_value: bfloat16 [2, 1536, 512], P('section'), may hold values from -0.15625 to 0.15625
- w_out: bfloat16 [2, 1536, 1536], P('section'), may hold values from -0.4375 to 0.4375
- gain_moe: bfloat16 [2, 1536], P('section'), may hold values from 0.5 to 1.5
- w_router: bfloat16 [2, 1536, 16], P('section'), may hold values from -0.078125 to 0.078125
- w_gate: bfloat16 [2, 16, 1536, 512], P('section', 'expert'), may hold values from -0.15625 to 0.15625
- w_up: bfloat16 [2, 16, 1536, 512], P('section', 'expert'), may hold values from -0.15625 to 0.15625
- w_down: bfloat16 [2, 16, 512, 1536], P('section', 'expert'), may hold values from -1 to 1
Outputs:
- layer_out: bfloat16 [2, 3072, 1536], P('section', ('dp', 'expert'))
- input_grad: float32 [2, 3072, 1536], P('section', ('dp', 'expert'))
- grad_gain_attn: float32 [2, 1536], P('section', ('dp', 'expert'))
- grad_w_query: float32 [2, 1536, 1536], P('section', ('dp', 'expert'))
- grad_w_key: float32 [2, 1536, 512], P('section', ('dp', 'expert'))
- grad_w_value: float32 [2, 1536, 512], P('section', ('dp', 'expert'))
- grad_w_out: float32 [2, 1536, 1536], P('section', ('dp', 'expert'))
- grad_gain_moe: float32 [2, 1536], P('section', ('dp', 'expert'))
- grad_w_router: float32 [2, 1536, 16], P('section', ('dp', 'expert'))
- grad_w_gate: float32 [2, 16, 1536, 512], P('section', 'expert', 'dp')
- grad_w_up: float32 [2, 16, 1536, 512], P('section', 'expert', 'dp')
- grad_w_down: float32 [2, 16, 512, 1536], P('section', 'expert', 'dp')
- balance_loss: float32 [2, 16], P('section')
Inputs may be any that keep to these rules, and one draw needn't show every extreme that they name: `routes`: each row names 8 different experts. In each aligned block of 96 rows (the rows of one micro-batch of one device in one layer) every expert is named, none by more than 64 rows, and some by exactly 64 rows. `segments`: ids never fall along a sequence; each document has 1 to 48 positions, and some has exactly 48.
All inputs are finite; a program needn't handle non-finite values.
Results may differ from a plain program's by a relative error of at most 0.025.
Values may be sent and summed in bfloat16 or wider, within the bound.
A program may use at most 256 MiB of HBM per device.

v0:
```python
import jax
import jax.numpy as jnp
from jax import lax
from jax.sharding import PartitionSpec as P

D = 1536
H = 24
KVH = 8
HD = 64
TOPK = 8
EXP_DEV = 4
MB = 2
SEQ = 96
CAP = 64


EPSILON = 1e-05
THETA = 10000.0
MASKED = -1e30


def passed_along(shard, axis, by):
    count = lax.axis_size(axis)
    pairs = [(i, i + by) for i in range(count) if 0 <= i + by < count]
    return lax.ppermute(shard, axis, pairs)


def in_blocks(shard, dim, count):
    lengths = shard.shape
    pieces = shard.reshape(*lengths[:dim], count, lengths[dim] // count, *lengths[dim + 1 :])
    return jnp.moveaxis(pieces, dim, 0)


def summed_on_arrival(shard, axis, dim):
    pieces = in_blocks(shard, dim, lax.axis_size(axis))
    arrived = lax.all_to_all(pieces, axis, split_axis=0, concat_axis=0, tiled=True)
    return arrived.astype(jnp.float32).sum(axis=0)


def sent_together(arrays, axis, dim, along):
    columns = [a.reshape(*a.shape[:along], -1) for a in arrays]
    both = jnp.concatenate(columns, axis=along)
    result, at, gathered = (summed_on_arrival(both, axis, dim), 0, [])
    for a, column in zip(arrays, columns):
        section = result[..., at : at + column.shape[along]]
        gathered.append(section.reshape(*section.shape[:along], *a.shape[along:]))
        at += column.shape[along]
    return tuple(gathered)


def matmul(left_side, right_side):
    return jnp.dot(left_side, right_side, preferred_element_type=jnp.float32)


def rotary_tables(length):
    half_width = HD // 2
    position = jnp.arange(length, dtype=jnp.float32)[:, None]
    freq_rate = THETA ** (-jnp.arange(half_width, dtype=jnp.float32) / half_width)
    angles = position * freq_rate[None, :]
    return (jnp.cos(angles)[:, None, :], jnp.sin(angles)[:, None, :])


def rotate(tensor, cosine_table, sine_table):
    half_width = HD // 2
    first_half = tensor[..., :half_width]
    second_half = tensor[..., half_width:]
    return jnp.concatenate(
        [
            first_half * cosine_table - second_half * sine_table,
            second_half * cosine_table + first_half * sine_table,
        ],
        axis=-1,
    )


def unrotate(gradient, cosine_table, sine_table):
    half_width = HD // 2
    first_half = gradient[..., :half_width]
    second_half = gradient[..., half_width:]
    return jnp.concatenate(
        [
            first_half * cosine_table + second_half * sine_table,
            second_half * cosine_table - first_half * sine_table,
        ],
        axis=-1,
    )


def norm_back(grad_normed, tensor, inverse, gain_vector):
    scaled = grad_normed * gain_vector
    grad_gain = jnp.sum(grad_normed * tensor * inverse, axis=0)
    grad_tensor = inverse * scaled - tensor * inverse**3 * jnp.mean(
        scaled * tensor, axis=-1, keepdims=True
    )
    return (grad_tensor, grad_gain)


def attention_scores(queries, key_rows, segment_row):
    length = queries.shape[0]
    grouped = queries.reshape(length, KVH, H // KVH, HD)
    scores = jnp.einsum(
        "qkgd,skd->kgqs", grouped, key_rows, preferred_element_type=jnp.float32
    ) * HD ** (-0.5)
    position = jnp.arange(length)
    allowed = (position[None, :] <= position[:, None]) & (
        segment_row[:, None] == segment_row[None, :]
    )
    return jnp.where(allowed[None, None], scores, MASKED)


def route_hot(route_rows, experts):
    return (route_rows[:, :, None] == jnp.arange(experts, dtype=jnp.int32)[None, None, :]).astype(
        jnp.float32
    )


def route_slots(route_rows, experts):
    flat_routes = route_rows.reshape(-1)
    one_hot = (flat_routes[:, None] == jnp.arange(experts, dtype=jnp.int32)[None, :]).astype(
        jnp.int32
    )
    before = jnp.cumsum(one_hot, axis=0) - one_hot
    rank_index = jnp.sum(before * one_hot, axis=1)
    return flat_routes * CAP + rank_index


def place_rows(token_rows, slot_index, experts):
    buffer = (
        jnp.zeros((experts * CAP, token_rows.shape[1]), token_rows.dtype)
        .at[slot_index]
        .set(token_rows)
    )
    return buffer.reshape(experts // EXP_DEV, EXP_DEV, CAP, token_rows.shape[1])


def forward_layer(inputs, weights, segment_row, route_rows):
    gain_attn, w_query, w_key, w_value, w_out, gain_moe, w_router, w_gate, w_up, w_down = weights
    length = inputs.shape[0]
    experts = w_router.shape[1]
    cosine_table, sine_table = rotary_tables(length)
    inverse_one = lax.rsqrt(jnp.mean(inputs * inputs, axis=-1, keepdims=True) + EPSILON)
    normed_one = (inputs * inverse_one * gain_attn).astype(jnp.bfloat16)
    queries = rotate(
        matmul(normed_one, w_query).reshape(length, H, HD), cosine_table, sine_table
    ).astype(jnp.bfloat16)
    key_rows = rotate(
        matmul(normed_one, w_key).reshape(length, KVH, HD), cosine_table, sine_table
    ).astype(jnp.bfloat16)
    values = matmul(normed_one, w_value).astype(jnp.bfloat16).reshape(length, KVH, HD)
    scores = attention_scores(queries, key_rows, segment_row)
    highest = jnp.max(scores, axis=-1, keepdims=True)
    exponent = jnp.exp(scores - highest)
    denominator = jnp.sum(exponent, axis=-1, keepdims=True)
    logsum = highest + jnp.log(denominator)
    weight_low = (exponent / denominator).astype(jnp.bfloat16)
    attended = jnp.einsum("kgqs,skd->qkgd", weight_low, values, preferred_element_type=jnp.float32)
    attended = attended.reshape(length, H * HD).astype(jnp.bfloat16)
    hidden = inputs + matmul(attended, w_out)
    inverse_two = lax.rsqrt(jnp.mean(hidden * hidden, axis=-1, keepdims=True) + EPSILON)
    normed_two = (hidden * inverse_two * gain_moe).astype(jnp.bfloat16)
    logits = matmul(normed_two, w_router)
    one_hot = route_hot(route_rows, experts)
    gate_weights = jax.nn.softmax(jnp.sum(one_hot * logits[:, None, :], axis=-1), axis=-1)
    probabilities = jnp.sum(jax.nn.softmax(logits, axis=-1), axis=0)
    slot_index = route_slots(route_rows, experts)
    outgoing = place_rows(jnp.repeat(normed_two, TOPK, axis=0), slot_index, experts)
    received = lax.all_to_all(outgoing, "expert", split_axis=0, concat_axis=0, tiled=True)
    gate_pre = jnp.einsum("secd,edf->secf", received, w_gate, preferred_element_type=jnp.float32)
    up_pre = jnp.einsum("secd,edf->secf", received, w_up, preferred_element_type=jnp.float32)
    active = (jax.nn.silu(gate_pre) * up_pre).astype(jnp.bfloat16)
    expert_out = jnp.einsum(
        "secf,efd->secd", active, w_down, preferred_element_type=jnp.float32
    ).astype(jnp.bfloat16)
    returned = lax.all_to_all(
        expert_out, "expert", split_axis=0, concat_axis=0, tiled=True
    ).reshape(experts * CAP, -1)
    picked = returned[slot_index].reshape(length, TOPK, -1)
    outputs = hidden + jnp.sum(gate_weights[:, :, None] * picked, axis=1)
    state = (
        inverse_one,
        queries,
        key_rows,
        values,
        logsum,
        attended,
        hidden,
        inverse_two,
        gate_weights,
        slot_index,
        received,
        gate_pre,
        up_pre,
        picked,
    )
    return (outputs, state, probabilities)


def backward_layer(grad_out, inputs, state, weights, segment_row, route_rows):
    gain_attn, w_query, w_key, w_value, w_out, gain_moe, w_router, w_gate, w_up, w_down = weights
    (
        inverse_one,
        queries,
        key_rows,
        values,
        logsum,
        attended,
        hidden,
        inverse_two,
        gate_weights,
        slot_index,
        received,
        gate_pre,
        up_pre,
        picked,
    ) = state
    length = inputs.shape[0]
    experts = w_router.shape[1]
    grad_rows = (
        (gate_weights[:, :, None] * grad_out[:, None, :])
        .astype(jnp.bfloat16)
        .reshape(length * TOPK, -1)
    )
    grad_gates = jnp.sum(picked * grad_out[:, None, :], axis=-1)
    grad_chosen = gate_weights * (
        grad_gates - jnp.sum(gate_weights * grad_gates, axis=-1, keepdims=True)
    )
    grad_logits = jnp.sum(grad_chosen[:, :, None] * route_hot(route_rows, experts), axis=1).astype(
        jnp.bfloat16
    )
    outgoing = place_rows(grad_rows, slot_index, experts)
    grad_expert_out = lax.all_to_all(outgoing, "expert", split_axis=0, concat_axis=0, tiled=True)
    sigmoid = jax.nn.sigmoid(gate_pre)
    silu_gate = gate_pre * sigmoid
    active = (silu_gate * up_pre).astype(jnp.bfloat16)
    grad_active = jnp.einsum(
        "secd,efd->secf", grad_expert_out, w_down, preferred_element_type=jnp.float32
    )
    grad_w_down = jnp.einsum(
        "secf,secd->efd", active, grad_expert_out, preferred_element_type=jnp.float32
    )
    grad_gate_pre = (grad_active * up_pre * sigmoid * (1.0 + gate_pre * (1.0 - sigmoid))).astype(
        jnp.bfloat16
    )
    grad_up_pre = (grad_active * silu_gate).astype(jnp.bfloat16)
    grad_w_gate = jnp.einsum(
        "secd,secf->edf", received, grad_gate_pre, preferred_element_type=jnp.float32
    )
    grad_w_up = jnp.einsum(
        "secd,secf->edf", received, grad_up_pre, preferred_element_type=jnp.float32
    )
    grad_route_in = (
        jnp.einsum("secf,edf->secd", grad_gate_pre, w_gate, preferred_element_type=jnp.float32)
        + jnp.einsum("secf,edf->secd", grad_up_pre, w_up, preferred_element_type=jnp.float32)
    ).astype(jnp.bfloat16)
    back_rows = lax.all_to_all(
        grad_route_in, "expert", split_axis=0, concat_axis=0, tiled=True
    ).reshape(experts * CAP, -1)
    normed_two = (hidden * inverse_two * gain_moe).astype(jnp.bfloat16)
    grad_normed_two = jnp.sum(
        back_rows[slot_index].reshape(length, TOPK, -1).astype(jnp.float32), axis=1
    )
    grad_normed_two = grad_normed_two + jnp.einsum(
        "te,de->td", grad_logits, w_router, preferred_element_type=jnp.float32
    )
    grad_w_router = jnp.einsum(
        "td,te->de", normed_two, grad_logits, preferred_element_type=jnp.float32
    )
    grad_norm_two, grad_gain_moe = norm_back(grad_normed_two, hidden, inverse_two, gain_moe)
    grad_hidden = grad_out + grad_norm_two
    grad_branch = grad_hidden.astype(jnp.bfloat16)
    grad_w_out = jnp.einsum("tc,td->cd", attended, grad_branch, preferred_element_type=jnp.float32)
    grad_attended = jnp.einsum("td,cd->tc", grad_branch, w_out, preferred_element_type=jnp.float32)
    grad_attended = grad_attended.astype(jnp.bfloat16).reshape(length, KVH, H // KVH, HD)
    weight = jnp.exp(attention_scores(queries, key_rows, segment_row) - logsum)
    grad_weight = jnp.einsum(
        "qkgd,skd->kgqs", grad_attended, values, preferred_element_type=jnp.float32
    )
    grad_values = jnp.einsum(
        "kgqs,qkgd->skd",
        weight.astype(jnp.bfloat16),
        grad_attended,
        preferred_element_type=jnp.float32,
    )
    grad_values = grad_values.astype(jnp.bfloat16).reshape(length, KVH * HD)
    grad_scores = (
        weight * (grad_weight - jnp.sum(weight * grad_weight, axis=-1, keepdims=True))
    ).astype(jnp.bfloat16)
    score_scale = HD ** (-0.5)
    grouped = queries.reshape(length, KVH, H // KVH, HD)
    grad_queries = jnp.einsum(
        "kgqs,skd->qkgd", grad_scores, key_rows, preferred_element_type=jnp.float32
    )
    grad_queries = grad_queries.reshape(length, H, HD) * score_scale
    grad_keys = (
        jnp.einsum("kgqs,qkgd->skd", grad_scores, grouped, preferred_element_type=jnp.float32)
        * score_scale
    )
    cosine_table, sine_table = rotary_tables(length)
    grad_query_pre = (
        unrotate(grad_queries, cosine_table, sine_table)
        .reshape(length, H * HD)
        .astype(jnp.bfloat16)
    )
    grad_key_pre = (
        unrotate(grad_keys, cosine_table, sine_table).reshape(length, KVH * HD).astype(jnp.bfloat16)
    )
    normed_one = (inputs * inverse_one * gain_attn).astype(jnp.bfloat16)
    grad_w_query = jnp.einsum(
        "tc,tq->cq", normed_one, grad_query_pre, preferred_element_type=jnp.float32
    )
    grad_w_key = jnp.einsum(
        "tc,tq->cq", normed_one, grad_key_pre, preferred_element_type=jnp.float32
    )
    grad_w_value = jnp.einsum(
        "tc,tq->cq", normed_one, grad_values, preferred_element_type=jnp.float32
    )
    grad_normed_one = (
        jnp.einsum("tq,cq->tc", grad_query_pre, w_query, preferred_element_type=jnp.float32)
        + jnp.einsum("tq,cq->tc", grad_key_pre, w_key, preferred_element_type=jnp.float32)
        + jnp.einsum("tq,cq->tc", grad_values, w_value, preferred_element_type=jnp.float32)
    )
    grad_norm_one, grad_gain_attn = norm_back(grad_normed_one, inputs, inverse_one, gain_attn)
    grad_inputs = grad_hidden + grad_norm_one
    return (
        grad_inputs,
        (
            grad_gain_attn,
            grad_w_query,
            grad_w_key,
            grad_w_value,
            grad_w_out,
            grad_gain_moe,
            grad_w_router,
            grad_w_gate,
            grad_w_up,
            grad_w_down,
        ),
    )


def body(
    tokens,
    cotangent,
    segments,
    routes,
    gain_attn,
    w_query,
    w_key,
    w_value,
    w_out,
    gain_moe,
    w_router,
    w_gate,
    w_up,
    w_down,
):
    weights = tuple(
        (
            weight_array[0]
            for weight_array in (
                gain_attn,
                w_query,
                w_key,
                w_value,
                w_out,
                gain_moe,
                w_router,
                w_gate,
                w_up,
                w_down,
            )
        )
    )
    section_index = lax.axis_index("section")
    route_all = routes[0]
    experts = w_router.shape[2]
    saved = []
    out_rows = jnp.zeros((MB, SEQ, D), jnp.bfloat16)
    arriving = jnp.zeros((SEQ, D), jnp.bfloat16)
    prob_total = jnp.zeros((experts,), jnp.float32)
    for tick_index in range(MB + 1):
        micro_index = jnp.clip(tick_index - section_index, 0, MB - 1)
        is_valid = (tick_index - section_index >= 0) & (tick_index - section_index < MB)
        own_start = min(tick_index, MB - 1) * SEQ
        own_rows = tokens[own_start : own_start + SEQ]
        inputs = jnp.where(section_index == 0, own_rows, arriving).astype(jnp.float32)
        segment_row = lax.dynamic_index_in_dim(segments, micro_index, 0, keepdims=False)
        route_rows = lax.dynamic_slice_in_dim(route_all, micro_index * SEQ, SEQ, 0)
        outputs, state, probabilities = forward_layer(inputs, weights, segment_row, route_rows)
        sent_rows = outputs.astype(jnp.bfloat16)
        out_rows = jnp.where(is_valid, out_rows.at[micro_index].set(sent_rows), out_rows)
        prob_total = prob_total + jnp.where(is_valid, probabilities, 0.0)
        saved.append((inputs, segment_row, route_rows, state))
        if tick_index < MB:
            arriving = passed_along(sent_rows, "section", 1)
    counts = jnp.sum(route_hot(route_all, experts), axis=(0, 1))
    count_all, prob_all = lax.psum((counts, prob_total), ("dp", "expert"))
    token_total = MB * SEQ * lax.axis_size("dp") * lax.axis_size("expert")
    balance_loss = experts * (count_all / (token_total * TOPK) * prob_all / token_total)
    in_grads = jnp.zeros((MB, SEQ, D), jnp.float32)
    arriving = jnp.zeros((SEQ, D), jnp.bfloat16)
    dense_totals = None
    expert_totals = None
    for turn_index in range(MB + 1):
        offset = MB - turn_index - section_index
        micro_index = jnp.clip(offset, 0, MB - 1)
        is_valid = (offset >= 0) & (offset < MB)
        inputs, segment_row, route_rows, state = saved[MB - turn_index]
        own_start = max(MB - 1 - turn_index, 0) * SEQ
        own_rows = cotangent[own_start : own_start + SEQ]
        incoming = jnp.where(section_index == 1, own_rows, arriving).astype(
            jnp.float32
        ) * is_valid.astype(jnp.float32)
        grad_inputs, layer_grads = backward_layer(
            incoming, inputs, state, weights, segment_row, route_rows
        )
        grad_sent = grad_inputs.astype(jnp.bfloat16)
        record = jnp.where(section_index == 0, grad_inputs, grad_sent.astype(jnp.float32))
        in_grads = jnp.where(is_valid, in_grads.at[micro_index].set(record), in_grads)
        if turn_index < MB:
            arriving = passed_along(grad_sent, "section", -1)
        dense_turn = tuple(layer_grads[:7])
        expert_turn = tuple(layer_grads[7:])
        if dense_totals is None:
            dense_totals = dense_turn
        else:
            dense_totals = jax.tree.map(jnp.add, dense_totals, dense_turn)
        if expert_totals is None:
            expert_totals = expert_turn
        else:
            expert_totals = jax.tree.map(jnp.add, expert_totals, expert_turn)
    dense_part = sent_together(
        (
            dense_totals[0].astype(jnp.bfloat16),
            dense_totals[1].astype(jnp.bfloat16),
            dense_totals[2].astype(jnp.bfloat16),
            dense_totals[3].astype(jnp.bfloat16),
            dense_totals[4].astype(jnp.bfloat16),
            dense_totals[5].astype(jnp.bfloat16),
            dense_totals[6].astype(jnp.bfloat16),
        ),
        ("dp", "expert"),
        0,
        1,
    )
    expert_part = (
        lax.psum_scatter(
            expert_totals[0].astype(jnp.bfloat16), "dp", scatter_dimension=1, tiled=True
        ).astype(jnp.float32),
        lax.psum_scatter(
            expert_totals[1].astype(jnp.bfloat16), "dp", scatter_dimension=1, tiled=True
        ).astype(jnp.float32),
        lax.psum_scatter(
            expert_totals[2].astype(jnp.bfloat16), "dp", scatter_dimension=1, tiled=True
        ).astype(jnp.float32),
    )
    grad_shards = tuple(dense_part) + tuple(expert_part)
    results = tuple((shard[None] for shard in grad_shards))
    return (
        (out_rows.reshape(MB * SEQ, D)[None], in_grads.reshape(MB * SEQ, D)[None])
        + results
        + (balance_loss[None],)
    )


def solution(mesh):
    return jax.shard_map(
        body,
        mesh=mesh,
        in_specs=(
            P(("dp", "expert"), None),
            P(("dp", "expert"), None),
            P(("dp", "expert"), None),
            P("section", ("dp", "expert"), None),
            P("section", None),
            P("section", None, None),
            P("section", None, None),
            P("section", None, None),
            P("section", None, None),
            P("section", None),
            P("section", None, None),
            P("section", "expert", None, None),
            P("section", "expert", None, None),
            P("section", "expert", None, None),
        ),
        out_specs=(
            P("section", ("dp", "expert"), None),
            P("section", ("dp", "expert"), None),
            P("section", ("dp", "expert")),
            P("section", ("dp", "expert"), None),
            P("section", ("dp", "expert"), None),
            P("section", ("dp", "expert"), None),
            P("section", ("dp", "expert"), None),
            P("section", ("dp", "expert")),
            P("section", ("dp", "expert"), None),
            P("section", "expert", "dp", None),
            P("section", "expert", "dp", None),
            P("section", "expert", "dp", None),
            P("section", None),
        ),
        check_vma=False,
    )
```

profile of v0, /device:TPU:0, one launch (start us, length us, event | category | flops | bytes accessed | tf_op | source)
XLA Modules:
  0.0 1716.5 jit_solution(15033721547080694941)
XLA Ops:
  13.3 6.7 copy.307
  40.0 8.5 scatter_custom_fusion
  48.5 77.5 %all_to_all.65 = bf16[4,4,64,1536]{3,2,1,0:T(8,128)(2,1)S(1)} all-to-all(bf16[4,4,64,1536]{3,2,1,0:T(8,128)(2,1)} %bitcast.804), channel_id=1, replica_groups=mesh['section'=2,'dp'=4,'expert'=4] {'expert'}, dimensions={0} | all-to-all | bytes 6291456 | tf_op jit(solution)/shard_map/all_to_all | solution.py:167
  126.0 5.8 fusion.39
  145.2 68.1 %all-to-all-done.1 = bf16[4,4,64,1536]{3,2,1,0:T(8,128)(2,1)} async-done(((bf16[4,4,64,1536]{3,2,1,0:T(8,128)(2,1)}), bf16[4,4,64,1536]{3,2,1,0:T(8,128)(2,1)}, u32[]{:S(2)}, u32[]{:S(2)}) %all-to-all-start.1) | async-done | bytes 3145760 | tf_op jit(solution)/shard_map/all_to_all | solution.py:174
  213.3 8.2 gather_fusion
  241.8 8.5 scatter_custom_fusion.1
  250.3 75.6 %all_to_all.66 = bf16[4,4,64,1536]{3,2,1,0:T(8,128)(2,1)S(1)} all-to-all(bf16[4,4,64,1536]{3,2,1,0:T(8,128)(2,1)} %bitcast.805), channel_id=1, replica_groups=mesh['section'=2,'dp'=4,'expert'=4] {'expert'}, dimensions={0} | all-to-all | bytes 6291456 | tf_op jit(solution)/shard_map/all_to_all | solution.py:167
  325.9 5.7 fusion.37
  355.9 57.8 %all-to-all-done.3 = bf16[4,4,64,1536]{3,2,1,0:T(8,128)(2,1)} async-done(((bf16[4,4,64,1536]{3,2,1,0:T(8,128)(2,1)}), bf16[4,4,64,1536]{3,2,1,0:T(8,128)(2,1)}, u32[]{:S(2)}, u32[]{:S(2)}) %all-to-all-start.3) | async-done | bytes 3145760 | tf_op jit(solution)/shard_map/all_to_all | solution.py:174
  413.7 8.3 gather_fusion.1
  454.1 8.4 scatter_custom_fusion.2
  475.0 9.5 scatter_custom_fusion.3
  484.4 52.7 %all-to-all-done.4 = bf16[4,4,64,1536]{3,2,1,0:T(8,128)(2,1)} async-done(((bf16[4,4,64,1536]{3,2,1,0:T(8,128)(2,1)}), bf16[4,4,64,1536]{3,2,1,0:T(8,128)(2,1)}, u32[]{:S(2)}, u32[]{:S(2)}) %all-to-all-start.4) | async-done | bytes 3145760 | tf_op jit(solution)/shard_map/all_to_all | solution.py:167
  541.8 6.9 fusion.23
  548.7 6.8 fusion.35
  555.5 56.5 %all-to-all-done.6 = bf16[4,4,64,1536]{3,2,1,0:T(8,128)(2,1)} async-done(((bf16[4,4,64,1536]{3,2,1,0:T(8,128)(2,1)}), bf16[4,4,64,1536]{3,2,1,0:T(8,128)(2,1)}, u32[]{:S(2)}, u32[]{:S(2)}) %all-to-all-start.6) | async-done | bytes 3145760 | tf_op jit(solution)/shard_map/all_to_all | solution.py:231
  612.0 8.6 fusion.173
  644.0 58.6 %all-to-all-done.5 = bf16[4,4,64,1536]{3,2,1,0:T(8,128)(2,1)} async-done(((bf16[4,4,64,1536]{3,2,1,0:T(8,128)(2,1)}), bf16[4,4,64,1536]{3,2,1,0:T(8,128)(2,1)}, u32[]{:S(2)}, u32[]{:S(2)}) %all-to-all-start.5) | async-done | bytes 3145760 | tf_op jit(solution)/shard_map/all_to_all | solution.py:174
  709.8 8.3 gather_fusion.2
  722.6 54.8 %all-to-all-done.7 = bf16[4,4,64,1536]{3,2,1,0:T(8,128)(2,1)} async-done(((bf16[4,4,64,1536]{3,2,1,0:T(8,128)(2,1)}), bf16[4,4,64,1536]{3,2,1,0:T(8,128)(2,1)}, u32[]{:S(2)}, u32[]{:S(2)}) %all-to-all-start.7) | async-done | bytes 3145760 | tf_op jit(solution)/shard_map/all_to_all | solution.py:255
  777.4 8.5 gather_fusion.3
  820.1 9.8 scatter_custom_fusion.4
  830.0 75.4 %all_to_all.67 = bf16[4,4,64,1536]{3,2,1,0:T(8,128)(2,1)S(1)} all-to-all(bf16[4,4,64,1536]{3,2,1,0:T(8,128)(2,1)} %bitcast.803), channel_id=1, replica_groups=mesh['section'=2,'dp'=4,'expert'=4] {'expert'}, dimensions={0} | all-to-all | bytes 6291456 | tf_op jit(solution)/shard_map/all_to_all | solution.py:231
  905.3 8.7 fusion.169
  937.4 64.5 %all-to-all-done.9 = bf16[4,4,64,1536]{3,2,1,0:T(8,128)(2,1)} async-done(((bf16[4,4,64,1536]{3,2,1,0:T(8,128)(2,1)}), bf16[4,4,64,1536]{3,2,1,0:T(8,128)(2,1)}, u32[]{:S(2)}, u32[]{:S(2)}) %all-to-all-start.9) | async-done | bytes 3145760 | tf_op jit(solution)/shard_map/all_to_all | solution.py:255
  1001.9 8.2 gather_fusion.4
  1037.8 12.3 scatter_custom_fusion.5
  1055.0 8.7 fusion.246
  1063.8 6.4 fusion.244
  1070.2 55.8 %all-to-all-done.10 = bf16[4,4,64,1536]{3,2,1,0:T(8,128)(2,1)} async-done(((bf16[4,4,64,1536]{3,2,1,0:T(8,128)(2,1)}), bf16[4,4,64,1536]{3,2,1,0:T(8,128)(2,1)}, u32[]{:S(2)}, u32[]{:S(2)}) %all-to-all-start.10) | async-done | bytes 3145760 | tf_op jit(solution)/shard_map/all_to_all | solution.py:231
  1125.9 8.4 fusion.165
  1134.3 14.0 fusion.2
  1149.1 9.2 fusion.241
  1168.9 6.3 fusion.308
  1175.4 6.7 fusion.239
  1200.9 9.0 convolution_add_fusion.3
  1217.0 14.1 fusion.1
  1231.2 33.1 %all-to-all-done.11 = bf16[4,4,64,1536]{3,2,1,0:T(8,128)(2,1)} async-done(((bf16[4,4,64,1536]{3,2,1,0:T(8,128)(2,1)}), bf16[4,4,64,1536]{3,2,1,0:T(8,128)(2,1)}, u32[]{:S(2)}, u32[]{:S(2)}) %all-to-all-start.11) | async-done | bytes 3145760 | tf_op jit(solution)/shard_map/all_to_all | solution.py:255
  1264.3 8.4 gather_fusion.5
  1301.6 7.6 fusion.3
  1312.7 24.1 %concatenate.115 = bf16[16,96,4114]{2,1,0:T(8,128)(2,1)} concatenate(bf16[16,96,1]{2,1,0:T(8,128)(2,1)} %convert_element_type.650, bf16[16,96,1536]{2,1,0:T(8,128)(2,1)} %bitcast.795, bf16[16,96,512]{2,1,0:T(8,128)(2,1)} %bitcast.806, bf16[16,96,512]{2,1,0:T(8,128)(2,1)} %bitcast.807, bf16[16,96,1536]{2,1,0:T(8,128)(2,1)} %bitcast.796, bf16[16,96,1]{2,1,0:T(8,128)(2,1)} %convert_element_type.651, ...), dimensions={2} | concatenate | bytes 25276416 | tf_op jit(solution)/shard_map/concatenate | solution.py:42
  1336.8 6.0 all-to-all-start.12
  1342.9 8.7 fusion.108
  1351.6 6.4 fusion.105
  1358.0 13.9 fusion
  1373.2 309.1 %all-reduce = (f32[16]{0:T(128)S(1)}, f32[16]{0:T(128)S(1)}) all-reduce(f32[16]{0:T(128)S(1)} %fusion.357, f32[16]{0:T(128)S(1)} %convert_reduce_fusion.4), channel_id=1, replica_groups=mesh['section'=2,'dp'=4,'expert'=4] {'dp','expert'}, use_global_device_ids=true, to_apply=%region_84.85 | all-reduce | flops 32 | bytes 256 | tf_op jit(solution)/shard_map/psum | solution.py:397
  1698.8 6.9 convert_reduce_fusion
  (714 shorter events, 347.3 us)
Async XLA Ops:
  8.8 135.4 %copy-start.127 = (s32[1,96,8]{1,2,0:T(8,128)}, s32[1,96,8]{1,2,0:T(8,128)S(1)}, u32[]{:S(2)}) copy-start(s32[1,96,8]{1,2,0:T(8,128)S(1)} %get-tuple-element.226) | copy-start | bytes 9220
  11.8 14.9 copy-start.151
  13.3 22.1 %copy-start.97 = (bf16[96,512]{0,1:T(8,128)(2,1)}, bf16[96,512]{0,1:T(8,128)(2,1)S(1)}, u32[]{:S(2)}) copy-start(bf16[96,512]{0,1:T(8,128)(2,1)S(1)} %copy.305) | copy-start | bytes 294916
  38.6 186.9 %copy-start.11 = (f32[96,1536]{1,0:T(8,128)}, f32[96,1536]{1,0:T(8,128)S(1)}, u32[]{:S(2)}) copy-start(f32[96,1536]{1,0:T(8,128)S(1)} %get-tuple-element.248) | copy-start | bytes 1769476
  39.9 103.6 %copy-start.32 = (bf16[96,1536]{1,0:T(8,128)(2,1)}, bf16[96,1536]{1,0:T(8,128)(2,1)S(1)}, u32[]{:S(2)}) copy-start(bf16[96,1536]{1,0:T(8,128)(2,1)S(1)} %multiply_convert_fusion.5) | copy-start | bytes 884740
  40.0 104.4 %copy-start.153 = (s32[768]{0:T(1024)}, s32[768]{0:T(1024)S(1)}, u32[]{:S(2)}) copy-start(s32[768]{0:T(1024)S(1)} %get-tuple-element.279) | copy-start | bytes 9220
  40.0 201.8 %copy-start.154 = (s32[768]{0:T(1024)}, s32[768]{0:T(1024)S(1)}, u32[]{:S(2)}) copy-start(s32[768]{0:T(1024)S(1)} %get-tuple-element.280) | copy-start | bytes 9220
  48.5 83.2 %slice-start.12 = ((s8[6291456]{0:T(1024)(128)(4,1)}), s8[4194304]{0:T(1024)(128)(4,1)S(1)}, s32[]{:S(2)}) async-start(s8[6291456]{0:T(1024)(128)(4,1)} %bitcast.779), calls=%async_computation.31 | async-start | bytes 8388608
  138.7 74.7 %all-to-all-start.1 = ((bf16[4,4,64,1536]{3,2,1,0:T(8,128)(2,1)}), bf16[4,4,64,1536]{3,2,1,0:T(8,128)(2,1)}, u32[]{:S(2)}, u32[]{:S(2)}) async-start(bf16[4,4,64,1536]{3,2,1,0:T(8,128)(2,1)} %copy.316), calls=%async_computation.1 | async-start | bytes 6291456 | tf_op jit(solution)/shard_map/all_to_all | solution.py:174
  144.2 77.4 %copy-start.117 = (f32[96,16]{0,1:T(8,128)}, f32[96,16]{0,1:T(8,128)S(1)}, u32[]{:S(2)}) copy-start(f32[96,16]{0,1:T(8,128)S(1)} %get-tuple-element.274) | copy-start | bytes 18436
  144.2 77.4 %copy-start.112 = (f32[96,8]{0,1:T(8,128)}, f32[96,8]{0,1:T(8,128)S(1)}, u32[]{:S(2)}) copy-start(f32[96,8]{0,1:T(8,128)S(1)} %select_reduce_fusion.5) | copy-start | bytes 9220
  144.2 77.4 %copy-start.156 = (f32[96]{0:T(128)}, f32[96]{0:T(128)S(1)}, u32[]{:S(2)}) copy-start(f32[96]{0:T(128)S(1)} %reduce_max.82) | copy-start | bytes 1156
  144.3 77.3 %copy-start.161 = (f32[96]{0:T(128)}, f32[96]{0:T(128)S(1)}, u32[]{:S(2)}) copy-start(f32[96]{0:T(128)S(1)} %fusion.341) | copy-start | bytes 1156
  144.4 77.2 %copy-start.101 = (f32[96,8]{1,0:T(8,128)}, f32[96,8]{1,0:T(8,128)S(1)}, u32[]{:S(2)}) copy-start(f32[96,8]{1,0:T(8,128)S(1)} %copy.309) | copy-start | bytes 9220
  144.4 77.2 %copy-start.141 = (s32[1024]{0:T(1024)}, s32[1024]{0:T(1024)S(1)}, u32[]{:S(2)}) copy-start(s32[1024]{0:T(1024)S(1)} %pad_clamp_fusion.2) | copy-start | bytes 12292
  226.1 2.5 collective-permute-start
  241.4 84.5 %copy-start.168 = (f32[96]{0:T(128)}, f32[96]{0:T(128)S(1)}, u32[]{:S(2)}) copy-start(f32[96]{0:T(128)S(1)} %get-tuple-element.237) | copy-start | bytes 1156
  241.8 110.9 %copy-start.34 = (bf16[96,1536]{1,0:T(8,128)(2,1)}, bf16[96,1536]{1,0:T(8,128)(2,1)S(1)}, u32[]{:S(2)}) copy-start(bf16[96,1536]{1,0:T(8,128)(2,1)S(1)} %multiply_convert_fusion.4) | copy-start | bytes 884740
  250.3 81.4 %slice-start.14 = ((s8[6291456]{0:T(1024)(128)(4,1)}), s8[4194304]{0:T(1024)(128)(4,1)S(1)}, s32[]{:S(2)}) async-start(s8[6291456]{0:T(1024)(128)(4,1)} %bitcast.781), calls=%async_computation.33 | async-start | bytes 8388608
  338.7 75.1 %all-to-all-start.3 = ((bf16[4,4,64,1536]{3,2,1,0:T(8,128)(2,1)}), bf16[4,4,64,1536]{3,2,1,0:T(8,128)(2,1)}, u32[]{:S(2)}, u32[]{:S(2)}) async-start(bf16[4,4,64,1536]{3,2,1,0:T(8,128)(2,1)} %copy.326), calls=%async_computation.3 | async-start | bytes 6291456 | tf_op jit(solution)/shard_map/all_to_all | solution.py:174
  355.9 66.1 %copy-start.103 = (f32[96,8]{1,0:T(8,128)}, f32[96,8]{1,0:T(8,128)S(1)}, u32[]{:S(2)}) copy-start(f32[96,8]{1,0:T(8,128)S(1)} %copy.319) | copy-start | bytes 9220
  427.5 5.9 collective-permute-start.1
  433.4 20.7 %copy-start.155 = (s32[768]{0:T(1024)}, s32[768]{0:T(1024)S(1)}, u32[]{:S(2)}) copy-start(s32[768]{0:T(1024)S(1)} %fusion.348) | copy-start | bytes 9220
  462.4 74.7 %all-to-all-start.4 = ((bf16[4,4,64,1536]{3,2,1,0:T(8,128)(2,1)}), bf16[4,4,64,1536]{3,2,1,0:T(8,128)(2,1)}, u32[]{:S(2)}, u32[]{:S(2)}) async-start(bf16[4,4,64,1536]{3,2,1,0:T(8,128)(2,1)} %bitcast.800), calls=%async_computation.4 | async-start | bytes 6291456 | tf_op jit(solution)/shard_map/all_to_all | solution.py:167
  537.1 74.9 %all-to-all-start.6 = ((bf16[4,4,64,1536]{3,2,1,0:T(8,128)(2,1)}), bf16[4,4,64,1536]{3,2,1,0:T(8,128)(2,1)}, u32[]{:S(2)}, u32[]{:S(2)}) async-start(bf16[4,4,64,1536]{3,2,1,0:T(8,128)(2,1)} %bitcast.802), calls=%async_computation.6 | async-start | bytes 6291456 | tf_op jit(solution)/shard_map/all_to_all | solution.py:231
  627.5 75.1 %all-to-all-start.5 = ((bf16[4,4,64,1536]{3,2,1,0:T(8,128)(2,1)}), bf16[4,4,64,1536]{3,2,1,0:T(8,128)(2,1)}, u32[]{:S(2)}, u32[]{:S(2)}) async-start(bf16[4,4,64,1536]{3,2,1,0:T(8,128)(2,1)} %copy.336), calls=%async_computation.5 | async-start | bytes 6291456 | tf_op jit(solution)/shard_map/all_to_all | solution.py:174
  702.5 74.9 %all-to-all-start.7 = ((bf16[4,4,64,1536]{3,2,1,0:T(8,128)(2,1)}), bf16[4,4,64,1536]{3,2,1,0:T(8,128)(2,1)}, u32[]{:S(2)}, u32[]{:S(2)}) async-start(bf16[4,4,64,1536]{3,2,1,0:T(8,128)(2,1)} %copy.339), calls=%async_computation.7 | async-start | bytes 6291456 | tf_op jit(solution)/shard_map/all_to_all | solution.py:255
  777.4 12.6 copy-start.106
  814.3 3.8 collective-permute-start.2
  829.9 84.1 %slice-start.16 = ((s8[6291456]{0:T(1024)(128)(4,1)}), s8[4194304]{0:T(1024)(128)(4,1)S(1)}, s32[]{:S(2)}) async-start(s8[6291456]{0:T(1024)(128)(4,1)} %bitcast.783), calls=%async_computation.35 | async-start | bytes 8388608
  829.9 89.8 %slice-start.20 = ((s8[6291456]{0:T(1024)(128)(4,1)}), s8[4194304]{0:T(1024)(128)(4,1)S(1)}, s32[]{:S(2)}) async-start(s8[6291456]{0:T(1024)(128)(4,1)} %bitcast.787), calls=%async_computation.39 | async-start | bytes 8388608
  905.3 14.4 slice-start.21
  926.7 75.2 %copy-start.143 = (s32[1024]{0:T(1024)S(1)}, s32[1024]{0:T(1024)}, u32[]{:S(2)}) copy-start(s32[1024]{0:T(1024)} %pad_clamp_fusion.1) | copy-start | bytes 12292
  926.7 75.2 %all-to-all-start.9 = ((bf16[4,4,64,1536]{3,2,1,0:T(8,128)(2,1)}), bf16[4,4,64,1536]{3,2,1,0:T(8,128)(2,1)}, u32[]{:S(2)}, u32[]{:S(2)}) async-start(bf16[4,4,64,1536]{3,2,1,0:T(8,128)(2,1)} %copy.348), calls=%async_computation.9 | async-start | bytes 6291456 | tf_op jit(solution)/shard_map/all_to_all | solution.py:255
  937.4 76.1 %copy-start.139 = (bf16[96,16]{0,1:T(8,128)(2,1)}, bf16[96,16]{0,1:T(8,128)(2,1)S(1)}, u32[]{:S(2)}) copy-start(bf16[96,16]{0,1:T(8,128)(2,1)S(1)} %select_reduce_fusion.1) | copy-start | bytes 9220
  1032.8 3.8 collective-permute-start.3
  1050.0 75.9 %all-to-all-start.10 = ((bf16[4,4,64,1536]{3,2,1,0:T(8,128)(2,1)}), bf16[4,4,64,1536]{3,2,1,0:T(8,128)(2,1)}, u32[]{:S(2)}, u32[]{:S(2)}) async-start(bf16[4,4,64,1536]{3,2,1,0:T(8,128)(2,1)} %bitcast.801), calls=%async_computation.10 | async-start | bytes 6291456 | tf_op jit(solution)/shard_map/all_to_all | solution.py:231
  1054.7 633.6 %reduce-scatter.4.cloned.1.call-start = ((), (), s32[]{:S(2)}) async-start(), calls=%async_computation.16 | async-start | bytes 7864320 | tf_op jit(solution)/shard_map/reduce_scatter | solution.py:447
  1168.8 13.3 slice-start.18
  1168.9 15.1 slice-start.22
  1189.0 75.2 %all-to-all-start.11 = ((bf16[4,4,64,1536]{3,2,1,0:T(8,128)(2,1)}), bf16[4,4,64,1536]{3,2,1,0:T(8,128)(2,1)}, u32[]{:S(2)}, u32[]{:S(2)}) async-start(bf16[4,4,64,1536]{3,2,1,0:T(8,128)(2,1)} %copy.357), calls=%async_computation.11 | async-start | bytes 6291456 | tf_op jit(solution)/shard_map/all_to_all | solution.py:255
  1193.9 498.0 %reduce-scatter.6.cloned.1.call-start = ((), (), s32[]{:S(2)}) async-start(), calls=%async_computation.17 | async-start | bytes 7864320 | tf_op jit(solution)/shard_map/reduce_scatter | solution.py:450
  1231.1 33.1 %copy-start.142 = (s32[1024]{0:T(1024)S(1)}, s32[1024]{0:T(1024)}, u32[]{:S(2)}) copy-start(s32[1024]{0:T(1024)} %copy-done.141) | copy-start | bytes 12292
  1293.6 15.6 slice-start.27
  1336.8 362.0 %all-to-all-start.12 = ((bf16[16,96,4114]{2,1,0:T(8,128)(2,1)}), bf16[16,96,4114]{2,1,0:T(8,128)(2,1)}, u32[]{:S(2)}, u32[]{:S(2)}) async-start(bf16[16,96,4114]{2,1,0:T(8,128)(2,1)} %concatenate.115), calls=%async_computation.12 | async-start | bytes 25952256 | tf_op jit(solution)/shard_map/all_to_all | solution.py:36
  1342.8 352.5 %reduce-scatter.8.cloned.1.call-start = ((), (), s32[]{:S(2)}) async-start(), calls=%async_computation.18 | async-start | bytes 7864320 | tf_op jit(solution)/shard_map/reduce_scatter | solution.py:453
  1371.9 310.9 %copy-start.14 = (f32[96,1536]{1,0:T(8,128)S(1)}, f32[96,1536]{1,0:T(8,128)}, u32[]{:S(2)}) copy-start(f32[96,1536]{1,0:T(8,128)} %copy-done.13) | copy-start | bytes 1769476
  1371.9 313.5 %copy-start.175 = (f32[96]{0:T(128)S(1)}, f32[96]{0:T(128)}, u32[]{:S(2)}) copy-start(f32[96]{0:T(128)} %get-tuple-element.230) | copy-start | bytes 1156
  (182 other events, 736.5 us)
Sparse Core Ops, SparseCore 0:
  1148.4 69.3 reduce-scatter.3
  1231.3 72.0 reduce-scatter.5
  1372.1 188.5 reduce-scatter.7
where the time goes:
time: 1730 us; the launch traced here: 1720 us
  blocking collectives  537 us (31%)
  waiting for transfers between devices  506 us (29%)
  matrix products  305 us (18%)
  local copies, waits for them, and re-layouts  162 us (9%)
  other arithmetic  133 us (8%)
  starting transfers between devices  56.3 us (3%)
    psum x1, blocking collectives, body(): count_all, prob_all = lax.psum((counts, prob_total), ('dp', 'expert'))  309 us
    all_to_all x3, waiting for transfers between devices, forward_layer(): lax.all_to_all(expert_out, 'expert', split_axis=0, concat_axis=0, tiled=T...  185 us
    all_to_all x2, blocking collectives, forward_layer(): lax.all_to_all(outgoing, 'expert', split_axis=0, concat_axis=0, tiled=True)  153 us
    all_to_all x3, waiting for transfers between devices, backward_layer(): lax.all_to_all(grad_route_in, 'expert', split_axis=0, concat_axis=0, tile...  152 us
    all_to_all x2, waiting for transfers between devices, backward_layer(): lax.all_to_all(outgoing, 'expert', split_axis=0, concat_axis=0, tiled=True)  112 us
    all_to_all x1, blocking collectives, backward_layer(): lax.all_to_all(outgoing, 'expert', split_axis=0, concat_axis=0, tiled=True)  75.4 us
    all_to_all x1, waiting for transfers between devices, forward_layer(): lax.all_to_all(outgoing, 'expert', split_axis=0, concat_axis=0, tiled=True)  52.7 us
  transfers between devices with their start and end apart: 17, of which 12 were waited for; matrix products, arithmetic and copies ran while one was open for 17% of the time, Pallas kernels for 0%

commit v1 on v0

v1 whole, which is shorter than its diff:
```python
import jax
import jax.numpy as jnp
from jax import lax
from jax.sharding import PartitionSpec as P

D = 1536
H = 24
KVH = 8
HD = 64
TOPK = 8
SEQ = 96


EPSILON = 1e-05
THETA = 10000.0
MASKED = -1e30


def matmul(left_side, right_side):
    return jnp.dot(left_side, right_side, preferred_element_type=jnp.float32)


def rotary_tables(length):
    half_width = HD // 2
    position = jnp.arange(length, dtype=jnp.float32)[:, None]
    freq_rate = THETA ** (-jnp.arange(half_width, dtype=jnp.float32) / half_width)
    angles = position * freq_rate[None, :]
    return (jnp.cos(angles)[:, None, :], jnp.sin(angles)[:, None, :])


def rotate(tensor, cosine_table, sine_table):
    half_width = HD // 2
    first_half = tensor[..., :half_width]
    second_half = tensor[..., half_width:]
    return jnp.concatenate(
        [
            first_half * cosine_table - second_half * sine_table,
            second_half * cosine_table + first_half * sine_table,
        ],
        axis=-1,
    )


def unrotate(gradient, cosine_table, sine_table):
    half_width = HD // 2
    first_half = gradient[..., :half_width]
    second_half = gradient[..., half_width:]
    return jnp.concatenate(
        [
            first_half * cosine_table + second_half * sine_table,
            second_half * cosine_table - first_half * sine_table,
        ],
        axis=-1,
    )


def norm_back(grad_normed, tensor, inverse, gain_vector):
    scaled = grad_normed * gain_vector
    grad_gain = jnp.sum(grad_normed * tensor * inverse, axis=0)
    grad_tensor = inverse * scaled - tensor * inverse**3 * jnp.mean(
        scaled * tensor, axis=-1, keepdims=True
    )
    return (grad_tensor, grad_gain)


def attention_scores(queries, key_rows, segment_row):
    length = queries.shape[0]
    grouped = queries.reshape(length, KVH, H // KVH, HD)
    scores = jnp.einsum(
        "qkgd,skd->kgqs", grouped, key_rows, preferred_element_type=jnp.float32
    ) * HD ** (-0.5)
    position = jnp.arange(length)
    allowed = (position[None, :] <= position[:, None]) & (
        segment_row[:, None] == segment_row[None, :]
    )
    return jnp.where(allowed[None, None], scores, MASKED)


def masked_softmax(logits, mask):
    highest = jnp.max(jnp.where(mask > 0, logits, MASKED), axis=-1, keepdims=True)
    exponent = jnp.where(mask > 0, jnp.exp(logits - highest), 0.0)
    return exponent / jnp.sum(exponent, axis=-1, keepdims=True)


def multi_hot(route_rows, experts):
    columns = jnp.arange(experts, dtype=jnp.int32)
    return jnp.sum(
        (route_rows[..., None] == columns).astype(jnp.float32), axis=-2
    )


def swapped(array):
    return lax.ppermute(array, "section", [(0, 1), (1, 0)])


def halved_over(arrays, axis, bit):
    count = lax.axis_size(axis)
    mine = (lax.axis_index(axis) >> bit) & 1
    pairs = [(i, i ^ (1 << bit)) for i in range(count)]
    results = []
    for array in arrays:
        keep = lax.dynamic_index_in_dim(array, mine, 0, keepdims=False)
        send = lax.dynamic_index_in_dim(array, 1 - mine, 0, keepdims=False)
        got = lax.ppermute(send, axis, pairs)
        results.append((keep.astype(jnp.float32) + got.astype(jnp.float32)).astype(jnp.bfloat16))
    return results


def scattered(array, steps):
    bits = len(steps)
    shape = array.shape[1:]
    array = array.reshape((2,) * bits + shape)
    left = sorted((place for _, _, place in steps))
    for axis, bit, place in steps:
        at = left.index(place)
        (array,) = halved_over([jnp.moveaxis(array, at, 0)], axis, bit)
        left.remove(place)
    return array.astype(jnp.float32)


def bits_of(count):
    return count.bit_length() - 1


def orders(axes):
    steps, place = [], 0
    per_axis = []
    for axis in axes:
        count = bits_of(lax.axis_size(axis))
        own = []
        for bit in range(count - 1, -1, -1):
            own.append((axis, bit, place))
            place += 1
        per_axis.append(own)
    first = [s for own in per_axis for s in own]
    second = [s for own in per_axis for s in reversed(own)]
    return second, first


def attention_forward(inputs, weights, segment_row):
    gain_attn, w_query, w_key, w_value, w_out, gain_moe = weights[:6]
    length = inputs.shape[0]
    cosine_table, sine_table = rotary_tables(length)
    inverse_one = lax.rsqrt(jnp.mean(inputs * inputs, axis=-1, keepdims=True) + EPSILON)
    normed_one = (inputs * inverse_one * gain_attn).astype(jnp.bfloat16)
    queries = rotate(
        matmul(normed_one, w_query).reshape(length, H, HD), cosine_table, sine_table
    ).astype(jnp.bfloat16)
    key_rows = rotate(
        matmul(normed_one, w_key).reshape(length, KVH, HD), cosine_table, sine_table
    ).astype(jnp.bfloat16)
    values = matmul(normed_one, w_value).astype(jnp.bfloat16).reshape(length, KVH, HD)
    scores = attention_scores(queries, key_rows, segment_row)
    highest = jnp.max(scores, axis=-1, keepdims=True)
    exponent = jnp.exp(scores - highest)
    denominator = jnp.sum(exponent, axis=-1, keepdims=True)
    weight = exponent / denominator
    attended = jnp.einsum(
        "kgqs,skd->qkgd", weight.astype(jnp.bfloat16), values, preferred_element_type=jnp.float32
    )
    attended = attended.reshape(length, H * HD).astype(jnp.bfloat16)
    hidden = inputs + matmul(attended, w_out)
    inverse_two = lax.rsqrt(jnp.mean(hidden * hidden, axis=-1, keepdims=True) + EPSILON)
    normed_two = (hidden * inverse_two * gain_moe).astype(jnp.bfloat16)
    state = (inverse_one, normed_one, queries, key_rows, values, weight, attended, hidden, inverse_two, normed_two)
    return state


def experts_forward(rows, mask, weights):
    w_router, w_gate, w_up, w_down = weights[6:]
    held = w_gate.shape[0]
    gates = masked_softmax(matmul(rows, w_router), mask)
    local = lax.dynamic_slice_in_dim(gates, lax.axis_index("expert") * held, held, 1)
    local = local.T[:, :, None]
    gate_pre = jnp.einsum("td,edf->etf", rows, w_gate, preferred_element_type=jnp.float32)
    up_pre = jnp.einsum("td,edf->etf", rows, w_up, preferred_element_type=jnp.float32)
    gated = (local * (jax.nn.silu(gate_pre) * up_pre)).astype(jnp.bfloat16)
    partial = jnp.einsum("etf,efd->td", gated, w_down, preferred_element_type=jnp.float32)
    return partial.astype(jnp.bfloat16), (rows, local, gate_pre, up_pre, gated)


def experts_backward(grad_rows, state, weights):
    w_router, w_gate, w_up, w_down = weights[6:]
    rows, local, gate_pre, up_pre, gated = state
    experts = w_router.shape[1]
    held = w_gate.shape[0]
    raw = jnp.einsum("td,efd->etf", grad_rows, w_down, preferred_element_type=jnp.float32)
    sigmoid = jax.nn.sigmoid(gate_pre)
    silu_gate = gate_pre * sigmoid
    grad_gates = jnp.sum(raw * (silu_gate * up_pre), axis=-1).T
    grad_gates = lax.dynamic_update_slice_in_dim(
        jnp.zeros((grad_gates.shape[0], experts), jnp.float32),
        grad_gates,
        lax.axis_index("expert") * held,
        1,
    )
    grad_active = local * raw
    grad_gate_pre = (grad_active * up_pre * sigmoid * (1.0 + gate_pre * (1.0 - sigmoid))).astype(
        jnp.bfloat16
    )
    grad_up_pre = (grad_active * silu_gate).astype(jnp.bfloat16)
    partial = jnp.einsum(
        "etf,edf->td", grad_gate_pre, w_gate, preferred_element_type=jnp.float32
    ) + jnp.einsum("etf,edf->td", grad_up_pre, w_up, preferred_element_type=jnp.float32)
    return partial.astype(jnp.bfloat16), grad_gates, grad_gate_pre, grad_up_pre


def attention_backward(grad_hidden, inputs, state, weights):
    gain_attn, w_query, w_key, w_value, w_out, gain_moe = weights[:6]
    (inverse_one, normed_one, queries, key_rows, values, weight, attended, hidden, inverse_two, normed_two) = state
    length = inputs.shape[0]
    grad_branch = grad_hidden.astype(jnp.bfloat16)
    grad_attended = jnp.einsum("td,cd->tc", grad_branch, w_out, preferred_element_type=jnp.float32)
    grad_attended = grad_attended.astype(jnp.bfloat16).reshape(length, KVH, H // KVH, HD)
    grad_weight = jnp.einsum(
        "qkgd,skd->kgqs", grad_attended, values, preferred_element_type=jnp.float32
    )
    grad_values = jnp.einsum(
        "kgqs,qkgd->skd",
        weight.astype(jnp.bfloat16),
        grad_attended,
        preferred_element_type=jnp.float32,
    )
    grad_values = grad_values.astype(jnp.bfloat16).reshape(length, KVH * HD)
    grad_scores = (
        weight * (grad_weight - jnp.sum(weight * grad_weight, axis=-1, keepdims=True))
    ).astype(jnp.bfloat16)
    score_scale = HD ** (-0.5)
    grouped = queries.reshape(length, KVH, H // KVH, HD)
    grad_queries = jnp.einsum(
        "kgqs,skd->qkgd", grad_scores, key_rows, preferred_element_type=jnp.float32
    )
    grad_queries = grad_queries.reshape(length, H, HD) * score_scale
    grad_keys = (
        jnp.einsum("kgqs,qkgd->skd", grad_scores, grouped, preferred_element_type=jnp.float32)
        * score_scale
    )
    cosine_table, sine_table = rotary_tables(length)
    grad_query_pre = (
        unrotate(grad_queries, cosine_table, sine_table)
        .reshape(length, H * HD)
        .astype(jnp.bfloat16)
    )
    grad_key_pre = (
        unrotate(grad_keys, cosine_table, sine_table).reshape(length, KVH * HD).astype(jnp.bfloat16)
    )
    grad_normed_one = (
        jnp.einsum("tq,cq->tc", grad_query_pre, w_query, preferred_element_type=jnp.float32)
        + jnp.einsum("tq,cq->tc", grad_key_pre, w_key, preferred_element_type=jnp.float32)
        + jnp.einsum("tq,cq->tc", grad_values, w_value, preferred_element_type=jnp.float32)
    )
    grad_norm_one, grad_gain_attn = norm_back(grad_normed_one, inputs, inverse_one, gain_attn)
    grad_inputs = grad_hidden + grad_norm_one
    grad_qkv = jnp.concatenate([grad_query_pre, grad_key_pre, grad_values], axis=1)
    return grad_inputs, grad_gain_attn, grad_qkv, grad_branch


def gather_rows(rows):
    return lax.all_gather(rows, "expert", axis=0, tiled=True)


def sum_rows(partial):
    return lax.psum_scatter(
        partial, "expert", scatter_dimension=0, tiled=True
    ).astype(jnp.float32)


def turned(left, right):
    return jnp.einsum("tc,tq->cq", left, right, preferred_element_type=jnp.float32)


def body(tokens, cotangent, segments, routes, *weight_arrays):
    core = lax.axis_index("section")
    first = core == 0
    experts = weight_arrays[6].shape[2]
    held = weight_arrays[7].shape[1]
    own = [array[0] for array in weight_arrays]
    other = [swapped(array) for array in own]
    weights = [
        [jnp.where(first, a, b) for a, b in zip(own, other)],
        [jnp.where(first, b, a) for a, b in zip(own, other)],
    ]
    inputs_low = lax.dynamic_slice_in_dim(tokens, core * SEQ, SEQ, 0)
    grad_low = lax.dynamic_slice_in_dim(cotangent, core * SEQ, SEQ, 0)
    segment_row = lax.dynamic_index_in_dim(segments, core, 0, keepdims=False)
    mine = lax.dynamic_slice_in_dim(routes[0], core * SEQ, SEQ, 0)
    got = swapped(lax.dynamic_slice_in_dim(routes[0], (1 - core) * SEQ, SEQ, 0))
    routes_here = jnp.stack([jnp.where(first, mine, got), jnp.where(first, got, mine)])
    routes_all = lax.all_gather(routes_here, "expert", axis=1, tiled=True)
    masks_here = multi_hot(routes_here, experts)
    masks_all = multi_hot(routes_all, experts)

    saved, outs, probabilities = [], [], []
    for s in range(2):
        inputs = inputs_low.astype(jnp.float32)
        state = attention_forward(inputs, weights[s], segment_row)
        hidden, normed_two = state[7], state[9]
        logits = matmul(normed_two, weights[s][6])
        gates = masked_softmax(logits, masks_here[s])
        probabilities.append(jnp.sum(jax.nn.softmax(logits, axis=-1), axis=0))
        partial, expert_state = experts_forward(gather_rows(normed_two), masks_all[s], weights[s])
        inputs_low = (hidden + sum_rows(partial)).astype(jnp.bfloat16)
        outs.append(inputs_low)
        saved.append((inputs, state, gates, expert_state))

    counts = jnp.sum(masks_here, axis=1)
    axes = ("section", "dp", "expert")
    count_all, prob_all = lax.psum((counts, jnp.stack(probabilities)), axes)
    token_total = SEQ * lax.axis_size(axes)
    balance = experts * (count_all / (token_total * TOPK) * prob_all / token_total)
    balance = lax.dynamic_index_in_dim(balance, core, 0)

    grads = [None, None]
    input_grads = [None, None]
    for s in (1, 0):
        inputs, state, gates, expert_state = saved[s]
        (inverse_one, normed_one, _, _, _, _, attended, hidden, inverse_two, normed_two) = state
        gain_moe, w_router = weights[s][5], weights[s][6]
        grad_all = gather_rows(grad_low)
        partial, grad_gates, grad_gate_pre, grad_up_pre = experts_backward(
            grad_all, expert_state, weights[s]
        )
        grad_gates = lax.psum_scatter(grad_gates, "expert", scatter_dimension=0, tiled=True)
        grad_chosen = gates * (grad_gates - jnp.sum(gates * grad_gates, axis=-1, keepdims=True))
        grad_logits = grad_chosen.astype(jnp.bfloat16)
        grad_normed_two = sum_rows(partial) + jnp.einsum(
            "te,de->td", grad_logits, w_router, preferred_element_type=jnp.float32
        )
        grad_norm_two, grad_gain_moe = norm_back(grad_normed_two, hidden, inverse_two, gain_moe)
        grad_hidden = grad_low.astype(jnp.float32) + grad_norm_two
        half = held // 2
        stacked = jnp.stack([expert_state[4], grad_gate_pre, grad_up_pre])
        keep = lax.dynamic_slice_in_dim(stacked, core * half, half, 1)
        send = lax.dynamic_slice_in_dim(stacked, (1 - core) * half, half, 1)
        arrived = swapped(send)
        both = jnp.concatenate([keep, arrived], axis=2)
        rows_both = jnp.concatenate([expert_state[0], swapped(expert_state[0])], axis=0)
        grad_both = jnp.concatenate([grad_all, swapped(grad_all)], axis=0)
        w_down_grad = jnp.einsum(
            "etf,td->efd", both[0], grad_both, preferred_element_type=jnp.float32
        ).astype(jnp.bfloat16)
        w_gate_grad = jnp.einsum(
            "td,etf->edf", rows_both, both[1], preferred_element_type=jnp.float32
        ).astype(jnp.bfloat16)
        w_up_grad = jnp.einsum(
            "td,etf->edf", rows_both, both[2], preferred_element_type=jnp.float32
        ).astype(jnp.bfloat16)

        grad_inputs, grad_gain_attn, grad_qkv, grad_branch = attention_backward(
            grad_hidden, inputs, state, weights[s]
        )
        def halves(array):
            width = array.shape[1] // 2
            return (
                lax.dynamic_slice_in_dim(array, core * width, width, 1),
                lax.dynamic_slice_in_dim(array, (1 - core) * width, width, 1),
            )
        qkv_keep, qkv_send = halves(grad_qkv)
        branch_keep, branch_send = halves(grad_branch)
        packed = swapped(jnp.concatenate([normed_one, attended, qkv_send, branch_send], axis=1))
        normed_got, attended_got = packed[:, :D], packed[:, D : 2 * D]
        qkv_got = packed[:, 2 * D : 2 * D + qkv_send.shape[1]]
        branch_got = packed[:, 2 * D + qkv_send.shape[1] :]
        grad_w_qkv = turned(
            jnp.concatenate([normed_one, normed_got]), jnp.concatenate([qkv_keep, qkv_got])
        ).astype(jnp.bfloat16)
        grad_w_out = turned(
            jnp.concatenate([attended, attended_got]), jnp.concatenate([branch_keep, branch_got])
        ).astype(jnp.bfloat16)
        grad_w_router = turned(normed_two, grad_logits)
        small = jnp.concatenate(
            [grad_gain_attn[:, None], grad_gain_moe[:, None], grad_w_router], axis=1
        ).astype(jnp.bfloat16)
        grads[s] = (w_gate_grad, w_up_grad, w_down_grad, grad_w_qkv, grad_w_out, small)
        input_grads[s] = grad_inputs
        grad_low = grad_inputs.astype(jnp.bfloat16)

    order_a, order_b = orders(("dp",))
    order_all_a, order_all_b = orders(("dp", "expert"))
    dp = lax.axis_size("dp")
    devices = dp * lax.axis_size("expert")
    reduced = []
    for s in (0, 1):
        w_gate_grad, w_up_grad, w_down_grad, grad_w_qkv, grad_w_out, small = grads[s]

        def by_dp(array):
            return jnp.moveaxis(
                array.reshape(array.shape[0], dp, array.shape[1] // dp, array.shape[2]), 1, 0
            )

        def by_all(array):
            return array.reshape(devices, array.shape[0] // devices, array.shape[1])

        reduced.append(
            (
                scattered(by_dp(w_gate_grad), order_a),
                scattered(by_dp(w_up_grad), order_b),
                scattered(by_dp(w_down_grad), order_a),
                scattered(by_all(grad_w_qkv), order_all_a),
                scattered(by_all(grad_w_out), order_all_b),
                scattered(by_all(small), order_all_a),
            )
        )
    final = []
    for a, b, dim in zip(reduced[0], reduced[1], (0, 0, 0, 1, 1, None)):
        keep = jnp.where(first, a, b)
        got = swapped(jnp.where(first, b, a).astype(jnp.bfloat16)).astype(jnp.float32)
        if dim is None:
            final.append(keep + got)
        else:
            final.append(
                jnp.concatenate(
                    [jnp.where(first, keep, got), jnp.where(first, got, keep)], axis=dim
                )
            )
    w_gate_grad, w_up_grad, w_down_grad, grad_w_qkv, grad_w_out, small = final
    heads, kv = H * HD, KVH * HD
    out_keep = jnp.where(first, outs[0], outs[1])
    out_got = swapped(jnp.where(first, outs[1], outs[0]))
    layer_out = jnp.where(
        first, jnp.concatenate([out_keep, out_got]), jnp.concatenate([out_got, out_keep])
    )
    low_one = input_grads[1].astype(jnp.bfloat16).astype(jnp.float32)
    grad_keep = jnp.where(first, input_grads[0], low_one)
    grad_got = swapped(jnp.where(first, low_one, input_grads[0]))
    input_grad = jnp.where(
        first, jnp.concatenate([grad_keep, grad_got]), jnp.concatenate([grad_got, grad_keep])
    )
    results = (
        layer_out,
        input_grad,
        small[:, 0],
        grad_w_qkv[:, :heads],
        grad_w_qkv[:, heads : heads + kv],
        grad_w_qkv[:, heads + kv :],
        grad_w_out,
        small[:, 1],
        small[:, 2:],
        w_gate_grad,
        w_up_grad,
        w_down_grad,
    )
    return tuple(result[None] for result in results) + (balance,)


def solution(mesh):
    return jax.shard_map(
        body,
        mesh=mesh,
        in_specs=(
            P(("dp", "expert"), None),
            P(("dp", "expert"), None),
            P(("dp", "expert"), None),
            P("section", ("dp", "expert"), None),
            P("section", None),
            P("section", None, None),
            P("section", None, None),
            P("section", None, None),
            P("section", None, None),
            P("section", None),
            P("section", None, None),
            P("section", "expert", None, None),
            P("section", "expert", None, None),
            P("section", "expert", None, None),
        ),
        out_specs=(
            P("section", ("dp", "expert"), None),
            P("section", ("dp", "expert"), None),
            P("section", ("dp", "expert")),
            P("section", ("dp", "expert"), None),
            P("section", ("dp", "expert"), None),
            P("section", ("dp", "expert"), None),
            P("section", ("dp", "expert"), None),
            P("section", ("dp", "expert")),
            P("section", ("dp", "expert"), None),
            P("section", "expert", "dp", None),
            P("section", "expert", "dp", None),
            P("section", "expert", "dp", None),
            P("section", None),
        ),
        check_vma=False,
    )
```

time: 1730 us -> 902 us (0.52)
  blocking collectives: 537 us -> 68.6 us
  waiting for transfers between devices: 506 us -> 387 us
  matrix products: 305 us -> 202 us
  other arithmetic: 133 us -> 62.1 us
  local copies, waits for them, and re-layouts: 162 us -> 105 us
    all_to_all x10 -> x0, waiting for transfers between devices: 502 us -> none  [the longest x3 185 us: forward_layer(): lax.all_to_all(expert_out, 'expert', split_axis=0, concat_axis=0, tiled=T...]
    ppermute x4 -> x63, waiting for transfers between devices: 4.12 us -> 292 us  [the longest x36 275 us: halved_over(): got = lax.ppermute(send, axis, pairs)]
    psum x1, blocking collectives: 309 us -> 47.1 us  [body(): count_all, prob_all = lax.psum((counts, jnp.stack(probabilities)), axes)]
    all_to_all x3 -> x0, blocking collectives: 228 us -> none  [the longest x2 153 us: forward_layer(): lax.all_to_all(outgoing, 'expert', split_axis=0, concat_axis=0, tiled=True)]
    dot_general x75 -> x44, matrix products: 273 us -> 168 us  [the longest x2 20.6 us: experts_forward(): jnp.einsum('td,edf->etf', rows, w_up, preferred_element_type=jnp.float32)]
    reduce_scatter x3 -> x4, waiting for transfers between devices: 0.01 us -> 62 us  [sum_rows(): lax.psum_scatter(partial, 'expert', scatter_dimension=0, tiled=True)]
    gather x6 -> x0, local copies, waits for them, and re-layouts: 50 us -> none  [the longest x3 25.1 us: backward_layer(): back_rows[slot_index].reshape(length, TOPK, -1).astype(jnp.float32)]
    all_to_all x10 -> x0, starting transfers between devices: 49 us -> none  [the longest x3 14.3 us: backward_layer(): lax.all_to_all(grad_route_in, 'expert', split_axis=0, concat_axis=0, tile...]
  transfers between devices with their start and end apart: 17 -> 73, of which waited for: 12 -> 29; matrix products, arithmetic and copies ran while one was open for 17% -> 39% of each run, Pallas kernels for 0% -> 0%
where the time goes in v1:
time: 902 us; the launch traced here: 894 us
  waiting for transfers between devices  387 us (43%)
  matrix products  202 us (22%)
  local copies, waits for them, and re-layouts  105 us (12%)
  blocking collectives  68.6 us (8%)
  other arithmetic  62.1 us (7%)
  starting transfers between devices  51.1 us (6%)
  between operations  17.4 us (2%)
    ppermute x36, waiting for transfers between devices, halved_over(): got = lax.ppermute(send, axis, pairs)  275 us
    reduce_scatter x4, waiting for transfers between devices, sum_rows(): lax.psum_scatter(partial, 'expert', scatter_dimension=0, tiled=True)  62 us
    psum x1, blocking collectives, body(): count_all, prob_all = lax.psum((counts, jnp.stack(probabilities)), axes)  47.1 us
    all_gather x4, waiting for transfers between devices, gather_rows(): return lax.all_gather(rows, 'expert', axis=0, tiled=True)  32.6 us
    ppermute x36, starting transfers between devices, halved_over(): got = lax.ppermute(send, axis, pairs)  32.5 us
    dot_general x12, matrix products, matmul(): return jnp.dot(left_side, right_side, preferred_element_type=jnp.float32)  32 us
    reshape x8, local copies, waits for them, and re-layouts, by_dp(): array.reshape(array.shape[0], dp, array.shape[1] // dp, array.shape[2])  31.7 us
    all_gather x1, blocking collectives, body(): routes_all = lax.all_gather(routes_here, 'expert', axis=1, tiled=True)  21.5 us
  transfers between devices with their start and end apart: 73, of which 29 were waited for; matrix products, arithmetic and copies ran while one was open for 39% of the time, Pallas kernels for 0%

profile of v1, /device:TPU:0, one launch (start us, length us, event | category | flops | bytes accessed | tf_op | source)
XLA Modules:
  0.0 893.5 jit_solution(12999696151799525860)
XLA Ops:
  44.6 9.0 %collective-permute-done.5 = s32[96,8]{0,1:T(8,128)S(1)} collective-permute-done((s32[96,8]{0,1:T(8,128)S(1)}, s32[96,8]{0,1:T(8,128)S(1)}, u32[]{:S(2)}, u32[]{:S(2)}) %collective-permute-start.5) | collective-permute-done | bytes 3104 | tf_op jit(solution)/shard_map/ppermute | solution.py:93
  53.8 21.5 %all_gather.15 = s32[2,384,8]{2,0,1:T(2,128)S(1)} all-gather(s32[2,96,8]{2,0,1:T(2,128)S(1)} %copy.199), channel_id=1, replica_groups=mesh['section'=2,'dp'=4,'expert'=4] {'expert'}, dimensions={1}, use_global_device_ids=true | all-gather | bytes 30720 | tf_op jit(solution)/shard_map/all_gather | solution.py:289
  76.1 7.4 all-gather.5.cloned.1.call-done
  85.4 6.1 fusion.38
  91.6 8.5 multiply_convert_fusion.3
  107.3 31.4 %reduce-scatter.11.cloned.1.call-done = bf16[96,1536]{1,0:T(8,128)(2,1)} async-done(((bf16[384,1536]{1,0:T(8,128)(2,1)}), bf16[96,1536]{1,0:T(8,128)(2,1)}) %reduce-scatter.11.cloned.1.call-update) | async-done | bytes 294928 | tf_op jit(solution)/shard_map/reduce_scatter | solution.py:263
  143.3 6.0 fusion.53
  155.2 5.0 multiply_reduce_fusion.6
  163.6 6.5 all-gather.9.cloned.1.call-done
  171.9 10.0 %fusion.43 = f32[4,512,384]{2,1,0:T(8,128)} fusion(bf16[4,512,1536]{2,1,0:T(8,128)(2,1)} %collective-permute-done.10, pred[]{:T(512)S(6)} %eq.26, bf16[384,1536]{1,0:T(8,128)(2,1)} %all-gather.9.cloned.1.call-done, bf16[1,4,512,1536]{3,2,1,0:T(8,128)(2,1)} %param.27), kind=kOutput, calls=%fused_computation.112 | convolution fusion | flops 2419064832 | bytes 16908288 | tf_op jit(solution)/shard_map/td,efd->etf/dot_general | solution.py:187
  182.9 18.8 %all-gather.7.cloned.1.call-done = bf16[384,1536]{1,0:T(8,128)(2,1)} async-done(((bf16[96,1536]{1,0:T(8,128)(2,1)}), bf16[384,1536]{1,0:T(8,128)(2,1)}) %all-gather.7.cloned.1.call-update) | async-done | bytes 1179664 | tf_op jit(solution)/shard_map/all_gather | solution.py:259
  203.5 8.6 fusion.40
  212.1 12.1 %fusion.18 = (bf16[4,384,512]{1,2,0:T(8,128)(2,1)}, f32[4,384]{1,0:T(4,128)S(1)}, bf16[4,384,512]{1,2,0:T(8,128)(2,1)}, bf16[4,384,512]{1,2,0:T(8,128)(2,1)}) fusion(f32[4,512,384]{2,1,0:T(8,128)S(1)} %fusion.40, f32[4,512,384]{2,1,0:T(8,128)S(1)} %copy-done.146, f32[4,384]{1,0:T(4,128)S(1)} %fusion.199, bf16[384,1536]{1,0:T(8,128)(2,1)S(1)} %copy-done.49, ...), kind=kOutput, calls=%fused_computation.65 | convolution fusion | flops 2434005504 | bytes 24784896 | tf_op jit(solution)/shard_map/td,edf->etf/dot_general | solution.py:176
  225.3 6.8 convolution_bitcast_fusion.2
  232.1 8.3 fusion.33
  247.5 6.7 fusion.35
  257.0 16.4 %reduce-scatter.15.cloned.1.call-done = bf16[96,1536]{1,0:T(8,128)(2,1)} async-done(((bf16[384,1536]{1,0:T(8,128)(2,1)}), bf16[96,1536]{1,0:T(8,128)(2,1)}) %reduce-scatter.15.cloned.1.call-update) | async-done | bytes 294928 | tf_op jit(solution)/shard_map/reduce_scatter | solution.py:263
  278.1 5.6 convolution_convert_fusion.11
  289.5 14.3 %reduce-scatter.13.cloned.1.call-done = bf16[96,1536]{1,0:T(8,128)(2,1)} async-done(((bf16[384,1536]{1,0:T(8,128)(2,1)}), bf16[96,1536]{1,0:T(8,128)(2,1)}) %reduce-scatter.13.cloned.1.call-update) | async-done | bytes 294928 | tf_op jit(solution)/shard_map/reduce_scatter | solution.py:263
  313.3 5.7 fusion.130
  324.6 4.9 fusion.5
  338.4 6.2 fusion.7
  355.0 6.2 reshape.578
  361.3 6.3 copy.247
  390.0 18.8 %collective-permute-done.53 = bf16[2,2,384,512]{3,2,1,0:T(8,128)(2,1)S(1)} collective-permute-done((bf16[2,2,384,512]{3,2,1,0:T(8,128)(2,1)S(1)}, bf16[2,2,384,512]{3,2,1,0:T(8,128)(2,1)S(1)}, u32[]{:S(2)}, u32[]{:S(2)}) %collective-permute-start.53) | collective-permute-done | bytes 1572896 | tf_op jit(solution)/shard_map/ppermute | solution.py:104
  417.9 10.1 %fusion.25 = (bf16[4,384,512]{1,2,0:T(8,128)(2,1)S(1)}, f32[4,384]{1,0:T(4,128)S(1)}, bf16[4,384,512]{1,2,0:T(8,128)(2,1)S(1)}) fusion(f32[4,512,384]{2,1,0:T(8,128)} %get-tuple-element.155, f32[4,512,384]{2,1,0:T(8,128)} %copy-done.145, f32[4,384]{1,0:T(4,128)S(1)} %copy-done.125, bf16[384,1536]{1,0:T(8,128)(2,1)} %all-gather.11.cloned.1.call-done, ...), kind=kOutput, calls=%fused_computation.77 | convolution fusion | flops 2432432640 | bytes 23212032 | tf_op jit(solution)/shard_map/td,efd->etf/dot_general | solution.py:187
  429.1 5.2 convolution_bitcast_fusion
  434.3 6.7 fusion.32
  453.9 47.1 %all-reduce = (f32[2,16]{1,0:T(2,128)S(1)}, f32[2,16]{1,0:T(2,128)S(1)}) all-reduce(f32[2,16]{1,0:T(2,128)S(1)} %pad_maximum_fusion.29, f32[2,16]{1,0:T(2,128)S(1)} %copy-done.133), channel_id=1, replica_groups=mesh['section'=2,'dp'=4,'expert'=4] {'section','dp','expert'}, use_global_device_ids=true, to_apply=%region_46.47 | all-reduce | flops 64 | bytes 512 | tf_op jit(solution)/shard_map/psum | solution.py:308
  503.1 13.7 %collective-permute-done.39 = bf16[2,96,768]{2,1,0:T(8,128)(2,1)S(1)} collective-permute-done((bf16[2,96,768]{2,1,0:T(8,128)(2,1)S(1)}, bf16[2,96,768]{2,1,0:T(8,128)(2,1)S(1)}, u32[]{:S(2)}, u32[]{:S(2)}) %collective-permute-start.39) | collective-permute-done | bytes 294944 | tf_op jit(solution)/shard_map/ppermute | solution.py:104
  532.4 5.0 fusion.120
  544.1 6.1 fusion.4
  550.2 6.1 fusion.6
  571.1 6.2 reshape.572
  577.4 5.9 copy.243
  588.5 6.2 reshape.576
  594.7 6.1 copy.246
  617.5 24.7 %collective-permute-done.44 = bf16[2,2,384,512]{3,2,1,0:T(8,128)(2,1)S(1)} collective-permute-done((bf16[2,2,384,512]{3,2,1,0:T(8,128)(2,1)}, bf16[2,2,384,512]{3,2,1,0:T(8,128)(2,1)S(1)}, u32[]{:S(2)}, u32[]{:S(2)}) %collective-permute-start.44) | collective-permute-done | bytes 1572896 | tf_op jit(solution)/shard_map/ppermute | solution.py:104
  648.0 27.2 %collective-permute-done.57 = bf16[2,2,128,1536]{3,2,1,0:T(8,128)(2,1)} collective-permute-done((bf16[2,2,128,1536]{3,2,1,0:T(8,128)(2,1)}, bf16[2,2,128,1536]{3,2,1,0:T(8,128)(2,1)}, u32[]{:S(2)}, u32[]{:S(2)}) %collective-permute-start.57) | collective-permute-done | bytes 1572896 | tf_op jit(solution)/shard_map/ppermute | solution.py:104
  681.7 6.3 collective-permute-done.45
  698.7 6.1 collective-permute-done.61
  704.9 15.3 %collective-permute-done.58 = bf16[2,128,1536]{2,1,0:T(8,128)(2,1)S(1)} collective-permute-done((bf16[2,128,1536]{2,1,0:T(8,128)(2,1)S(1)}, bf16[2,128,1536]{2,1,0:T(8,128)(2,1)S(1)}, u32[]{:S(2)}, u32[]{:S(2)}) %collective-permute-start.58) | collective-permute-done | bytes 786464 | tf_op jit(solution)/shard_map/ppermute | solution.py:104
  720.7 70.1 %collective-permute-done.34 = bf16[2,2,96,768]{3,2,1,0:T(8,128)(2,1)S(1)} collective-permute-done((bf16[2,2,96,768]{3,2,1,0:T(8,128)(2,1)S(1)}, bf16[2,2,96,768]{3,2,1,0:T(8,128)(2,1)S(1)}, u32[]{:S(2)}, u32[]{:S(2)}) %collective-permute-start.34) | collective-permute-done | bytes 589856 | tf_op jit(solution)/shard_map/ppermute | solution.py:104
  793.3 14.4 %collective-permute-done.35 = bf16[2,96,768]{2,1,0:T(8,128)(2,1)S(1)} collective-permute-done((bf16[2,96,768]{2,1,0:T(8,128)(2,1)S(1)}, bf16[2,96,768]{2,1,0:T(8,128)(2,1)S(1)}, u32[]{:S(2)}, u32[]{:S(2)}) %collective-permute-start.35) | collective-permute-done | bytes 294944 | tf_op jit(solution)/shard_map/ppermute | solution.py:104
  815.4 17.0 %collective-permute-done.29 = bf16[2,2,96,1280]{3,2,0,1:T(8,128)(2,1)S(1)} collective-permute-done((bf16[2,2,96,1280]{3,2,0,1:T(8,128)(2,1)S(1)}, bf16[2,2,96,1280]{3,2,0,1:T(8,128)(2,1)S(1)}, u32[]{:S(2)}, u32[]{:S(2)}) %collective-permute-start.29) | collective-permute-done | bytes 983072 | tf_op jit(solution)/shard_map/ppermute | solution.py:104
  832.8 19.8 %collective-permute-done.24 = bf16[2,2,96,1280]{3,2,0,1:T(8,128)(2,1)S(1)} collective-permute-done((bf16[2,2,96,1280]{3,2,0,1:T(8,128)(2,1)S(1)}, bf16[2,2,96,1280]{3,2,0,1:T(8,128)(2,1)S(1)}, u32[]{:S(2)}, u32[]{:S(2)}) %collective-permute-start.24) | collective-permute-done | bytes 983072 | tf_op jit(solution)/shard_map/ppermute | solution.py:104
  855.6 14.9 %collective-permute-done.25 = bf16[2,96,1280]{2,1,0:T(8,128)(2,1)S(1)} collective-permute-done((bf16[2,96,1280]{2,1,0:T(8,128)(2,1)S(1)}, bf16[2,96,1280]{2,1,0:T(8,128)(2,1)S(1)}, u32[]{:S(2)}, u32[]{:S(2)}) %collective-permute-start.25) | collective-permute-done | bytes 491552 | tf_op jit(solution)/shard_map/ppermute | solution.py:104
  872.9 9.9 %collective-permute-done.26 = bf16[96,1280]{1,0:T(8,128)(2,1)S(1)} collective-permute-done((bf16[96,1280]{1,0:T(8,128)(2,1)S(1)}, bf16[96,1280]{1,0:T(8,128)(2,1)S(1)}, u32[]{:S(2)}, u32[]{:S(2)}) %collective-permute-start.26) | collective-permute-done | bytes 245792 | tf_op jit(solution)/shard_map/ppermute | solution.py:104
  (689 shorter events, 269.0 us)
Async XLA Ops:
  7.2 76.3 %all-gather.5.cloned.1.call-start = ((), (), s32[]{:S(2)}) async-start(), calls=%async_computation.6 | async-start | bytes 1474560 | tf_op jit(solution)/shard_map/all_gather | solution.py:259
  7.8 26.6 %collective-permute-start.4 = (bf16[1536,1536]{1,0:T(8,128)(2,1)}, bf16[1536,1536]{1,0:T(8,128)(2,1)}, u32[]{:S(2)}, u32[]{:S(2)}) collective-permute-start(bf16[1536,1536]{1,0:T(8,128)(2,1)} %bitcast.804), channel_id=1, source_target_pairs={{0,16},{16,0},{1,17},{17,1},{2,18},{18,2},{3,19},{19,3},{4,20},{20... | collective-permute-start | bytes 14155784 | tf_op jit(solution)/shard_map/ppermute | solution.py:93
  19.8 65.5 %collective-permute-start.8 = (bf16[4,1536,512]{2,1,0:T(8,128)(2,1)}, bf16[4,1536,512]{2,1,0:T(8,128)(2,1)}, u32[]{:S(2)}, u32[]{:S(2)}) collective-permute-start(bf16[4,1536,512]{2,1,0:T(8,128)(2,1)} %bitcast.886), channel_id=1, source_target_pairs={{0,16},{16,0},{1,17},{17,1},{2,18},{18,2},{3,19},{19,3},{4,20},{20... | collective-permute-start | bytes 18874376 | tf_op jit(solution)/shard_map/ppermute | solution.py:93
  21.4 70.2 %collective-permute-start.9 = (bf16[4,1536,512]{2,1,0:T(8,128)(2,1)}, bf16[4,1536,512]{2,1,0:T(8,128)(2,1)}, u32[]{:S(2)}, u32[]{:S(2)}) collective-permute-start(bf16[4,1536,512]{2,1,0:T(8,128)(2,1)} %bitcast.883), channel_id=1, source_target_pairs={{0,16},{16,0},{1,17},{17,1},{2,18},{18,2},{3,19},{19,3},{4,20},{20... | collective-permute-start | bytes 18874376 | tf_op jit(solution)/shard_map/ppermute | solution.py:93
  26.9 73.2 %collective-permute-start.10 = (bf16[4,512,1536]{2,1,0:T(8,128)(2,1)}, bf16[4,512,1536]{2,1,0:T(8,128)(2,1)}, u32[]{:S(2)}, u32[]{:S(2)}) collective-permute-start(bf16[4,512,1536]{2,1,0:T(8,128)(2,1)} %bitcast.878), channel_id=1, source_target_pairs={{0,16},{16,0},{1,17},{17,1},{2,18},{18,2},{3,19},{19,3},{4,20},{20... | collective-permute-start | bytes 18874376 | tf_op jit(solution)/shard_map/ppermute | solution.py:93
  39.9 98.8 %reduce-scatter.11.cloned.1.call-start = ((), (), s32[]{:S(2)}) async-start(), calls=%async_computation.7 | async-start | bytes 1474560 | tf_op jit(solution)/shard_map/reduce_scatter | solution.py:263
  44.5 31.0 %collective-permute-start.7 = (bf16[1536,16]{0,1:T(8,128)(2,1)S(1)}, bf16[1536,16]{0,1:T(8,128)(2,1)S(1)}, u32[]{:S(2)}, u32[]{:S(2)}) collective-permute-start(bf16[1536,16]{0,1:T(8,128)(2,1)S(1)} %bitcast.875), channel_id=1, source_target_pairs={{0,16},{16,0},{1,17},{17,1},{2,18},{18,2},{3,19},{19,3},{4,20},{20... | collective-permute-start | bytes 147464 | tf_op jit(solution)/shard_map/ppermute | solution.py:93
  105.1 64.9 %all-gather.9.cloned.1.call-start = ((), (), s32[]{:S(2)}) async-start(), calls=%async_computation.10 | async-start | bytes 1474560 | tf_op jit(solution)/shard_map/all_gather | solution.py:259
  107.0 94.6 %all-gather.7.cloned.1.call-start = ((), (), s32[]{:S(2)}) async-start(), calls=%async_computation.8 | async-start | bytes 1474560 | tf_op jit(solution)/shard_map/all_gather | solution.py:259
  161.6 92.9 %reduce-scatter.19.cloned.1.call-start = ((), (), s32[]{:S(2)}) async-start(), calls=%async_computation.14 | async-start | bytes 245760
  170.0 174.6 %collective-permute-start.59 = (bf16[384,1536]{1,0:T(8,128)(2,1)}, bf16[384,1536]{1,0:T(8,128)(2,1)}, u32[]{:S(2)}, u32[]{:S(2)}) collective-permute-start(bf16[384,1536]{1,0:T(8,128)(2,1)} %all-gather.9.cloned.1.call-done), channel_id=1, source_target_pairs={{0,16},{16,0},{1,17},{17,1},{2,18},{18,2},{3,19},{19,3},{4,20},{20... | collective-permute-start | bytes 3538952 | tf_op jit(solution)/shard_map/ppermute | solution.py:93
  182.0 360.0 %collective-permute-start.43 = (bf16[384,1536]{1,0:T(8,128)(2,1)}, bf16[384,1536]{1,0:T(8,128)(2,1)}, u32[]{:S(2)}, u32[]{:S(2)}) collective-permute-start(bf16[384,1536]{1,0:T(8,128)(2,1)} %all-gather.5.cloned.1.call-done), channel_id=1, source_target_pairs={{0,16},{16,0},{1,17},{17,1},{2,18},{18,2},{3,19},{19,3},{4,20},{20... | collective-permute-start | bytes 3538952 | tf_op jit(solution)/shard_map/ppermute | solution.py:93
  225.0 48.3 %reduce-scatter.15.cloned.1.call-start = ((), (), s32[]{:S(2)}) async-start(), calls=%async_computation.11 | async-start | bytes 1474560 | tf_op jit(solution)/shard_map/reduce_scatter | solution.py:263
  240.4 63.3 %reduce-scatter.13.cloned.1.call-start = ((), (), s32[]{:S(2)}) async-start(), calls=%async_computation.9 | async-start | bytes 1474560 | tf_op jit(solution)/shard_map/reduce_scatter | solution.py:263
  246.9 77.6 %collective-permute-start.46 = (bf16[3,2,384,512]{2,3,1,0:T(8,128)(2,1)}, bf16[3,2,384,512]{2,3,1,0:T(8,128)(2,1)}, u32[]{:S(2)}, u32[]{:S(2)}) collective-permute-start(bf16[3,2,384,512]{2,3,1,0:T(8,128)(2,1)} %get-tuple-element.77), channel_id=1, source_target_pairs={{0,16},{16,0},{1,17},{17,1},{2,18},{18,2},{3,19},{19,3},{4,20},{20... | collective-permute-start | bytes 7077896 | tf_op jit(solution)/shard_map/ppermute | solution.py:93
  254.2 163.7 %all-gather.11.cloned.1.call-start = ((), (), s32[]{:S(2)}) async-start(), calls=%async_computation.12 | async-start | bytes 1474560 | tf_op jit(solution)/shard_map/all_gather | solution.py:259
  254.5 68.6 %collective-permute-start.47 = (bf16[384,1536]{1,0:T(8,128)(2,1)}, bf16[384,1536]{1,0:T(8,128)(2,1)}, u32[]{:S(2)}, u32[]{:S(2)}) collective-permute-start(bf16[384,1536]{1,0:T(8,128)(2,1)} %all-gather.7.cloned.1.call-done), channel_id=1, source_target_pairs={{0,16},{16,0},{1,17},{17,1},{2,18},{18,2},{3,19},{19,3},{4,20},{20... | collective-permute-start | bytes 3538952 | tf_op jit(solution)/shard_map/ppermute | solution.py:93
  305.6 67.0 %collective-permute-start.11 = (bf16[96,1536]{1,0:T(8,128)(2,1)}, bf16[96,1536]{1,0:T(8,128)(2,1)}, u32[]{:S(2)}, u32[]{:S(2)}) collective-permute-start(bf16[96,1536]{1,0:T(8,128)(2,1)} %get-tuple-element.92), channel_id=1, source_target_pairs={{0,16},{16,0},{1,17},{17,1},{2,18},{18,2},{3,19},{19,3},{4,20},{20... | collective-permute-start | bytes 884744 | tf_op jit(solution)/shard_map/ppermute | solution.py:93
  320.0 130.3 %reduce-scatter.21.cloned.1.call-start = ((), (), s32[]{:S(2)}) async-start(), calls=%async_computation.15 | async-start | bytes 245760
  323.1 27.8 %collective-permute-start.17 = (bf16[2,2,2,96,18]{3,4,1,2,0:T(8,128)(2,1)}, bf16[2,2,2,96,18]{3,4,1,2,0:T(8,128)(2,1)}, u32[]{:S(2)}, u32[]{:S(2)}) collective-permute-start(bf16[2,2,2,96,18]{3,4,1,2,0:T(8,128)(2,1)} %dynamic-slice_bitcast_fusion.26), channel_id=1, source_target_pairs={{0,4},{4,0},{8,12},{12,8},{1,5},{5,1},{9,13},{13,9},{2,6},{6,2},{1... | collective-permute-start | bytes 82952 | tf_op jit(solution)/shard_map/ppermute | solution.py:104
  324.5 51.7 %collective-permute-start.27 = (bf16[96,5120]{1,0:T(8,128)(2,1)}, bf16[96,5120]{1,0:T(8,128)(2,1)}, u32[]{:S(2)}, u32[]{:S(2)}) collective-permute-start(bf16[96,5120]{1,0:T(8,128)(2,1)} %pad_maximum_fusion.5), channel_id=1, source_target_pairs={{0,16},{16,0},{1,17},{17,1},{2,18},{18,2},{3,19},{19,3},{4,20},{20... | collective-permute-start | bytes 2949128 | tf_op jit(solution)/shard_map/ppermute | solution.py:93
  344.6 40.7 %collective-permute-start.48 = (bf16[2,2,384,512]{3,2,1,0:T(8,128)(2,1)}, bf16[2,2,384,512]{3,2,1,0:T(8,128)(2,1)}, u32[]{:S(2)}, u32[]{:S(2)}) collective-permute-start(bf16[2,2,384,512]{3,2,1,0:T(8,128)(2,1)} %dynamic-slice_bitcast_fusion.4), channel_id=1, source_target_pairs={{0,4},{4,0},{8,12},{12,8},{1,5},{5,1},{9,13},{13,9},{2,6},{6,2},{1... | collective-permute-start | bytes 4718600 | tf_op jit(solution)/shard_map/ppermute | solution.py:104
  371.4 37.3 %collective-permute-start.53 = (bf16[2,2,384,512]{3,2,1,0:T(8,128)(2,1)S(1)}, bf16[2,2,384,512]{3,2,1,0:T(8,128)(2,1)S(1)}, u32[]{:S(2)}, u32[]{:S(2)}) collective-permute-start(bf16[2,2,384,512]{3,2,1,0:T(8,128)(2,1)S(1)} %dynamic-slice_bitcast_fusion.2), channel_id=1, source_target_pairs={{0,8},{4,12},{8,0},{12,4},{1,9},{5,13},{9,1},{13,5},{2,10},{6,14},... | collective-permute-start | bytes 4718600 | tf_op jit(solution)/shard_map/ppermute | solution.py:104
  372.6 42.7 %collective-permute-start.60 = (bf16[2,2,128,1536]{3,2,1,0:T(8,128)(2,1)S(1)}, bf16[2,2,128,1536]{3,2,1,0:T(8,128)(2,1)S(1)}, u32[]{:S(2)}, u32[]{:S(2)}) collective-permute-start(bf16[2,2,128,1536]{3,2,1,0:T(8,128)(2,1)S(1)} %copy-done.40), channel_id=1, source_target_pairs={{0,4},{4,0},{8,12},{12,8},{1,5},{5,1},{9,13},{13,9},{2,6},{6,2},{1... | collective-permute-start | bytes 4718600 | tf_op jit(solution)/shard_map/ppermute | solution.py:104
  376.2 224.6 %collective-permute-start.20 = (bf16[96,18]{0,1:T(8,128)(2,1)}, bf16[96,18]{0,1:T(8,128)(2,1)}, u32[]{:S(2)}, u32[]{:S(2)}) collective-permute-start(bf16[96,18]{0,1:T(8,128)(2,1)} %fusion.198), channel_id=1, source_target_pairs={{0,2},{1,3},{2,0},{3,1},{4,6},{5,7},{6,4},{7,5},{8,10},{9,11},{10,... | collective-permute-start | bytes 10376 | tf_op jit(solution)/shard_map/ppermute | solution.py:104
  385.4 65.9 %collective-permute-start.37 = (bf16[2,2,2,96,768]{4,3,2,1,0:T(8,128)(2,1)}, bf16[2,2,2,96,768]{4,3,2,1,0:T(8,128)(2,1)}, u32[]{:S(2)}, u32[]{:S(2)}) collective-permute-start(bf16[2,2,2,96,768]{4,3,2,1,0:T(8,128)(2,1)} %dynamic-slice_bitcast_fusion.6), channel_id=1, source_target_pairs={{0,8},{4,12},{8,0},{12,4},{1,9},{5,13},{9,1},{13,5},{2,10},{6,14},... | collective-permute-start | bytes 3538952 | tf_op jit(solution)/shard_map/ppermute | solution.py:104
  408.8 269.8 %collective-permute-start.49 = (bf16[2,384,512]{2,1,0:T(8,128)(2,1)}, bf16[2,384,512]{2,1,0:T(8,128)(2,1)}, u32[]{:S(2)}, u32[]{:S(2)}) collective-permute-start(bf16[2,384,512]{2,1,0:T(8,128)(2,1)} %dynamic-slice_bitcast_fusion.14), channel_id=1, source_target_pairs={{0,8},{4,12},{8,0},{12,4},{1,9},{5,13},{9,1},{13,5},{2,10},{6,14},... | collective-permute-start | bytes 2359304 | tf_op jit(solution)/shard_map/ppermute | solution.py:104
  429.0 89.3 %reduce-scatter.17.cloned.1.call-start = ((), (), s32[]{:S(2)}) async-start(), calls=%async_computation.13 | async-start | bytes 1474560 | tf_op jit(solution)/shard_map/reduce_scatter | solution.py:263
  445.6 97.8 %collective-permute-start.42 = (bf16[3,2,384,512]{2,3,1,0:T(8,128)(2,1)}, bf16[3,2,384,512]{2,3,1,0:T(8,128)(2,1)}, u32[]{:S(2)}, u32[]{:S(2)}) collective-permute-start(bf16[3,2,384,512]{2,3,1,0:T(8,128)(2,1)} %get-tuple-element.75), channel_id=1, source_target_pairs={{0,16},{16,0},{1,17},{17,1},{2,18},{18,2},{3,19},{19,3},{4,20},{20... | collective-permute-start | bytes 7077896 | tf_op jit(solution)/shard_map/ppermute | solution.py:93
  453.2 48.1 %collective-permute-start.38 = (bf16[2,2,96,768]{3,2,1,0:T(8,128)(2,1)S(1)}, bf16[2,2,96,768]{3,2,1,0:T(8,128)(2,1)S(1)}, u32[]{:S(2)}, u32[]{:S(2)}) collective-permute-start(bf16[2,2,96,768]{3,2,1,0:T(8,128)(2,1)S(1)} %dynamic-slice_bitcast_fusion.16), channel_id=1, source_target_pairs={{0,4},{4,0},{8,12},{12,8},{1,5},{5,1},{9,13},{13,9},{2,6},{6,2},{1... | collective-permute-start | bytes 1769480 | tf_op jit(solution)/shard_map/ppermute | solution.py:104
  516.8 46.8 %collective-permute-start.56 = (bf16[384,1536]{1,0:T(8,128)(2,1)}, bf16[384,1536]{1,0:T(8,128)(2,1)}, u32[]{:S(2)}, u32[]{:S(2)}) collective-permute-start(bf16[384,1536]{1,0:T(8,128)(2,1)} %all-gather.11.cloned.1.call-done), channel_id=1, source_target_pairs={{0,16},{16,0},{1,17},{17,1},{2,18},{18,2},{3,19},{19,3},{4,20},{20... | collective-permute-start | bytes 3538952 | tf_op jit(solution)/shard_map/ppermute | solution.py:93
  542.0 137.3 %collective-permute-start.54 = (bf16[2,384,512]{2,1,0:T(8,128)(2,1)}, bf16[2,384,512]{2,1,0:T(8,128)(2,1)}, u32[]{:S(2)}, u32[]{:S(2)}) collective-permute-start(bf16[2,384,512]{2,1,0:T(8,128)(2,1)} %dynamic-slice_bitcast_fusion.12), channel_id=1, source_target_pairs={{0,4},{4,0},{8,12},{12,8},{1,5},{5,1},{9,13},{13,9},{2,6},{6,2},{1... | collective-permute-start | bytes 2359304 | tf_op jit(solution)/shard_map/ppermute | solution.py:104
  560.1 47.9 %collective-permute-start.12 = (f32[96,1536]{1,0:T(8,128)}, f32[96,1536]{1,0:T(8,128)}, u32[]{:S(2)}, u32[]{:S(2)}) collective-permute-start(f32[96,1536]{1,0:T(8,128)} %get-tuple-element.90), channel_id=1, source_target_pairs={{0,16},{16,0},{1,17},{17,1},{2,18},{18,2},{3,19},{19,3},{4,20},{20... | collective-permute-start | bytes 1769480 | tf_op jit(solution)/shard_map/ppermute | solution.py:93
  604.8 37.5 %collective-permute-start.44 = (bf16[2,2,384,512]{3,2,1,0:T(8,128)(2,1)}, bf16[2,2,384,512]{3,2,1,0:T(8,128)(2,1)S(1)}, u32[]{:S(2)}, u32[]{:S(2)}) collective-permute-start(bf16[2,2,384,512]{3,2,1,0:T(8,128)(2,1)} %dynamic-slice_bitcast_fusion.5), channel_id=1, source_target_pairs={{0,4},{4,0},{8,12},{12,8},{1,5},{5,1},{9,13},{13,9},{2,6},{6,2},{1... | collective-permute-start | bytes 4718600 | tf_op jit(solution)/shard_map/ppermute | solution.py:104
  608.0 37.4 %collective-permute-start.51 = (bf16[2,2,384,512]{3,2,1,0:T(8,128)(2,1)}, bf16[2,2,384,512]{3,2,1,0:T(8,128)(2,1)}, u32[]{:S(2)}, u32[]{:S(2)}) collective-permute-start(bf16[2,2,384,512]{3,2,1,0:T(8,128)(2,1)} %dynamic-slice_bitcast_fusion.3), channel_id=1, source_target_pairs={{0,8},{4,12},{8,0},{12,4},{1,9},{5,13},{9,1},{13,5},{2,10},{6,14},... | collective-permute-start | bytes 4718600 | tf_op jit(solution)/shard_map/ppermute | solution.py:104
  611.1 64.1 %collective-permute-start.57 = (bf16[2,2,128,1536]{3,2,1,0:T(8,128)(2,1)}, bf16[2,2,128,1536]{3,2,1,0:T(8,128)(2,1)}, u32[]{:S(2)}, u32[]{:S(2)}) collective-permute-start(bf16[2,2,128,1536]{3,2,1,0:T(8,128)(2,1)} %dynamic-slice_bitcast_fusion.1), channel_id=1, source_target_pairs={{0,4},{4,0},{8,12},{12,8},{1,5},{5,1},{9,13},{13,9},{2,6},{6,2},{1... | collective-permute-start | bytes 4718600 | tf_op jit(solution)/shard_map/ppermute | solution.py:104
  642.2 37.6 %collective-permute-start.33 = (bf16[2,2,2,96,768]{4,3,2,1,0:T(8,128)(2,1)S(1)}, bf16[2,2,2,96,768]{4,3,2,1,0:T(8,128)(2,1)S(1)}, u32[]{:S(2)}, u32[]{:S(2)}) collective-permute-start(bf16[2,2,2,96,768]{4,3,2,1,0:T(8,128)(2,1)S(1)} %dynamic-slice_bitcast_fusion.7), channel_id=1, source_target_pairs={{0,8},{4,12},{8,0},{12,4},{1,9},{5,13},{9,1},{13,5},{2,10},{6,14},... | collective-permute-start | bytes 3538952 | tf_op jit(solution)/shard_map/ppermute | solution.py:104
  645.4 42.6 %collective-permute-start.45 = (bf16[2,384,512]{2,1,0:T(8,128)(2,1)S(1)}, bf16[2,384,512]{2,1,0:T(8,128)(2,1)S(1)}, u32[]{:S(2)}, u32[]{:S(2)}) collective-permute-start(bf16[2,384,512]{2,1,0:T(8,128)(2,1)S(1)} %dynamic-slice_bitcast_fusion.15), channel_id=1, source_target_pairs={{0,8},{4,12},{8,0},{12,4},{1,9},{5,13},{9,1},{13,5},{2,10},{6,14},... | collective-permute-start | bytes 2359304 | tf_op jit(solution)/shard_map/ppermute | solution.py:104
  678.6 26.3 %collective-permute-start.61 = (bf16[2,128,1536]{2,1,0:T(8,128)(2,1)S(1)}, bf16[2,128,1536]{2,1,0:T(8,128)(2,1)S(1)}, u32[]{:S(2)}, u32[]{:S(2)}) collective-permute-start(bf16[2,128,1536]{2,1,0:T(8,128)(2,1)S(1)} %copy-done.72), channel_id=1, source_target_pairs={{0,8},{4,12},{8,0},{12,4},{1,9},{5,13},{9,1},{13,5},{2,10},{6,14},... | collective-permute-start | bytes 2359304 | tf_op jit(solution)/shard_map/ppermute | solution.py:104
  679.3 111.7 %collective-permute-start.28 = (bf16[2,2,2,96,1280]{4,3,1,2,0:T(8,128)(2,1)S(1)}, bf16[2,2,2,96,1280]{4,3,1,2,0:T(8,128)(2,1)S(1)}, u32[]{:S(2)}, u32[]{:S(2)}) collective-permute-start(bf16[2,2,2,96,1280]{4,3,1,2,0:T(8,128)(2,1)S(1)} %bitcast.832), channel_id=1, source_target_pairs={{0,4},{4,0},{8,12},{12,8},{1,5},{5,1},{9,13},{13,9},{2,6},{6,2},{1... | collective-permute-start | bytes 5898248 | tf_op jit(solution)/shard_map/ppermute | solution.py:104
  679.9 40.3 %collective-permute-start.58 = (bf16[2,128,1536]{2,1,0:T(8,128)(2,1)S(1)}, bf16[2,128,1536]{2,1,0:T(8,128)(2,1)S(1)}, u32[]{:S(2)}, u32[]{:S(2)}) collective-permute-start(bf16[2,128,1536]{2,1,0:T(8,128)(2,1)S(1)} %dynamic-slice_bitcast_fusion.11), channel_id=1, source_target_pairs={{0,8},{4,12},{8,0},{12,4},{1,9},{5,13},{9,1},{13,5},{2,10},{6,14},... | collective-permute-start | bytes 2359304 | tf_op jit(solution)/shard_map/ppermute | solution.py:104
  688.0 104.1 %collective-permute-start.23 = (bf16[2,2,2,96,1280]{4,3,1,2,0:T(8,128)(2,1)S(1)}, bf16[2,2,2,96,1280]{4,3,1,2,0:T(8,128)(2,1)S(1)}, u32[]{:S(2)}, u32[]{:S(2)}) collective-permute-start(bf16[2,2,2,96,1280]{4,3,1,2,0:T(8,128)(2,1)S(1)} %bitcast.831), channel_id=1, source_target_pairs={{0,4},{4,0},{8,12},{12,8},{1,5},{5,1},{9,13},{13,9},{2,6},{6,2},{1... | collective-permute-start | bytes 5898248 | tf_op jit(solution)/shard_map/ppermute | solution.py:104
  695.7 95.1 %collective-permute-start.34 = (bf16[2,2,96,768]{3,2,1,0:T(8,128)(2,1)S(1)}, bf16[2,2,96,768]{3,2,1,0:T(8,128)(2,1)S(1)}, u32[]{:S(2)}, u32[]{:S(2)}) collective-permute-start(bf16[2,2,96,768]{3,2,1,0:T(8,128)(2,1)S(1)} %dynamic-slice_bitcast_fusion.17), channel_id=1, source_target_pairs={{0,4},{4,0},{8,12},{12,8},{1,5},{5,1},{9,13},{13,9},{2,6},{6,2},{1... | collective-permute-start | bytes 1769480 | tf_op jit(solution)/shard_map/ppermute | solution.py:104
  704.8 167.9 %collective-permute-start.40 = (bf16[96,768]{1,0:T(8,128)(2,1)S(1)}, bf16[96,768]{1,0:T(8,128)(2,1)S(1)}, u32[]{:S(2)}, u32[]{:S(2)}) collective-permute-start(bf16[96,768]{1,0:T(8,128)(2,1)S(1)} %copy-done.95), channel_id=1, source_target_pairs={{0,1},{1,0},{2,3},{3,2},{4,5},{5,4},{6,7},{7,6},{8,9},{9,8},{10,11... | collective-permute-start | bytes 442376 | tf_op jit(solution)/shard_map/ppermute | solution.py:104
  720.2 90.3 %collective-permute-start.50 = (bf16[2,384,512]{2,1,0:T(8,128)(2,1)S(1)}, bf16[2,384,512]{2,1,0:T(8,128)(2,1)S(1)}, u32[]{:S(2)}, u32[]{:S(2)}) collective-permute-start(bf16[2,384,512]{2,1,0:T(8,128)(2,1)S(1)} %get-tuple-element.43), channel_id=1, source_target_pairs={{0,16},{16,0},{1,17},{17,1},{2,18},{18,2},{3,19},{19,3},{4,20},{20... | collective-permute-start | bytes 2359304 | tf_op jit(solution)/shard_map/ppermute | solution.py:93
  807.8 24.6 %collective-permute-start.29 = (bf16[2,2,96,1280]{3,2,0,1:T(8,128)(2,1)S(1)}, bf16[2,2,96,1280]{3,2,0,1:T(8,128)(2,1)S(1)}, u32[]{:S(2)}, u32[]{:S(2)}) collective-permute-start(bf16[2,2,96,1280]{3,2,0,1:T(8,128)(2,1)S(1)} %dynamic-slice_bitcast_fusion.8), channel_id=1, source_target_pairs={{0,8},{4,12},{8,0},{12,4},{1,9},{5,13},{9,1},{13,5},{2,10},{6,14},... | collective-permute-start | bytes 2949128 | tf_op jit(solution)/shard_map/ppermute | solution.py:104
  808.5 44.0 %collective-permute-start.24 = (bf16[2,2,96,1280]{3,2,0,1:T(8,128)(2,1)S(1)}, bf16[2,2,96,1280]{3,2,0,1:T(8,128)(2,1)S(1)}, u32[]{:S(2)}, u32[]{:S(2)}) collective-permute-start(bf16[2,2,96,1280]{3,2,0,1:T(8,128)(2,1)S(1)} %dynamic-slice_bitcast_fusion.9), channel_id=1, source_target_pairs={{0,8},{4,12},{8,0},{12,4},{1,9},{5,13},{9,1},{13,5},{2,10},{6,14},... | collective-permute-start | bytes 2949128 | tf_op jit(solution)/shard_map/ppermute | solution.py:104
  810.5 62.2 %collective-permute-start.36 = (bf16[96,768]{1,0:T(8,128)(2,1)S(1)}, bf16[96,768]{1,0:T(8,128)(2,1)S(1)}, u32[]{:S(2)}, u32[]{:S(2)}) collective-permute-start(bf16[96,768]{1,0:T(8,128)(2,1)S(1)} %dynamic-slice_bitcast_fusion.25), channel_id=1, source_target_pairs={{0,1},{1,0},{2,3},{3,2},{4,5},{5,4},{6,7},{7,6},{8,9},{9,8},{10,11... | collective-permute-start | bytes 442376 | tf_op jit(solution)/shard_map/ppermute | solution.py:104
  (179 other events, 2103.2 us)
Sparse Core Ops, SparseCore 0:
  40.0 43.4 all-gather.4
  105.2 33.3 reduce-scatter.10
  140.8 29.1 all-gather.8
  172.0 29.5 all-gather.6
  225.2 18.4 reduce-scatter.18
  246.0 27.3 reduce-scatter.14
  275.8 27.8 reduce-scatter.12
  320.1 29.1 all-gather.10
  429.1 18.2 reduce-scatter.20
  450.2 27.3 reduce-scatter.16

commit v2 on v1

--- a/solution.py
+++ b/solution.py
@@ -1,6 +1,11 @@
+import functools
+import itertools
+
 import jax
 import jax.numpy as jnp
 from jax import lax
+from jax.experimental import pallas as pl
+from jax.experimental.pallas import tpu as pltpu
 from jax.sharding import PartitionSpec as P
 
 D = 1536
@@ -93,48 +98,226 @@
     return lax.ppermute(array, "section", [(0, 1), (1, 0)])
 
 
-def halved_over(arrays, axis, bit):
-    count = lax.axis_size(axis)
-    mine = (lax.axis_index(axis) >> bit) & 1
-    pairs = [(i, i ^ (1 << bit)) for i in range(count)]
-    results = []
-    for array in arrays:
-        keep = lax.dynamic_index_in_dim(array, mine, 0, keepdims=False)
-        send = lax.dynamic_index_in_dim(array, 1 - mine, 0, keepdims=False)
-        got = lax.ppermute(send, axis, pairs)
-        results.append((keep.astype(jnp.float32) + got.astype(jnp.float32)).astype(jnp.bfloat16))
-    return results
-
-
-def scattered(array, steps):
-    bits = len(steps)
-    shape = array.shape[1:]
-    array = array.reshape((2,) * bits + shape)
-    left = sorted((place for _, _, place in steps))
-    for axis, bit, place in steps:
-        at = left.index(place)
-        (array,) = halved_over([jnp.moveaxis(array, at, 0)], axis, bit)
-        left.remove(place)
-    return array.astype(jnp.float32)
-
-
-def bits_of(count):
-    return count.bit_length() - 1
-
-
-def orders(axes):
-    steps, place = [], 0
-    per_axis = []
-    for axis in axes:
-        count = bits_of(lax.axis_size(axis))
-        own = []
-        for bit in range(count - 1, -1, -1):
-            own.append((axis, bit, place))
-            place += 1
-        per_axis.append(own)
-    first = [s for own in per_axis for s in own]
-    second = [s for own in per_axis for s in reversed(own)]
-    return second, first
+def add_slab(total, arrived):
+    *lead, rows, _ = total.shape
+    step = 16 if rows % 16 == 0 else rows
+    for where in itertools.product(*(range(n) for n in lead)):
+
+        def add(i, carry):
+            at = (*where, pl.ds(pl.multiple_of(i * step, step), step), slice(None))
+            both = total[at].astype(jnp.float32) + arrived[at].astype(jnp.float32)
+            total[at] = both.astype(jnp.bfloat16)
+            return carry
+
+        lax.fori_loop(0, rows // step, add, 0)
+
+
+def sum_scatter_kernel(plan, *refs):
+    lanes, ins, copies = plan
+    sources = refs[:ins]
+    outs = refs[ins : ins + len(lanes)]
+    scratch = list(refs[ins + len(lanes) :])
+    send_sem, recv_sem, local_sem = scratch[-3:]
+    partners = []
+    for lane in lanes:
+        for axis, bits in lane["phases"]:
+            partners += [(axis, bit) for bit in bits if (axis, bit) not in partners]
+    index = {axis: lax.axis_index(axis) for axis, _ in partners}
+    mine = {(axis, bit): (index[axis] >> bit) & 1 for axis, bit in partners}
+    far = {key: index[key[0]] + (1 - 2 * mine[key]) * (1 << key[1]) for key in partners}
+    barrier = pltpu.get_barrier_semaphore()
+    for axis, bit in partners:
+        pl.semaphore_signal(
+            barrier, inc=1, device_id={axis: far[axis, bit]}, device_id_type=pl.DeviceIdType.MESH
+        )
+    pl.semaphore_wait(barrier, len(partners))
+
+    counter = itertools.count()
+
+    def send(source, target, key):
+        number = next(counter)
+        copy = pltpu.make_async_remote_copy(
+            src_ref=source,
+            dst_ref=target,
+            send_sem=send_sem.at[number],
+            recv_sem=recv_sem.at[number],
+            device_id={key[0]: far[key]},
+            device_id_type=pl.DeviceIdType.MESH,
+        )
+        copy.start()
+        return copy
+
+    def place(axis, values):
+        total = 0
+        for bit, value in values.items():
+            total = total + value * (1 << bit)
+        return total
+
+    started = []
+    states = []
+    for number, lane in enumerate(lanes):
+        count = len(lane["buffers"])
+        buffers, scratch = scratch[:count], scratch[count:]
+        source = sources[lane["source"]]
+        if lane["prefix"] is not None:
+            source = source.at[lane["prefix"]]
+        axis, bits = lane["phases"][0]
+        total, arrived = buffers[0], buffers[1:]
+        rest = [bit for bit in bits[1:]]
+        pending = []
+        for choice in itertools.product((0, 1), repeat=len(rest)):
+            values = dict(zip(rest, choice))
+            slot = sum(value << i for i, value in enumerate(choice))
+            far_at = place(axis, {**values, bits[0]: 1 - mine[axis, bits[0]]})
+            here_at = place(axis, {**values, bits[0]: mine[axis, bits[0]]})
+            copy = send(source.at[far_at], arrived[0].at[slot], (axis, bits[0]))
+            pending.append((copy, slot))
+            started.append(copy)
+            states.append((number, here_at, slot, source, total))
+        lane_state = {"total": total, "arrived": arrived, "pending": pending, "rest": rest}
+        lane["state"] = lane_state
+    locals_ = {}
+    for at, (number, here_at, slot, source, total) in enumerate(states):
+        copy = pltpu.make_async_copy(source.at[here_at], total.at[slot], local_sem.at[at])
+        copy.start()
+        locals_[number, slot] = copy
+    longest = max(sum(len(bits) for _, bits in lane["phases"]) for lane in lanes)
+    for step in range(1, longest + 1):
+        for number, lane in enumerate(lanes):
+            state = lane["state"]
+            sizes = [len(bits) for _, bits in lane["phases"]]
+            if step > sum(sizes):
+                continue
+            if step <= sizes[0]:
+                axis, bits = lane["phases"][0]
+                resolved, rest = bits[:step], bits[step:]
+
+                def slot_of(values):
+                    found = 0
+                    for i, bit in enumerate(bits[1:]):
+                        found = found + values.get(bit, mine[axis, bit]) * (1 << i)
+                    return found
+
+                for copy, slot in state["pending"]:
+                    copy.wait_recv()
+                    if step == 1:
+                        locals_[number, slot].wait()
+                state["pending_next"] = []
+                for choice in itertools.product((0, 1), repeat=len(rest)):
+                    values = dict(zip(rest, choice))
+                    got = sum(value << i for i, value in enumerate(choice))
+                    add_slab(
+                        state["total"].at[slot_of(values)], state["arrived"][step - 1].at[got]
+                    )
+                if rest:
+                    following = rest[1:]
+                    for choice in itertools.product((0, 1), repeat=len(following)):
+                        values = dict(zip(following, choice))
+                        got = sum(value << i for i, value in enumerate(choice))
+                        values[rest[0]] = 1 - mine[axis, rest[0]]
+                        copy = send(
+                            state["total"].at[slot_of(values)],
+                            state["arrived"][step].at[got],
+                            (axis, rest[0]),
+                        )
+                        state["pending_next"].append((copy, got))
+                        started.append(copy)
+                final = state["total"].at[slot_of({})] if not rest else None
+            else:
+                axis, bits = lane["phases"][1]
+                done = step - sizes[0]
+                rest = bits[done:]
+                final = state["final"]
+                for copy, _ in state["pending"]:
+                    copy.wait_recv()
+                state["pending_next"] = []
+                for choice in itertools.product((0, 1), repeat=len(rest)):
+                    values = dict(zip(rest, choice))
+                    got = sum(value << i for i, value in enumerate(choice))
+                    at = place(axis, {bit: values.get(bit, mine[axis, bit]) for bit in bits})
+                    add_slab(final.at[at], state["arrived"][step - 1].at[got])
+                if not rest:
+                    at = place(axis, {bit: mine[axis, bit] for bit in bits})
+                    final = final.at[at]
+            if final is not None and step >= sizes[0]:
+                state["final"] = final
+                if step == sum(sizes):
+                    outs[number][...] = final[...]
+                elif step < sum(sizes):
+                    axis, bits = lane["phases"][1]
+                    done = step - sizes[0]
+                    bit, following = bits[done], bits[done + 1 :]
+                    for choice in itertools.product((0, 1), repeat=len(following)):
+                        values = dict(zip(following, choice))
+                        got = sum(value << i for i, value in enumerate(choice))
+                        at = place(
+                            axis,
+                            {
+                                b: values.get(b, 1 - mine[axis, b] if b == bit else mine[axis, b])
+                                for b in bits
+                            },
+                        )
+                        copy = send(final.at[at], state["arrived"][step].at[got], (axis, bit))
+                        state["pending_next"].append((copy, got))
+                        started.append(copy)
+            state["pending"] = state["pending_next"]
+    for copy in started:
+        copy.wait_send()
+
+
+def sum_scatter(arrays, lanes, collective):
+    plans, scratch, shapes, copies, locals_ = [], [], [], 0, 0
+    for source, prefix, phases in lanes:
+        shape = arrays[source].shape
+        if prefix is not None:
+            shape = shape[1:]
+        buffers = [(shape[0] // 2, *shape[1:])]
+        for step in range(1, len(phases[0][1]) + 1):
+            buffers.append((shape[0] >> step, *shape[1:]))
+            copies += shape[0] >> step
+        locals_ += shape[0] // 2
+        if len(phases) > 1:
+            for step in range(1, len(phases[1][1]) + 1):
+                buffers.append((shape[1] >> step, *shape[2:]))
+                copies += shape[1] >> step
+        plans.append({"source": source, "prefix": prefix, "phases": phases, "buffers": buffers})
+        scratch += [pltpu.VMEM(buffer, jnp.bfloat16) for buffer in buffers]
+        shapes.append(jax.ShapeDtypeStruct(shape[-2:], jnp.bfloat16))
+    scratch += [
+        pltpu.SemaphoreType.DMA((copies,)),
+        pltpu.SemaphoreType.DMA((copies,)),
+        pltpu.SemaphoreType.DMA((locals_,)),
+    ]
+    return pl.pallas_call(
+        functools.partial(sum_scatter_kernel, (plans, len(arrays), copies)),
+        out_shape=shapes,
+        in_specs=[pl.BlockSpec(memory_space=pl.ANY)] * len(arrays),
+        out_specs=[pl.BlockSpec(memory_space=pltpu.VMEM)] * len(lanes),
+        scratch_shapes=scratch,
+        compiler_params=pltpu.CompilerParams(
+            collective_id=collective, has_side_effects=True, vmem_limit_bytes=60 * 2**20
+        ),
+    )(*arrays)
+
+
+def bits_of(axis):
+    return list(range(lax.axis_size(axis).bit_length() - 1))
+
+
+def layer_lanes(first):
+    up, down, deep = bits_of("dp"), bits_of("dp")[::-1], bits_of("expert")
+    one, two = [("dp", up)], [("dp", down)]
+    return [
+        (first, 0, one),
+        (first + 1, 0, two),
+        (first, 1, one),
+        (first + 1, 1, two),
+        (first + 2, 0, one),
+        (first + 2, 1, two),
+        (first + 3, None, [("expert", deep), ("dp", up)]),
+        (first + 4, None, [("dp", down), ("expert", deep)]),
+        (first + 5, None, [("dp", up), ("expert", deep)]),
+    ]
 
 
 def attention_forward(inputs, weights, segment_row):
@@ -375,36 +558,33 @@
         input_grads[s] = grad_inputs
         grad_low = grad_inputs.astype(jnp.bfloat16)
 
-    order_a, order_b = orders(("dp",))
-    order_all_a, order_all_b = orders(("dp", "expert"))
-    dp = lax.axis_size("dp")
-    devices = dp * lax.axis_size("expert")
+    dp, deep = lax.axis_size("dp"), lax.axis_size("expert")
+    arrays, lanes = [], []
+    for s in (1, 0):
+        w_gate_grad, w_up_grad, w_down_grad, grad_w_qkv, grad_w_out, small = grads[s]
+        lanes += layer_lanes(len(arrays))
+        for array in (w_gate_grad, w_up_grad, w_down_grad):
+            arrays.append(array.reshape(array.shape[0], dp, array.shape[1] // dp, array.shape[2]))
+        small = jnp.pad(small, ((0, 0), (0, 128 - small.shape[1])))
+        for array in (grad_w_qkv, grad_w_out, small):
+            arrays.append(array.reshape(dp, deep, array.shape[0] // (dp * deep), array.shape[1]))
+        arrays[-3] = jnp.swapaxes(arrays[-3], 0, 1)
+    sums = sum_scatter(arrays, lanes, 0)
     reduced = []
-    for s in (0, 1):
-        w_gate_grad, w_up_grad, w_down_grad, grad_w_qkv, grad_w_out, small = grads[s]
-
-        def by_dp(array):
-            return jnp.moveaxis(
-                array.reshape(array.shape[0], dp, array.shape[1] // dp, array.shape[2]), 1, 0
-            )
-
-        def by_all(array):
-            return array.reshape(devices, array.shape[0] // devices, array.shape[1])
-
+    for piece in (sums[9:], sums[:9]):
         reduced.append(
             (
-                scattered(by_dp(w_gate_grad), order_a),
-                scattered(by_dp(w_up_grad), order_b),
-                scattered(by_dp(w_down_grad), order_a),
-                scattered(by_all(grad_w_qkv), order_all_a),
-                scattered(by_all(grad_w_out), order_all_b),
-                scattered(by_all(small), order_all_a),
+                jnp.stack([piece[0], piece[2]]),
+                jnp.stack([piece[1], piece[3]]),
+                jnp.stack([piece[4], piece[5]]),
+                *piece[6:],
             )
         )
     final = []
     for a, b, dim in zip(reduced[0], reduced[1], (0, 0, 0, 1, 1, None)):
         keep = jnp.where(first, a, b)
-        got = swapped(jnp.where(first, b, a).astype(jnp.bfloat16)).astype(jnp.float32)
+        got = swapped(jnp.where(first, b, a))
+        keep, got = keep.astype(jnp.float32), got.astype(jnp.float32)
         if dim is None:
             final.append(keep + got)
         else:
@@ -435,7 +615,7 @@
         grad_w_qkv[:, heads + kv :],
         grad_w_out,
         small[:, 1],
-        small[:, 2:],
+        small[:, 2 : 2 + experts],
         w_gate_grad,
         w_up_grad,
         w_down_grad,

time: 902 us -> 783 us (0.87)
  waiting for transfers between devices: 387 us -> 111 us
  Pallas kernels: 0 us -> 234 us
  local copies, waits for them, and re-layouts: 105 us -> 63.6 us
  starting transfers between devices: 51.1 us -> 18.4 us
    ppermute x36 -> x0, waiting for transfers between devices: 275 us -> none  [halved_over(): got = lax.ppermute(send, axis, pairs)]
    pallas_call x0 -> x1, Pallas kernels: none -> 234 us  [sum_scatter(): pl.pallas_call(functools.partial(sum_scatter_kernel, (plans, len(arrays),...]
    ppermute x36 -> x0, starting transfers between devices: 32.5 us -> none  [halved_over(): got = lax.ppermute(send, axis, pairs)]
    reshape x8 -> x2, local copies, waits for them, and re-layouts: 31.7 us -> 4.45 us  [body(): array.reshape(dp, deep, array.shape[0] // (dp * deep), array.shape[1])]
    convert_element_type x30 -> x0, other arithmetic: 17.6 us -> none  [the longest x24 12.8 us: halved_over(): (keep.astype(jnp.float32) + got.astype(jnp.float32)).astype(jnp.bfloat16)]
    squeeze x34 -> x0, local copies, waits for them, and re-layouts: 17.5 us -> none  [halved_over(): send = lax.dynamic_index_in_dim(array, 1 - mine, 0, keepdims=False)]
    convert_element_type x0 -> x4, local copies, waits for them, and re-layouts: none -> 17 us  [the longest x2 9.37 us: body(): w_gate_grad = jnp.einsum('td,etf->edf', rows_both, both[1], preferred_ele...]
    reduce_scatter x4, waiting for transfers between devices: 62 us -> 48.9 us  [sum_rows(): lax.psum_scatter(partial, 'expert', scatter_dimension=0, tiled=True)]
  transfers between devices with their start and end apart: 73 -> 37, of which waited for: 29 -> 10; matrix products, arithmetic and copies ran while one was open for 39% -> 40% of each run, Pallas kernels for 0% -> 0%
where the time goes in v2:
time: 783 us; the launch traced here: 775 us
  Pallas kernels  234 us (30%)
  matrix products  210 us (27%)
  waiting for transfers between devices  111 us (14%)
  local copies, waits for them, and re-layouts  63.6 us (8%)
  blocking collectives  61.6 us (8%)
  other arithmetic  60.6 us (8%)
  starting transfers between devices  18.4 us (2%)
  between operations  16.6 us (2%)
    pallas_call x1, Pallas kernels, sum_scatter(): pl.pallas_call(functools.partial(sum_scatter_kernel, (plans, len(arrays),...  234 us
    reduce_scatter x4, waiting for transfers between devices, sum_rows(): lax.psum_scatter(partial, 'expert', scatter_dimension=0, tiled=True)  48.9 us
    all_gather x4, waiting for transfers between devices, gather_rows(): return lax.all_gather(rows, 'expert', axis=0, tiled=True)  42.5 us
    psum x1, blocking collectives, body(): count_all, prob_all = lax.psum((counts, jnp.stack(probabilities)), axes)  40.1 us
    dot_general x12, matrix products, matmul(): return jnp.dot(left_side, right_side, preferred_element_type=jnp.float32)  31.8 us
    dot_general x2, matrix products, experts_backward(): jnp.einsum('td,efd->etf', grad_rows, w_down, preferred_element_type=jnp.f...  22 us
    all_gather x1, blocking collectives, body(): routes_all = lax.all_gather(routes_here, 'expert', axis=1, tiled=True)  21.5 us
    dot_general x2, matrix products, experts_forward(): jnp.einsum('td,edf->etf', rows, w_up, preferred_element_type=jnp.float32)  20.6 us
  transfers between devices with their start and end apart: 37, of which 10 were waited for; matrix products, arithmetic and copies ran while one was open for 40% of the time, Pallas kernels for 0%

profile of v2, /device:TPU:0, one launch (start us, length us, event | category | flops | bytes accessed | tf_op | source)
XLA Modules:
  0.0 775.5 jit_solution(11263503617018527783)
XLA Ops:
  12.2 3.1 collective-permute-done
  15.7 4.1 collective-permute-done.6
  24.0 2.8 collective-permute-done.2
  29.2 4.4 fusion.40
  35.8 3.6 multiply_reduce_fusion.7
  41.0 3.6 collective-permute-start.5
  44.6 8.9 %collective-permute-done.5 = s32[96,8]{0,1:T(8,128)S(1)} collective-permute-done((s32[96,8]{0,1:T(8,128)S(1)}, s32[96,8]{0,1:T(8,128)S(1)}, u32[]{:S(2)}, u32[]{:S(2)}) %collective-permute-start.5) | collective-permute-done | bytes 3104 | tf_op jit(solution)/shard_map/ppermute | solution.py:98
  53.8 21.5 %all_gather.15 = s32[2,384,8]{2,0,1:T(2,128)S(1)} all-gather(s32[2,96,8]{2,0,1:T(2,128)S(1)} %copy.180), channel_id=1, replica_groups=mesh['section'=2,'dp'=4,'expert'=4] {'expert'}, dimensions={1}, use_global_device_ids=true | all-gather | bytes 30720 | tf_op jit(solution)/shard_map/all_gather | solution.py:472
  75.5 8.1 %all-gather.5.cloned.1.call-done = bf16[384,1536]{1,0:T(8,128)(2,1)} async-done(((bf16[96,1536]{1,0:T(8,128)(2,1)}), bf16[384,1536]{1,0:T(8,128)(2,1)}) %all-gather.5.cloned.1.call-update) | async-done | bytes 1179664 | tf_op jit(solution)/shard_map/all_gather | solution.py:442
  85.4 6.1 fusion.30
  91.6 8.5 %multiply_convert_fusion.3 = (bf16[4,384,512]{1,2,0:T(8,128)(2,1)S(1)}, f32[4,512,384]{2,1,0:T(8,128)}) fusion(f32[4,384]{1,0:T(4,128)S(1)} %fusion.146, f32[4,512,384]{2,1,0:T(8,128)S(1)} %fusion.30, bf16[384,1536]{1,0:T(8,128)(2,1)} %all-gather.5.cloned.1.call-done, bf16[4,1536,512]{2,1,0:T(8,128)(2,1)} %collective-permute-done.9, pred[]{:T(512)S(6)} %eq.26, ...), kind=kOutput, calls=%fused_computation.74 | convolution fusion | flops 2424569856 | bytes 21633024 | tf_op jit(solution)/shard_map/td,edf->etf/dot_general | solution.py:359
  101.3 3.9 fusion.26
  106.3 32.5 %reduce-scatter.11.cloned.1.call-done = bf16[96,1536]{1,0:T(8,128)(2,1)} async-done(((bf16[384,1536]{1,0:T(8,128)(2,1)}), bf16[96,1536]{1,0:T(8,128)(2,1)}) %reduce-scatter.11.cloned.1.call-update) | async-done | bytes 294928 | tf_op jit(solution)/shard_map/reduce_scatter | solution.py:446
  143.5 6.0 fusion.41
  155.3 5.2 multiply_reduce_fusion.6
  163.0 7.2 all-gather.9.cloned.1.call-done
  172.2 10.1 %fusion.35 = f32[4,512,384]{2,1,0:T(8,128)} fusion(bf16[4,512,1536]{2,1,0:T(8,128)(2,1)} %collective-permute-done.10, pred[]{:T(512)S(6)} %eq.26, bf16[384,1536]{1,0:T(8,128)(2,1)} %all-gather.9.cloned.1.call-done, bf16[1,4,512,1536]{3,2,1,0:T(8,128)(2,1)} %param.27), kind=kOutput, calls=%fused_computation.98 | convolution fusion | flops 2419064832 | bytes 16908288 | tf_op jit(solution)/shard_map/td,efd->etf/dot_general | solution.py:370
  184.3 16.9 %all-gather.7.cloned.1.call-done = bf16[384,1536]{1,0:T(8,128)(2,1)} async-done(((bf16[96,1536]{1,0:T(8,128)(2,1)}), bf16[384,1536]{1,0:T(8,128)(2,1)}) %all-gather.7.cloned.1.call-update) | async-done | bytes 1179664 | tf_op jit(solution)/shard_map/all_gather | solution.py:442
  203.8 8.5 %fusion.32 = f32[4,512,384]{2,1,0:T(8,128)S(1)} fusion(bf16[4,1536,512]{2,1,0:T(8,128)(2,1)} %collective-permute-done.8, pred[]{:T(512)S(6)} %eq.26, bf16[384,1536]{1,0:T(8,128)(2,1)} %all-gather.7.cloned.1.call-done, bf16[1,4,1536,512]{3,2,1,0:T(8,128)(2,1)} %param.25), kind=kOutput, calls=%fused_computation.95 | convolution fusion | flops 2419064832 | bytes 16908288 | tf_op jit(solution)/shard_map/td,edf->etf/dot_general | solution.py:358
  212.3 12.1 %fusion.10 = (bf16[4,384,512]{1,2,0:T(8,128)(2,1)}, f32[4,384]{1,0:T(4,128)S(1)}, bf16[4,384,512]{1,2,0:T(8,128)(2,1)}, bf16[4,384,512]{1,2,0:T(8,128)(2,1)}) fusion(f32[4,512,384]{2,1,0:T(8,128)S(1)} %fusion.32, f32[4,512,384]{2,1,0:T(8,128)S(1)} %copy-done.125, f32[4,384]{1,0:T(4,128)S(1)} %fusion.147, bf16[384,1536]{1,0:T(8,128)(2,1)S(1)} %copy-done.39, ...), kind=kOutput, calls=%fused_computation.51 | convolution fusion | flops 2434005504 | bytes 24784896 | tf_op jit(solution)/shard_map/td,edf->etf/dot_general | solution.py:359
  225.5 6.8 convolution_bitcast_fusion.2
  232.3 8.3 %fusion.25 = bf16[384,1536]{1,0:T(8,128)(2,1)} fusion(f32[384,1536]{1,0:T(8,128)S(1)} %convolution_bitcast_fusion.2, bf16[4,384,512]{1,2,0:T(8,128)(2,1)S(1)} %copy-done.23, bf16[4,1536,512]{2,1,0:T(8,128)(2,1)} %collective-permute-done.8, pred[]{:T(512)S(6)} %eq.26, bf16[1,4,1536,512]{3,2,1,0:T(8,128)(2,1)} %param.25), kind=kOutput, calls=%fused_computation.84 | convolution fusion | flops 2420244480 | bytes 17694720 | tf_op jit(solution)/shard_map/etf,edf->td/dot_general | solution.py:385
  242.5 2.8 pad_maximum_fusion
  248.6 6.9 fusion.27
  257.2 16.4 %reduce-scatter.15.cloned.1.call-done = bf16[96,1536]{1,0:T(8,128)(2,1)} async-done(((bf16[384,1536]{1,0:T(8,128)(2,1)}), bf16[96,1536]{1,0:T(8,128)(2,1)}) %reduce-scatter.15.cloned.1.call-update) | async-done | bytes 294928 | tf_op jit(solution)/shard_map/reduce_scatter | solution.py:446
  277.9 6.3 convolution_convert_fusion.11
  293.8 5.8 fusion.105
  306.5 6.5 convolution_convert_fusion.5
  313.0 5.8 fusion.2
  318.7 5.8 fusion.3
  324.5 10.3 %all-gather.11.cloned.1.call-done = bf16[384,1536]{1,0:T(8,128)(2,1)} async-done(((bf16[96,1536]{1,0:T(8,128)(2,1)}), bf16[384,1536]{1,0:T(8,128)(2,1)}) %all-gather.11.cloned.1.call-update) | async-done | bytes 1179664 | tf_op jit(solution)/shard_map/all_gather | solution.py:442
  334.8 11.8 %fusion.17 = (bf16[4,384,512]{1,2,0:T(8,128)(2,1)}, f32[4,384]{1,0:T(4,128)S(1)}, bf16[4,384,512]{1,2,0:T(8,128)(2,1)}) fusion(f32[4,512,384]{2,1,0:T(8,128)} %get-tuple-element.224, f32[4,512,384]{2,1,0:T(8,128)} %copy-done.124, f32[4,384]{1,0:T(4,128)S(1)} %copy-done.105, bf16[384,1536]{1,0:T(8,128)(2,1)} %all-gather.11.cloned.1.call-done, ...), kind=kOutput, calls=%fused_computation.63 | convolution fusion | flops 2432432640 | bytes 23212032 | tf_op jit(solution)/shard_map/td,efd->etf/dot_general | solution.py:370
  348.0 5.5 convolution_bitcast_fusion
  353.5 6.5 fusion.24
  361.0 4.6 copy.204
  365.6 4.7 copy.205
  380.9 4.1 collective-permute-start.17
  386.1 40.1 %all-reduce.2 = (f32[2,16]{1,0:T(2,128)S(1)}, f32[2,16]{1,0:T(2,128)S(1)}) all-reduce(f32[2,16]{1,0:T(2,128)S(1)} %pad_maximum_fusion.35, f32[2,16]{1,0:T(2,128)S(1)} %copy-done.113), channel_id=1, replica_groups=mesh['section'=2,'dp'=4,'expert'=4] {'section','dp','expert'}, use_global_device_ids=true, to_apply=%region_46.47 | all-reduce | flops 64 | bytes 512 | tf_op jit(solution)/shard_map/psum | solution.py:491
  430.3 4.7 convolution_convert_fusion.10
  447.3 4.2 fusion.95
  453.0 3.8 collective-permute-start.12
  461.1 6.1 fusion.4
  467.3 4.5 fusion.5
  471.8 6.1 convolution_convert_fusion.2
  478.0 4.7 copy.213
  482.7 3.0 copy.214
  486.8 2.8 maximum_select_fusion
  507.1 234.0 %shard_map.237 = (bf16[384,512]{1,0:T(8,128)(2,1)}, bf16[384,512]{1,0:T(8,128)(2,1)}, bf16[384,512]{1,0:T(8,128)(2,1)}, bf16[384,512]{1,0:T(8,128)(2,1)}, bf16[1...) custom-call(bf16[2,4,384,512]{3,2,1,0:T(8,128)(2,1)} %bitcast.583, ...), custom_call_target="tpu_custom_call" | custom-call | tf_op jit(solution)/shard_map/pallas_call | solution.py:291
  (506 shorter events, 148.9 us)
Async XLA Ops:
  7.2 76.4 %all-gather.5.cloned.1.call-start = ((), (), s32[]{:S(2)}) async-start(), calls=%async_computation.6 | async-start | bytes 1474560 | tf_op jit(solution)/shard_map/all_gather | solution.py:442
  7.2 21.9 %collective-permute-start.3 = (bf16[1536,1536]{1,0:T(8,128)(2,1)}, bf16[1536,1536]{1,0:T(8,128)(2,1)}, u32[]{:S(2)}, u32[]{:S(2)}) collective-permute-start(bf16[1536,1536]{1,0:T(8,128)(2,1)} %bitcast.679), channel_id=1, source_target_pairs={{0,16},{16,0},{1,17},{17,1},{2,18},{18,2},{3,19},{19,3},{4,20},{20... | collective-permute-start | bytes 14155784 | tf_op jit(solution)/shard_map/ppermute | solution.py:98
  7.8 26.9 %collective-permute-start.4 = (bf16[1536,1536]{1,0:T(8,128)(2,1)}, bf16[1536,1536]{1,0:T(8,128)(2,1)}, u32[]{:S(2)}, u32[]{:S(2)}) collective-permute-start(bf16[1536,1536]{1,0:T(8,128)(2,1)} %bitcast.580), channel_id=1, source_target_pairs={{0,16},{16,0},{1,17},{17,1},{2,18},{18,2},{3,19},{19,3},{4,20},{20... | collective-permute-start | bytes 14155784 | tf_op jit(solution)/shard_map/ppermute | solution.py:98
  8.6 6.7 collective-permute-start
  9.1 12.3 %collective-permute-start.1 = (bf16[1536,512]{1,0:T(8,128)(2,1)}, bf16[1536,512]{1,0:T(8,128)(2,1)S(1)}, u32[]{:S(2)}, u32[]{:S(2)}) collective-permute-start(bf16[1536,512]{1,0:T(8,128)(2,1)} %bitcast.587), channel_id=1, source_target_pairs={{0,16},{16,0},{1,17},{17,1},{2,18},{18,2},{3,19},{19,3},{4,20},{20... | collective-permute-start | bytes 4718600 | tf_op jit(solution)/shard_map/ppermute | solution.py:98
  9.1 17.8 %collective-permute-start.2 = (bf16[1536,512]{1,0:T(8,128)(2,1)}, bf16[1536,512]{1,0:T(8,128)(2,1)}, u32[]{:S(2)}, u32[]{:S(2)}) collective-permute-start(bf16[1536,512]{1,0:T(8,128)(2,1)} %bitcast.588), channel_id=1, source_target_pairs={{0,16},{16,0},{1,17},{17,1},{2,18},{18,2},{3,19},{19,3},{4,20},{20... | collective-permute-start | bytes 4718600 | tf_op jit(solution)/shard_map/ppermute | solution.py:98
  15.3 4.5 collective-permute-start.6
  19.8 65.6 %collective-permute-start.8 = (bf16[4,1536,512]{2,1,0:T(8,128)(2,1)}, bf16[4,1536,512]{2,1,0:T(8,128)(2,1)}, u32[]{:S(2)}, u32[]{:S(2)}) collective-permute-start(bf16[4,1536,512]{2,1,0:T(8,128)(2,1)} %bitcast.678), channel_id=1, source_target_pairs={{0,16},{16,0},{1,17},{17,1},{2,18},{18,2},{3,19},{19,3},{4,20},{20... | collective-permute-start | bytes 18874376 | tf_op jit(solution)/shard_map/ppermute | solution.py:98
  20.2 19.8 %copy-start.90 = (f32[1536]{0:T(1024)}, f32[1536]{0:T(1024)S(1)}, u32[]{:S(2)}) copy-start(f32[1536]{0:T(1024)S(1)} %get-tuple-element.206) | copy-start | bytes 18436
  21.3 70.2 %collective-permute-start.9 = (bf16[4,1536,512]{2,1,0:T(8,128)(2,1)}, bf16[4,1536,512]{2,1,0:T(8,128)(2,1)}, u32[]{:S(2)}, u32[]{:S(2)}) collective-permute-start(bf16[4,1536,512]{2,1,0:T(8,128)(2,1)} %bitcast.675), channel_id=1, source_target_pairs={{0,16},{16,0},{1,17},{17,1},{2,18},{18,2},{3,19},{19,3},{4,20},{20... | collective-permute-start | bytes 18874376 | tf_op jit(solution)/shard_map/ppermute | solution.py:98
  26.9 73.2 %collective-permute-start.10 = (bf16[4,512,1536]{2,1,0:T(8,128)(2,1)}, bf16[4,512,1536]{2,1,0:T(8,128)(2,1)}, u32[]{:S(2)}, u32[]{:S(2)}) collective-permute-start(bf16[4,512,1536]{2,1,0:T(8,128)(2,1)} %bitcast.670), channel_id=1, source_target_pairs={{0,16},{16,0},{1,17},{17,1},{2,18},{18,2},{3,19},{19,3},{4,20},{20... | collective-permute-start | bytes 18874376 | tf_op jit(solution)/shard_map/ppermute | solution.py:98
  40.8 98.0 %reduce-scatter.11.cloned.1.call-start = ((), (), s32[]{:S(2)}) async-start(), calls=%async_computation.7 | async-start | bytes 1474560 | tf_op jit(solution)/shard_map/reduce_scatter | solution.py:446
  41.0 12.6 %collective-permute-start.5 = (s32[96,8]{0,1:T(8,128)S(1)}, s32[96,8]{0,1:T(8,128)S(1)}, u32[]{:S(2)}, u32[]{:S(2)}) collective-permute-start(s32[96,8]{0,1:T(8,128)S(1)} %fusion.153), channel_id=1, source_target_pairs={{0,16},{16,0},{1,17},{17,1},{2,18},{18,2},{3,19},{19,3},{4,20},{20... | collective-permute-start | bytes 9224 | tf_op jit(solution)/shard_map/ppermute | solution.py:98
  44.5 30.9 %collective-permute-start.7 = (bf16[1536,16]{0,1:T(8,128)(2,1)S(1)}, bf16[1536,16]{0,1:T(8,128)(2,1)S(1)}, u32[]{:S(2)}, u32[]{:S(2)}) collective-permute-start(bf16[1536,16]{0,1:T(8,128)(2,1)S(1)} %bitcast.665), channel_id=1, source_target_pairs={{0,16},{16,0},{1,17},{17,1},{2,18},{18,2},{3,19},{19,3},{4,20},{20... | collective-permute-start | bytes 147464 | tf_op jit(solution)/shard_map/ppermute | solution.py:98
  75.5 96.6 %copy-start.65 = (bf16[1536,16]{0,1:T(8,128)(2,1)}, bf16[1536,16]{0,1:T(8,128)(2,1)S(1)}, u32[]{:S(2)}) copy-start(bf16[1536,16]{0,1:T(8,128)(2,1)S(1)} %get-tuple-element.199) | copy-start | bytes 147460
  105.2 35.5 %copy-start.2 = (bf16[1,1536,512]{2,1,0:T(8,128)(2,1)S(1)}, bf16[1,1536,512]{2,1,0:T(8,128)(2,1)}, u32[]{:S(2)}) copy-start(bf16[1,1536,512]{2,1,0:T(8,128)(2,1)} %param.21) | copy-start | bytes 4718596
  105.2 65.0 %all-gather.9.cloned.1.call-start = ((), (), s32[]{:S(2)}) async-start(), calls=%async_computation.10 | async-start | bytes 1474560 | tf_op jit(solution)/shard_map/all_gather | solution.py:442
  106.0 95.2 %all-gather.7.cloned.1.call-start = ((), (), s32[]{:S(2)}) async-start(), calls=%async_computation.8 | async-start | bytes 1474560 | tf_op jit(solution)/shard_map/all_gather | solution.py:442
  161.0 21.3 %copy-start.106 = (f32[96]{0:T(128)}, f32[96]{0:T(128)S(1)}, u32[]{:S(2)}) copy-start(f32[96]{0:T(128)S(1)} %get-tuple-element.216) | copy-start | bytes 1156
  161.9 93.7 %reduce-scatter.19.cloned.1.call-start = ((), (), s32[]{:S(2)}) async-start(), calls=%async_computation.14 | async-start | bytes 245760
  170.2 136.2 %collective-permute-start.15 = (bf16[384,1536]{1,0:T(8,128)(2,1)}, bf16[384,1536]{1,0:T(8,128)(2,1)}, u32[]{:S(2)}, u32[]{:S(2)}) collective-permute-start(bf16[384,1536]{1,0:T(8,128)(2,1)} %all-gather.9.cloned.1.call-done), channel_id=1, source_target_pairs={{0,16},{16,0},{1,17},{17,1},{2,18},{18,2},{3,19},{19,3},{4,20},{20... | collective-permute-start | bytes 3538952 | tf_op jit(solution)/shard_map/ppermute | solution.py:98
  182.4 278.3 %collective-permute-start.18 = (bf16[384,1536]{1,0:T(8,128)(2,1)}, bf16[384,1536]{1,0:T(8,128)(2,1)}, u32[]{:S(2)}, u32[]{:S(2)}) collective-permute-start(bf16[384,1536]{1,0:T(8,128)(2,1)} %all-gather.5.cloned.1.call-done), channel_id=1, source_target_pairs={{0,16},{16,0},{1,17},{17,1},{2,18},{18,2},{3,19},{19,3},{4,20},{20... | collective-permute-start | bytes 3538952 | tf_op jit(solution)/shard_map/ppermute | solution.py:98
  225.3 48.3 %reduce-scatter.15.cloned.1.call-start = ((), (), s32[]{:S(2)}) async-start(), calls=%async_computation.11 | async-start | bytes 1474560 | tf_op jit(solution)/shard_map/reduce_scatter | solution.py:446
  240.6 63.9 %reduce-scatter.13.cloned.1.call-start = ((), (), s32[]{:S(2)}) async-start(), calls=%async_computation.9 | async-start | bytes 1474560 | tf_op jit(solution)/shard_map/reduce_scatter | solution.py:446
  248.1 25.6 %copy-start.107 = (f32[96]{0:T(128)S(1)}, f32[96]{0:T(128)}, u32[]{:S(2)}) copy-start(f32[96]{0:T(128)} %copy-done.106) | copy-start | bytes 1156
  248.1 58.4 %collective-permute-start.13 = (bf16[3,2,384,512]{2,3,1,0:T(8,128)(2,1)}, bf16[3,2,384,512]{2,3,1,0:T(8,128)(2,1)}, u32[]{:S(2)}, u32[]{:S(2)}) collective-permute-start(bf16[3,2,384,512]{2,3,1,0:T(8,128)(2,1)} %get-tuple-element.152), channel_id=1, source_target_pairs={{0,16},{16,0},{1,17},{17,1},{2,18},{18,2},{3,19},{19,3},{4,20},{20... | collective-permute-start | bytes 7077896 | tf_op jit(solution)/shard_map/ppermute | solution.py:98
  255.5 19.6 %copy-start.121 = (f32[96]{0:T(128)S(1)}, f32[96]{0:T(128)}, u32[]{:S(2)}) copy-start(f32[96]{0:T(128)} %get-tuple-element.215) | copy-start | bytes 1156
  255.5 79.3 %all-gather.11.cloned.1.call-start = ((), (), s32[]{:S(2)}) async-start(), calls=%async_computation.12 | async-start | bytes 1474560 | tf_op jit(solution)/shard_map/all_gather | solution.py:442
  255.6 57.4 %collective-permute-start.14 = (bf16[384,1536]{1,0:T(8,128)(2,1)}, bf16[384,1536]{1,0:T(8,128)(2,1)}, u32[]{:S(2)}, u32[]{:S(2)}) collective-permute-start(bf16[384,1536]{1,0:T(8,128)(2,1)} %all-gather.7.cloned.1.call-done), channel_id=1, source_target_pairs={{0,16},{16,0},{1,17},{17,1},{2,18},{18,2},{3,19},{19,3},{4,20},{20... | collective-permute-start | bytes 3538952 | tf_op jit(solution)/shard_map/ppermute | solution.py:98
  300.6 84.5 %reduce-scatter.21.cloned.1.call-start = ((), (), s32[]{:S(2)}) async-start(), calls=%async_computation.15 | async-start | bytes 245760
  306.4 67.6 %collective-permute-start.11 = (bf16[96,1536]{1,0:T(8,128)(2,1)}, bf16[96,1536]{1,0:T(8,128)(2,1)}, u32[]{:S(2)}, u32[]{:S(2)}) collective-permute-start(bf16[96,1536]{1,0:T(8,128)(2,1)} %get-tuple-element.163), channel_id=1, source_target_pairs={{0,16},{16,0},{1,17},{17,1},{2,18},{18,2},{3,19},{19,3},{4,20},{20... | collective-permute-start | bytes 884744 | tf_op jit(solution)/shard_map/ppermute | solution.py:98
  347.5 80.1 %reduce-scatter.17.cloned.1.call-start = ((), (), s32[]{:S(2)}) async-start(), calls=%async_computation.13 | async-start | bytes 1474560 | tf_op jit(solution)/shard_map/reduce_scatter | solution.py:446
  378.1 49.5 %copy-start.66 = (bf16[1536,16]{0,1:T(8,128)(2,1)S(1)}, bf16[1536,16]{0,1:T(8,128)(2,1)}, u32[]{:S(2)}) copy-start(bf16[1536,16]{0,1:T(8,128)(2,1)} %copy-done.65) | copy-start | bytes 147460
  378.1 49.5 %copy-start.91 = (f32[1536]{0:T(1024)S(1)}, f32[1536]{0:T(1024)}, u32[]{:S(2)}) copy-start(f32[1536]{0:T(1024)} %copy-done.90) | copy-start | bytes 18436
  378.1 49.4 %copy-start.112 = (f32[96]{0:T(128)S(1)}, f32[96]{0:T(128)}, u32[]{:S(2)}) copy-start(f32[96]{0:T(128)} %copy-done.111) | copy-start | bytes 1156
  378.2 50.9 %copy-start.9 = (bf16[96,1536]{1,0:T(8,128)(2,1)S(1)}, bf16[96,1536]{1,0:T(8,128)(2,1)}, u32[]{:S(2)}) copy-start(bf16[96,1536]{1,0:T(8,128)(2,1)} %fusion.102) | copy-start | bytes 884740
  378.2 50.9 %copy-start.123 = (f32[96]{0:T(128)S(1)}, f32[96]{0:T(128)}, u32[]{:S(2)}) copy-start(f32[96]{0:T(128)} %get-tuple-element.211) | copy-start | bytes 1156
  380.9 80.2 %collective-permute-start.17 = (bf16[3,2,384,512]{2,3,1,0:T(8,128)(2,1)}, bf16[3,2,384,512]{2,3,1,0:T(8,128)(2,1)}, u32[]{:S(2)}, u32[]{:S(2)}) collective-permute-start(bf16[3,2,384,512]{2,3,1,0:T(8,128)(2,1)} %get-tuple-element.150), channel_id=1, source_target_pairs={{0,16},{16,0},{1,17},{17,1},{2,18},{18,2},{3,19},{19,3},{4,20},{20... | collective-permute-start | bytes 7077896 | tf_op jit(solution)/shard_map/ppermute | solution.py:98
  385.1 86.7 %collective-permute-start.19 = (bf16[384,1536]{1,0:T(8,128)(2,1)}, bf16[384,1536]{1,0:T(8,128)(2,1)}, u32[]{:S(2)}, u32[]{:S(2)}) collective-permute-start(bf16[384,1536]{1,0:T(8,128)(2,1)} %all-gather.11.cloned.1.call-done), channel_id=1, source_target_pairs={{0,16},{16,0},{1,17},{17,1},{2,18},{18,2},{3,19},{19,3},{4,20},{20... | collective-permute-start | bytes 3538952 | tf_op jit(solution)/shard_map/ppermute | solution.py:98
  453.0 33.8 %collective-permute-start.12 = (f32[96,1536]{1,0:T(8,128)}, f32[96,1536]{1,0:T(8,128)}, u32[]{:S(2)}, u32[]{:S(2)}) collective-permute-start(f32[96,1536]{1,0:T(8,128)} %get-tuple-element.161), channel_id=1, source_target_pairs={{0,16},{16,0},{1,17},{17,1},{2,18},{18,2},{3,19},{19,3},{4,20},{20... | collective-permute-start | bytes 1769480 | tf_op jit(solution)/shard_map/ppermute | solution.py:98
  458.9 30.7 %collective-permute-start.16 = (bf16[96,5120]{1,0:T(8,128)(2,1)}, bf16[96,5120]{1,0:T(8,128)(2,1)}, u32[]{:S(2)}, u32[]{:S(2)}) collective-permute-start(bf16[96,5120]{1,0:T(8,128)(2,1)} %pad_maximum_fusion.4), channel_id=1, source_target_pairs={{0,16},{16,0},{1,17},{17,1},{2,18},{18,2},{3,19},{19,3},{4,20},{20... | collective-permute-start | bytes 2949128 | tf_op jit(solution)/shard_map/ppermute | solution.py:98
  460.6 34.5 %collective-permute-start.20 = (bf16[96,5120]{1,0:T(8,128)(2,1)}, bf16[96,5120]{1,0:T(8,128)(2,1)}, u32[]{:S(2)}, u32[]{:S(2)}) collective-permute-start(bf16[96,5120]{1,0:T(8,128)(2,1)} %pad_maximum_fusion.5), channel_id=1, source_target_pairs={{0,16},{16,0},{1,17},{17,1},{2,18},{18,2},{3,19},{19,3},{4,20},{20... | collective-permute-start | bytes 2949128 | tf_op jit(solution)/shard_map/ppermute | solution.py:98
  742.1 8.9 %collective-permute-start.21 = (bf16[96,128]{1,0:T(8,128)(2,1)S(1)}, bf16[96,128]{1,0:T(8,128)(2,1)S(1)}, u32[]{:S(2)}, u32[]{:S(2)}) collective-permute-start(bf16[96,128]{1,0:T(8,128)(2,1)S(1)} %broadcast_select_fusion.55), channel_id=1, source_target_pairs={{0,16},{16,0},{1,17},{17,1},{2,18},{18,2},{3,19},{19,3},{4,20},{20... | collective-permute-start | bytes 73736 | tf_op jit(solution)/shard_map/ppermute | solution.py:98
  743.8 11.1 %collective-permute-start.22 = (bf16[96,1280]{1,0:T(8,128)(2,1)}, bf16[96,1280]{1,0:T(8,128)(2,1)}, u32[]{:S(2)}, u32[]{:S(2)}) collective-permute-start(bf16[96,1280]{1,0:T(8,128)(2,1)} %broadcast_select_fusion.49), channel_id=1, source_target_pairs={{0,16},{16,0},{1,17},{17,1},{2,18},{18,2},{3,19},{19,3},{4,20},{20... | collective-permute-start | bytes 737288 | tf_op jit(solution)/shard_map/ppermute | solution.py:98
  745.9 7.1 collective-permute-start.23
  748.4 9.3 %collective-permute-start.24 = (bf16[2,384,512]{2,1,0:T(8,128)(2,1)}, bf16[2,384,512]{2,1,0:T(8,128)(2,1)}, u32[]{:S(2)}, u32[]{:S(2)}) collective-permute-start(bf16[2,384,512]{2,1,0:T(8,128)(2,1)} %broadcast_select_fusion.38), channel_id=1, source_target_pairs={{0,16},{16,0},{1,17},{17,1},{2,18},{18,2},{3,19},{19,3},{4,20},{20... | collective-permute-start | bytes 2359304 | tf_op jit(solution)/shard_map/ppermute | solution.py:98
  749.9 11.4 %collective-permute-start.25 = (bf16[2,384,512]{2,1,0:T(8,128)(2,1)}, bf16[2,384,512]{2,1,0:T(8,128)(2,1)}, u32[]{:S(2)}, u32[]{:S(2)}) collective-permute-start(bf16[2,384,512]{2,1,0:T(8,128)(2,1)} %broadcast_select_fusion.36), channel_id=1, source_target_pairs={{0,16},{16,0},{1,17},{17,1},{2,18},{18,2},{3,19},{19,3},{4,20},{20... | collective-permute-start | bytes 2359304 | tf_op jit(solution)/shard_map/ppermute | solution.py:98
  751.0 13.9 %collective-permute-start.26 = (bf16[2,128,1536]{2,1,0:T(8,128)(2,1)}, bf16[2,128,1536]{2,1,0:T(8,128)(2,1)}, u32[]{:S(2)}, u32[]{:S(2)}) collective-permute-start(bf16[2,128,1536]{2,1,0:T(8,128)(2,1)} %broadcast_select_fusion.34), channel_id=1, source_target_pairs={{0,16},{16,0},{1,17},{17,1},{2,18},{18,2},{3,19},{19,3},{4,20},{20... | collective-permute-start | bytes 2359304 | tf_op jit(solution)/shard_map/ppermute | solution.py:98
  (121 other events, 615.1 us)
Sparse Core Ops, SparseCore 0:
  40.9 42.5 all-gather.4
  105.3 33.4 reduce-scatter.10
  141.0 29.1 all-gather.8
  171.6 29.5 all-gather.6
  225.4 18.4 reduce-scatter.18
  246.2 27.3 reduce-scatter.14
  276.0 27.8 reduce-scatter.12
  305.6 29.1 all-gather.10
  347.6 20.0 reduce-scatter.20
  370.4 27.3 reduce-scatter.16

commit v3 on v2

--- a/solution.py
+++ b/solution.py
@@ -81,12 +81,6 @@
     return jnp.where(allowed[None, None], scores, MASKED)
 
 
-def masked_softmax(logits, mask):
-    highest = jnp.max(jnp.where(mask > 0, logits, MASKED), axis=-1, keepdims=True)
-    exponent = jnp.where(mask > 0, jnp.exp(logits - highest), 0.0)
-    return exponent / jnp.sum(exponent, axis=-1, keepdims=True)
-
-
 def multi_hot(route_rows, experts):
     columns = jnp.arange(experts, dtype=jnp.int32)
     return jnp.sum(
@@ -115,13 +109,16 @@
 def sum_scatter_kernel(plan, *refs):
     lanes, ins, copies = plan
     sources = refs[:ins]
-    outs = refs[ins : ins + len(lanes)]
-    scratch = list(refs[ins + len(lanes) :])
-    send_sem, recv_sem, local_sem = scratch[-3:]
+    stats_in = refs[ins]
+    outs = refs[ins + 1 : ins + 1 + len(lanes)]
+    stats = refs[ins + 1 + len(lanes)]
+    scratch = list(refs[ins + 2 + len(lanes) :])
+    send_sem, recv_sem, local_sem, stats_got, stats_send, stats_recv = scratch[-6:]
     partners = []
     for lane in lanes:
         for axis, bits in lane["phases"]:
             partners += [(axis, bit) for bit in bits if (axis, bit) not in partners]
+    partners.append(("section", 0))
     index = {axis: lax.axis_index(axis) for axis, _ in partners}
     mine = {(axis, bit): (index[axis] >> bit) & 1 for axis, bit in partners}
     far = {key: index[key[0]] + (1 - 2 * mine[key]) * (1 << key[1]) for key in partners}
@@ -153,6 +150,24 @@
             total = total + value * (1 << bit)
         return total
 
+    stats[...] = stats_in[...]
+
+    def sum_stats():
+        for at, key in enumerate(partners):
+            copy = pltpu.make_async_remote_copy(
+                src_ref=stats,
+                dst_ref=stats_got.at[at],
+                send_sem=stats_send.at[at],
+                recv_sem=stats_recv.at[at],
+                device_id={key[0]: far[key]},
+                device_id_type=pl.DeviceIdType.MESH,
+            )
+            copy.start()
+            yield
+            copy.wait()
+            stats[...] += stats_got[at]
+
+    summing = sum_stats()
     started = []
     states = []
     for number, lane in enumerate(lanes):
@@ -184,6 +199,7 @@
     longest = max(sum(len(bits) for _, bits in lane["phases"]) for lane in lanes)
     for step in range(1, longest + 1):
         for number, lane in enumerate(lanes):
+            next(summing, None)
             state = lane["state"]
             sizes = [len(bits) for _, bits in lane["phases"]]
             if step > sum(sizes):
@@ -261,11 +277,13 @@
                         state["pending_next"].append((copy, got))
                         started.append(copy)
             state["pending"] = state["pending_next"]
+    for _ in summing:
+        pass
     for copy in started:
         copy.wait_send()
 
 
-def sum_scatter(arrays, lanes, collective):
+def sum_scatter(arrays, lanes, stats, collective):
     plans, scratch, shapes, copies, locals_ = [], [], [], 0, 0
     for source, prefix, phases in lanes:
         shape = arrays[source].shape
@@ -288,16 +306,24 @@
         pltpu.SemaphoreType.DMA((copies,)),
         pltpu.SemaphoreType.DMA((locals_,)),
     ]
+    hops = 1 + len(bits_of("dp")) + len(bits_of("expert"))
+    scratch += [
+        pltpu.VMEM((hops, *stats.shape), jnp.float32),
+        pltpu.SemaphoreType.DMA((hops,)),
+        pltpu.SemaphoreType.DMA((hops,)),
+    ]
+    shapes.append(jax.ShapeDtypeStruct(stats.shape, jnp.float32))
     return pl.pallas_call(
         functools.partial(sum_scatter_kernel, (plans, len(arrays), copies)),
         out_shape=shapes,
-        in_specs=[pl.BlockSpec(memory_space=pl.ANY)] * len(arrays),
-        out_specs=[pl.BlockSpec(memory_space=pltpu.VMEM)] * len(lanes),
+        in_specs=[pl.BlockSpec(memory_space=pl.ANY)] * len(arrays)
+        + [pl.BlockSpec(memory_space=pltpu.VMEM)],
+        out_specs=[pl.BlockSpec(memory_space=pltpu.VMEM)] * (len(lanes) + 1),
         scratch_shapes=scratch,
         compiler_params=pltpu.CompilerParams(
             collective_id=collective, has_side_effects=True, vmem_limit_bytes=60 * 2**20
         ),
-    )(*arrays)
+    )(*arrays, stats)
 
 
 def bits_of(axis):
@@ -349,43 +375,375 @@
     return state
 
 
-def experts_forward(rows, mask, weights):
-    w_router, w_gate, w_up, w_down = weights[6:]
-    held = w_gate.shape[0]
-    gates = masked_softmax(matmul(rows, w_router), mask)
-    local = lax.dynamic_slice_in_dim(gates, lax.axis_index("expert") * held, held, 1)
-    local = local.T[:, :, None]
-    gate_pre = jnp.einsum("td,edf->etf", rows, w_gate, preferred_element_type=jnp.float32)
-    up_pre = jnp.einsum("td,edf->etf", rows, w_up, preferred_element_type=jnp.float32)
-    gated = (local * (jax.nn.silu(gate_pre) * up_pre)).astype(jnp.bfloat16)
-    partial = jnp.einsum("etf,efd->td", gated, w_down, preferred_element_type=jnp.float32)
-    return partial.astype(jnp.bfloat16), (rows, local, gate_pre, up_pre, gated)
-
-
-def experts_backward(grad_rows, state, weights):
-    w_router, w_gate, w_up, w_down = weights[6:]
-    rows, local, gate_pre, up_pre, gated = state
-    experts = w_router.shape[1]
-    held = w_gate.shape[0]
-    raw = jnp.einsum("td,efd->etf", grad_rows, w_down, preferred_element_type=jnp.float32)
-    sigmoid = jax.nn.sigmoid(gate_pre)
-    silu_gate = gate_pre * sigmoid
-    grad_gates = jnp.sum(raw * (silu_gate * up_pre), axis=-1).T
-    grad_gates = lax.dynamic_update_slice_in_dim(
-        jnp.zeros((grad_gates.shape[0], experts), jnp.float32),
-        grad_gates,
-        lax.axis_index("expert") * held,
-        1,
-    )
-    grad_active = local * raw
-    grad_gate_pre = (grad_active * up_pre * sigmoid * (1.0 + gate_pre * (1.0 - sigmoid))).astype(
-        jnp.bfloat16
-    )
-    grad_up_pre = (grad_active * silu_gate).astype(jnp.bfloat16)
-    partial = jnp.einsum(
-        "etf,edf->td", grad_gate_pre, w_gate, preferred_element_type=jnp.float32
-    ) + jnp.einsum("etf,edf->td", grad_up_pre, w_up, preferred_element_type=jnp.float32)
-    return partial.astype(jnp.bfloat16), grad_gates, grad_gate_pre, grad_up_pre
+MESH = pl.DeviceIdType.MESH
+COLUMNS = 128
+
+
+def move_rows(refs, compute, z, n):
+    sources, held, sums, returned, sems = refs
+    row_send, row_recv, sum_send, sum_recv = sems
+    barrier = pltpu.get_barrier_semaphore()
+    for k in range(1, n):
+        peer = lax.rem(z + k, n)
+        pl.semaphore_signal(barrier, inc=1, device_id={"expert": peer}, device_id_type=MESH)
+    pl.semaphore_wait(barrier, n - 1)
+
+    def row_copy(kind, way, hop, source=None):
+        step = 1 - 2 * way
+        block = jnp.clip(z - step * hop, 0, n - 1)
+        peer = jnp.clip(z + step, 0, n - 1)
+        return pltpu.make_async_remote_copy(
+            src_ref=held[kind].at[block] if source is None else source,
+            dst_ref=held[kind].at[block],
+            send_sem=row_send.at[kind, way, hop],
+            recv_sem=row_recv.at[kind, way, hop],
+            device_id={"expert": peer},
+            device_id_type=MESH,
+        )
+
+    def sends(way, hop):
+        step = 1 - 2 * way
+        block, peer = z - step * hop, z + step
+        return (block >= 0) & (block < n) & (peer >= 0) & (peer < n)
+
+    def arrives(way, hop):
+        block = z - (1 - 2 * way) * (hop + 1)
+        return (block >= 0) & (block < n)
+
+    def start(kind):
+        for way in range(2):
+            @pl.when(sends(way, 0))
+            def _():
+                row_copy(kind, way, 0, sources[kind]).start()
+
+    def take(hop):
+        for kind in range(len(held)):
+            for way in range(2):
+                @pl.when(arrives(way, hop))
+                def _():
+                    row_copy(kind, way, hop).wait_recv()
+
+                @pl.when(sends(way, hop + 1) & (hop + 1 < n - 1))
+                def _():
+                    row_copy(kind, way, hop + 1).start()
+
+    def sum_copy(kind, peer):
+        return pltpu.make_async_remote_copy(
+            src_ref=sums[kind].at[peer],
+            dst_ref=returned[kind].at[z],
+            send_sem=sum_send.at[kind, peer],
+            recv_sem=sum_recv.at[kind, z],
+            device_id={"expert": peer},
+            device_id_type=MESH,
+        )
+
+    def came_back(kind, peer):
+        return pltpu.make_async_remote_copy(
+            src_ref=sums[kind].at[peer],
+            dst_ref=returned[kind].at[peer],
+            send_sem=sum_send.at[kind, peer],
+            recv_sem=sum_recv.at[kind, peer],
+            device_id={"expert": peer},
+            device_id_type=MESH,
+        )
+
+    def run():
+        def turn(k, carry):
+            hop = lax.div(k + 1, 2) - 1
+            block = z + (1 + hop) * (1 - 2 * lax.rem(k, 2))
+
+            @pl.when(lax.rem(k, 2) == 1)
+            def _():
+                take(hop)
+
+            @pl.when((block >= 0) & (block < n))
+            def _():
+                compute(block)
+
+                @pl.when(block != z)
+                def _():
+                    for kind in range(len(sums)):
+                        sum_copy(kind, block).start()
+
+            return carry
+
+        lax.fori_loop(0, 2 * n - 1, turn, 0)
+
+    def finish():
+        for kind in range(len(held)):
+            for way in range(2):
+                for hop in range(n - 1):
+                    @pl.when(sends(way, hop))
+                    def _():
+                        row_copy(kind, way, hop).wait_send()
+        for kind in range(len(sums)):
+            for k in range(1, n):
+                sum_copy(kind, lax.rem(z + k, n)).wait_send()
+
+    def collect(kind, k):
+        peer = lax.rem(z + k, n)
+        came_back(kind, peer).wait_recv()
+        return peer
+
+    return start, run, collect, finish
+
+
+def fetch_weights(layer, own, other, places, sem):
+    count = places[0].shape[0]
+    mine = lax.axis_index("section") == layer
+
+    def copy(group, kind, e):
+        return pltpu.make_async_copy(
+            group[kind].at[e], places[kind].at[e], sem.at[kind * count + e]
+        )
+
+    for kind in range(len(places)):
+        for e in range(count):
+            @pl.when(mine)
+            def _():
+                copy(own, kind, e).start()
+
+            @pl.when(jnp.logical_not(mine))
+            def _():
+                copy(other, kind, e).start()
+
+    def wait():
+        for kind in range(len(places)):
+            for e in range(count):
+                copy(own, kind, e).wait()
+
+    return wait
+
+
+def sigmoid_of(value):
+    return 1.0 / (1.0 + jnp.exp(-value))
+
+
+def column_of(block, column):
+    here = lax.broadcasted_iota(jnp.int32, block.shape, 1) == column
+    return jnp.sum(jnp.where(here, block, 0.0), axis=1, keepdims=True)
+
+
+def experts_forward_kernel(
+    layer, experts, x, mask, hidden, router, *refs
+):
+    own, other, refs = refs[:3], refs[3:6], refs[6:]
+    out, rows, gates, gate_keep, up_keep, gated, stats = refs[:7]
+    w_gate, w_up, w_down, sums, returned, mixed, total = refs[7:14]
+    weight_sem, *sems = refs[14:]
+    n, held = rows.shape[0], w_gate.shape[0]
+    z = lax.axis_index("expert")
+
+    def compute(block):
+        picked = rows[block]
+        gate_block = gates[block]
+
+        def one(e, carry):
+            gate_pre = jnp.dot(picked, w_gate[e], preferred_element_type=jnp.float32)
+            up_pre = jnp.dot(picked, w_up[e], preferred_element_type=jnp.float32)
+            gate_keep[e, block] = gate_pre.astype(jnp.bfloat16)
+            up_keep[e, block] = up_pre.astype(jnp.bfloat16)
+            active = gate_pre * sigmoid_of(gate_pre) * up_pre
+            share = (column_of(gate_block, z * held + e) * active).astype(jnp.bfloat16)
+            gated[e, block] = share
+            mixed[e] = share
+            return carry
+
+        lax.fori_loop(0, held, one, 0)
+        width = out.shape[1] // 3
+        for part in range(3):
+            at = pl.ds(part * width, width)
+            result = jnp.zeros((out.shape[0], width), jnp.float32)
+            for e in range(held):
+                result += jnp.dot(mixed[e], w_down[e, :, at], preferred_element_type=jnp.float32)
+
+            @pl.when(block == z)
+            def _():
+                total[:, at] = hidden[:, at] + result
+
+            @pl.when(block != z)
+            def _():
+                sums[block, :, at] = result.astype(jnp.bfloat16)
+
+    own_gates = gates.at[z]
+    start, run, collect, finish = move_rows(
+        ((x, own_gates), (rows, gates), (sums,), (returned,), sems), compute, z, n
+    )
+    start(0)
+    wait_weights = fetch_weights(layer, own, other, (w_gate, w_up, w_down), weight_sem)
+    logits = jnp.dot(x[...], router[...], preferred_element_type=jnp.float32)
+    chosen = mask[...] > 0
+    highest = jnp.max(jnp.where(chosen, logits, MASKED), axis=1, keepdims=True)
+    exponent = jnp.where(chosen, jnp.exp(logits - highest), 0.0)
+    own_gates[...] = exponent / jnp.sum(exponent, axis=1, keepdims=True)
+    start(1)
+    real = lax.broadcasted_iota(jnp.int32, logits.shape, 1) < experts
+    highest = jnp.max(jnp.where(real, logits, MASKED), axis=1, keepdims=True)
+    exponent = jnp.where(real, jnp.exp(logits - highest), 0.0)
+    chance = exponent / jnp.sum(exponent, axis=1, keepdims=True)
+    line = lax.broadcasted_iota(jnp.int32, stats.shape, 0)
+    stats[...] = jnp.where(
+        line == 0,
+        jnp.sum(chance, axis=0, keepdims=True),
+        jnp.where(line == 1, jnp.sum(mask[...], axis=0, keepdims=True), 0.0),
+    )
+    rows[z] = x[...]
+    wait_weights()
+    run()
+    for k in range(1, n):
+        peer = collect(0, k)
+        total[...] += returned[peer].astype(jnp.float32)
+    out[...] = total[...].astype(jnp.bfloat16)
+    finish()
+
+
+def experts_backward_kernel(layer, grad, gates, gate_keep, up_keep, *refs):
+    own, other, refs = refs[:3], refs[3:6], refs[6:]
+    out, out_gates, rows, grad_gate, grad_up = refs[:5]
+    w_gate, w_up, w_down, sums, sum_gates, returned, returned_gates = refs[5:12]
+    weight_sem, *sems = refs[12:]
+    n, held = rows.shape[0], w_gate.shape[0]
+    z = lax.axis_index("expert")
+    turned_dims = (((1,), (1,)), ((), ()))
+
+    def compute(block):
+        picked = rows[block]
+        gate_block = gates[block]
+        sum_gates[block] = jnp.zeros(sum_gates.shape[1:], jnp.float32)
+
+        def one(e, carry):
+            raw = lax.dot_general(
+                picked, w_down[e], turned_dims, preferred_element_type=jnp.float32
+            )
+            gate_pre = gate_keep[e, block].astype(jnp.float32)
+            up_pre = up_keep[e, block].astype(jnp.float32)
+            sigmoid = sigmoid_of(gate_pre)
+            silu = gate_pre * sigmoid
+            column = z * held + e
+            dot = jnp.sum(raw * (silu * up_pre), axis=1, keepdims=True)
+            here = lax.broadcasted_iota(jnp.int32, sum_gates.shape[1:], 1) == column
+            sum_gates[block] += jnp.where(here, dot, 0.0)
+            active = column_of(gate_block, column) * raw
+            grad_gate[e, block] = (
+                active * up_pre * sigmoid * (1.0 + gate_pre * (1.0 - sigmoid))
+            ).astype(jnp.bfloat16)
+            grad_up[e, block] = (active * silu).astype(jnp.bfloat16)
+            return carry
+
+        lax.fori_loop(0, held, one, 0)
+        width = out.shape[1] // 3
+        for part in range(3):
+            at = pl.ds(part * width, width)
+            result = jnp.zeros((out.shape[0], width), jnp.float32)
+            for e in range(held):
+                for left, right in ((grad_gate, w_gate), (grad_up, w_up)):
+                    result += lax.dot_general(
+                        left[e, block],
+                        right[e, at, :],
+                        turned_dims,
+                        preferred_element_type=jnp.float32,
+                    )
+
+            @pl.when(block == z)
+            def _():
+                out[:, at] = result
+
+            @pl.when(block != z)
+            def _():
+                sums[block, :, at] = result.astype(jnp.bfloat16)
+
+    start, run, collect, finish = move_rows(
+        ((grad,), (rows,), (sums, sum_gates), (returned, returned_gates), sems), compute, z, n
+    )
+    start(0)
+    wait_weights = fetch_weights(layer, own, other, (w_gate, w_up, w_down), weight_sem)
+    rows[z] = grad[...]
+    wait_weights()
+    run()
+    out_gates[...] = sum_gates[z]
+    for k in range(1, n):
+        peer = collect(0, k)
+        out[...] += returned[peer].astype(jnp.float32)
+        peer = collect(1, k)
+        out_gates[...] += returned_gates[peer]
+    finish()
+
+
+def exchange_scratch(n, kinds_out, kinds_back):
+    return [
+        pltpu.SemaphoreType.DMA((kinds_out, 2, n)),
+        pltpu.SemaphoreType.DMA((kinds_out, 2, n)),
+        pltpu.SemaphoreType.DMA((kinds_back, n)),
+        pltpu.SemaphoreType.DMA((kinds_back, n)),
+    ]
+
+
+def expert_call(kernel, operands, own, other, shapes, scratch, collective):
+    vmem, free = pl.BlockSpec(memory_space=pltpu.VMEM), pl.BlockSpec(memory_space=pl.ANY)
+    weights = [pltpu.VMEM(array.shape, jnp.bfloat16) for array in own]
+    return pl.pallas_call(
+        kernel,
+        out_shape=shapes,
+        in_specs=[vmem] * len(operands) + [free] * 6,
+        out_specs=[vmem] * len(shapes),
+        scratch_shapes=weights + scratch,
+        compiler_params=pltpu.CompilerParams(
+            collective_id=collective, has_side_effects=True, vmem_limit_bytes=50 * 2**20
+        ),
+    )(*operands, *own, *other)
+
+
+def experts_forward(layer, normed_two, mask, hidden, router, own, other, experts):
+    n, held = lax.axis_size("expert"), own[0].shape[0]
+    length, width = normed_two.shape
+    inner = own[0].shape[2]
+    low, full = jnp.bfloat16, jnp.float32
+    kept = jax.ShapeDtypeStruct((held, n, length, inner), low)
+    shapes = [
+        jax.ShapeDtypeStruct((length, width), low),
+        jax.ShapeDtypeStruct((n, length, width), low),
+        jax.ShapeDtypeStruct((n, length, COLUMNS), full),
+        kept,
+        kept,
+        kept,
+        jax.ShapeDtypeStruct((8, COLUMNS), full),
+    ]
+    scratch = [
+        pltpu.VMEM((n, length, width), low),
+        pltpu.VMEM((n, length, width), low),
+        pltpu.VMEM((held, length, inner), low),
+        pltpu.VMEM((length, width), full),
+        pltpu.SemaphoreType.DMA((3 * held,)),
+    ] + exchange_scratch(n, 2, 1)
+    kernel = functools.partial(experts_forward_kernel, layer, experts)
+    return expert_call(
+        kernel, (normed_two, mask, hidden, router), own, other, shapes, scratch, 1 + layer
+    )
+
+
+def experts_backward(layer, grad_low, gates, gate_keep, up_keep, own, other):
+    held, n, length, inner = gate_keep.shape
+    width = grad_low.shape[1]
+    low, full = jnp.bfloat16, jnp.float32
+    kept = jax.ShapeDtypeStruct((held, n, length, inner), low)
+    shapes = [
+        jax.ShapeDtypeStruct((length, width), full),
+        jax.ShapeDtypeStruct((length, COLUMNS), full),
+        jax.ShapeDtypeStruct((n, length, width), low),
+        kept,
+        kept,
+    ]
+    scratch = [
+        pltpu.VMEM((n, length, width), low),
+        pltpu.VMEM((n, length, COLUMNS), full),
+        pltpu.VMEM((n, length, width), low),
+        pltpu.VMEM((n, length, COLUMNS), full),
+        pltpu.SemaphoreType.DMA((3 * held,)),
+    ] + exchange_scratch(n, 1, 2)
+    kernel = functools.partial(experts_backward_kernel, layer)
+    return expert_call(
+        kernel, (grad_low, gates, gate_keep, up_keep), own, other, shapes, scratch, 3 + layer
+    )
 
 
 def attention_backward(grad_hidden, inputs, state, weights):
@@ -438,16 +796,6 @@
     return grad_inputs, grad_gain_attn, grad_qkv, grad_branch
 
 
-def gather_rows(rows):
-    return lax.all_gather(rows, "expert", axis=0, tiled=True)
-
-
-def sum_rows(partial):
-    return lax.psum_scatter(
-        partial, "expert", scatter_dimension=0, tiled=True
-    ).astype(jnp.float32)
-
-
 def turned(left, right):
     return jnp.einsum("tc,tq->cq", left, right, preferred_element_type=jnp.float32)
 
@@ -460,8 +808,8 @@
     own = [array[0] for array in weight_arrays]
     other = [swapped(array) for array in own]
     weights = [
-        [jnp.where(first, a, b) for a, b in zip(own, other)],
-        [jnp.where(first, b, a) for a, b in zip(own, other)],
+        [jnp.where(first, a, b) for a, b in zip(own[:7], other[:7])],
+        [jnp.where(first, b, a) for a, b in zip(own[:7], other[:7])],
     ]
     inputs_low = lax.dynamic_slice_in_dim(tokens, core * SEQ, SEQ, 0)
     grad_low = lax.dynamic_slice_in_dim(cotangent, core * SEQ, SEQ, 0)
@@ -469,55 +817,51 @@
     mine = lax.dynamic_slice_in_dim(routes[0], core * SEQ, SEQ, 0)
     got = swapped(lax.dynamic_slice_in_dim(routes[0], (1 - core) * SEQ, SEQ, 0))
     routes_here = jnp.stack([jnp.where(first, mine, got), jnp.where(first, got, mine)])
-    routes_all = lax.all_gather(routes_here, "expert", axis=1, tiled=True)
-    masks_here = multi_hot(routes_here, experts)
-    masks_all = multi_hot(routes_all, experts)
-
-    saved, outs, probabilities = [], [], []
+    masks = multi_hot(routes_here, COLUMNS)
+    own_experts, other_experts = own[7:], other[7:]
+
+    saved, outs, stats = [], [], []
     for s in range(2):
         inputs = inputs_low.astype(jnp.float32)
         state = attention_forward(inputs, weights[s], segment_row)
         hidden, normed_two = state[7], state[9]
-        logits = matmul(normed_two, weights[s][6])
-        gates = masked_softmax(logits, masks_here[s])
-        probabilities.append(jnp.sum(jax.nn.softmax(logits, axis=-1), axis=0))
-        partial, expert_state = experts_forward(gather_rows(normed_two), masks_all[s], weights[s])
-        inputs_low = (hidden + sum_rows(partial)).astype(jnp.bfloat16)
+        router = jnp.pad(weights[s][6], ((0, 0), (0, COLUMNS - experts)))
+        inputs_low, *expert_state, stat = experts_forward(
+            s, normed_two, masks[s], hidden, router, own_experts, other_experts, experts
+        )
         outs.append(inputs_low)
-        saved.append((inputs, state, gates, expert_state))
-
-    counts = jnp.sum(masks_here, axis=1)
-    axes = ("section", "dp", "expert")
-    count_all, prob_all = lax.psum((counts, jnp.stack(probabilities)), axes)
-    token_total = SEQ * lax.axis_size(axes)
-    balance = experts * (count_all / (token_total * TOPK) * prob_all / token_total)
-    balance = lax.dynamic_index_in_dim(balance, core, 0)
+        stats.append(stat)
+        saved.append((inputs, state, expert_state))
 
     grads = [None, None]
     input_grads = [None, None]
     for s in (1, 0):
-        inputs, state, gates, expert_state = saved[s]
+        inputs, state, expert_state = saved[s]
         (inverse_one, normed_one, _, _, _, _, attended, hidden, inverse_two, normed_two) = state
+        rows_all, gates_all, gate_keep, up_keep, gated = expert_state
         gain_moe, w_router = weights[s][5], weights[s][6]
-        grad_all = gather_rows(grad_low)
-        partial, grad_gates, grad_gate_pre, grad_up_pre = experts_backward(
-            grad_all, expert_state, weights[s]
+        grad_sum, grad_gates, grad_all, grad_gate_pre, grad_up_pre = experts_backward(
+            s, grad_low, gates_all, gate_keep, up_keep, own_experts, other_experts
         )
-        grad_gates = lax.psum_scatter(grad_gates, "expert", scatter_dimension=0, tiled=True)
+        gates = lax.dynamic_index_in_dim(gates_all, lax.axis_index("expert"), 0, keepdims=False)
+        gates, grad_gates = gates[:, :experts], grad_gates[:, :experts]
         grad_chosen = gates * (grad_gates - jnp.sum(gates * grad_gates, axis=-1, keepdims=True))
         grad_logits = grad_chosen.astype(jnp.bfloat16)
-        grad_normed_two = sum_rows(partial) + jnp.einsum(
+        grad_normed_two = grad_sum + jnp.einsum(
             "te,de->td", grad_logits, w_router, preferred_element_type=jnp.float32
         )
         grad_norm_two, grad_gain_moe = norm_back(grad_normed_two, hidden, inverse_two, gain_moe)
         grad_hidden = grad_low.astype(jnp.float32) + grad_norm_two
         half = held // 2
-        stacked = jnp.stack([expert_state[4], grad_gate_pre, grad_up_pre])
+        inner = gated.shape[3]
+        flat = [a.reshape(held, -1, inner) for a in (gated, grad_gate_pre, grad_up_pre)]
+        rows_all, grad_all = rows_all.reshape(-1, D), grad_all.reshape(-1, D)
+        stacked = jnp.stack(flat)
         keep = lax.dynamic_slice_in_dim(stacked, core * half, half, 1)
         send = lax.dynamic_slice_in_dim(stacked, (1 - core) * half, half, 1)
         arrived = swapped(send)
         both = jnp.concatenate([keep, arrived], axis=2)
-        rows_both = jnp.concatenate([expert_state[0], swapped(expert_state[0])], axis=0)
+        rows_both = jnp.concatenate([rows_all, swapped(rows_all)], axis=0)
         grad_both = jnp.concatenate([grad_all, swapped(grad_all)], axis=0)
         w_down_grad = jnp.einsum(
             "etf,td->efd", both[0], grad_both, preferred_element_type=jnp.float32
@@ -569,7 +913,11 @@
         for array in (grad_w_qkv, grad_w_out, small):
             arrays.append(array.reshape(dp, deep, array.shape[0] // (dp * deep), array.shape[1]))
         arrays[-3] = jnp.swapaxes(arrays[-3], 0, 1)
-    sums = sum_scatter(arrays, lanes, 0)
+    *sums, stats = sum_scatter(arrays, lanes, jnp.concatenate(stats, axis=0), 0)
+    stats = lax.dynamic_index_in_dim(stats.reshape(2, 8, COLUMNS), core, 0)
+    token_total = SEQ * lax.axis_size(("section", "dp", "expert"))
+    counts, chances = stats[:, 1, :experts], stats[:, 0, :experts]
+    balance = experts * (counts / (token_total * TOPK) * chances / token_total)
     reduced = []
     for piece in (sums[9:], sums[:9]):
         reduced.append(

time: 783 us -> 799 us (1.020)
  Pallas kernels: 234 us -> 520 us
  matrix products: 210 us -> 103 us
  waiting for transfers between devices: 111 us -> 13.9 us
  blocking collectives: 61.6 us -> 0 us
  local copies, waits for them, and re-layouts: 63.6 us -> 87.8 us
  between operations: 16.6 us -> 3.29 us
  starting transfers between devices: 18.4 us -> 7.74 us
    pallas_call x0 -> x4, Pallas kernels: none -> 232 us  [expert_call(): pl.pallas_call(kernel, out_shape=shapes, in_specs=[vmem] * len(operands)...]
    dot_general x12 -> x0, matrix products: 95.1 us -> none  [the longest x2 22 us: experts_backward(): jnp.einsum('td,efd->etf', grad_rows, w_down, preferred_element_type=jnp.f...]
    pallas_call x1, Pallas kernels: 234 us -> 288 us  [sum_scatter(): pl.pallas_call(functools.partial(sum_scatter_kernel, (plans, len(arrays),...]
    reduce_scatter x4 -> x0, waiting for transfers between devices: 48.9 us -> none  [sum_rows(): lax.psum_scatter(partial, 'expert', scatter_dimension=0, tiled=True)]
    all_gather x4 -> x0, waiting for transfers between devices: 42.5 us -> none  [gather_rows(): return lax.all_gather(rows, 'expert', axis=0, tiled=True)]
    psum x1 -> x0, blocking collectives: 40.1 us -> none  [body(): count_all, prob_all = lax.psum((counts, jnp.stack(probabilities)), axes)]
    all_gather x1 -> x0, blocking collectives: 21.5 us -> none  [body(): routes_all = lax.all_gather(routes_here, 'expert', axis=1, tiled=True)]
    another operation x2 -> x6, local copies, waits for them, and re-layouts: 0.01 us -> 14.7 us  [body(): stacked = jnp.stack(flat)]
  transfers between devices with their start and end apart: 37 -> 27, of which waited for: 10 -> 3; matrix products, arithmetic and copies ran while one was open for 40% -> 19% of each run, Pallas kernels for 0% -> 0%
where the time goes in v3:
time: 799 us; the launch traced here: 791 us
  Pallas kernels  520 us (65%)
  matrix products  103 us (13%)
  local copies, waits for them, and re-layouts  87.8 us (11%)
  other arithmetic  54.8 us (7%)
  waiting for transfers between devices  13.9 us (2%)
    pallas_call x1, Pallas kernels, sum_scatter(): pl.pallas_call(functools.partial(sum_scatter_kernel, (plans, len(arrays),...  288 us
    pallas_call x4, Pallas kernels, expert_call(): pl.pallas_call(kernel, out_shape=shapes, in_specs=[vmem] * len(operands)...  232 us
    dot_general x8, matrix products, matmul(): return jnp.dot(left_side, right_side, preferred_element_type=jnp.float32)  20.2 us
  transfers between devices with their start and end apart: 27, of which 3 were waited for; matrix products, arithmetic and copies ran while one was open for 19% of the time, Pallas kernels for 0%

profile of v3, /device:TPU:0, one launch (start us, length us, event | category | flops | bytes accessed | tf_op | source)
XLA Modules:
  0.0 791.0 jit_solution(9907819090699772383)
XLA Ops:
  9.5 4.9 collective-permute-done.7
  32.1 4.4 fusion.12
  40.7 7.1 collective-permute-done.4
  47.9 3.6 multiply_reduce_fusion.7
  52.2 52.7 %shard_map.237 = (bf16[96,1536]{1,0:T(8,128)(2,1)S(1)}, bf16[4,96,1536]{2,1,0:T(8,128)(2,1)S(1)}, f32[4,96,128]{2,1,0:T(8,128)S(1)}, bf16[4,4,96,512]{3,2,1,0:T(...) custom-call(bf16[96,1536]{1,0:T(8,128)(2,1)S(1)} %multiply_convert_fusion.3.x, ...), custom_call_target="tpu_custom_call" | custom-call | tf_op jit(solution)/shard_map/pallas_call | solution.py:684
  107.5 4.7 fusion.13
  117.2 5.1 multiply_reduce_fusion.6
  122.6 55.4 %shard_map.238 = (bf16[96,1536]{1,0:T(8,128)(2,1)S(1)}, bf16[4,96,1536]{2,1,0:T(8,128)(2,1)S(1)}, f32[4,96,128]{2,1,0:T(8,128)S(1)}, bf16[4,4,96,512]{3,2,1,0:T(...) custom-call(bf16[96,1536]{1,0:T(8,128)(2,1)S(1)} %multiply_convert_fusion.2.x, ...), custom_call_target="tpu_custom_call" | custom-call | tf_op jit(solution)/shard_map/pallas_call | solution.py:684
  179.0 63.7 %shard_map.239 = (f32[96,1536]{1,0:T(8,128)S(1)}, f32[96,128]{1,0:T(8,128)S(1)}, bf16[4,96,1536]{2,1,0:T(8,128)(2,1)S(1)}, bf16[4,4,96,512]{3,2,1,0:T(8,128)(2,1)S(1)}, bf16[4,4,96,512]{3,2,1,0:T(8,128)(2,1)}) custom-call(bf16[96,1536]{1,0:T(8,128)(2,1)S(1)} %copy-done.3, f32[4,96,128]{2,1,0:T(8,128)S(1)} %get-tuple-element.58.gates, ...), custom_call_target="tpu_custom_call" | custom-call | tf_op jit(solution)/shard_map/pallas_call | solution.py:684
  245.3 4.8 convolution_convert_fusion.11
  250.1 1.9 copy.130
  252.0 1.9 multiply_reduce_fusion.1
  259.8 6.3 fusion.71
  266.4 60.5 %shard_map.240 = (f32[96,1536]{1,0:T(8,128)S(1)}, f32[96,128]{1,0:T(8,128)S(1)}, bf16[4,96,1536]{2,1,0:T(8,128)(2,1)}, bf16[4,4,96,512]{3,2,1,0:T(8,128)(2,1)S(1)}, bf16[4,4,96,512]{3,2,1,0:T(8,128)(2,1)}) custom-call(bf16[96,1536]{1,0:T(8,128)(2,1)S(1)} %fusion.68.grad, f32[4,96,128]{2,1,0:T(8,128)S(1)} %get-tuple-element.63.gates, ...), custom_call_target="tpu_custom_call" | custom-call | tf_op jit(solution)/shard_map/pallas_call | solution.py:684
  330.1 2.4 convolution_convert_fusion.10
  339.7 2.0 copy.143
  348.4 1.9 copy.146
  353.9 2.2 fusion.47
  357.4 5.6 fusion.61
  366.4 2.6 copy.151
  369.0 2.6 copy.152
  371.5 2.6 copy.150
  374.1 2.6 pad_maximum_fusion.1
  376.8 2.8 constant_dynamic-slice_fusion.5
  382.8 2.6 copy.140
  385.4 2.8 copy.138
  388.2 2.4 pad_maximum_fusion
  390.6 2.8 constant_dynamic-slice_fusion.11
  399.6 2.3 maximum_select_fusion.1
  402.4 2.5 maximum_select_fusion
  412.2 2.2 copy.187
  414.4 2.2 copy.188
  418.5 2.2 convolution_convert_fusion.8
  420.8 2.2 convolution_convert_fusion.9
  423.1 5.4 fusion.5
  428.5 5.4 fusion.4
  433.9 4.7 copy.154
  438.6 5.0 copy.153
  443.6 6.0 fusion.3
  449.6 4.6 copy.142
  454.2 6.0 fusion.2
  460.2 4.6 copy.141
  464.9 6.5 convolution_convert_fusion.2
  471.4 5.8 convolution_convert_fusion.5
  477.2 288.1 %shard_map.241 = (bf16[384,512]{1,0:T(8,128)(2,1)}, bf16[384,512]{1,0:T(8,128)(2,1)}, bf16[384,512]{1,0:T(8,128)(2,1)}, bf16[384,512]{1,0:T(8,128)(2,1)}, bf16[1...) custom-call(bf16[2,4,384,512]{3,2,1,0:T(8,128)(2,1)} %bitcast.400, ...), custom_call_target="tpu_custom_call" | custom-call | tf_op jit(solution)/shard_map/pallas_call | solution.py:316
  765.4 2.5 broadcast_select_fusion.16
  781.4 2.0 maximum_bitcast_fusion.1
  788.5 2.0 maximum_bitcast_fusion
  (519 shorter events, 110.6 us)
Async XLA Ops:
  0.7 14.1 %collective-permute-start.2 = (bf16[1536,512]{1,0:T(8,128)(2,1)}, bf16[1536,512]{1,0:T(8,128)(2,1)S(1)}, u32[]{:S(2)}, u32[]{:S(2)}) collective-permute-start(bf16[1536,512]{1,0:T(8,128)(2,1)} %bitcast.401), channel_id=1, source_target_pairs={{0,16},{16,0},{1,17},{17,1},{2,18},{18,2},{3,19},{19,3},{4,20},{20... | collective-permute-start | bytes 4718600 | tf_op jit(solution)/shard_map/ppermute | solution.py:92
  1.2 16.2 %collective-permute-start.1 = (bf16[1536,512]{1,0:T(8,128)(2,1)}, bf16[1536,512]{1,0:T(8,128)(2,1)S(1)}, u32[]{:S(2)}, u32[]{:S(2)}) collective-permute-start(bf16[1536,512]{1,0:T(8,128)(2,1)} %bitcast.402), channel_id=1, source_target_pairs={{0,16},{16,0},{1,17},{17,1},{2,18},{18,2},{3,19},{19,3},{4,20},{20... | collective-permute-start | bytes 4718600 | tf_op jit(solution)/shard_map/ppermute | solution.py:92
  1.3 30.8 %collective-permute-start.3 = (bf16[1536,1536]{1,0:T(8,128)(2,1)}, bf16[1536,1536]{1,0:T(8,128)(2,1)}, u32[]{:S(2)}, u32[]{:S(2)}) collective-permute-start(bf16[1536,1536]{1,0:T(8,128)(2,1)} %bitcast.482), channel_id=1, source_target_pairs={{0,16},{16,0},{1,17},{17,1},{2,18},{18,2},{3,19},{19,3},{4,20},{20... | collective-permute-start | bytes 14155784 | tf_op jit(solution)/shard_map/ppermute | solution.py:92
  2.4 4.5 collective-permute-start
  3.3 17.6 %copy-start.141 = (bf16[1536]{0:T(1024)(128)(2,1)}, bf16[1536]{0:T(1024)(128)(2,1)S(1)}, u32[]{:S(2)}) copy-start(bf16[1536]{0:T(1024)(128)(2,1)S(1)} %reduce.1) | copy-start | bytes 9220
  3.3 5.6 collective-permute-start.5
  6.9 13.9 %copy-start.146 = (bf16[1536]{0:T(1024)(128)(2,1)}, bf16[1536]{0:T(1024)(128)(2,1)S(1)}, u32[]{:S(2)}) copy-start(bf16[1536]{0:T(1024)(128)(2,1)S(1)} %collective-permute-done) | copy-start | bytes 9220
  7.0 2.3 collective-permute-start.6
  8.9 5.5 collective-permute-start.7
  9.3 42.8 %collective-permute-start.10 = (bf16[4,512,1536]{2,1,0:T(8,128)(2,1)}, bf16[4,512,1536]{2,1,0:T(8,128)(2,1)}, u32[]{:S(2)}, u32[]{:S(2)}) collective-permute-start(bf16[4,512,1536]{2,1,0:T(8,128)(2,1)} %bitcast.385), channel_id=1, source_target_pairs={{0,16},{16,0},{1,17},{17,1},{2,18},{18,2},{3,19},{19,3},{4,20},{20... | collective-permute-start | bytes 18874376 | tf_op jit(solution)/shard_map/ppermute | solution.py:92
  14.4 37.8 %collective-permute-start.8 = (bf16[4,1536,512]{2,1,0:T(8,128)(2,1)}, bf16[4,1536,512]{2,1,0:T(8,128)(2,1)}, u32[]{:S(2)}, u32[]{:S(2)}) collective-permute-start(bf16[4,1536,512]{2,1,0:T(8,128)(2,1)} %bitcast.375), channel_id=1, source_target_pairs={{0,16},{16,0},{1,17},{17,1},{2,18},{18,2},{3,19},{19,3},{4,20},{20... | collective-permute-start | bytes 18874376 | tf_op jit(solution)/shard_map/ppermute | solution.py:92
  15.1 13.6 %copy-start.21 = (bf16[1536,512]{1,0:T(8,128)(2,1)}, bf16[1536,512]{1,0:T(8,128)(2,1)S(1)}, u32[]{:S(2)}) copy-start(bf16[1536,512]{1,0:T(8,128)(2,1)S(1)} %collective-permute-done.2) | copy-start | bytes 4718596
  15.1 37.0 %collective-permute-start.9 = (bf16[4,1536,512]{2,1,0:T(8,128)(2,1)}, bf16[4,1536,512]{2,1,0:T(8,128)(2,1)}, u32[]{:S(2)}, u32[]{:S(2)}) collective-permute-start(bf16[4,1536,512]{2,1,0:T(8,128)(2,1)} %bitcast.380), channel_id=1, source_target_pairs={{0,16},{16,0},{1,17},{17,1},{2,18},{18,2},{3,19},{19,3},{4,20},{20... | collective-permute-start | bytes 18874376 | tf_op jit(solution)/shard_map/ppermute | solution.py:92
  17.4 30.5 %collective-permute-start.4 = (bf16[1536,1536]{1,0:T(8,128)(2,1)}, bf16[1536,1536]{1,0:T(8,128)(2,1)}, u32[]{:S(2)}, u32[]{:S(2)}) collective-permute-start(bf16[1536,1536]{1,0:T(8,128)(2,1)} %bitcast.390), channel_id=1, source_target_pairs={{0,16},{16,0},{1,17},{17,1},{2,18},{18,2},{3,19},{19,3},{4,20},{20... | collective-permute-start | bytes 14155784 | tf_op jit(solution)/shard_map/ppermute | solution.py:92
  52.0 52.9 %copy-start.144 = (f32[96]{0:T(128)}, f32[96]{0:T(128)S(1)}, u32[]{:S(2)}) copy-start(f32[96]{0:T(128)S(1)} %get-tuple-element.213) | copy-start | bytes 1156
  52.0 55.4 %slice-start.4 = ((s8[4718592]{0:T(1024)(128)(4,1)}), s8[4194304]{0:T(1024)(128)(4,1)S(1)}, s32[]{:S(2)}) async-start(s8[4718592]{0:T(1024)(128)(4,1)} %bitcast.483), calls=%async_computation.4 | async-start | bytes 8388608
  52.1 53.7 %copy-start.130 = (f32[1536]{0:T(1024)S(1)}, f32[1536]{0:T(1024)}, u32[]{:S(2)}) copy-start(f32[1536]{0:T(1024)} %get-tuple-element.208) | copy-start | bytes 18436
  52.2 53.8 %copy-start.15 = (bf16[1,1536,512]{2,1,0:T(8,128)(2,1)S(1)}, bf16[1,1536,512]{2,1,0:T(8,128)(2,1)}, u32[]{:S(2)}) copy-start(bf16[1,1536,512]{2,1,0:T(8,128)(2,1)} %param.20) | copy-start | bytes 4718596
  52.2 53.8 %copy-start.22 = (bf16[1536,512]{1,0:T(8,128)(2,1)S(1)}, bf16[1536,512]{1,0:T(8,128)(2,1)}, u32[]{:S(2)}) copy-start(bf16[1536,512]{1,0:T(8,128)(2,1)} %copy-done.21) | copy-start | bytes 4718596
  52.2 55.3 %slice-start.5 = ((s8[4718592]{0:T(1024)(128)(4,1)}), s8[524288]{0:T(1024)(128)(4,1)S(1)}, s32[]{:S(2)}) async-start(s8[4718592]{0:T(1024)(128)(4,1)} %bitcast.483), calls=%async_computation.5 | async-start | bytes 1048576
  122.5 56.4 %copy-start.3 = (bf16[96,1536]{1,0:T(8,128)(2,1)S(1)}, bf16[96,1536]{1,0:T(8,128)(2,1)}, u32[]{:S(2)}) copy-start(bf16[96,1536]{1,0:T(8,128)(2,1)} %constant_dynamic-slice_fusion.13.grad) | copy-start | bytes 884740
  122.6 122.7 %slice-start = ((s8[4718592]{0:T(1024)(128)(4,1)}), s8[4194304]{0:T(1024)(128)(4,1)S(1)}, s32[]{:S(2)}) async-start(s8[4718592]{0:T(1024)(128)(4,1)} %bitcast.391), calls=%async_computation | async-start | bytes 8388608
  178.9 63.7 %copy-start.4 = (bf16[96,1536]{1,0:T(8,128)(2,1)}, bf16[96,1536]{1,0:T(8,128)(2,1)S(1)}, u32[]{:S(2)}) copy-start(bf16[96,1536]{1,0:T(8,128)(2,1)S(1)} %get-tuple-element.57) | copy-start | bytes 884740
  179.0 64.0 %copy-start.32 = (bf16[1536,16]{1,0:T(8,128)(2,1)S(1)}, bf16[1536,16]{1,0:T(8,128)(2,1)}, u32[]{:S(2)}) copy-start(bf16[1536,16]{1,0:T(8,128)(2,1)} %copy-done.31) | copy-start | bytes 147460
  179.0 66.3 %slice-start.1 = ((s8[4718592]{0:T(1024)(128)(4,1)}), s8[524288]{0:T(1024)(128)(4,1)S(1)}, s32[]{:S(2)}) async-start(s8[4718592]{0:T(1024)(128)(4,1)} %bitcast.391), calls=%async_computation.1 | async-start | bytes 1048576
  259.8 70.3 %slice-start.2 = ((s8[4718592]{0:T(1024)(128)(4,1)}), s8[4194304]{0:T(1024)(128)(4,1)S(1)}, s32[]{:S(2)}) async-start(s8[4718592]{0:T(1024)(128)(4,1)} %bitcast.393), calls=%async_computation.2 | async-start | bytes 8388608
  266.4 61.7 %copy-start.30 = (bf16[1536,16]{1,0:T(8,128)(2,1)S(1)}, bf16[1536,16]{1,0:T(8,128)(2,1)}, u32[]{:S(2)}) copy-start(bf16[1536,16]{1,0:T(8,128)(2,1)} %copy-done.29) | copy-start | bytes 147460
  266.4 61.7 %copy-start.145 = (f32[96]{0:T(128)S(1)}, f32[96]{0:T(128)}, u32[]{:S(2)}) copy-start(f32[96]{0:T(128)} %copy-done.144) | copy-start | bytes 1156
  266.4 63.7 %slice-start.3 = ((s8[4718592]{0:T(1024)(128)(4,1)}), s8[524288]{0:T(1024)(128)(4,1)S(1)}, s32[]{:S(2)}) async-start(s8[4718592]{0:T(1024)(128)(4,1)} %bitcast.393), calls=%async_computation.3 | async-start | bytes 1048576
  339.7 10.5 %copy-start.33 = (f32[8,64,3,96]{3,1,2,0:T(8,128)S(1)}, f32[8,64,3,96]{3,1,2,0:T(8,128)}, u32[]{:S(2)}) copy-start(f32[8,64,3,96]{3,1,2,0:T(8,128)} %convolution_multiply_fusion.2) | copy-start | bytes 1769476
  339.7 10.5 %copy-start.56 = (f32[96,32]{0,1:T(8,128)S(1)}, f32[96,32]{0,1:T(8,128)}, u32[]{:S(2)}) copy-start(f32[96,32]{0,1:T(8,128)} %get-tuple-element.218) | copy-start | bytes 36868
  339.7 10.5 %copy-start.59 = (f32[96,32]{0,1:T(8,128)S(1)}, f32[96,32]{0,1:T(8,128)}, u32[]{:S(2)}) copy-start(f32[96,32]{0,1:T(8,128)} %get-tuple-element.219) | copy-start | bytes 36868
  366.4 38.5 %collective-permute-start.20 = (bf16[96,5120]{1,0:T(8,128)(2,1)}, bf16[96,5120]{1,0:T(8,128)(2,1)}, u32[]{:S(2)}, u32[]{:S(2)}) collective-permute-start(bf16[96,5120]{1,0:T(8,128)(2,1)} %pad_maximum_fusion.5), channel_id=1, source_target_pairs={{0,16},{16,0},{1,17},{17,1},{2,18},{18,2},{3,19},{19,3},{4,20},{20... | collective-permute-start | bytes 2949128 | tf_op jit(solution)/shard_map/ppermute | solution.py:92
  379.6 43.4 %collective-permute-start.17 = (bf16[3,2,384,512]{2,3,1,0:T(8,128)(2,1)}, bf16[3,2,384,512]{2,3,1,0:T(8,128)(2,1)}, u32[]{:S(2)}, u32[]{:S(2)}) collective-permute-start(bf16[3,2,384,512]{2,3,1,0:T(8,128)(2,1)} %get-tuple-element.152), channel_id=1, source_target_pairs={{0,16},{16,0},{1,17},{17,1},{2,18},{18,2},{3,19},{19,3},{4,20},{20... | collective-permute-start | bytes 7077896 | tf_op jit(solution)/shard_map/ppermute | solution.py:92
  381.2 24.7 %collective-permute-start.16 = (bf16[96,5120]{1,0:T(8,128)(2,1)}, bf16[96,5120]{1,0:T(8,128)(2,1)}, u32[]{:S(2)}, u32[]{:S(2)}) collective-permute-start(bf16[96,5120]{1,0:T(8,128)(2,1)} %pad_maximum_fusion.4), channel_id=1, source_target_pairs={{0,16},{16,0},{1,17},{17,1},{2,18},{18,2},{3,19},{19,3},{4,20},{20... | collective-permute-start | bytes 2949128 | tf_op jit(solution)/shard_map/ppermute | solution.py:92
  394.7 7.2 collective-permute-start.12
  396.0 2.9 collective-permute-start.11
  398.9 66.0 %collective-permute-start.19 = (bf16[384,1536]{1,0:T(8,128)(2,1)}, bf16[384,1536]{1,0:T(8,128)(2,1)}, u32[]{:S(2)}, u32[]{:S(2)}) collective-permute-start(bf16[384,1536]{1,0:T(8,128)(2,1)} %bitcast.112), channel_id=1, source_target_pairs={{0,16},{16,0},{1,17},{17,1},{2,18},{18,2},{3,19},{19,3},{4,20},{20... | collective-permute-start | bytes 3538952 | tf_op jit(solution)/shard_map/ppermute | solution.py:92
  401.9 21.1 %collective-permute-start.18 = (bf16[384,1536]{1,0:T(8,128)(2,1)S(1)}, bf16[384,1536]{1,0:T(8,128)(2,1)S(1)}, u32[]{:S(2)}, u32[]{:S(2)}) collective-permute-start(bf16[384,1536]{1,0:T(8,128)(2,1)S(1)} %bitcast.367), channel_id=1, source_target_pairs={{0,16},{16,0},{1,17},{17,1},{2,18},{18,2},{3,19},{19,3},{4,20},{20... | collective-permute-start | bytes 3538952 | tf_op jit(solution)/shard_map/ppermute | solution.py:92
  404.9 38.6 %collective-permute-start.13 = (bf16[3,2,384,512]{2,3,1,0:T(8,128)(2,1)}, bf16[3,2,384,512]{2,3,1,0:T(8,128)(2,1)}, u32[]{:S(2)}, u32[]{:S(2)}) collective-permute-start(bf16[3,2,384,512]{2,3,1,0:T(8,128)(2,1)} %get-tuple-element.154), channel_id=1, source_target_pairs={{0,16},{16,0},{1,17},{17,1},{2,18},{18,2},{3,19},{19,3},{4,20},{20... | collective-permute-start | bytes 7077896 | tf_op jit(solution)/shard_map/ppermute | solution.py:92
  405.9 37.6 %collective-permute-start.14 = (bf16[384,1536]{1,0:T(8,128)(2,1)S(1)}, bf16[384,1536]{1,0:T(8,128)(2,1)}, u32[]{:S(2)}, u32[]{:S(2)}) collective-permute-start(bf16[384,1536]{1,0:T(8,128)(2,1)S(1)} %bitcast.372), channel_id=1, source_target_pairs={{0,16},{16,0},{1,17},{17,1},{2,18},{18,2},{3,19},{19,3},{4,20},{20... | collective-permute-start | bytes 3538952 | tf_op jit(solution)/shard_map/ppermute | solution.py:92
  423.0 48.3 %collective-permute-start.15 = (bf16[384,1536]{1,0:T(8,128)(2,1)S(1)}, bf16[384,1536]{1,0:T(8,128)(2,1)}, u32[]{:S(2)}, u32[]{:S(2)}) collective-permute-start(bf16[384,1536]{1,0:T(8,128)(2,1)S(1)} %bitcast.370), channel_id=1, source_target_pairs={{0,16},{16,0},{1,17},{17,1},{2,18},{18,2},{3,19},{19,3},{4,20},{20... | collective-permute-start | bytes 3538952 | tf_op jit(solution)/shard_map/ppermute | solution.py:92
  767.9 15.5 %collective-permute-start.26 = (bf16[2,128,1536]{2,1,0:T(8,128)(2,1)}, bf16[2,128,1536]{2,1,0:T(8,128)(2,1)}, u32[]{:S(2)}, u32[]{:S(2)}) collective-permute-start(bf16[2,128,1536]{2,1,0:T(8,128)(2,1)} %broadcast_select_fusion.16), channel_id=1, source_target_pairs={{0,16},{16,0},{1,17},{17,1},{2,18},{18,2},{3,19},{19,3},{4,20},{20... | collective-permute-start | bytes 2359304 | tf_op jit(solution)/shard_map/ppermute | solution.py:92
  769.0 10.7 %collective-permute-start.25 = (bf16[2,384,512]{2,1,0:T(8,128)(2,1)}, bf16[2,384,512]{2,1,0:T(8,128)(2,1)}, u32[]{:S(2)}, u32[]{:S(2)}) collective-permute-start(bf16[2,384,512]{2,1,0:T(8,128)(2,1)} %broadcast_select_fusion.18), channel_id=1, source_target_pairs={{0,16},{16,0},{1,17},{17,1},{2,18},{18,2},{3,19},{19,3},{4,20},{20... | collective-permute-start | bytes 2359304 | tf_op jit(solution)/shard_map/ppermute | solution.py:92
  770.6 16.3 %collective-permute-start.24 = (bf16[2,384,512]{2,1,0:T(8,128)(2,1)}, bf16[2,384,512]{2,1,0:T(8,128)(2,1)}, u32[]{:S(2)}, u32[]{:S(2)}) collective-permute-start(bf16[2,384,512]{2,1,0:T(8,128)(2,1)} %broadcast_select_fusion.20), channel_id=1, source_target_pairs={{0,16},{16,0},{1,17},{17,1},{2,18},{18,2},{3,19},{19,3},{4,20},{20... | collective-permute-start | bytes 2359304 | tf_op jit(solution)/shard_map/ppermute | solution.py:92
  771.3 3.8 collective-permute-start.23
  771.8 1.4 collective-permute-start.21
  773.1 3.8 collective-permute-start.22
  (143 other events, 452.5 us)

commit v4 on v3

--- a/solution.py
+++ b/solution.py
@@ -123,11 +123,14 @@
     mine = {(axis, bit): (index[axis] >> bit) & 1 for axis, bit in partners}
     far = {key: index[key[0]] + (1 - 2 * mine[key]) * (1 << key[1]) for key in partners}
     barrier = pltpu.get_barrier_semaphore()
-    for axis, bit in partners:
+    peers = [{axis: far[axis, bit]} for axis, bit in partners if axis != "dp"]
+    groups = lax.axis_size("dp")
+    peers += [{"dp": lax.rem(lax.axis_index("dp") + k, groups)} for k in range(1, groups)]
+    for peer in peers:
         pl.semaphore_signal(
-            barrier, inc=1, device_id={axis: far[axis, bit]}, device_id_type=pl.DeviceIdType.MESH
-        )
-    pl.semaphore_wait(barrier, len(partners))
+            barrier, inc=1, device_id=peer, device_id_type=pl.DeviceIdType.MESH
+        )
+    pl.semaphore_wait(barrier, len(peers))
 
     counter = itertools.count()
 
@@ -150,32 +153,53 @@
             total = total + value * (1 << bit)
         return total
 
-    stats[...] = stats_in[...]
-
     def sum_stats():
-        for at, key in enumerate(partners):
-            copy = pltpu.make_async_remote_copy(
-                src_ref=stats,
-                dst_ref=stats_got.at[at],
+        count = lax.axis_size("dp")
+        me = lax.axis_index("dp")
+
+        def copy(at, source, slot, target):
+            return pltpu.make_async_remote_copy(
+                src_ref=source,
+                dst_ref=stats_got.at[slot],
                 send_sem=stats_send.at[at],
-                recv_sem=stats_recv.at[at],
-                device_id={key[0]: far[key]},
+                recv_sem=stats_recv.at[slot],
+                device_id=target,
                 device_id_type=pl.DeviceIdType.MESH,
             )
-            copy.start()
-            yield
-            copy.wait()
-            stats[...] += stats_got[at]
+
+        for k in range(1, count):
+            copy(k, stats_in, me, {"dp": lax.rem(me + k, count)}).start()
+        yield
+        stats[...] = stats_in[...]
+        for k in range(1, count):
+            peer = lax.rem(me + k, count)
+            copy(k, stats_in, peer, {"dp": peer}).wait_recv()
+            stats[...] += stats_got[peer]
+        both = copy(0, stats, count, {"section": far["section", 0]})
+        both.start()
+        yield
+        both.wait()
+        stats[...] += stats_got[count]
+        for k in range(1, count):
+            copy(k, stats_in, me, {"dp": lax.rem(me + k, count)}).wait_send()
 
     summing = sum_stats()
+    next(summing)
     started = []
     states = []
     for number, lane in enumerate(lanes):
         count = len(lane["buffers"])
         buffers, scratch = scratch[:count], scratch[count:]
         source = sources[lane["source"]]
-        if lane["prefix"] is not None:
-            source = source.at[lane["prefix"]]
+        prefix = lane["prefix"]
+        if isinstance(prefix, int):
+            source = source.at[prefix]
+
+        def part(at, source=source, prefix=prefix):
+            if isinstance(prefix, tuple):
+                return source.at[at, :, pl.ds(*prefix)]
+            return source.at[at]
+
         axis, bits = lane["phases"][0]
         total, arrived = buffers[0], buffers[1:]
         rest = [bit for bit in bits[1:]]
@@ -185,21 +209,22 @@
             slot = sum(value << i for i, value in enumerate(choice))
             far_at = place(axis, {**values, bits[0]: 1 - mine[axis, bits[0]]})
             here_at = place(axis, {**values, bits[0]: mine[axis, bits[0]]})
-            copy = send(source.at[far_at], arrived[0].at[slot], (axis, bits[0]))
+            copy = send(part(far_at), arrived[0].at[slot], (axis, bits[0]))
             pending.append((copy, slot))
             started.append(copy)
-            states.append((number, here_at, slot, source, total))
+            states.append((number, part(here_at), slot, total))
         lane_state = {"total": total, "arrived": arrived, "pending": pending, "rest": rest}
         lane["state"] = lane_state
     locals_ = {}
-    for at, (number, here_at, slot, source, total) in enumerate(states):
-        copy = pltpu.make_async_copy(source.at[here_at], total.at[slot], local_sem.at[at])
+    for at, (number, here, slot, total) in enumerate(states):
+        copy = pltpu.make_async_copy(here, total.at[slot], local_sem.at[at])
         copy.start()
         locals_[number, slot] = copy
     longest = max(sum(len(bits) for _, bits in lane["phases"]) for lane in lanes)
     for step in range(1, longest + 1):
+        if step == 2:
+            next(summing)
         for number, lane in enumerate(lanes):
-            next(summing, None)
             state = lane["state"]
             sizes = [len(bits) for _, bits in lane["phases"]]
             if step > sum(sizes):
@@ -287,8 +312,10 @@
     plans, scratch, shapes, copies, locals_ = [], [], [], 0, 0
     for source, prefix, phases in lanes:
         shape = arrays[source].shape
-        if prefix is not None:
+        if isinstance(prefix, int):
             shape = shape[1:]
+        elif prefix is not None:
+            shape = (*shape[:-1], prefix[1])
         buffers = [(shape[0] // 2, *shape[1:])]
         for step in range(1, len(phases[0][1]) + 1):
             buffers.append((shape[0] >> step, *shape[1:]))
@@ -306,7 +333,7 @@
         pltpu.SemaphoreType.DMA((copies,)),
         pltpu.SemaphoreType.DMA((locals_,)),
     ]
-    hops = 1 + len(bits_of("dp")) + len(bits_of("expert"))
+    hops = lax.axis_size("dp") + 1
     scratch += [
         pltpu.VMEM((hops, *stats.shape), jnp.float32),
         pltpu.SemaphoreType.DMA((hops,)),
@@ -330,19 +357,25 @@
     return list(range(lax.axis_size(axis).bit_length() - 1))
 
 
-def layer_lanes(first):
-    up, down, deep = bits_of("dp"), bits_of("dp")[::-1], bits_of("expert")
+def expert_lanes(first, inner):
+    up, down = bits_of("dp"), bits_of("dp")[::-1]
     one, two = [("dp", up)], [("dp", down)]
     return [
-        (first, 0, one),
-        (first + 1, 0, two),
-        (first, 1, one),
+        (first, (0, inner), one),
+        (first, (2 * inner, inner), two),
+        (first, (inner, inner), one),
+        (first, (3 * inner, inner), two),
+        (first + 1, 0, one),
         (first + 1, 1, two),
-        (first + 2, 0, one),
-        (first + 2, 1, two),
-        (first + 3, None, [("expert", deep), ("dp", up)]),
-        (first + 4, None, [("dp", down), ("expert", deep)]),
-        (first + 5, None, [("dp", up), ("expert", deep)]),
+    ]
+
+
+def dense_lanes(first):
+    up, down, deep = bits_of("dp"), bits_of("dp")[::-1], bits_of("expert")
+    return [
+        (first, None, [("expert", deep), ("dp", up)]),
+        (first + 1, None, [("dp", down), ("expert", deep)]),
+        (first + 2, None, [("dp", up), ("expert", deep)]),
     ]
 
 
@@ -379,14 +412,16 @@
 COLUMNS = 128
 
 
-def move_rows(refs, compute, z, n):
+def move_rows(refs, compute, z, n, others):
     sources, held, sums, returned, sems = refs
     row_send, row_recv, sum_send, sum_recv = sems
     barrier = pltpu.get_barrier_semaphore()
     for k in range(1, n):
         peer = lax.rem(z + k, n)
         pl.semaphore_signal(barrier, inc=1, device_id={"expert": peer}, device_id_type=MESH)
-    pl.semaphore_wait(barrier, n - 1)
+    for peer in others:
+        pl.semaphore_signal(barrier, inc=1, device_id=peer, device_id_type=MESH)
+    pl.semaphore_wait(barrier, n - 1 + len(others))
 
     def row_copy(kind, way, hop, source=None):
         step = 1 - 2 * way
@@ -529,8 +564,8 @@
 ):
     own, other, refs = refs[:3], refs[3:6], refs[6:]
     out, rows, gates, gate_keep, up_keep, gated, stats = refs[:7]
-    w_gate, w_up, w_down, sums, returned, mixed, total = refs[7:14]
-    weight_sem, *sems = refs[14:]
+    w_gate, w_up, w_down, sums, returned, mixed, total, stats_all = refs[7:15]
+    weight_sem, *sems = refs[15:]
     n, held = rows.shape[0], w_gate.shape[0]
     z = lax.axis_index("expert")
 
@@ -545,7 +580,8 @@
             up_keep[e, block] = up_pre.astype(jnp.bfloat16)
             active = gate_pre * sigmoid_of(gate_pre) * up_pre
             share = (column_of(gate_block, z * held + e) * active).astype(jnp.bfloat16)
-            gated[e, block] = share
+            inner = share.shape[1]
+            gated[block, :, pl.ds(pl.multiple_of(e * inner, inner), inner)] = share
             mixed[e] = share
             return carry
 
@@ -567,7 +603,11 @@
 
     own_gates = gates.at[z]
     start, run, collect, finish = move_rows(
-        ((x, own_gates), (rows, gates), (sums,), (returned,), sems), compute, z, n
+        ((x, own_gates, stats_all.at[z]), (rows, gates, stats_all), (sums,), (returned,), sems),
+        compute,
+        z,
+        n,
+        [],
     )
     start(0)
     wait_weights = fetch_weights(layer, own, other, (w_gate, w_up, w_down), weight_sem)
@@ -582,14 +622,16 @@
     exponent = jnp.where(real, jnp.exp(logits - highest), 0.0)
     chance = exponent / jnp.sum(exponent, axis=1, keepdims=True)
     line = lax.broadcasted_iota(jnp.int32, stats.shape, 0)
-    stats[...] = jnp.where(
+    stats_all[z] = jnp.where(
         line == 0,
         jnp.sum(chance, axis=0, keepdims=True),
         jnp.where(line == 1, jnp.sum(mask[...], axis=0, keepdims=True), 0.0),
     )
+    start(2)
     rows[z] = x[...]
     wait_weights()
     run()
+    stats[...] = jnp.sum(stats_all[...], axis=0)
     for k in range(1, n):
         peer = collect(0, k)
         total[...] += returned[peer].astype(jnp.float32)
@@ -598,20 +640,56 @@
 
 
 def experts_backward_kernel(layer, grad, gates, gate_keep, up_keep, *refs):
-    own, other, refs = refs[:3], refs[3:6], refs[6:]
-    out, out_gates, rows, grad_gate, grad_up = refs[:5]
-    w_gate, w_up, w_down, sums, sum_gates, returned, returned_gates = refs[5:12]
-    weight_sem, *sems = refs[12:]
-    n, held = rows.shape[0], w_gate.shape[0]
+    own, other, saved_rows, saved_gated, refs = refs[:3], refs[3:6], refs[6], refs[7], refs[8:]
+    out, out_gates, rows_both, gated_both, grad_both, pre_both = refs[:6]
+    w_gate, w_up, w_down, sums, sum_gates, returned, returned_gates, away = refs[6:14]
+    weight_sem, core_send, core_recv, core_local, *sems = refs[14:]
+    n, held = gates.shape[0], w_gate.shape[0]
+    half, inner = held // 2, w_gate.shape[2]
+    core = lax.axis_index("section")
     z = lax.axis_index("expert")
     turned_dims = (((1,), (1,)), ((), ()))
+    rows = grad_both.at[core]
+
+    def to_core(number, source, target):
+        return pltpu.make_async_remote_copy(
+            src_ref=source,
+            dst_ref=target,
+            send_sem=core_send.at[number],
+            recv_sem=core_recv.at[number],
+            device_id={"section": 1 - core},
+            device_id_type=MESH,
+        )
+
+    def block_copies(block):
+        return (
+            to_core(2 + block, rows.at[block], rows.at[block]),
+            to_core(2 + n + block, away.at[block], pre_both.at[core, block]),
+        )
+
+    def columns(at):
+        return pl.ds(pl.multiple_of(at * half * inner, half * inner), half * inner)
+
+    def whole_copies():
+        return (
+            to_core(0, saved_rows, rows_both.at[core]),
+            to_core(1, saved_gated.at[:, :, columns(1 - core)], gated_both.at[core]),
+        )
+
+    def local_copies():
+        return (
+            pltpu.make_async_copy(saved_rows, rows_both.at[core], core_local.at[0]),
+            pltpu.make_async_copy(
+                saved_gated.at[:, :, columns(core)], gated_both.at[core], core_local.at[1]
+            ),
+        )
 
     def compute(block):
         picked = rows[block]
         gate_block = gates[block]
         sum_gates[block] = jnp.zeros(sum_gates.shape[1:], jnp.float32)
 
-        def one(e, carry):
+        def one(e, place, j):
             raw = lax.dot_general(
                 picked, w_down[e], turned_dims, preferred_element_type=jnp.float32
             )
@@ -624,25 +702,39 @@
             here = lax.broadcasted_iota(jnp.int32, sum_gates.shape[1:], 1) == column
             sum_gates[block] += jnp.where(here, dot, 0.0)
             active = column_of(gate_block, column) * raw
-            grad_gate[e, block] = (
+            place[:, pl.ds(pl.multiple_of(j * inner, inner), inner)] = (
                 active * up_pre * sigmoid * (1.0 + gate_pre * (1.0 - sigmoid))
             ).astype(jnp.bfloat16)
-            grad_up[e, block] = (active * silu).astype(jnp.bfloat16)
+            place[:, pl.ds(pl.multiple_of((half + j) * inner, inner), inner)] = (
+                active * silu
+            ).astype(jnp.bfloat16)
+
+        def own_half(j, carry):
+            one(core * half + j, pre_both.at[core, block], j)
             return carry
 
-        lax.fori_loop(0, held, one, 0)
+        def other_half(j, carry):
+            one((1 - core) * half + j, away.at[block], j)
+            return carry
+
+        lax.fori_loop(0, half, other_half, 0)
+        for copy in block_copies(block):
+            copy.start()
+        lax.fori_loop(0, half, own_half, 0)
         width = out.shape[1] // 3
         for part in range(3):
             at = pl.ds(part * width, width)
             result = jnp.zeros((out.shape[0], width), jnp.float32)
-            for e in range(held):
-                for left, right in ((grad_gate, w_gate), (grad_up, w_up)):
-                    result += lax.dot_general(
-                        left[e, block],
-                        right[e, at, :],
-                        turned_dims,
-                        preferred_element_type=jnp.float32,
-                    )
+            for place, side in ((away.at[block], 1 - core), (pre_both.at[core, block], core)):
+                for kind, right in enumerate((w_gate, w_up)):
+                    for j in range(half):
+                        left = place[:, pl.ds((kind * half + j) * inner, inner)]
+                        result += lax.dot_general(
+                            left,
+                            right[side * half + j, at, :],
+                            turned_dims,
+                            preferred_element_type=jnp.float32,
+                        )
 
             @pl.when(block == z)
             def _():
@@ -653,10 +745,16 @@
                 sums[block, :, at] = result.astype(jnp.bfloat16)
 
     start, run, collect, finish = move_rows(
-        ((grad,), (rows,), (sums, sum_gates), (returned, returned_gates), sems), compute, z, n
+        ((grad,), (rows,), (sums, sum_gates), (returned, returned_gates), sems),
+        compute,
+        z,
+        n,
+        [{"section": 1 - core}],
     )
     start(0)
     wait_weights = fetch_weights(layer, own, other, (w_gate, w_up, w_down), weight_sem)
+    for copy in whole_copies() + local_copies():
+        copy.start()
     rows[z] = grad[...]
     wait_weights()
     run()
@@ -667,6 +765,13 @@
         peer = collect(1, k)
         out_gates[...] += returned_gates[peer]
     finish()
+    for copy in local_copies():
+        copy.wait()
+    for copy in whole_copies():
+        copy.wait()
+    for block in range(n):
+        for copy in block_copies(block):
+            copy.wait()
 
 
 def exchange_scratch(n, kinds_out, kinds_back):
@@ -678,19 +783,22 @@
     ]
 
 
-def expert_call(kernel, operands, own, other, shapes, scratch, collective):
+def expert_call(kernel, operands, own, other, extra, shapes, scratch, collective):
     vmem, free = pl.BlockSpec(memory_space=pltpu.VMEM), pl.BlockSpec(memory_space=pl.ANY)
     weights = [pltpu.VMEM(array.shape, jnp.bfloat16) for array in own]
     return pl.pallas_call(
         kernel,
         out_shape=shapes,
-        in_specs=[vmem] * len(operands) + [free] * 6,
+        in_specs=[vmem] * len(operands) + [free] * (6 + len(extra)),
         out_specs=[vmem] * len(shapes),
         scratch_shapes=weights + scratch,
         compiler_params=pltpu.CompilerParams(
             collective_id=collective, has_side_effects=True, vmem_limit_bytes=50 * 2**20
         ),
-    )(*operands, *own, *other)
+        cost_estimate=pl.CostEstimate(
+            flops=5 * 10**10, bytes_accessed=10**8, transcendentals=0
+        ),
+    )(*operands, *own, *other, *extra)
 
 
 def experts_forward(layer, normed_two, mask, hidden, router, own, other, experts):
@@ -705,7 +813,7 @@
         jax.ShapeDtypeStruct((n, length, COLUMNS), full),
         kept,
         kept,
-        kept,
+        jax.ShapeDtypeStruct((n, length, held * inner), low),
         jax.ShapeDtypeStruct((8, COLUMNS), full),
     ]
     scratch = [
@@ -713,36 +821,48 @@
         pltpu.VMEM((n, length, width), low),
         pltpu.VMEM((held, length, inner), low),
         pltpu.VMEM((length, width), full),
+        pltpu.VMEM((n, 8, COLUMNS), full),
         pltpu.SemaphoreType.DMA((3 * held,)),
-    ] + exchange_scratch(n, 2, 1)
+    ] + exchange_scratch(n, 3, 1)
     kernel = functools.partial(experts_forward_kernel, layer, experts)
     return expert_call(
-        kernel, (normed_two, mask, hidden, router), own, other, shapes, scratch, 1 + layer
-    )
-
-
-def experts_backward(layer, grad_low, gates, gate_keep, up_keep, own, other):
+        kernel, (normed_two, mask, hidden, router), own, other, (), shapes, scratch, 1 + layer
+    )
+
+
+def experts_backward(layer, grad_low, gates, gate_keep, up_keep, rows, gated, own, other):
     held, n, length, inner = gate_keep.shape
     width = grad_low.shape[1]
     low, full = jnp.bfloat16, jnp.float32
-    kept = jax.ShapeDtypeStruct((held, n, length, inner), low)
     shapes = [
         jax.ShapeDtypeStruct((length, width), full),
         jax.ShapeDtypeStruct((length, COLUMNS), full),
-        jax.ShapeDtypeStruct((n, length, width), low),
-        kept,
-        kept,
+        jax.ShapeDtypeStruct((2, n, length, width), low),
+        jax.ShapeDtypeStruct((2, n, length, held // 2 * inner), low),
+        jax.ShapeDtypeStruct((2, n, length, width), low),
+        jax.ShapeDtypeStruct((2, n, length, held * inner), low),
     ]
     scratch = [
         pltpu.VMEM((n, length, width), low),
         pltpu.VMEM((n, length, COLUMNS), full),
         pltpu.VMEM((n, length, width), low),
         pltpu.VMEM((n, length, COLUMNS), full),
+        pltpu.VMEM((n, length, held * inner), low),
         pltpu.SemaphoreType.DMA((3 * held,)),
+        pltpu.SemaphoreType.DMA((2 + 2 * n,)),
+        pltpu.SemaphoreType.DMA((2 + 2 * n,)),
+        pltpu.SemaphoreType.DMA((2,)),
     ] + exchange_scratch(n, 1, 2)
     kernel = functools.partial(experts_backward_kernel, layer)
     return expert_call(
-        kernel, (grad_low, gates, gate_keep, up_keep), own, other, shapes, scratch, 3 + layer
+        kernel,
+        (grad_low, gates, gate_keep, up_keep),
+        own,
+        other,
+        (rows, gated),
+        shapes,
+        scratch,
+        3 + layer,
     )
 
 
@@ -804,7 +924,8 @@
     core = lax.axis_index("section")
     first = core == 0
     experts = weight_arrays[6].shape[2]
-    held = weight_arrays[7].shape[1]
+    w_gate = weight_arrays[7]
+    held = w_gate.shape[1]
     own = [array[0] for array in weight_arrays]
     other = [swapped(array) for array in own]
     weights = [
@@ -840,8 +961,26 @@
         (inverse_one, normed_one, _, _, _, _, attended, hidden, inverse_two, normed_two) = state
         rows_all, gates_all, gate_keep, up_keep, gated = expert_state
         gain_moe, w_router = weights[s][5], weights[s][6]
-        grad_sum, grad_gates, grad_all, grad_gate_pre, grad_up_pre = experts_backward(
-            s, grad_low, gates_all, gate_keep, up_keep, own_experts, other_experts
+        grad_sum, grad_gates, rows_both, gated_both, grad_both, pre_both = experts_backward(
+            s,
+            grad_low,
+            gates_all,
+            gate_keep,
+            up_keep,
+            rows_all,
+            gated,
+            own_experts,
+            other_experts,
+        )
+        inner = w_gate.shape[3]
+        grad_gate_up = turned(
+            rows_both.reshape(-1, D), pre_both.reshape(-1, held * inner)
+        ).astype(jnp.bfloat16)
+        grad_down = turned(
+            gated_both.reshape(-1, held // 2 * inner), grad_both.reshape(-1, D)
+        ).astype(jnp.bfloat16)
+        grad_sum, grad_gate_up, grad_down = lax.optimization_barrier(
+            (grad_sum, grad_gate_up, grad_down)
         )
         gates = lax.dynamic_index_in_dim(gates_all, lax.axis_index("expert"), 0, keepdims=False)
         gates, grad_gates = gates[:, :experts], grad_gates[:, :experts]
@@ -852,27 +991,6 @@
         )
         grad_norm_two, grad_gain_moe = norm_back(grad_normed_two, hidden, inverse_two, gain_moe)
         grad_hidden = grad_low.astype(jnp.float32) + grad_norm_two
-        half = held // 2
-        inner = gated.shape[3]
-        flat = [a.reshape(held, -1, inner) for a in (gated, grad_gate_pre, grad_up_pre)]
-        rows_all, grad_all = rows_all.reshape(-1, D), grad_all.reshape(-1, D)
-        stacked = jnp.stack(flat)
-        keep = lax.dynamic_slice_in_dim(stacked, core * half, half, 1)
-        send = lax.dynamic_slice_in_dim(stacked, (1 - core) * half, half, 1)
-        arrived = swapped(send)
-        both = jnp.concatenate([keep, arrived], axis=2)
-        rows_both = jnp.concatenate([rows_all, swapped(rows_all)], axis=0)
-        grad_both = jnp.concatenate([grad_all, swapped(grad_all)], axis=0)
-        w_down_grad = jnp.einsum(
-            "etf,td->efd", both[0], grad_both, preferred_element_type=jnp.float32
-        ).astype(jnp.bfloat16)
-        w_gate_grad = jnp.einsum(
-            "td,etf->edf", rows_both, both[1], preferred_element_type=jnp.float32
-        ).astype(jnp.bfloat16)
-        w_up_grad = jnp.einsum(
-            "td,etf->edf", rows_both, both[2], preferred_element_type=jnp.float32
-        ).astype(jnp.bfloat16)
-
         grad_inputs, grad_gain_attn, grad_qkv, grad_branch = attention_backward(
             grad_hidden, inputs, state, weights[s]
         )
@@ -898,17 +1016,28 @@
         small = jnp.concatenate(
             [grad_gain_attn[:, None], grad_gain_moe[:, None], grad_w_router], axis=1
         ).astype(jnp.bfloat16)
-        grads[s] = (w_gate_grad, w_up_grad, w_down_grad, grad_w_qkv, grad_w_out, small)
+        grads[s] = (grad_gate_up, grad_down, grad_w_qkv, grad_w_out, small)
         input_grads[s] = grad_inputs
         grad_low = grad_inputs.astype(jnp.bfloat16)
 
     dp, deep = lax.axis_size("dp"), lax.axis_size("expert")
+    half, inner = held // 2, w_gate.shape[3]
+    grad_gate_up, grad_down = grads[1][:2]
+    second_pre = lax.psum_scatter(grad_gate_up, "dp", scatter_dimension=0, tiled=True)
+    second_down = [
+        lax.psum_scatter(
+            grad_down[j * inner : (j + 1) * inner], "dp", scatter_dimension=0, tiled=True
+        )
+        for j in range(half)
+    ]
     arrays, lanes = [], []
-    for s in (1, 0):
-        w_gate_grad, w_up_grad, w_down_grad, grad_w_qkv, grad_w_out, small = grads[s]
-        lanes += layer_lanes(len(arrays))
-        for array in (w_gate_grad, w_up_grad, w_down_grad):
-            arrays.append(array.reshape(array.shape[0], dp, array.shape[1] // dp, array.shape[2]))
+    for s in (0, 1):
+        grad_gate_up, grad_down, grad_w_qkv, grad_w_out, small = grads[s]
+        if s == 0:
+            lanes += expert_lanes(len(arrays), inner)
+            arrays.append(grad_gate_up.reshape(dp, D // dp, held * inner))
+            arrays.append(grad_down.reshape(half, dp, inner // dp, D))
+        lanes += dense_lanes(len(arrays))
         small = jnp.pad(small, ((0, 0), (0, 128 - small.shape[1])))
         for array in (grad_w_qkv, grad_w_out, small):
             arrays.append(array.reshape(dp, deep, array.shape[0] // (dp * deep), array.shape[1]))
@@ -918,16 +1047,16 @@
     token_total = SEQ * lax.axis_size(("section", "dp", "expert"))
     counts, chances = stats[:, 1, :experts], stats[:, 0, :experts]
     balance = experts * (counts / (token_total * TOPK) * chances / token_total)
-    reduced = []
-    for piece in (sums[9:], sums[:9]):
-        reduced.append(
-            (
-                jnp.stack([piece[0], piece[2]]),
-                jnp.stack([piece[1], piece[3]]),
-                jnp.stack([piece[4], piece[5]]),
-                *piece[6:],
-            )
-        )
+    first_experts = (
+        jnp.stack([sums[0], sums[2]]),
+        jnp.stack([sums[1], sums[3]]),
+        jnp.stack([sums[4], sums[5]]),
+    )
+    columns = [second_pre[:, i * inner : (i + 1) * inner] for i in range(2 * half)]
+    second_experts = (
+        jnp.stack(columns[:half]), jnp.stack(columns[half:]), jnp.stack(second_down)
+    )
+    reduced = [(*first_experts, *sums[6:9]), (*second_experts, *sums[9:])]
     final = []
     for a, b, dim in zip(reduced[0], reduced[1], (0, 0, 0, 1, 1, None)):
         keep = jnp.where(first, a, b)

time: 799 us -> 667 us (0.83)
  Pallas kernels: 520 us -> 434 us
  local copies, waits for them, and re-layouts: 87.8 us -> 35.4 us
  other arithmetic: 54.8 us -> 39.4 us
  between operations: 3.29 us -> 16 us
  waiting for transfers between devices: 13.9 us -> 22.3 us
    pallas_call x1, Pallas kernels: 288 us -> 191 us  [sum_scatter(): pl.pallas_call(functools.partial(sum_scatter_kernel, (plans, len(arrays),...]
    dot_general x6 -> x0, matrix products: 35.1 us -> none  [the longest x2 12.3 us: body(): jnp.einsum('etf,td->efd', both[0], grad_both, preferred_element_type=jnp....]
    dot_general x6 -> x10, matrix products: 8.7 us -> 34.7 us  [turned(): jnp.einsum('tc,tq->cq', left, right, preferred_element_type=jnp.float32)]
    convert_element_type x4 -> x0, local copies, waits for them, and re-layouts: 18.9 us -> none  [the longest x2 9.61 us: body(): w_gate_grad = jnp.einsum('td,etf->edf', rows_both, both[1], preferred_ele...]
    another operation x6 -> x1, local copies, waits for them, and re-layouts: 14.7 us -> 1.54 us  [body(): jnp.stack(columns[half:])]
    pallas_call x4, Pallas kernels: 232 us -> 243 us  [expert_call(): pl.pallas_call(kernel, out_shape=shapes, in_specs=[vmem] * len(operands)...]
    ppermute x27 -> x21, waiting for transfers between devices: 13.9 us -> 22.3 us  [swapped(): return lax.ppermute(array, 'section', [(0, 1), (1, 0)])]
  transfers between devices with their start and end apart: 27 -> 24, of which waited for: 3 -> 3; matrix products, arithmetic and copies ran while one was open for 19% -> 18% of each run, Pallas kernels for 0% -> 39%
where the time goes in v4:
time: 667 us; the launch traced here: 658 us
  Pallas kernels  434 us (65%)
  matrix products  105 us (16%)
  other arithmetic  39.4 us (6%)
  local copies, waits for them, and re-layouts  35.4 us (5%)
  waiting for transfers between devices  22.3 us (3%)
  between operations  16 us (2%)
    pallas_call x4, Pallas kernels, expert_call(): pl.pallas_call(kernel, out_shape=shapes, in_specs=[vmem] * len(operands)...  243 us
    pallas_call x1, Pallas kernels, sum_scatter(): pl.pallas_call(functools.partial(sum_scatter_kernel, (plans, len(arrays),...  191 us
    dot_general x10, matrix products, turned(): jnp.einsum('tc,tq->cq', left, right, preferred_element_type=jnp.float32)  34.7 us
    dot_general x8, matrix products, matmul(): return jnp.dot(left_side, right_side, preferred_element_type=jnp.float32)  25.6 us
    ppermute x21, waiting for transfers between devices, swapped(): return lax.ppermute(array, 'section', [(0, 1), (1, 0)])  22.3 us
  transfers between devices with their start and end apart: 24, of which 3 were waited for; matrix products, arithmetic and copies ran while one was open for 18% of the time, Pallas kernels for 39%

profile of v4, /device:TPU:0, one launch (start us, length us, event | category | flops | bytes accessed | tf_op | source)
XLA Modules:
  0.0 657.6 jit_solution(921844794155971008)
XLA Ops:
  12.6 2.6 collective-permute-done
  15.8 5.1 collective-permute-done.7
  29.5 1.8 fusion.22
  31.4 4.3 fusion.4
  35.9 1.6 fusion.122
  37.5 1.6 convolution_convert_fusion.9
  40.0 14.5 %collective-permute-done.4 = bf16[1536,1536]{1,0:T(8,128)(2,1)} collective-permute-done((bf16[1536,1536]{1,0:T(8,128)(2,1)}, bf16[1536,1536]{1,0:T(8,128)(2,1)}, u32[]{:S(2)}, u32[]{:S(2)}) %collective-permute-start.4) | collective-permute-done | bytes 4718624 | tf_op jit(solution)/shard_map/ppermute | solution.py:92
  54.5 3.5 multiply_reduce_fusion.7
  58.8 58.7 %shard_map.237 = (bf16[96,1536]{1,0:T(8,128)(2,1)S(1)}, bf16[4,96,1536]{2,1,0:T(8,128)(2,1)S(1)}, f32[4,96,128]{2,1,0:T(8,128)S(1)}, bf16[4,4,96,512]{3,2,1,0:T(...) custom-call(bf16[96,1536]{1,0:T(8,128)(2,1)S(1)} %multiply_convert_fusion.3.x, ...), custom_call_target="tpu_custom_call" | custom-call | flops 49999998976 | bytes 100000000 | tf_op jit(solution)/shard_map/pallas_call | solution.py:789
  118.4 1.9 convolution_convert_fusion.10
  120.4 2.7 fusion.25
  123.2 5.8 fusion.5
  129.2 1.6 fusion.123
  130.8 1.5 convolution_convert_fusion.8
  132.4 5.1 multiply_reduce_fusion.6
  138.5 57.4 %shard_map.238 = (bf16[96,1536]{1,0:T(8,128)(2,1)S(1)}, bf16[4,96,1536]{2,1,0:T(8,128)(2,1)S(1)}, f32[4,96,128]{2,1,0:T(8,128)S(1)}, bf16[4,4,96,512]{3,2,1,0:T(...) custom-call(bf16[96,1536]{1,0:T(8,128)(2,1)S(1)} %multiply_convert_fusion.2.x, ...), custom_call_target="tpu_custom_call" | custom-call | flops 49999998976 | bytes 100000000 | tf_op jit(solution)/shard_map/pallas_call | solution.py:789
  196.8 58.9 %shard_map.239 = (f32[96,1536]{1,0:T(8,128)S(1)}, f32[96,128]{1,0:T(8,128)S(1)}, bf16[2,4,96,1536]{3,2,1,0:T(8,128)(2,1)}, bf16[2,4,96,1024]{3,2,1,0:T(8,128)(2,...) custom-call(bf16[96,1536]{1,0:T(8,128)(2,1)S(1)} %constant_dynamic-slice_fusion.9.grad, ...), custom_call_target="tpu_custom_call" | custom-call | flops 49999998976 | bytes 100000000 | tf_op jit(solution)/shard_map/pallas_call | solution.py:789
  255.9 5.8 bitcast_convert_fusion.3
  261.7 7.0 %bitcast_convert_fusion.1 = bf16[1536,2048]{1,0:T(8,128)(2,1)} fusion(bf16[2,4,96,1536]{3,2,1,0:T(8,128)(2,1)S(1)} %copy-done.120, bf16[2,4,96,2048]{3,2,1,0:T(8,128)(2,1)S(1)} %copy-done.119), kind=kOutput, calls=%fused_computation.3 | convolution fusion | flops 4834983936 | bytes 11796480 | tf_op jit(solution)/shard_map/tc,tq->cq/dot_general | solution.py:920
  270.9 5.4 convolution_convert_fusion.5
  276.5 2.8 multiply_reduce_fusion.1
  279.3 1.9 fusion.119
  281.5 1.6 fusion.18
  284.8 1.9 multiply_convert_fusion.1
  288.2 1.4 fusion.15
  289.7 2.7 fusion.23
  293.4 6.5 fusion.45
  301.0 1.3 fusion.42.grad
  302.3 68.2 %shard_map.240 = (f32[96,1536]{1,0:T(8,128)S(1)}, f32[96,128]{1,0:T(8,128)S(1)}, bf16[2,4,96,1536]{3,2,1,0:T(8,128)(2,1)}, bf16[2,4,96,1024]{3,2,1,0:T(8,128)(2,...) custom-call(bf16[96,1536]{1,0:T(8,128)(2,1)S(1)} %fusion.42.grad, ...), custom_call_target="tpu_custom_call" | custom-call | flops 49999998976 | bytes 100000000 | tf_op jit(solution)/shard_map/pallas_call | solution.py:789
  370.6 9.4 %bitcast_convert_fusion = bf16[1536,2048]{1,0:T(8,128)(2,1)} fusion(bf16[2,4,96,1536]{3,2,1,0:T(8,128)(2,1)} %get-tuple-element.78, bf16[2,4,96,2048]{3,2,1,0:T(8,128)(2,1)} %get-tuple-element.79), kind=kOutput, calls=%fused_computation.2 | convolution fusion | flops 4834983936 | bytes 11796480 | tf_op jit(solution)/shard_map/tc,tq->cq/dot_general | solution.py:920
  379.9 4.3 bitcast_convert_fusion.2
  385.7 4.0 convolution_convert_fusion.4
  390.0 1.7 fusion.19
  391.8 1.4 multiply_reduce_fusion
  393.2 1.9 multiply_convert_fusion
  400.3 1.7 fusion.20
  404.2 4.7 fusion.35
  420.1 2.0 maximum_select_fusion.1
  422.1 2.5 maximum_select_fusion
  425.9 2.1 copy.161
  430.5 2.2 copy.162
  432.8 2.5 convolution_convert_fusion.2
  435.3 2.2 convolution_convert_fusion.3
  437.5 191.1 %shard_map.241 = (bf16[384,512]{1,0:T(8,128)(2,1)}, bf16[384,512]{1,0:T(8,128)(2,1)}, bf16[384,512]{1,0:T(8,128)(2,1)}, bf16[384,512]{1,0:T(8,128)(2,1)}, bf16[1...) custom-call(bf16[4,384,2048]{2,1,0:T(8,128)(2,1)} %bitcast.345, ...), custom_call_target="tpu_custom_call" | custom-call | tf_op jit(solution)/shard_map/pallas_call | solution.py:343
  640.4 1.5 slice_bitcast_fusion.1
  643.8 1.9 maximum_bitcast_fusion.2
  646.2 2.0 maximum_bitcast_fusion.1
  648.7 2.0 maximum_bitcast_fusion
  (414 shorter events, 65.2 us)
Async XLA Ops:
  7.2 8.2 %copy-start = (s32[2,96]{1,0:T(2,128)S(1)}, s32[2,96]{1,0:T(2,128)}, u32[]{:S(2)}) copy-start(s32[2,96]{1,0:T(2,128)} %param.16) | copy-start | bytes 2308
  7.2 18.9 %copy-start.23 = (bf16[192,1536]{1,0:T(8,128)(2,1)S(1)}, bf16[192,1536]{1,0:T(8,128)(2,1)}, u32[]{:S(2)}) copy-start(bf16[192,1536]{1,0:T(8,128)(2,1)} %param.14) | copy-start | bytes 1769476
  7.2 629.4 %reduce-scatter.6.cloned.1.call-start = ((), (), s32[]{:S(2)}) async-start(), calls=%async_computation.4 | async-start | bytes 1966080 | tf_op jit(solution)/shard_map/reduce_scatter | solution.py:1028
  7.3 14.1 %collective-permute-start.1 = (bf16[1536,512]{1,0:T(8,128)(2,1)}, bf16[1536,512]{1,0:T(8,128)(2,1)}, u32[]{:S(2)}, u32[]{:S(2)}) collective-permute-start(bf16[1536,512]{1,0:T(8,128)(2,1)} %bitcast.343), channel_id=1, source_target_pairs={{0,16},{16,0},{1,17},{17,1},{2,18},{18,2},{3,19},{19,3},{4,20},{20... | collective-permute-start | bytes 4718600 | tf_op jit(solution)/shard_map/ppermute | solution.py:92
  7.8 14.9 %collective-permute-start.2 = (bf16[1536,512]{1,0:T(8,128)(2,1)}, bf16[1536,512]{1,0:T(8,128)(2,1)S(1)}, u32[]{:S(2)}, u32[]{:S(2)}) collective-permute-start(bf16[1536,512]{1,0:T(8,128)(2,1)} %bitcast.344), channel_id=1, source_target_pairs={{0,16},{16,0},{1,17},{17,1},{2,18},{18,2},{3,19},{19,3},{4,20},{20... | collective-permute-start | bytes 4718600 | tf_op jit(solution)/shard_map/ppermute | solution.py:92
  7.9 23.5 %collective-permute-start.3 = (bf16[1536,1536]{1,0:T(8,128)(2,1)}, bf16[1536,1536]{1,0:T(8,128)(2,1)}, u32[]{:S(2)}, u32[]{:S(2)}) collective-permute-start(bf16[1536,1536]{1,0:T(8,128)(2,1)} %bitcast.426), channel_id=1, source_target_pairs={{0,16},{16,0},{1,17},{17,1},{2,18},{18,2},{3,19},{19,3},{4,20},{20... | collective-permute-start | bytes 14155784 | tf_op jit(solution)/shard_map/ppermute | solution.py:92
  9.0 3.3 collective-permute-start.5
  9.9 5.4 collective-permute-start
  10.5 118.5 %copy-start.36 = (f32[96,32]{0,1:T(8,128)}, f32[96,32]{0,1:T(8,128)S(1)}, u32[]{:S(2)}) copy-start(f32[96,32]{0,1:T(8,128)S(1)} %get-tuple-element.224) | copy-start | bytes 36868
  10.5 118.5 %copy-start.38 = (f32[96,32]{0,1:T(8,128)}, f32[96,32]{0,1:T(8,128)S(1)}, u32[]{:S(2)}) copy-start(f32[96,32]{0,1:T(8,128)S(1)} %get-tuple-element.225) | copy-start | bytes 36868
  12.4 3.0 collective-permute-start.6
  15.2 5.7 collective-permute-start.7
  15.4 43.3 %collective-permute-start.8 = (bf16[4,1536,512]{2,1,0:T(8,128)(2,1)}, bf16[4,1536,512]{2,1,0:T(8,128)(2,1)}, u32[]{:S(2)}, u32[]{:S(2)}) collective-permute-start(bf16[4,1536,512]{2,1,0:T(8,128)(2,1)} %bitcast.411), channel_id=1, source_target_pairs={{0,16},{16,0},{1,17},{17,1},{2,18},{18,2},{3,19},{19,3},{4,20},{20... | collective-permute-start | bytes 18874376 | tf_op jit(solution)/shard_map/ppermute | solution.py:92
  20.9 37.8 %collective-permute-start.9 = (bf16[4,1536,512]{2,1,0:T(8,128)(2,1)}, bf16[4,1536,512]{2,1,0:T(8,128)(2,1)}, u32[]{:S(2)}, u32[]{:S(2)}) collective-permute-start(bf16[4,1536,512]{2,1,0:T(8,128)(2,1)} %bitcast.416), channel_id=1, source_target_pairs={{0,16},{16,0},{1,17},{17,1},{2,18},{18,2},{3,19},{19,3},{4,20},{20... | collective-permute-start | bytes 18874376 | tf_op jit(solution)/shard_map/ppermute | solution.py:92
  21.3 37.4 %collective-permute-start.10 = (bf16[4,512,1536]{2,1,0:T(8,128)(2,1)}, bf16[4,512,1536]{2,1,0:T(8,128)(2,1)}, u32[]{:S(2)}, u32[]{:S(2)}) collective-permute-start(bf16[4,512,1536]{2,1,0:T(8,128)(2,1)} %bitcast.421), channel_id=1, source_target_pairs={{0,16},{16,0},{1,17},{17,1},{2,18},{18,2},{3,19},{19,3},{4,20},{20... | collective-permute-start | bytes 18874376 | tf_op jit(solution)/shard_map/ppermute | solution.py:92
  22.7 31.8 %collective-permute-start.4 = (bf16[1536,1536]{1,0:T(8,128)(2,1)}, bf16[1536,1536]{1,0:T(8,128)(2,1)}, u32[]{:S(2)}, u32[]{:S(2)}) collective-permute-start(bf16[1536,1536]{1,0:T(8,128)(2,1)} %bitcast.340), channel_id=1, source_target_pairs={{0,16},{16,0},{1,17},{17,1},{2,18},{18,2},{3,19},{19,3},{4,20},{20... | collective-permute-start | bytes 14155784 | tf_op jit(solution)/shard_map/ppermute | solution.py:92
  26.1 32.5 %copy-start.88 = (f32[1536]{0:T(1024)}, f32[1536]{0:T(1024)S(1)}, u32[]{:S(2)}) copy-start(f32[1536]{0:T(1024)S(1)} %get-tuple-element.213) | copy-start | bytes 18436
  26.1 92.1 %copy-start.96 = (f32[1536]{0:T(1024)}, f32[1536]{0:T(1024)S(1)}, u32[]{:S(2)}) copy-start(f32[1536]{0:T(1024)S(1)} %get-tuple-element.214) | copy-start | bytes 18436
  29.5 8.0 %copy-start.90 = (bf16[96,512]{0,1:T(8,128)(2,1)}, bf16[96,512]{0,1:T(8,128)(2,1)S(1)}, u32[]{:S(2)}) copy-start(bf16[96,512]{0,1:T(8,128)(2,1)S(1)} %copy.100) | copy-start | bytes 294916
  37.5 17.0 %copy-start.24 = (bf16[192,1536]{1,0:T(8,128)(2,1)S(1)}, bf16[192,1536]{1,0:T(8,128)(2,1)}, u32[]{:S(2)}) copy-start(bf16[192,1536]{1,0:T(8,128)(2,1)} %param.14) | copy-start | bytes 1769476
  58.0 59.5 %copy-start.2 = (f32[96,1536]{1,0:T(8,128)}, f32[96,1536]{1,0:T(8,128)S(1)}, u32[]{:S(2)}) copy-start(f32[96,1536]{1,0:T(8,128)S(1)} %get-tuple-element.229.hidden) | copy-start | bytes 1769476
  58.6 58.9 %copy-start.105 = (f32[96]{0:T(128)}, f32[96]{0:T(128)S(1)}, u32[]{:S(2)}) copy-start(f32[96]{0:T(128)S(1)} %get-tuple-element.219) | copy-start | bytes 1156
  58.7 58.8 %copy-start.4 = (bf16[96,1536]{1,0:T(8,128)(2,1)}, bf16[96,1536]{1,0:T(8,128)(2,1)S(1)}, u32[]{:S(2)}) copy-start(bf16[96,1536]{1,0:T(8,128)(2,1)S(1)} %multiply_convert_fusion.3.x) | copy-start | bytes 884740
  58.8 59.6 %copy-start.9 = (bf16[1,1536,512]{2,1,0:T(8,128)(2,1)S(1)}, bf16[1,1536,512]{2,1,0:T(8,128)(2,1)}, u32[]{:S(2)}) copy-start(bf16[1,1536,512]{2,1,0:T(8,128)(2,1)} %param.21) | copy-start | bytes 4718596
  120.4 10.4 %copy-start.92 = (bf16[96,512]{0,1:T(8,128)(2,1)}, bf16[96,512]{0,1:T(8,128)(2,1)S(1)}, u32[]{:S(2)}) copy-start(bf16[96,512]{0,1:T(8,128)(2,1)S(1)} %copy.106) | copy-start | bytes 294916
  123.2 6.0 copy-start.76
  123.2 6.0 copy-start.78
  138.5 57.4 %copy-start.6 = (bf16[96,1536]{1,0:T(8,128)(2,1)}, bf16[96,1536]{1,0:T(8,128)(2,1)S(1)}, u32[]{:S(2)}) copy-start(bf16[96,1536]{1,0:T(8,128)(2,1)S(1)} %multiply_convert_fusion.2.x) | copy-start | bytes 884740
  255.9 12.9 %copy-start.82 = (bf16[96,16]{1,0:T(8,128)(2,1)}, bf16[96,16]{1,0:T(8,128)(2,1)S(1)}, u32[]{:S(2)}) copy-start(bf16[96,16]{1,0:T(8,128)(2,1)S(1)} %multiply_convert_fusion.5) | copy-start | bytes 9220
  255.9 5.9 copy-start.119
  255.9 5.9 copy-start.120
  261.7 7.0 %copy-start.20 = (bf16[1536,16]{1,0:T(8,128)(2,1)S(1)}, bf16[1536,16]{1,0:T(8,128)(2,1)}, u32[]{:S(2)}) copy-start(bf16[1536,16]{1,0:T(8,128)(2,1)} %copy-done.19) | copy-start | bytes 147460
  261.7 7.0 %copy-start.108 = (f32[96]{0:T(128)S(1)}, f32[96]{0:T(128)}, u32[]{:S(2)}) copy-start(f32[96]{0:T(128)} %copy-done.107) | copy-start | bytes 1156
  281.2 355.4 %reduce-scatter.8.cloned.1.call-start = ((), (), s32[]{:S(2)}) async-start(), calls=%async_computation.5 | async-start | bytes 1966080 | tf_op jit(solution)/shard_map/reduce_scatter | solution.py:1028
  284.0 136.0 %collective-permute-start.11 = (bf16[96,1536]{1,0:T(8,128)(2,1)}, bf16[96,1536]{1,0:T(8,128)(2,1)}, u32[]{:S(2)}, u32[]{:S(2)}) collective-permute-start(bf16[96,1536]{1,0:T(8,128)(2,1)} %get-tuple-element.187), channel_id=1, source_target_pairs={{0,16},{16,0},{1,17},{17,1},{2,18},{18,2},{3,19},{19,3},{4,20},{20... | collective-permute-start | bytes 884744 | tf_op jit(solution)/shard_map/ppermute | solution.py:92
  300.0 340.4 %reduce-scatter.4.cloned.1.call-start = ((), (), s32[]{:S(2)}) async-start(), calls=%async_computation.3 | async-start | bytes 7864320 | tf_op jit(solution)/shard_map/reduce_scatter | solution.py:1026
  370.5 9.4 %copy-start.118 = (bf16[2,4,96,1536]{3,2,1,0:T(8,128)(2,1)S(1)}, bf16[2,4,96,1536]{3,2,1,0:T(8,128)(2,1)}, u32[]{:S(2)}) copy-start(bf16[2,4,96,1536]{3,2,1,0:T(8,128)(2,1)} %get-tuple-element.81) | copy-start | bytes 7077892
  410.2 11.9 %collective-permute-start.12 = (f32[96,1536]{1,0:T(8,128)}, f32[96,1536]{1,0:T(8,128)}, u32[]{:S(2)}, u32[]{:S(2)}) collective-permute-start(f32[96,1536]{1,0:T(8,128)} %get-tuple-element.165), channel_id=1, source_target_pairs={{0,16},{16,0},{1,17},{17,1},{2,18},{18,2},{3,19},{19,3},{4,20},{20... | collective-permute-start | bytes 1769480 | tf_op jit(solution)/shard_map/ppermute | solution.py:92
  413.0 11.5 %collective-permute-start.14 = (bf16[96,5120]{1,0:T(8,128)(2,1)}, bf16[96,5120]{1,0:T(8,128)(2,1)S(1)}, u32[]{:S(2)}, u32[]{:S(2)}) collective-permute-start(bf16[96,5120]{1,0:T(8,128)(2,1)} %pad_maximum_fusion.1), channel_id=1, source_target_pairs={{0,16},{16,0},{1,17},{17,1},{2,18},{18,2},{3,19},{19,3},{4,20},{20... | collective-permute-start | bytes 2949128 | tf_op jit(solution)/shard_map/ppermute | solution.py:92
  419.5 8.6 %collective-permute-start.13 = (bf16[96,5120]{1,0:T(8,128)(2,1)}, bf16[96,5120]{1,0:T(8,128)(2,1)S(1)}, u32[]{:S(2)}, u32[]{:S(2)}) collective-permute-start(bf16[96,5120]{1,0:T(8,128)(2,1)} %pad_maximum_fusion), channel_id=1, source_target_pairs={{0,16},{16,0},{1,17},{17,1},{2,18},{18,2},{3,19},{19,3},{4,20},{20... | collective-permute-start | bytes 2949128 | tf_op jit(solution)/shard_map/ppermute | solution.py:92
  628.7 6.9 %copy-start.63 = (bf16[96,768]{1,0:T(8,128)(2,1)S(1)}, bf16[96,768]{1,0:T(8,128)(2,1)}, u32[]{:S(2)}) copy-start(bf16[96,768]{1,0:T(8,128)(2,1)} %get-tuple-element.92) | copy-start | bytes 442372
  628.7 6.9 %copy-start.64 = (bf16[96,768]{1,0:T(8,128)(2,1)S(1)}, bf16[96,768]{1,0:T(8,128)(2,1)}, u32[]{:S(2)}) copy-start(bf16[96,768]{1,0:T(8,128)(2,1)} %get-tuple-element.93) | copy-start | bytes 442372
  629.5 3.8 collective-permute-start.15
  630.4 5.1 collective-permute-start.17
  633.2 3.3 collective-permute-start.16
  638.2 4.1 collective-permute-start.20
  642.2 3.5 collective-permute-start.19
  643.7 4.4 collective-permute-start.18
  (98 other events, 238.7 us)
Sparse Core Ops, SparseCore 0:
  281.4 34.8 reduce-scatter.5
  319.2 30.9 reduce-scatter.7
  393.3 88.5 reduce-scatter.3

commit v5 on v4

--- a/solution.py
+++ b/solution.py
@@ -198,6 +198,8 @@
         def part(at, source=source, prefix=prefix):
             if isinstance(prefix, tuple):
                 return source.at[at, :, pl.ds(*prefix)]
+            if prefix == "inner":
+                return source.at[:, at]
             return source.at[at]
 
         axis, bits = lane["phases"][0]
@@ -314,6 +316,8 @@
         shape = arrays[source].shape
         if isinstance(prefix, int):
             shape = shape[1:]
+        elif prefix == "inner":
+            shape = (shape[1], shape[0], *shape[2:])
         elif prefix is not None:
             shape = (*shape[:-1], prefix[1])
         buffers = [(shape[0] // 2, *shape[1:])]
@@ -373,7 +377,7 @@
 def dense_lanes(first):
     up, down, deep = bits_of("dp"), bits_of("dp")[::-1], bits_of("expert")
     return [
-        (first, None, [("expert", deep), ("dp", up)]),
+        (first, "inner", [("expert", deep), ("dp", up)]),
         (first + 1, None, [("dp", down), ("expert", deep)]),
         (first + 2, None, [("dp", up), ("expert", deep)]),
     ]
@@ -976,12 +980,11 @@
         grad_gate_up = turned(
             rows_both.reshape(-1, D), pre_both.reshape(-1, held * inner)
         ).astype(jnp.bfloat16)
-        grad_down = turned(
-            gated_both.reshape(-1, held // 2 * inner), grad_both.reshape(-1, D)
-        ).astype(jnp.bfloat16)
-        grad_sum, grad_gate_up, grad_down = lax.optimization_barrier(
-            (grad_sum, grad_gate_up, grad_down)
-        )
+        if s == 1:
+            grad_sum, grad_gate_up = lax.optimization_barrier((grad_sum, grad_gate_up))
+            second_pre = lax.psum_scatter(grad_gate_up, "dp", scatter_dimension=0, tiled=True)
+        else:
+            grad_sum, second_pre = lax.optimization_barrier((grad_sum, second_pre))
         gates = lax.dynamic_index_in_dim(gates_all, lax.axis_index("expert"), 0, keepdims=False)
         gates, grad_gates = gates[:, :experts], grad_gates[:, :experts]
         grad_chosen = gates * (grad_gates - jnp.sum(gates * grad_gates, axis=-1, keepdims=True))
@@ -994,6 +997,12 @@
         grad_inputs, grad_gain_attn, grad_qkv, grad_branch = attention_backward(
             grad_hidden, inputs, state, weights[s]
         )
+        if s == 1:
+            grad_inputs, gated_both = lax.optimization_barrier((grad_inputs, gated_both))
+        grad_down = turned(
+            gated_both.reshape(-1, held // 2 * inner), grad_both.reshape(-1, D)
+        ).astype(jnp.bfloat16)
+
         def halves(array):
             width = array.shape[1] // 2
             return (
@@ -1016,32 +1025,31 @@
         small = jnp.concatenate(
             [grad_gain_attn[:, None], grad_gain_moe[:, None], grad_w_router], axis=1
         ).astype(jnp.bfloat16)
+        small = jnp.pad(small, ((0, 0), (0, COLUMNS - small.shape[1])))
+        if s == 1:
+            axes = ("dp", "expert")
+            dp = lax.axis_size("dp")
+            parts = grad_down.reshape(held // 2, dp, inner // dp, D)
+            parts = jnp.moveaxis(parts, 1, 0).reshape(-1, D)
+            dense = jnp.concatenate([grad_w_qkv, grad_w_out, small], axis=1)
+            grad_inputs, parts, dense = lax.optimization_barrier((grad_inputs, parts, dense))
+            second_down = lax.psum_scatter(parts, "dp", scatter_dimension=0, tiled=True)
+            second_dense = lax.psum_scatter(dense, axes, scatter_dimension=0, tiled=True)
         grads[s] = (grad_gate_up, grad_down, grad_w_qkv, grad_w_out, small)
         input_grads[s] = grad_inputs
         grad_low = grad_inputs.astype(jnp.bfloat16)
 
     dp, deep = lax.axis_size("dp"), lax.axis_size("expert")
     half, inner = held // 2, w_gate.shape[3]
-    grad_gate_up, grad_down = grads[1][:2]
-    second_pre = lax.psum_scatter(grad_gate_up, "dp", scatter_dimension=0, tiled=True)
-    second_down = [
-        lax.psum_scatter(
-            grad_down[j * inner : (j + 1) * inner], "dp", scatter_dimension=0, tiled=True
-        )
-        for j in range(half)
-    ]
     arrays, lanes = [], []
-    for s in (0, 1):
-        grad_gate_up, grad_down, grad_w_qkv, grad_w_out, small = grads[s]
-        if s == 0:
-            lanes += expert_lanes(len(arrays), inner)
-            arrays.append(grad_gate_up.reshape(dp, D // dp, held * inner))
-            arrays.append(grad_down.reshape(half, dp, inner // dp, D))
-        lanes += dense_lanes(len(arrays))
-        small = jnp.pad(small, ((0, 0), (0, 128 - small.shape[1])))
-        for array in (grad_w_qkv, grad_w_out, small):
-            arrays.append(array.reshape(dp, deep, array.shape[0] // (dp * deep), array.shape[1]))
-        arrays[-3] = jnp.swapaxes(arrays[-3], 0, 1)
+    grad_gate_up, grad_down, grad_w_qkv, grad_w_out, small = grads[0]
+    lanes += expert_lanes(len(arrays), inner)
+    arrays.append(grad_gate_up.reshape(dp, D // dp, held * inner))
+    arrays.append(grad_down.reshape(half, dp, inner // dp, D))
+    lanes += dense_lanes(len(arrays))
+    for array in (grad_w_qkv, grad_w_out, small):
+        arrays.append(array.reshape(dp, deep, array.shape[0] // (dp * deep), array.shape[1]))
+    *arrays, second_down = lax.optimization_barrier((*arrays, second_down))
     *sums, stats = sum_scatter(arrays, lanes, jnp.concatenate(stats, axis=0), 0)
     stats = lax.dynamic_index_in_dim(stats.reshape(2, 8, COLUMNS), core, 0)
     token_total = SEQ * lax.axis_size(("section", "dp", "expert"))
@@ -1054,9 +1062,15 @@
     )
     columns = [second_pre[:, i * inner : (i + 1) * inner] for i in range(2 * half)]
     second_experts = (
-        jnp.stack(columns[:half]), jnp.stack(columns[half:]), jnp.stack(second_down)
-    )
-    reduced = [(*first_experts, *sums[6:9]), (*second_experts, *sums[9:])]
+        jnp.stack(columns[:half]),
+        jnp.stack(columns[half:]),
+        second_down.reshape(half, inner // dp, D),
+    )
+    qkv, out = grads[0][2].shape[1], grads[0][3].shape[1]
+    second_dense = (
+        second_dense[:, :qkv], second_dense[:, qkv : qkv + out], second_dense[:, qkv + out :]
+    )
+    reduced = [(*first_experts, *sums[6:9]), (*second_experts, *second_dense)]
     final = []
     for a, b, dim in zip(reduced[0], reduced[1], (0, 0, 0, 1, 1, None)):
         keep = jnp.where(first, a, b)

time: 667 us -> 635 us (0.952)
  Pallas kernels: 434 us -> 405 us
  matrix products: 105 us -> 93.9 us
  other arithmetic: 39.4 us -> 48.5 us
    pallas_call x1, Pallas kernels: 191 us -> 159 us  [sum_scatter(): pl.pallas_call(functools.partial(sum_scatter_kernel, (plans, len(arrays),...]
    unnamed x246 -> x219, local copies, waits for them, and re-layouts: 11.4 us -> 13.4 us
  transfers between devices with their start and end apart: 24 -> 24, of which waited for: 3 -> 3; matrix products, arithmetic and copies ran while one was open for 18% -> 22% of each run, Pallas kernels for 39% -> 37%
where the time goes in v5:
time: 635 us; the launch traced here: 628 us
  Pallas kernels  405 us (64%)
  matrix products  93.9 us (15%)
  other arithmetic  48.5 us (8%)
  local copies, waits for them, and re-layouts  36.9 us (6%)
  waiting for transfers between devices  18.4 us (3%)
  between operations  15.7 us (2%)
  starting transfers between devices  9.19 us (1%)
    pallas_call x4, Pallas kernels, expert_call(): pl.pallas_call(kernel, out_shape=shapes, in_specs=[vmem] * len(operands)...  246 us
    pallas_call x1, Pallas kernels, sum_scatter(): pl.pallas_call(functools.partial(sum_scatter_kernel, (plans, len(arrays),...  159 us
    dot_general x10, matrix products, turned(): jnp.einsum('tc,tq->cq', left, right, preferred_element_type=jnp.float32)  35.2 us
    dot_general x8, matrix products, matmul(): return jnp.dot(left_side, right_side, preferred_element_type=jnp.float32)  24.6 us
    ppermute x21, waiting for transfers between devices, swapped(): return lax.ppermute(array, 'section', [(0, 1), (1, 0)])  18.3 us
    unnamed x219, local copies, waits for them, and re-layouts  13.4 us
  transfers between devices with their start and end apart: 24, of which 3 were waited for; matrix products, arithmetic and copies ran while one was open for 22% of the time, Pallas kernels for 37%

profile of v5, /device:TPU:0, one launch (start us, length us, event | category | flops | bytes accessed | tf_op | source)
XLA Modules:
  0.0 627.9 jit_solution(10755115544189871564)
XLA Ops:
  11.1 1.4 dynamic-slice_bitcast_fusion.2
  13.7 1.8 collective-permute-done
  16.1 4.9 collective-permute-done.7
  29.1 1.3 broadcast_select_fusion.30
  32.7 2.2 fusion.24
  35.0 4.4 fusion.6
  39.5 1.6 fusion.122
  41.1 1.7 convolution_convert_fusion.9
  42.8 11.6 %collective-permute-done.4 = bf16[1536,1536]{1,0:T(8,128)(2,1)} collective-permute-done((bf16[1536,1536]{1,0:T(8,128)(2,1)}, bf16[1536,1536]{1,0:T(8,128)(2,1)}, u32[]{:S(2)}, u32[]{:S(2)}) %collective-permute-start.4) | collective-permute-done | bytes 4718624 | tf_op jit(solution)/shard_map/ppermute | solution.py:92
  54.5 3.6 multiply_reduce_fusion.7
  59.1 59.0 %shard_map.237 = (bf16[96,1536]{1,0:T(8,128)(2,1)S(1)}, bf16[4,96,1536]{2,1,0:T(8,128)(2,1)S(1)}, f32[4,96,128]{2,1,0:T(8,128)S(1)}, bf16[4,4,96,512]{3,2,1,0:T(...) custom-call(bf16[96,1536]{1,0:T(8,128)(2,1)S(1)} %multiply_convert_fusion.3.x, ...), custom_call_target="tpu_custom_call" | custom-call | flops 49999998976 | bytes 100000000 | tf_op jit(solution)/shard_map/pallas_call | solution.py:793
  121.3 2.6 fusion.27
  124.0 5.8 fusion.7
  130.6 1.3 convolution_convert_fusion.8
  132.0 5.1 multiply_reduce_fusion.6
  137.2 57.6 %shard_map.238 = (bf16[96,1536]{1,0:T(8,128)(2,1)S(1)}, bf16[4,96,1536]{2,1,0:T(8,128)(2,1)S(1)}, f32[4,96,128]{2,1,0:T(8,128)S(1)}, bf16[4,4,96,512]{3,2,1,0:T(...) custom-call(bf16[96,1536]{1,0:T(8,128)(2,1)S(1)} %multiply_convert_fusion.2.x, ...), custom_call_target="tpu_custom_call" | custom-call | flops 49999998976 | bytes 100000000 | tf_op jit(solution)/shard_map/pallas_call | solution.py:793
  194.8 58.8 %shard_map.239 = (f32[96,1536]{1,0:T(8,128)S(1)}, f32[96,128]{1,0:T(8,128)S(1)}, bf16[2,4,96,1536]{3,2,1,0:T(8,128)(2,1)}, bf16[2,4,96,1024]{3,2,1,0:T(8,128)(2,...) custom-call(bf16[96,1536]{1,0:T(8,128)(2,1)S(1)} %constant_dynamic-slice_fusion.9.grad, ...), custom_call_target="tpu_custom_call" | custom-call | flops 49999998976 | bytes 100000000 | tf_op jit(solution)/shard_map/pallas_call | solution.py:793
  254.8 9.1 %bitcast_convert_fusion.1 = bf16[1536,2048]{1,0:T(8,128)(2,1)} fusion(bf16[2,4,96,1536]{3,2,1,0:T(8,128)(2,1)} %get-tuple-element.72, bf16[2,4,96,2048]{3,2,1,0:T(8,128)(2,1)} %get-tuple-element.73), kind=kOutput, calls=%fused_computation.5 | convolution fusion | flops 4834983936 | bytes 11796480 | tf_op jit(solution)/shard_map/tc,tq->cq/dot_general | solution.py:924
  264.0 1.9 copy.158
  268.2 6.2 convolution_convert_fusion.5
  276.1 1.3 multiply_reduce_fusion.1
  285.1 5.8 fusion.46
  292.7 4.7 bitcast_convert_fusion.3
  297.4 1.9 copy.154
  303.4 1.2 convolution_convert_fusion.1
  304.6 3.1 fusion.3
  311.2 1.2 copy-done.9
  312.5 70.4 %shard_map.240 = (f32[96,1536]{1,0:T(8,128)S(1)}, f32[96,128]{1,0:T(8,128)S(1)}, bf16[2,4,96,1536]{3,2,1,0:T(8,128)(2,1)}, bf16[2,4,96,1024]{3,2,1,0:T(8,128)(2,...) custom-call(bf16[96,1536]{1,0:T(8,128)(2,1)S(1)} %get-tuple-element.80.grad, ...), custom_call_target="tpu_custom_call" | custom-call | flops 49999998976 | bytes 100000000 | tf_op jit(solution)/shard_map/pallas_call | solution.py:793
  383.1 5.9 bitcast_convert_fusion.2
  389.1 7.5 %bitcast_convert_fusion = bf16[1536,2048]{1,0:T(8,128)(2,1)} fusion(bf16[2,4,96,1536]{3,2,1,0:T(8,128)(2,1)S(1)} %copy-done.107, bf16[2,4,96,2048]{3,2,1,0:T(8,128)(2,1)S(1)} %copy-done.106), kind=kOutput, calls=%fused_computation.4 | convolution fusion | flops 4834983936 | bytes 11796480 | tf_op jit(solution)/shard_map/tc,tq->cq/dot_general | solution.py:924
  397.5 4.0 convolution_convert_fusion.4
  407.0 1.7 fusion.22
  410.1 4.4 fusion.37
  415.7 2.8 collective-permute-start.13
  421.9 1.5 slice_bitcast_fusion.1
  423.4 2.5 maximum_select_fusion
  428.9 2.2 convolution_convert_fusion.2
  431.1 3.1 convolution_convert_fusion
  434.3 159.5 %shard_map.241 = (bf16[384,512]{1,0:T(8,128)(2,1)}, bf16[384,512]{1,0:T(8,128)(2,1)}, bf16[384,512]{1,0:T(8,128)(2,1)}, bf16[384,512]{1,0:T(8,128)(2,1)}, bf16[1...) custom-call(bf16[4,384,2048]{2,1,0:T(8,128)(2,1)} %bitcast.336, ...), custom_call_target="tpu_custom_call" | custom-call | tf_op jit(solution)/shard_map/pallas_call | solution.py:347
  593.8 2.2 broadcast_select_fusion.16
  600.4 1.6 broadcast_select_fusion.35
  602.0 1.7 broadcast_select_fusion.33
  604.3 1.7 convert_select_fusion.3
  606.0 2.0 maximum_bitcast_fusion.1
  608.0 1.6 convert_select_fusion.1
  609.6 1.9 maximum_bitcast_fusion.2
  611.5 1.6 convert_select_fusion.5
  613.1 2.0 maximum_bitcast_fusion
  (385 shorter events, 69.3 us)
Async XLA Ops:
  7.2 8.6 %copy-start = (s32[2,96]{1,0:T(2,128)S(1)}, s32[2,96]{1,0:T(2,128)}, u32[]{:S(2)}) copy-start(s32[2,96]{1,0:T(2,128)} %param.16) | copy-start | bytes 2308
  7.2 389.4 %reduce-scatter.4.cloned.1.call-start = ((), (), s32[]{:S(2)}) async-start(), calls=%async_computation.3 | async-start | bytes 7864320 | tf_op jit(solution)/shard_map/reduce_scatter | solution.py:985
  7.2 14.1 %collective-permute-start.1 = (bf16[1536,512]{1,0:T(8,128)(2,1)}, bf16[1536,512]{1,0:T(8,128)(2,1)S(1)}, u32[]{:S(2)}, u32[]{:S(2)}) collective-permute-start(bf16[1536,512]{1,0:T(8,128)(2,1)} %bitcast.337), channel_id=1, source_target_pairs={{0,16},{16,0},{1,17},{17,1},{2,18},{18,2},{3,19},{19,3},{4,20},{20... | collective-permute-start | bytes 4718600 | tf_op jit(solution)/shard_map/ppermute | solution.py:92
  7.8 16.2 %collective-permute-start.2 = (bf16[1536,512]{1,0:T(8,128)(2,1)}, bf16[1536,512]{1,0:T(8,128)(2,1)S(1)}, u32[]{:S(2)}, u32[]{:S(2)}) collective-permute-start(bf16[1536,512]{1,0:T(8,128)(2,1)} %bitcast.338), channel_id=1, source_target_pairs={{0,16},{16,0},{1,17},{17,1},{2,18},{18,2},{3,19},{19,3},{4,20},{20... | collective-permute-start | bytes 4718600 | tf_op jit(solution)/shard_map/ppermute | solution.py:92
  7.8 27.1 %collective-permute-start.3 = (bf16[1536,1536]{1,0:T(8,128)(2,1)}, bf16[1536,1536]{1,0:T(8,128)(2,1)}, u32[]{:S(2)}, u32[]{:S(2)}) collective-permute-start(bf16[1536,1536]{1,0:T(8,128)(2,1)} %bitcast.416), channel_id=1, source_target_pairs={{0,16},{16,0},{1,17},{17,1},{2,18},{18,2},{3,19},{19,3},{4,20},{20... | collective-permute-start | bytes 14155784 | tf_op jit(solution)/shard_map/ppermute | solution.py:92
  9.0 4.5 collective-permute-start.5
  9.9 5.6 collective-permute-start
  13.5 14.4 %copy-start.40 = (bf16[1,1536,16]{2,1,0:T(8,128)(2,1)}, bf16[1,1536,16]{2,1,0:T(8,128)(2,1)S(1)}, u32[]{:S(2)}) copy-start(bf16[1,1536,16]{2,1,0:T(8,128)(2,1)S(1)} %copy.145) | copy-start | bytes 147460
  13.5 2.3 collective-permute-start.6
  15.4 5.5 collective-permute-start.7
  15.8 42.9 %collective-permute-start.8 = (bf16[4,1536,512]{2,1,0:T(8,128)(2,1)}, bf16[4,1536,512]{2,1,0:T(8,128)(2,1)}, u32[]{:S(2)}, u32[]{:S(2)}) collective-permute-start(bf16[4,1536,512]{2,1,0:T(8,128)(2,1)} %bitcast.401), channel_id=1, source_target_pairs={{0,16},{16,0},{1,17},{17,1},{2,18},{18,2},{3,19},{19,3},{4,20},{20... | collective-permute-start | bytes 18874376 | tf_op jit(solution)/shard_map/ppermute | solution.py:92
  20.9 37.8 %collective-permute-start.9 = (bf16[4,1536,512]{2,1,0:T(8,128)(2,1)}, bf16[4,1536,512]{2,1,0:T(8,128)(2,1)}, u32[]{:S(2)}, u32[]{:S(2)}) collective-permute-start(bf16[4,1536,512]{2,1,0:T(8,128)(2,1)} %bitcast.406), channel_id=1, source_target_pairs={{0,16},{16,0},{1,17},{17,1},{2,18},{18,2},{3,19},{19,3},{4,20},{20... | collective-permute-start | bytes 18874376 | tf_op jit(solution)/shard_map/ppermute | solution.py:92
  21.7 37.1 %collective-permute-start.10 = (bf16[4,512,1536]{2,1,0:T(8,128)(2,1)}, bf16[4,512,1536]{2,1,0:T(8,128)(2,1)}, u32[]{:S(2)}, u32[]{:S(2)}) collective-permute-start(bf16[4,512,1536]{2,1,0:T(8,128)(2,1)} %bitcast.411), channel_id=1, source_target_pairs={{0,16},{16,0},{1,17},{17,1},{2,18},{18,2},{3,19},{19,3},{4,20},{20... | collective-permute-start | bytes 18874376 | tf_op jit(solution)/shard_map/ppermute | solution.py:92
  23.9 30.5 %collective-permute-start.4 = (bf16[1536,1536]{1,0:T(8,128)(2,1)}, bf16[1536,1536]{1,0:T(8,128)(2,1)}, u32[]{:S(2)}, u32[]{:S(2)}) collective-permute-start(bf16[1536,1536]{1,0:T(8,128)(2,1)} %bitcast.334), channel_id=1, source_target_pairs={{0,16},{16,0},{1,17},{17,1},{2,18},{18,2},{3,19},{19,3},{4,20},{20... | collective-permute-start | bytes 14155784 | tf_op jit(solution)/shard_map/ppermute | solution.py:92
  27.2 31.4 %copy-start.80 = (f32[1536]{0:T(1024)}, f32[1536]{0:T(1024)S(1)}, u32[]{:S(2)}) copy-start(f32[1536]{0:T(1024)S(1)} %get-tuple-element.237) | copy-start | bytes 18436
  27.2 109.9 %copy-start.82 = (f32[1536]{0:T(1024)}, f32[1536]{0:T(1024)S(1)}, u32[]{:S(2)}) copy-start(f32[1536]{0:T(1024)S(1)} %get-tuple-element.236) | copy-start | bytes 18436
  27.9 92.0 %copy-start.88 = (f32[1536]{0:T(1024)}, f32[1536]{0:T(1024)S(1)}, u32[]{:S(2)}) copy-start(f32[1536]{0:T(1024)S(1)} %get-tuple-element.238) | copy-start | bytes 18436
  29.1 5.9 copy-start.43
  41.1 13.4 %copy-start.27 = (bf16[192,1536]{1,0:T(8,128)(2,1)S(1)}, bf16[192,1536]{1,0:T(8,128)(2,1)}, u32[]{:S(2)}) copy-start(bf16[192,1536]{1,0:T(8,128)(2,1)} %param.14) | copy-start | bytes 1769476
  42.8 15.2 %copy-start.31 = (bf16[8,64,3,96]{3,1,2,0:T(8,128)(2,1)}, bf16[8,64,3,96]{3,1,2,0:T(8,128)(2,1)S(1)}, u32[]{:S(2)}) copy-start(bf16[8,64,3,96]{3,1,2,0:T(8,128)(2,1)S(1)} %convolution_convert_fusion.9) | copy-start | bytes 884740
  58.0 60.2 %copy-start.2 = (f32[96,1536]{1,0:T(8,128)}, f32[96,1536]{1,0:T(8,128)S(1)}, u32[]{:S(2)}) copy-start(f32[96,1536]{1,0:T(8,128)S(1)} %get-tuple-element.253.hidden) | copy-start | bytes 1769476
  58.7 59.5 %copy-start.4 = (bf16[96,1536]{1,0:T(8,128)(2,1)}, bf16[96,1536]{1,0:T(8,128)(2,1)S(1)}, u32[]{:S(2)}) copy-start(bf16[96,1536]{1,0:T(8,128)(2,1)S(1)} %multiply_convert_fusion.3.x) | copy-start | bytes 884740
  59.1 60.9 %copy-start.17 = (bf16[1536,512]{1,0:T(8,128)(2,1)S(1)}, bf16[1536,512]{1,0:T(8,128)(2,1)}, u32[]{:S(2)}) copy-start(bf16[1536,512]{1,0:T(8,128)(2,1)} %copy-done.15) | copy-start | bytes 4718596
  124.0 6.0 copy-start.74
  124.0 6.0 copy-start.76
  130.6 145.0 %copy-start.92 = (f32[8,3,96]{2,1,0:T(4,128)}, f32[8,3,96]{2,1,0:T(4,128)S(1)}, u32[]{:S(2)}) copy-start(f32[8,3,96]{2,1,0:T(4,128)S(1)} %get-tuple-element.254) | copy-start | bytes 27652
  264.0 170.3 %reduce-scatter.6.cloned.1.call-start = ((), (), s32[]{:S(2)}) async-start(), calls=%async_computation.4 | async-start | bytes 3932160 | tf_op jit(solution)/shard_map/reduce_scatter | solution.py:1036
  268.2 7.4 %copy-start.51 = (f32[8,3,96,96]{2,3,1,0:T(8,128)S(1)}, f32[8,3,96,96]{2,3,1,0:T(8,128)}, u32[]{:S(2)}) copy-start(f32[8,3,96,96]{2,3,1,0:T(8,128)} %copy-done.50) | copy-start | bytes 2654212
  282.4 16.9 %collective-permute-start.12 = (bf16[96,5120]{1,0:T(8,128)(2,1)}, bf16[96,5120]{1,0:T(8,128)(2,1)}, u32[]{:S(2)}, u32[]{:S(2)}) collective-permute-start(bf16[96,5120]{1,0:T(8,128)(2,1)} %pad_maximum_fusion), channel_id=1, source_target_pairs={{0,16},{16,0},{1,17},{17,1},{2,18},{18,2},{3,19},{19,3},{4,20},{20... | collective-permute-start | bytes 2949128 | tf_op jit(solution)/shard_map/ppermute | solution.py:92
  285.1 5.9 copy-start.29
  285.1 5.9 copy-start.104
  307.7 291.4 %reduce-scatter.8.cloned.1.call-start = ((), (), s32[]{:S(2)}) async-start(), calls=%async_computation.5 | async-start | bytes 7102464 | tf_op jit(solution)/shard_map/reduce_scatter | solution.py:1037
  308.6 1.6 collective-permute-start.11
  383.1 6.0 copy-start.106
  383.1 6.0 copy-start.107
  389.1 7.6 %copy-start.3 = (f32[96,1536]{1,0:T(8,128)S(1)}, f32[96,1536]{1,0:T(8,128)}, u32[]{:S(2)}) copy-start(f32[96,1536]{1,0:T(8,128)} %copy-done.2) | copy-start | bytes 1769476
  389.1 7.6 %copy-start.23 = (bf16[1536,16]{1,0:T(8,128)(2,1)S(1)}, bf16[1536,16]{1,0:T(8,128)(2,1)}, u32[]{:S(2)}) copy-start(bf16[1536,16]{1,0:T(8,128)(2,1)} %copy-done.22) | copy-start | bytes 147460
  389.1 7.6 %copy-start.81 = (f32[1536]{0:T(1024)S(1)}, f32[1536]{0:T(1024)}, u32[]{:S(2)}) copy-start(f32[1536]{0:T(1024)} %copy-done.80) | copy-start | bytes 18436
  389.1 7.6 %copy-start.97 = (f32[96]{0:T(128)S(1)}, f32[96]{0:T(128)}, u32[]{:S(2)}) copy-start(f32[96]{0:T(128)} %copy-done.96) | copy-start | bytes 1156
  415.7 7.8 %collective-permute-start.13 = (f32[96,1536]{1,0:T(8,128)}, f32[96,1536]{1,0:T(8,128)}, u32[]{:S(2)}, u32[]{:S(2)}) collective-permute-start(f32[96,1536]{1,0:T(8,128)} %get-tuple-element.188), channel_id=1, source_target_pairs={{0,16},{16,0},{1,17},{17,1},{2,18},{18,2},{3,19},{19,3},{4,20},{20... | collective-permute-start | bytes 1769480 | tf_op jit(solution)/shard_map/ppermute | solution.py:92
  419.6 6.3 collective-permute-start.14
  434.3 159.5 %copy-start.26 = (bf16[256,1536]{1,0:T(8,128)(2,1)S(1)}, bf16[256,1536]{1,0:T(8,128)(2,1)}, u32[]{:S(2)}) copy-start(bf16[256,1536]{1,0:T(8,128)(2,1)} %reduce-scatter.6.cloned.1.call-done) | copy-start | bytes 2359300
  596.0 12.0 %collective-permute-start.20 = (bf16[2,128,1536]{2,1,0:T(8,128)(2,1)}, bf16[2,128,1536]{2,1,0:T(8,128)(2,1)}, u32[]{:S(2)}, u32[]{:S(2)}) collective-permute-start(bf16[2,128,1536]{2,1,0:T(8,128)(2,1)} %broadcast_select_fusion.16), channel_id=1, source_target_pairs={{0,16},{16,0},{1,17},{17,1},{2,18},{18,2},{3,19},{19,3},{4,20},{20... | collective-permute-start | bytes 2359304 | tf_op jit(solution)/shard_map/ppermute | solution.py:92
  597.1 6.6 %collective-permute-start.19 = (bf16[2,384,512]{2,1,0:T(8,128)(2,1)}, bf16[2,384,512]{2,1,0:T(8,128)(2,1)}, u32[]{:S(2)}, u32[]{:S(2)}) collective-permute-start(bf16[2,384,512]{2,1,0:T(8,128)(2,1)} %broadcast_select_fusion.18), channel_id=1, source_target_pairs={{0,16},{16,0},{1,17},{17,1},{2,18},{18,2},{3,19},{19,3},{4,20},{20... | collective-permute-start | bytes 2359304 | tf_op jit(solution)/shard_map/ppermute | solution.py:92
  598.6 12.9 %collective-permute-start.18 = (bf16[2,384,512]{2,1,0:T(8,128)(2,1)}, bf16[2,384,512]{2,1,0:T(8,128)(2,1)}, u32[]{:S(2)}, u32[]{:S(2)}) collective-permute-start(bf16[2,384,512]{2,1,0:T(8,128)(2,1)} %broadcast_select_fusion.20), channel_id=1, source_target_pairs={{0,16},{16,0},{1,17},{17,1},{2,18},{18,2},{3,19},{19,3},{4,20},{20... | collective-permute-start | bytes 2359304 | tf_op jit(solution)/shard_map/ppermute | solution.py:92
  599.9 15.3 %collective-permute-start.15 = (bf16[96,128]{1,0:T(8,128)(2,1)S(1)}, bf16[96,128]{1,0:T(8,128)(2,1)S(1)}, u32[]{:S(2)}, u32[]{:S(2)}) collective-permute-start(bf16[96,128]{1,0:T(8,128)(2,1)S(1)} %broadcast_select_fusion.37), channel_id=1, source_target_pairs={{0,16},{16,0},{1,17},{17,1},{2,18},{18,2},{3,19},{19,3},{4,20},{20... | collective-permute-start | bytes 73736 | tf_op jit(solution)/shard_map/ppermute | solution.py:92
  602.0 14.6 %collective-permute-start.17 = (bf16[96,768]{1,0:T(8,128)(2,1)}, bf16[96,768]{1,0:T(8,128)(2,1)}, u32[]{:S(2)}, u32[]{:S(2)}) collective-permute-start(bf16[96,768]{1,0:T(8,128)(2,1)} %broadcast_select_fusion.35), channel_id=1, source_target_pairs={{0,16},{16,0},{1,17},{17,1},{2,18},{18,2},{3,19},{19,3},{4,20},{20... | collective-permute-start | bytes 442376 | tf_op jit(solution)/shard_map/ppermute | solution.py:92
  603.7 14.8 %collective-permute-start.16 = (bf16[96,1280]{1,0:T(8,128)(2,1)}, bf16[96,1280]{1,0:T(8,128)(2,1)}, u32[]{:S(2)}, u32[]{:S(2)}) collective-permute-start(bf16[96,1280]{1,0:T(8,128)(2,1)} %broadcast_select_fusion.33), channel_id=1, source_target_pairs={{0,16},{16,0},{1,17},{17,1},{2,18},{18,2},{3,19},{19,3},{4,20},{20... | collective-permute-start | bytes 737288 | tf_op jit(solution)/shard_map/ppermute | solution.py:92
  (84 other events, 173.5 us)
Sparse Core Ops, SparseCore 0:
  264.1 72.6 reduce-scatter.3
  340.3 43.9 reduce-scatter.5
  389.6 187.9 reduce-scatter.7

commit v6 on v5

--- a/solution.py
+++ b/solution.py
@@ -414,10 +414,10 @@
 
 MESH = pl.DeviceIdType.MESH
 COLUMNS = 128
-
-
-def move_rows(refs, compute, z, n, others):
-    sources, held, sums, returned, sems = refs
+PARTS = 3
+
+
+def move_rows(sources, held, pieces, sems, compute, z, n, others):
     row_send, row_recv, sum_send, sum_recv = sems
     barrier = pltpu.get_barrier_semaphore()
     for k in range(1, n):
@@ -466,47 +466,75 @@
                 def _():
                     row_copy(kind, way, hop + 1).start()
 
-    def sum_copy(kind, peer):
+    def behind(way):
+        peer = z - (1 - 2 * way)
+        return (peer >= 0) & (peer < n)
+
+    def sum_copy(way, block, p):
+        mine, arrived = pieces[p]
         return pltpu.make_async_remote_copy(
-            src_ref=sums[kind].at[peer],
-            dst_ref=returned[kind].at[z],
-            send_sem=sum_send.at[kind, peer],
-            recv_sem=sum_recv.at[kind, z],
-            device_id={"expert": peer},
+            src_ref=mine(block),
+            dst_ref=arrived(way, block),
+            send_sem=sum_send.at[block, p],
+            recv_sem=sum_recv.at[way, block, p],
+            device_id={"expert": jnp.clip(z + 1 - 2 * way, 0, n - 1)},
             device_id_type=MESH,
         )
 
-    def came_back(kind, peer):
-        return pltpu.make_async_remote_copy(
-            src_ref=sums[kind].at[peer],
-            dst_ref=returned[kind].at[peer],
-            send_sem=sum_send.at[kind, peer],
-            recv_sem=sum_recv.at[kind, peer],
-            device_id={"expert": peer},
-            device_id_type=MESH,
-        )
+    def sent(block, p):
+        way = jnp.where(block > z, 0, 1)
+
+        @pl.when((block != z) & jnp.logical_not(behind(way)))
+        def _():
+            sum_copy(way, block, p).start()
 
     def run():
+        def both(hop):
+            return (hop >= 0) & (z - 1 - hop >= 0) & (z + 1 + hop < n)
+
         def turn(k, carry):
             hop = lax.div(k + 1, 2) - 1
             block = z + (1 + hop) * (1 - 2 * lax.rem(k, 2))
-
-            @pl.when(lax.rem(k, 2) == 1)
+            odd = lax.rem(k, 2) == 1
+
+            @pl.when(odd & jnp.logical_not(both(hop - 1)))
             def _():
                 take(hop)
 
+            @pl.when(jnp.logical_not(odd) & both(hop) & (hop + 1 < n - 1))
+            def _():
+                take(hop + 1)
+
             @pl.when((block >= 0) & (block < n))
             def _():
-                compute(block)
-
-                @pl.when(block != z)
+                compute(block, sent)
+
+            return carry
+
+        lax.fori_loop(0, 2 * n - 1, turn, 0)
+
+        first = jnp.where(2 * z < n, 0, 1)
+        for way in (first, 1 - first):
+            for k in range(1, n):
+                block = z + (1 - 2 * way) * k
+
+                @pl.when(behind(way) & (block >= 0) & (block < n))
                 def _():
-                    for kind in range(len(sums)):
-                        sum_copy(kind, block).start()
-
-            return carry
-
-        lax.fori_loop(0, 2 * n - 1, turn, 0)
+                    for p, (mine, arrived) in enumerate(pieces):
+                        sum_copy(way, block, p).wait_recv()
+                        own, other = mine(block), arrived(way, block)
+                        own[...] = (
+                            own[...].astype(jnp.float32) + other[...].astype(jnp.float32)
+                        ).astype(jnp.bfloat16)
+                        sum_copy(way, block, p).start()
+
+    def collect(add):
+        for way in range(2):
+            @pl.when(behind(way))
+            def _():
+                for p, (_, arrived) in enumerate(pieces):
+                    sum_copy(way, z, p).wait_recv()
+                    add(p, arrived(way, z)[...].astype(jnp.float32))
 
     def finish():
         for kind in range(len(held)):
@@ -515,16 +543,24 @@
                     @pl.when(sends(way, hop))
                     def _():
                         row_copy(kind, way, hop).wait_send()
-        for kind in range(len(sums)):
-            for k in range(1, n):
-                sum_copy(kind, lax.rem(z + k, n)).wait_send()
-
-    def collect(kind, k):
-        peer = lax.rem(z + k, n)
-        came_back(kind, peer).wait_recv()
-        return peer
+        for k in range(1, n):
+            for p in range(len(pieces)):
+                sum_copy(0, lax.rem(z + k, n), p).wait_send()
 
     return start, run, collect, finish
+
+
+def row_pieces(sums, returned, parts):
+    width = sums.shape[2] // parts
+
+    def piece(p):
+        at = pl.ds(p * width, width)
+        return (
+            lambda block: sums.at[block, :, at],
+            lambda way, block: returned.at[way, block, :, at],
+        )
+
+    return [piece(p) for p in range(parts)]
 
 
 def fetch_weights(layer, own, other, places, sem):
@@ -567,15 +603,15 @@
     layer, experts, x, mask, hidden, router, *refs
 ):
     own, other, refs = refs[:3], refs[3:6], refs[6:]
-    out, rows, gates, gate_keep, up_keep, gated, stats = refs[:7]
-    w_gate, w_up, w_down, sums, returned, mixed, total, stats_all = refs[7:15]
-    weight_sem, *sems = refs[15:]
+    out, rows, gates_all, gates, gate_keep, up_keep, gated, stats = refs[:8]
+    w_gate, w_up, w_down, sums, returned, mixed, total, stats_all = refs[8:16]
+    weight_sem, *sems = refs[16:]
     n, held = rows.shape[0], w_gate.shape[0]
     z = lax.axis_index("expert")
 
-    def compute(block):
+    def compute(block, sent):
         picked = rows[block]
-        gate_block = gates[block]
+        gate_block = gates_all[block].astype(jnp.float32)
 
         def one(e, carry):
             gate_pre = jnp.dot(picked, w_gate[e], preferred_element_type=jnp.float32)
@@ -590,8 +626,8 @@
             return carry
 
         lax.fori_loop(0, held, one, 0)
-        width = out.shape[1] // 3
-        for part in range(3):
+        width = out.shape[1] // PARTS
+        for part in range(PARTS):
             at = pl.ds(part * width, width)
             result = jnp.zeros((out.shape[0], width), jnp.float32)
             for e in range(held):
@@ -605,9 +641,14 @@
             def _():
                 sums[block, :, at] = result.astype(jnp.bfloat16)
 
-    own_gates = gates.at[z]
+            sent(block, part)
+
+    own_gates = gates_all.at[z]
     start, run, collect, finish = move_rows(
-        ((x, own_gates, stats_all.at[z]), (rows, gates, stats_all), (sums,), (returned,), sems),
+        (x, own_gates, stats_all.at[z]),
+        (rows, gates_all, stats_all),
+        row_pieces(sums, returned, PARTS),
+        sems,
         compute,
         z,
         n,
@@ -619,7 +660,8 @@
     chosen = mask[...] > 0
     highest = jnp.max(jnp.where(chosen, logits, MASKED), axis=1, keepdims=True)
     exponent = jnp.where(chosen, jnp.exp(logits - highest), 0.0)
-    own_gates[...] = exponent / jnp.sum(exponent, axis=1, keepdims=True)
+    gates[...] = exponent / jnp.sum(exponent, axis=1, keepdims=True)
+    own_gates[...] = gates[...].astype(jnp.bfloat16)
     start(1)
     real = lax.broadcasted_iota(jnp.int32, logits.shape, 1) < experts
     highest = jnp.max(jnp.where(real, logits, MASKED), axis=1, keepdims=True)
@@ -636,9 +678,12 @@
     wait_weights()
     run()
     stats[...] = jnp.sum(stats_all[...], axis=0)
-    for k in range(1, n):
-        peer = collect(0, k)
-        total[...] += returned[peer].astype(jnp.float32)
+    width = out.shape[1] // PARTS
+
+    def add(p, value):
+        total[:, p * width : (p + 1) * width] += value
+
+    collect(add)
     out[...] = total[...].astype(jnp.bfloat16)
     finish()
 
@@ -646,8 +691,8 @@
 def experts_backward_kernel(layer, grad, gates, gate_keep, up_keep, *refs):
     own, other, saved_rows, saved_gated, refs = refs[:3], refs[3:6], refs[6], refs[7], refs[8:]
     out, out_gates, rows_both, gated_both, grad_both, pre_both = refs[:6]
-    w_gate, w_up, w_down, sums, sum_gates, returned, returned_gates, away = refs[6:14]
-    weight_sem, core_send, core_recv, core_local, *sems = refs[14:]
+    w_gate, w_up, w_down, sums, sum_gates, returned, returned_gates, away, dots = refs[6:15]
+    weight_sem, core_send, core_recv, core_local, *sems = refs[15:]
     n, held = gates.shape[0], w_gate.shape[0]
     half, inner = held // 2, w_gate.shape[2]
     core = lax.axis_index("section")
@@ -688,10 +733,10 @@
             ),
         )
 
-    def compute(block):
+    def compute(block, sent):
         picked = rows[block]
-        gate_block = gates[block]
-        sum_gates[block] = jnp.zeros(sum_gates.shape[1:], jnp.float32)
+        gate_block = gates[block].astype(jnp.float32)
+        dots[...] = jnp.zeros(dots.shape, jnp.float32)
 
         def one(e, place, j):
             raw = lax.dot_general(
@@ -703,8 +748,8 @@
             silu = gate_pre * sigmoid
             column = z * held + e
             dot = jnp.sum(raw * (silu * up_pre), axis=1, keepdims=True)
-            here = lax.broadcasted_iota(jnp.int32, sum_gates.shape[1:], 1) == column
-            sum_gates[block] += jnp.where(here, dot, 0.0)
+            here = lax.broadcasted_iota(jnp.int32, dots.shape, 1) == column
+            dots[...] += jnp.where(here, dot, 0.0)
             active = column_of(gate_block, column) * raw
             place[:, pl.ds(pl.multiple_of(j * inner, inner), inner)] = (
                 active * up_pre * sigmoid * (1.0 + gate_pre * (1.0 - sigmoid))
@@ -725,8 +770,15 @@
         for copy in block_copies(block):
             copy.start()
         lax.fori_loop(0, half, own_half, 0)
-        width = out.shape[1] // 3
-        for part in range(3):
+        sum_gates[block] = dots[...].astype(jnp.bfloat16)
+
+        @pl.when(block == z)
+        def _():
+            out_gates[...] = dots[...]
+
+        sent(block, PARTS)
+        width = out.shape[1] // PARTS
+        for part in range(PARTS):
             at = pl.ds(part * width, width)
             result = jnp.zeros((out.shape[0], width), jnp.float32)
             for place, side in ((away.at[block], 1 - core), (pre_both.at[core, block], core)):
@@ -748,8 +800,14 @@
             def _():
                 sums[block, :, at] = result.astype(jnp.bfloat16)
 
+            sent(block, part)
+
+    gate_piece = (lambda block: sum_gates.at[block], lambda way, block: returned_gates.at[way, block])
     start, run, collect, finish = move_rows(
-        ((grad,), (rows,), (sums, sum_gates), (returned, returned_gates), sems),
+        (grad,),
+        (rows,),
+        row_pieces(sums, returned, PARTS) + [gate_piece],
+        sems,
         compute,
         z,
         n,
@@ -762,12 +820,15 @@
     rows[z] = grad[...]
     wait_weights()
     run()
-    out_gates[...] = sum_gates[z]
-    for k in range(1, n):
-        peer = collect(0, k)
-        out[...] += returned[peer].astype(jnp.float32)
-        peer = collect(1, k)
-        out_gates[...] += returned_gates[peer]
+    width = out.shape[1] // PARTS
+
+    def add(p, value):
+        if p == PARTS:
+            out_gates[...] += value
+        else:
+            out[:, p * width : (p + 1) * width] += value
+
+    collect(add)
     finish()
     for copy in local_copies():
         copy.wait()
@@ -782,8 +843,8 @@
     return [
         pltpu.SemaphoreType.DMA((kinds_out, 2, n)),
         pltpu.SemaphoreType.DMA((kinds_out, 2, n)),
-        pltpu.SemaphoreType.DMA((kinds_back, n)),
-        pltpu.SemaphoreType.DMA((kinds_back, n)),
+        pltpu.SemaphoreType.DMA((n, kinds_back)),
+        pltpu.SemaphoreType.DMA((2, n, kinds_back)),
     ]
 
 
@@ -814,7 +875,8 @@
     shapes = [
         jax.ShapeDtypeStruct((length, width), low),
         jax.ShapeDtypeStruct((n, length, width), low),
-        jax.ShapeDtypeStruct((n, length, COLUMNS), full),
+        jax.ShapeDtypeStruct((n, length, COLUMNS), low),
+        jax.ShapeDtypeStruct((length, COLUMNS), full),
         kept,
         kept,
         jax.ShapeDtypeStruct((n, length, held * inner), low),
@@ -822,12 +884,12 @@
     ]
     scratch = [
         pltpu.VMEM((n, length, width), low),
-        pltpu.VMEM((n, length, width), low),
+        pltpu.VMEM((2, n, length, width), low),
         pltpu.VMEM((held, length, inner), low),
         pltpu.VMEM((length, width), full),
         pltpu.VMEM((n, 8, COLUMNS), full),
         pltpu.SemaphoreType.DMA((3 * held,)),
-    ] + exchange_scratch(n, 3, 1)
+    ] + exchange_scratch(n, 3, PARTS)
     kernel = functools.partial(experts_forward_kernel, layer, experts)
     return expert_call(
         kernel, (normed_two, mask, hidden, router), own, other, (), shapes, scratch, 1 + layer
@@ -848,15 +910,16 @@
     ]
     scratch = [
         pltpu.VMEM((n, length, width), low),
-        pltpu.VMEM((n, length, COLUMNS), full),
-        pltpu.VMEM((n, length, width), low),
-        pltpu.VMEM((n, length, COLUMNS), full),
+        pltpu.VMEM((n, length, COLUMNS), low),
+        pltpu.VMEM((2, n, length, width), low),
+        pltpu.VMEM((2, n, length, COLUMNS), low),
         pltpu.VMEM((n, length, held * inner), low),
+        pltpu.VMEM((length, COLUMNS), full),
         pltpu.SemaphoreType.DMA((3 * held,)),
         pltpu.SemaphoreType.DMA((2 + 2 * n,)),
         pltpu.SemaphoreType.DMA((2 + 2 * n,)),
         pltpu.SemaphoreType.DMA((2,)),
-    ] + exchange_scratch(n, 1, 2)
+    ] + exchange_scratch(n, 1, PARTS + 1)
     kernel = functools.partial(experts_backward_kernel, layer)
     return expert_call(
         kernel,
@@ -963,7 +1026,7 @@
     for s in (1, 0):
         inputs, state, expert_state = saved[s]
         (inverse_one, normed_one, _, _, _, _, attended, hidden, inverse_two, normed_two) = state
-        rows_all, gates_all, gate_keep, up_keep, gated = expert_state
+        rows_all, gates_all, gates, gate_keep, up_keep, gated = expert_state
         gain_moe, w_router = weights[s][5], weights[s][6]
         grad_sum, grad_gates, rows_both, gated_both, grad_both, pre_both = experts_backward(
             s,
@@ -985,7 +1048,6 @@
             second_pre = lax.psum_scatter(grad_gate_up, "dp", scatter_dimension=0, tiled=True)
         else:
             grad_sum, second_pre = lax.optimization_barrier((grad_sum, second_pre))
-        gates = lax.dynamic_index_in_dim(gates_all, lax.axis_index("expert"), 0, keepdims=False)
         gates, grad_gates = gates[:, :experts], grad_gates[:, :experts]
         grad_chosen = gates * (grad_gates - jnp.sum(gates * grad_gates, axis=-1, keepdims=True))
         grad_logits = grad_chosen.astype(jnp.bfloat16)
@@ -1027,14 +1089,13 @@
         ).astype(jnp.bfloat16)
         small = jnp.pad(small, ((0, 0), (0, COLUMNS - small.shape[1])))
         if s == 1:
-            axes = ("dp", "expert")
             dp = lax.axis_size("dp")
             parts = grad_down.reshape(held // 2, dp, inner // dp, D)
             parts = jnp.moveaxis(parts, 1, 0).reshape(-1, D)
             dense = jnp.concatenate([grad_w_qkv, grad_w_out, small], axis=1)
             grad_inputs, parts, dense = lax.optimization_barrier((grad_inputs, parts, dense))
+            second_dense = lax.psum_scatter(dense, "dp", scatter_dimension=0, tiled=True)
             second_down = lax.psum_scatter(parts, "dp", scatter_dimension=0, tiled=True)
-            second_dense = lax.psum_scatter(dense, axes, scatter_dimension=0, tiled=True)
         grads[s] = (grad_gate_up, grad_down, grad_w_qkv, grad_w_out, small)
         input_grads[s] = grad_inputs
         grad_low = grad_inputs.astype(jnp.bfloat16)
@@ -1049,7 +1110,9 @@
     lanes += dense_lanes(len(arrays))
     for array in (grad_w_qkv, grad_w_out, small):
         arrays.append(array.reshape(dp, deep, array.shape[0] // (dp * deep), array.shape[1]))
-    *arrays, second_down = lax.optimization_barrier((*arrays, second_down))
+    lanes.append((len(arrays), None, [("expert", bits_of("expert"))]))
+    rows_each = second_dense.shape[0] // deep
+    arrays.append(second_dense.reshape(deep, rows_each, second_dense.shape[1]))
     *sums, stats = sum_scatter(arrays, lanes, jnp.concatenate(stats, axis=0), 0)
     stats = lax.dynamic_index_in_dim(stats.reshape(2, 8, COLUMNS), core, 0)
     token_total = SEQ * lax.axis_size(("section", "dp", "expert"))
@@ -1067,6 +1130,7 @@
         second_down.reshape(half, inner // dp, D),
     )
     qkv, out = grads[0][2].shape[1], grads[0][3].shape[1]
+    second_dense = sums[9]
     second_dense = (
         second_dense[:, :qkv], second_dense[:, qkv : qkv + out], second_dense[:, qkv + out :]
     )

time: 635 us -> 622 us (0.980)
  Pallas kernels: 405 us -> 376 us
  local copies, waits for them, and re-layouts: 36.9 us -> 48 us
    pallas_call x1, Pallas kernels: 159 us -> 143 us  [sum_scatter(): pl.pallas_call(functools.partial(sum_scatter_kernel, (plans, len(arrays),...]
    unnamed x219 -> x226, local copies, waits for them, and re-layouts: 13.4 us -> 28.2 us
    pallas_call x4, Pallas kernels: 246 us -> 232 us  [expert_call(): pl.pallas_call(kernel, out_shape=shapes, in_specs=[vmem] * len(operands)...]
  transfers between devices with their start and end apart: 24 -> 24, of which waited for: 3 -> 3; matrix products, arithmetic and copies ran while one was open for 22% -> 24% of each run, Pallas kernels for 37% -> 35%
where the time goes in v6:
time: 622 us; the launch traced here: 611 us
  Pallas kernels  376 us (60%)
  matrix products  93.4 us (15%)
  other arithmetic  50.8 us (8%)
  local copies, waits for them, and re-layouts  48 us (8%)
  waiting for transfers between devices  17.6 us (3%)
  between operations  15.8 us (3%)
  starting transfers between devices  10.5 us (2%)
    pallas_call x4, Pallas kernels, expert_call(): pl.pallas_call(kernel, out_shape=shapes, in_specs=[vmem] * len(operands)...  232 us
    pallas_call x1, Pallas kernels, sum_scatter(): pl.pallas_call(functools.partial(sum_scatter_kernel, (plans, len(arrays),...  143 us
    dot_general x10, matrix products, turned(): jnp.einsum('tc,tq->cq', left, right, preferred_element_type=jnp.float32)  33.2 us
    unnamed x226, local copies, waits for them, and re-layouts  28.2 us
    dot_general x8, matrix products, matmul(): return jnp.dot(left_side, right_side, preferred_element_type=jnp.float32)  24.7 us
    ppermute x21, waiting for transfers between devices, swapped(): return lax.ppermute(array, 'section', [(0, 1), (1, 0)])  17.5 us
  transfers between devices with their start and end apart: 24, of which 3 were waited for; matrix products, arithmetic and copies ran while one was open for 24% of the time, Pallas kernels for 35%

profile of v6, /device:TPU:0, one launch (start us, length us, event | category | flops | bytes accessed | tf_op | source)
XLA Modules:
  0.0 611.5 jit_solution(15492452595096781431)
XLA Ops:
  13.7 1.7 collective-permute-done
  16.1 4.9 collective-permute-done.7
  33.5 2.2 fusion.25
  35.8 4.4 fusion.4
  40.4 1.6 fusion.125
  41.9 1.6 convolution_convert_fusion.9
  43.6 10.9 %collective-permute-done.4 = bf16[1536,1536]{1,0:T(8,128)(2,1)} collective-permute-done((bf16[1536,1536]{1,0:T(8,128)(2,1)}, bf16[1536,1536]{1,0:T(8,128)(2,1)}, u32[]{:S(2)}, u32[]{:S(2)}) %collective-permute-start.4) | collective-permute-done | bytes 4718624 | tf_op jit(solution)/shard_map/ppermute | solution.py:92
  54.5 3.6 multiply_reduce_fusion.7
  59.2 55.8 %shard_map.237 = (bf16[96,1536]{1,0:T(8,128)(2,1)S(1)}, bf16[4,96,1536]{2,1,0:T(8,128)(2,1)S(1)}, bf16[4,96,128]{2,1,0:T(8,128)(2,1)S(1)}, f32[96,128]{1,0:T(8,1...) custom-call(bf16[96,1536]{1,0:T(8,128)(2,1)S(1)} %multiply_convert_f, ...), custom_call_target="tpu_custom_call" | custom-call | flops 49999998976 | bytes 100000000 | tf_op jit(solution)/shard_map/pallas_call | solution.py:854
  117.5 2.7 fusion.28
  120.3 5.8 fusion.5
  127.9 5.1 multiply_reduce_fusion.6
  133.2 46.1 %shard_map.238 = (bf16[96,1536]{1,0:T(8,128)(2,1)S(1)}, bf16[4,96,1536]{2,1,0:T(8,128)(2,1)S(1)}, bf16[4,96,128]{2,1,0:T(8,128)(2,1)S(1)}, f32[96,128]{1,0:T(8,1...) custom-call(bf16[96,1536]{1,0:T(8,128)(2,1)S(1)} %multiply_convert_f, ...), custom_call_target="tpu_custom_call" | custom-call | flops 49999998976 | bytes 100000000 | tf_op jit(solution)/shard_map/pallas_call | solution.py:854
  179.3 60.5 %shard_map.239 = (f32[96,1536]{1,0:T(8,128)S(1)}, f32[96,128]{1,0:T(8,128)S(1)}, bf16[2,4,96,1536]{3,2,1,0:T(8,128)(2,1)}, bf16[2,4,96,1024]{3,2,1,0:T(8,128)(2,...) custom-call(bf16[96,1536]{1,0:T(8,128)(2,1)S(1)} %constant_dynamic-slice_fusion.9.grad, ...), custom_call_target="tpu_custom_call" | custom-call | flops 49999998976 | bytes 100000000 | tf_op jit(solution)/shard_map/pallas_call | solution.py:854
  240.9 9.1 %bitcast_convert_fusion.1 = bf16[1536,2048]{1,0:T(8,128)(2,1)} fusion(bf16[2,4,96,1536]{3,2,1,0:T(8,128)(2,1)} %get-tuple-element.69, bf16[2,4,96,2048]{3,2,1,0:T(8,128)(2,1)} %get-tuple-element.70), kind=kOutput, calls=%fused_computation.3 | convolution fusion | flops 4834983936 | bytes 11796480 | tf_op jit(solution)/shard_map/tc,tq->cq/dot_general | solution.py:987
  253.5 6.2 %convolution_convert_fusion.5 = bf16[96,1536]{1,0:T(8,128)(2,1)} fusion(bf16[96,1536]{1,0:T(8,128)(2,1)S(1)} %get-tuple-element.173, bf16[1536,1536]{1,0:T(8,128)(2,1)} %collective-permute-done.4, pred[]{:T(512)S(6)} %eq.20, bf16[1,1536,1536]{2,1,0:T(8,128)(2,1)} %param.22), kind=kOutput, calls=%fused_computation.25 | convolution fusion | flops 455491584 | bytes 10027009 | tf_op jit(solution)/shard_map/td,cd->tc/dot_general | solution.py:941
  266.4 1.9 copy.147
  268.3 2.2 fusion.26
  271.7 6.0 fusion.47
  281.2 2.9 bitcast_convert_fusion.3
  284.2 1.9 copy.146
  288.5 3.2 pad_maximum_fusion
  291.7 9.4 %copy.188 = bf16[1536,2176]{1,0:T(8,128)(2,1)} copy(bf16[1536,2176]{0,1:T(8,128)(2,1)} %pad_maximum_fusion) | data formatting | bytes 13369344
  304.6 1.6 copy-done.11
  306.3 69.8 %shard_map.240 = (f32[96,1536]{1,0:T(8,128)S(1)}, f32[96,128]{1,0:T(8,128)S(1)}, bf16[2,4,96,1536]{3,2,1,0:T(8,128)(2,1)}, bf16[2,4,96,1024]{3,2,1,0:T(8,128)(2,...) custom-call(bf16[96,1536]{1,0:T(8,128)(2,1)S(1)} %get-tuple-element.78.grad, ...), custom_call_target="tpu_custom_call" | custom-call | flops 49999998976 | bytes 100000000 | tf_op jit(solution)/shard_map/pallas_call | solution.py:854
  377.4 1.4 copy-done.9
  378.8 5.8 bitcast_convert_fusion.2
  384.6 7.4 %bitcast_convert_fusion = bf16[1536,2048]{1,0:T(8,128)(2,1)} fusion(bf16[2,4,96,1536]{3,2,1,0:T(8,128)(2,1)S(1)} %copy-done.110, bf16[2,4,96,2048]{3,2,1,0:T(8,128)(2,1)S(1)} %copy-done.109), kind=kOutput, calls=%fused_computation.2 | convolution fusion | flops 4834983936 | bytes 11796480 | tf_op jit(solution)/shard_map/tc,tq->cq/dot_general | solution.py:987
  393.8 4.0 convolution_convert_fusion.4
  399.8 1.4 multiply_reduce_fusion
  404.0 1.5 fusion.23
  405.8 2.1 fusion.24
  408.0 4.3 fusion.38
  413.5 4.2 collective-permute-start.13
  421.2 1.5 slice_bitcast_fusion.1
  422.7 2.5 maximum_select_fusion
  428.2 2.2 convolution_convert_fusion.2
  430.4 3.2 convolution_convert_fusion
  433.6 143.3 %shard_map.241 = (bf16[384,512]{1,0:T(8,128)(2,1)}, bf16[384,512]{1,0:T(8,128)(2,1)}, bf16[384,512]{1,0:T(8,128)(2,1)}, bf16[384,512]{1,0:T(8,128)(2,1)}, bf16[1...) custom-call(bf16[4,384,2048]{2,1,0:T(8,128)(2,1)} %bitcast.334, ...), custom_call_target="tpu_custom_call" | custom-call | tf_op jit(solution)/shard_map/pallas_call | solution.py:347
  577.7 1.6 broadcast_select_fusion.35
  579.9 1.7 broadcast_select_fusion.33
  582.9 2.3 broadcast_select_fusion.16
  594.1 1.6 convert_select_fusion.3
  595.7 2.0 maximum_bitcast_fusion.1
  597.7 1.6 convert_select_fusion.1
  599.3 1.9 maximum_bitcast_fusion.2
  601.2 1.6 convert_select_fusion.5
  602.8 2.0 maximum_bitcast_fusion
  (389 shorter events, 73.5 us)
Async XLA Ops:
  7.2 8.6 %copy-start = (s32[2,96]{1,0:T(2,128)S(1)}, s32[2,96]{1,0:T(2,128)}, u32[]{:S(2)}) copy-start(s32[2,96]{1,0:T(2,128)} %param.16) | copy-start | bytes 2308
  7.2 384.9 %reduce-scatter.6.cloned.1.call-start = ((), (), s32[]{:S(2)}) async-start(), calls=%async_computation.3 | async-start | bytes 7864320 | tf_op jit(solution)/shard_map/reduce_scatter | solution.py:1048
  7.2 14.1 %collective-permute-start.1 = (bf16[1536,512]{1,0:T(8,128)(2,1)}, bf16[1536,512]{1,0:T(8,128)(2,1)S(1)}, u32[]{:S(2)}, u32[]{:S(2)}) collective-permute-start(bf16[1536,512]{1,0:T(8,128)(2,1)} %bitcast.335), channel_id=1, source_target_pairs={{0,16},{16,0},{1,17},{17,1},{2,18},{18,2},{3,19},{19,3},{4,20},{20... | collective-permute-start | bytes 4718600 | tf_op jit(solution)/shard_map/ppermute | solution.py:92
  7.8 16.2 %collective-permute-start.2 = (bf16[1536,512]{1,0:T(8,128)(2,1)}, bf16[1536,512]{1,0:T(8,128)(2,1)S(1)}, u32[]{:S(2)}, u32[]{:S(2)}) collective-permute-start(bf16[1536,512]{1,0:T(8,128)(2,1)} %bitcast.336), channel_id=1, source_target_pairs={{0,16},{16,0},{1,17},{17,1},{2,18},{18,2},{3,19},{19,3},{4,20},{20... | collective-permute-start | bytes 4718600 | tf_op jit(solution)/shard_map/ppermute | solution.py:92
  7.8 28.0 %collective-permute-start.3 = (bf16[1536,1536]{1,0:T(8,128)(2,1)}, bf16[1536,1536]{1,0:T(8,128)(2,1)}, u32[]{:S(2)}, u32[]{:S(2)}) collective-permute-start(bf16[1536,1536]{1,0:T(8,128)(2,1)} %bitcast.415), channel_id=1, source_target_pairs={{0,16},{16,0},{1,17},{17,1},{2,18},{18,2},{3,19},{19,3},{4,20},{20... | collective-permute-start | bytes 14155784 | tf_op jit(solution)/shard_map/ppermute | solution.py:92
  9.0 4.5 collective-permute-start.5
  9.9 17.1 %copy-start.97 = (bf16[1536]{0:T(1024)(128)(2,1)}, bf16[1536]{0:T(1024)(128)(2,1)S(1)}, u32[]{:S(2)}) copy-start(bf16[1536]{0:T(1024)(128)(2,1)S(1)} %reduce) | copy-start | bytes 9220
  9.9 5.6 collective-permute-start
  13.5 15.8 %copy-start.43 = (bf16[1,1536,16]{2,1,0:T(8,128)(2,1)}, bf16[1,1536,16]{2,1,0:T(8,128)(2,1)S(1)}, u32[]{:S(2)}) copy-start(bf16[1,1536,16]{2,1,0:T(8,128)(2,1)S(1)} %copy.137) | copy-start | bytes 147460
  13.5 11.5 %copy-start.102 = (bf16[1536]{0:T(1024)(128)(2,1)}, bf16[1536]{0:T(1024)(128)(2,1)S(1)}, u32[]{:S(2)}) copy-start(bf16[1536]{0:T(1024)(128)(2,1)S(1)} %collective-permute-done.5) | copy-start | bytes 9220
  13.6 2.3 collective-permute-start.6
  15.4 5.5 collective-permute-start.7
  15.8 42.9 %collective-permute-start.8 = (bf16[4,1536,512]{2,1,0:T(8,128)(2,1)}, bf16[4,1536,512]{2,1,0:T(8,128)(2,1)}, u32[]{:S(2)}, u32[]{:S(2)}) collective-permute-start(bf16[4,1536,512]{2,1,0:T(8,128)(2,1)} %bitcast.400), channel_id=1, source_target_pairs={{0,16},{16,0},{1,17},{17,1},{2,18},{18,2},{3,19},{19,3},{4,20},{20... | collective-permute-start | bytes 18874376 | tf_op jit(solution)/shard_map/ppermute | solution.py:92
  20.9 37.8 %collective-permute-start.9 = (bf16[4,1536,512]{2,1,0:T(8,128)(2,1)}, bf16[4,1536,512]{2,1,0:T(8,128)(2,1)}, u32[]{:S(2)}, u32[]{:S(2)}) collective-permute-start(bf16[4,1536,512]{2,1,0:T(8,128)(2,1)} %bitcast.405), channel_id=1, source_target_pairs={{0,16},{16,0},{1,17},{17,1},{2,18},{18,2},{3,19},{19,3},{4,20},{20... | collective-permute-start | bytes 18874376 | tf_op jit(solution)/shard_map/ppermute | solution.py:92
  21.7 7.6 %copy-start.18 = (bf16[1536,512]{1,0:T(8,128)(2,1)}, bf16[1536,512]{1,0:T(8,128)(2,1)S(1)}, u32[]{:S(2)}) copy-start(bf16[1536,512]{1,0:T(8,128)(2,1)S(1)} %collective-permute-done.1) | copy-start | bytes 4718596
  21.7 37.1 %collective-permute-start.10 = (bf16[4,512,1536]{2,1,0:T(8,128)(2,1)}, bf16[4,512,1536]{2,1,0:T(8,128)(2,1)}, u32[]{:S(2)}, u32[]{:S(2)}) collective-permute-start(bf16[4,512,1536]{2,1,0:T(8,128)(2,1)} %bitcast.410), channel_id=1, source_target_pairs={{0,16},{16,0},{1,17},{17,1},{2,18},{18,2},{3,19},{19,3},{4,20},{20... | collective-permute-start | bytes 18874376 | tf_op jit(solution)/shard_map/ppermute | solution.py:92
  23.9 30.5 %collective-permute-start.4 = (bf16[1536,1536]{1,0:T(8,128)(2,1)}, bf16[1536,1536]{1,0:T(8,128)(2,1)}, u32[]{:S(2)}, u32[]{:S(2)}) collective-permute-start(bf16[1536,1536]{1,0:T(8,128)(2,1)} %bitcast.332), channel_id=1, source_target_pairs={{0,16},{16,0},{1,17},{17,1},{2,18},{18,2},{3,19},{19,3},{4,20},{20... | collective-permute-start | bytes 14155784 | tf_op jit(solution)/shard_map/ppermute | solution.py:92
  28.0 30.6 %copy-start.83 = (f32[1536]{0:T(1024)}, f32[1536]{0:T(1024)S(1)}, u32[]{:S(2)}) copy-start(f32[1536]{0:T(1024)S(1)} %get-tuple-element.231) | copy-start | bytes 18436
  33.4 8.5 %copy-start.85 = (bf16[96,512]{0,1:T(8,128)(2,1)}, bf16[96,512]{0,1:T(8,128)(2,1)S(1)}, u32[]{:S(2)}) copy-start(bf16[96,512]{0,1:T(8,128)(2,1)S(1)} %copy.132) | copy-start | bytes 294916
  41.9 12.5 %copy-start.28 = (bf16[192,1536]{1,0:T(8,128)(2,1)S(1)}, bf16[192,1536]{1,0:T(8,128)(2,1)}, u32[]{:S(2)}) copy-start(bf16[192,1536]{1,0:T(8,128)(2,1)} %param.14) | copy-start | bytes 1769476
  43.6 14.4 %copy-start.33 = (bf16[8,64,3,96]{3,1,2,0:T(8,128)(2,1)}, bf16[8,64,3,96]{3,1,2,0:T(8,128)(2,1)S(1)}, u32[]{:S(2)}) copy-start(bf16[8,64,3,96]{3,1,2,0:T(8,128)(2,1)S(1)} %convolution_convert_fusion.9) | copy-start | bytes 884740
  58.0 57.0 %copy-start.2 = (f32[96,1536]{1,0:T(8,128)}, f32[96,1536]{1,0:T(8,128)S(1)}, u32[]{:S(2)}) copy-start(f32[96,1536]{1,0:T(8,128)S(1)} %get-tuple-element.247.hidden) | copy-start | bytes 1769476
  58.8 56.3 %copy-start.4 = (bf16[96,1536]{1,0:T(8,128)(2,1)}, bf16[96,1536]{1,0:T(8,128)(2,1)S(1)}, u32[]{:S(2)}) copy-start(bf16[96,1536]{1,0:T(8,128)(2,1)S(1)} %multiply_convert_fusion.3.x) | copy-start | bytes 884740
  59.2 57.6 %copy-start.92 = (f32[1536]{0:T(1024)S(1)}, f32[1536]{0:T(1024)}, u32[]{:S(2)}) copy-start(f32[1536]{0:T(1024)} %get-tuple-element.232) | copy-start | bytes 18436
  59.2 57.7 %copy-start.20 = (bf16[1536,512]{1,0:T(8,128)(2,1)S(1)}, bf16[1536,512]{1,0:T(8,128)(2,1)}, u32[]{:S(2)}) copy-start(bf16[1536,512]{1,0:T(8,128)(2,1)} %copy-done.18) | copy-start | bytes 4718596
  117.5 9.4 %copy-start.87 = (bf16[96,512]{0,1:T(8,128)(2,1)}, bf16[96,512]{0,1:T(8,128)(2,1)S(1)}, u32[]{:S(2)}) copy-start(bf16[96,512]{0,1:T(8,128)(2,1)S(1)} %copy.138) | copy-start | bytes 294916
  250.1 183.5 %reduce-scatter.10.cloned.1.call-start = ((), (), s32[]{:S(2)}) async-start(), calls=%async_computation.5 | async-start | bytes 8355840 | tf_op jit(solution)/shard_map/reduce_scatter | solution.py:1097
  253.5 6.2 %copy-start.49 = (bf16[96,1536]{1,0:T(8,128)(2,1)}, bf16[96,1536]{1,0:T(8,128)(2,1)S(1)}, u32[]{:S(2)}) copy-start(bf16[96,1536]{1,0:T(8,128)(2,1)S(1)} %get-tuple-element.173) | copy-start | bytes 884740
  253.5 7.4 %copy-start.55 = (f32[8,3,96,96]{2,3,1,0:T(8,128)S(1)}, f32[8,3,96,96]{2,3,1,0:T(8,128)}, u32[]{:S(2)}) copy-start(f32[8,3,96,96]{2,3,1,0:T(8,128)} %copy-done.54) | copy-start | bytes 2654212
  253.5 7.4 %copy-start.96 = (f32[8,3,96]{2,1,0:T(4,128)S(1)}, f32[8,3,96]{2,1,0:T(4,128)}, u32[]{:S(2)}) copy-start(f32[8,3,96]{2,1,0:T(4,128)} %copy-done.95) | copy-start | bytes 27652
  271.7 6.1 copy-start.30
  271.7 6.1 copy-start.106
  280.0 6.3 %collective-permute-start.12 = (bf16[96,5120]{1,0:T(8,128)(2,1)S(1)}, bf16[96,5120]{1,0:T(8,128)(2,1)S(1)}, u32[]{:S(2)}, u32[]{:S(2)}) collective-permute-start(bf16[96,5120]{1,0:T(8,128)(2,1)S(1)} %pad_maximum_fusion.1), channel_id=1, source_target_pairs={{0,16},{16,0},{1,17},{17,1},{2,18},{18,2},{3,19},{19,3},{4,20},{20... | collective-permute-start | bytes 2949128 | tf_op jit(solution)/shard_map/ppermute | solution.py:92
  301.1 281.8 %reduce-scatter.8.cloned.1.call-start = ((), (), s32[]{:S(2)}) async-start(), calls=%async_computation.4 | async-start | bytes 3932160 | tf_op jit(solution)/shard_map/reduce_scatter | solution.py:1098
  302.1 1.6 collective-permute-start.11
  384.6 7.5 %copy-start.3 = (f32[96,1536]{1,0:T(8,128)S(1)}, f32[96,1536]{1,0:T(8,128)}, u32[]{:S(2)}) copy-start(f32[96,1536]{1,0:T(8,128)} %copy-done.2) | copy-start | bytes 1769476
  384.6 7.5 %copy-start.22 = (bf16[1536,16]{1,0:T(8,128)(2,1)S(1)}, bf16[1536,16]{1,0:T(8,128)(2,1)}, u32[]{:S(2)}) copy-start(bf16[1536,16]{1,0:T(8,128)(2,1)} %copy-done.21) | copy-start | bytes 147460
  384.6 7.5 %copy-start.84 = (f32[1536]{0:T(1024)S(1)}, f32[1536]{0:T(1024)}, u32[]{:S(2)}) copy-start(f32[1536]{0:T(1024)} %copy-done.83) | copy-start | bytes 18436
  384.6 7.5 %copy-start.101 = (f32[96]{0:T(128)S(1)}, f32[96]{0:T(128)}, u32[]{:S(2)}) copy-start(f32[96]{0:T(128)} %copy-done.100) | copy-start | bytes 1156
  413.5 9.2 %collective-permute-start.13 = (f32[96,1536]{1,0:T(8,128)}, f32[96,1536]{1,0:T(8,128)}, u32[]{:S(2)}, u32[]{:S(2)}) collective-permute-start(f32[96,1536]{1,0:T(8,128)} %get-tuple-element.182), channel_id=1, source_target_pairs={{0,16},{16,0},{1,17},{17,1},{2,18},{18,2},{3,19},{19,3},{4,20},{20... | collective-permute-start | bytes 1769480 | tf_op jit(solution)/shard_map/ppermute | solution.py:92
  418.9 6.3 %collective-permute-start.14 = (bf16[96,5120]{1,0:T(8,128)(2,1)}, bf16[96,5120]{1,0:T(8,128)(2,1)}, u32[]{:S(2)}, u32[]{:S(2)}) collective-permute-start(bf16[96,5120]{1,0:T(8,128)(2,1)} %pad_maximum_fusion.2), channel_id=1, source_target_pairs={{0,16},{16,0},{1,17},{17,1},{2,18},{18,2},{3,19},{19,3},{4,20},{20... | collective-permute-start | bytes 2949128 | tf_op jit(solution)/shard_map/ppermute | solution.py:92
  577.7 10.2 %collective-permute-start.15 = (bf16[96,128]{1,0:T(8,128)(2,1)S(1)}, bf16[96,128]{1,0:T(8,128)(2,1)S(1)}, u32[]{:S(2)}, u32[]{:S(2)}) collective-permute-start(bf16[96,128]{1,0:T(8,128)(2,1)S(1)} %broadcast_select_fusion.37), channel_id=1, source_target_pairs={{0,16},{16,0},{1,17},{17,1},{2,18},{18,2},{3,19},{19,3},{4,20},{20... | collective-permute-start | bytes 73736 | tf_op jit(solution)/shard_map/ppermute | solution.py:92
  579.3 6.1 copy-start.41
  579.3 10.1 %collective-permute-start.17 = (bf16[96,768]{1,0:T(8,128)(2,1)}, bf16[96,768]{1,0:T(8,128)(2,1)}, u32[]{:S(2)}, u32[]{:S(2)}) collective-permute-start(bf16[96,768]{1,0:T(8,128)(2,1)} %broadcast_select_fusion.35), channel_id=1, source_target_pairs={{0,16},{16,0},{1,17},{17,1},{2,18},{18,2},{3,19},{19,3},{4,20},{20... | collective-permute-start | bytes 442376 | tf_op jit(solution)/shard_map/ppermute | solution.py:92
  581.5 9.8 %collective-permute-start.16 = (bf16[96,1280]{1,0:T(8,128)(2,1)}, bf16[96,1280]{1,0:T(8,128)(2,1)}, u32[]{:S(2)}, u32[]{:S(2)}) collective-permute-start(bf16[96,1280]{1,0:T(8,128)(2,1)} %broadcast_select_fusion.33), channel_id=1, source_target_pairs={{0,16},{16,0},{1,17},{17,1},{2,18},{18,2},{3,19},{19,3},{4,20},{20... | collective-permute-start | bytes 737288 | tf_op jit(solution)/shard_map/ppermute | solution.py:92
  585.3 12.4 %collective-permute-start.20 = (bf16[2,128,1536]{2,1,0:T(8,128)(2,1)}, bf16[2,128,1536]{2,1,0:T(8,128)(2,1)}, u32[]{:S(2)}, u32[]{:S(2)}) collective-permute-start(bf16[2,128,1536]{2,1,0:T(8,128)(2,1)} %broadcast_select_fusion.16), channel_id=1, source_target_pairs={{0,16},{16,0},{1,17},{17,1},{2,18},{18,2},{3,19},{19,3},{4,20},{20... | collective-permute-start | bytes 2359304 | tf_op jit(solution)/shard_map/ppermute | solution.py:92
  586.4 7.7 %collective-permute-start.19 = (bf16[2,384,512]{2,1,0:T(8,128)(2,1)}, bf16[2,384,512]{2,1,0:T(8,128)(2,1)}, u32[]{:S(2)}, u32[]{:S(2)}) collective-permute-start(bf16[2,384,512]{2,1,0:T(8,128)(2,1)} %broadcast_select_fusion.18), channel_id=1, source_target_pairs={{0,16},{16,0},{1,17},{17,1},{2,18},{18,2},{3,19},{19,3},{4,20},{20... | collective-permute-start | bytes 2359304 | tf_op jit(solution)/shard_map/ppermute | solution.py:92
  587.9 13.3 %collective-permute-start.18 = (bf16[2,384,512]{2,1,0:T(8,128)(2,1)}, bf16[2,384,512]{2,1,0:T(8,128)(2,1)}, u32[]{:S(2)}, u32[]{:S(2)}) collective-permute-start(bf16[2,384,512]{2,1,0:T(8,128)(2,1)} %broadcast_select_fusion.20), channel_id=1, source_target_pairs={{0,16},{16,0},{1,17},{17,1},{2,18},{18,2},{3,19},{19,3},{4,20},{20... | collective-permute-start | bytes 2359304 | tf_op jit(solution)/shard_map/ppermute | solution.py:92
  (87 other events, 210.0 us)
Sparse Core Ops, SparseCore 0:
  250.2 75.7 reduce-scatter.5
  329.1 73.5 reduce-scatter.9
  406.3 52.4 reduce-scatter.7

commit v7 on v6

--- a/solution.py
+++ b/solution.py
@@ -489,29 +489,18 @@
             sum_copy(way, block, p).start()
 
     def run():
-        def both(hop):
-            return (hop >= 0) & (z - 1 - hop >= 0) & (z + 1 + hop < n)
-
-        def turn(k, carry):
-            hop = lax.div(k + 1, 2) - 1
-            block = z + (1 + hop) * (1 - 2 * lax.rem(k, 2))
-            odd = lax.rem(k, 2) == 1
-
-            @pl.when(odd & jnp.logical_not(both(hop - 1)))
-            def _():
-                take(hop)
-
-            @pl.when(jnp.logical_not(odd) & both(hop) & (hop + 1 < n - 1))
-            def _():
-                take(hop + 1)
-
-            @pl.when((block >= 0) & (block < n))
-            def _():
-                compute(block, sent)
-
-            return carry
-
-        lax.fori_loop(0, 2 * n - 1, turn, 0)
+        inward = jnp.where(2 * z < n, 1, -1)
+        outer = (z - inward >= 0) & (z - inward < n)
+        take(0)
+        compute(z, z + inward, True, sent)
+        for hop in range(1, n - 1):
+            take(hop)
+        compute(
+            jnp.where(outer, z - inward, z + 2 * inward),
+            jnp.where(outer, z + 2 * inward, z + 3 * inward),
+            False,
+            sent,
+        )
 
         first = jnp.where(2 * z < n, 0, 1)
         for way in (first, 1 - first):
@@ -563,7 +552,7 @@
     return [piece(p) for p in range(parts)]
 
 
-def fetch_weights(layer, own, other, places, sem):
+def fetch_weights(layer, own, other, places, sem, order):
     count = places[0].shape[0]
     mine = lax.axis_index("section") == layer
 
@@ -572,8 +561,8 @@
             group[kind].at[e], places[kind].at[e], sem.at[kind * count + e]
         )
 
-    for kind in range(len(places)):
-        for e in range(count):
+    for kinds in order:
+        for e, kind in itertools.product(range(count), kinds):
             @pl.when(mine)
             def _():
                 copy(own, kind, e).start()
@@ -582,10 +571,8 @@
             def _():
                 copy(other, kind, e).start()
 
-    def wait():
-        for kind in range(len(places)):
-            for e in range(count):
-                copy(own, kind, e).wait()
+    def wait(kind, e):
+        copy(own, kind, e).wait()
 
     return wait
 
@@ -604,44 +591,52 @@
 ):
     own, other, refs = refs[:3], refs[3:6], refs[6:]
     out, rows, gates_all, gates, gate_keep, up_keep, gated, stats = refs[:8]
-    w_gate, w_up, w_down, sums, returned, mixed, total, stats_all = refs[8:16]
-    weight_sem, *sems = refs[16:]
+    w_gate, w_up, w_down, sums, returned, mixed, stacked, total, stats_all = refs[8:17]
+    weight_sem, *sems = refs[17:]
     n, held = rows.shape[0], w_gate.shape[0]
     z = lax.axis_index("expert")
 
-    def compute(block, sent):
-        picked = rows[block]
-        gate_block = gates_all[block].astype(jnp.float32)
+    length = x.shape[0]
+
+    def compute(a, b, first, sent):
+        stacked[:length] = rows[a]
+        stacked[length:] = rows[b]
+        gate_block = jnp.concatenate([gates_all[a], gates_all[b]], axis=0).astype(jnp.float32)
 
         def one(e, carry):
-            gate_pre = jnp.dot(picked, w_gate[e], preferred_element_type=jnp.float32)
-            up_pre = jnp.dot(picked, w_up[e], preferred_element_type=jnp.float32)
-            gate_keep[e, block] = gate_pre.astype(jnp.bfloat16)
-            up_keep[e, block] = up_pre.astype(jnp.bfloat16)
+            if first:
+                wait_weight(0, e)
+                wait_weight(1, e)
+            gate_pre = jnp.dot(stacked[...], w_gate[e], preferred_element_type=jnp.float32)
+            up_pre = jnp.dot(stacked[...], w_up[e], preferred_element_type=jnp.float32)
             active = gate_pre * sigmoid_of(gate_pre) * up_pre
             share = (column_of(gate_block, z * held + e) * active).astype(jnp.bfloat16)
+            mixed[e] = share
             inner = share.shape[1]
-            gated[block, :, pl.ds(pl.multiple_of(e * inner, inner), inner)] = share
-            mixed[e] = share
+            at = pl.ds(pl.multiple_of(e * inner, inner), inner)
+            for block, half in ((a, slice(0, length)), (b, slice(length, 2 * length))):
+                gate_keep[e, block] = gate_pre[half].astype(jnp.bfloat16)
+                up_keep[e, block] = up_pre[half].astype(jnp.bfloat16)
+                gated[block, :, at] = share[half]
             return carry
 
         lax.fori_loop(0, held, one, 0)
+        if first:
+            for e in range(held):
+                wait_weight(2, e)
         width = out.shape[1] // PARTS
         for part in range(PARTS):
             at = pl.ds(part * width, width)
-            result = jnp.zeros((out.shape[0], width), jnp.float32)
+            result = jnp.zeros((2 * length, width), jnp.float32)
             for e in range(held):
                 result += jnp.dot(mixed[e], w_down[e, :, at], preferred_element_type=jnp.float32)
-
-            @pl.when(block == z)
-            def _():
-                total[:, at] = hidden[:, at] + result
-
-            @pl.when(block != z)
-            def _():
-                sums[block, :, at] = result.astype(jnp.bfloat16)
-
-            sent(block, part)
+            sums[b, :, at] = result[length:].astype(jnp.bfloat16)
+            sent(b, part)
+            if first:
+                total[:, at] = hidden[:, at] + result[:length]
+            else:
+                sums[a, :, at] = result[:length].astype(jnp.bfloat16)
+                sent(a, part)
 
     own_gates = gates_all.at[z]
     start, run, collect, finish = move_rows(
@@ -655,7 +650,9 @@
         [],
     )
     start(0)
-    wait_weights = fetch_weights(layer, own, other, (w_gate, w_up, w_down), weight_sem)
+    wait_weight = fetch_weights(
+        layer, own, other, (w_gate, w_up, w_down), weight_sem, ((0, 1), (2,))
+    )
     logits = jnp.dot(x[...], router[...], preferred_element_type=jnp.float32)
     chosen = mask[...] > 0
     highest = jnp.max(jnp.where(chosen, logits, MASKED), axis=1, keepdims=True)
@@ -675,7 +672,6 @@
     )
     start(2)
     rows[z] = x[...]
-    wait_weights()
     run()
     stats[...] = jnp.sum(stats_all[...], axis=0)
     width = out.shape[1] // PARTS
@@ -692,7 +688,7 @@
     own, other, saved_rows, saved_gated, refs = refs[:3], refs[3:6], refs[6], refs[7], refs[8:]
     out, out_gates, rows_both, gated_both, grad_both, pre_both = refs[:6]
     w_gate, w_up, w_down, sums, sum_gates, returned, returned_gates, away, dots = refs[6:15]
-    weight_sem, core_send, core_recv, core_local, *sems = refs[15:]
+    mixed, stacked, weight_sem, core_send, core_recv, core_local, *sems = refs[15:]
     n, held = gates.shape[0], w_gate.shape[0]
     half, inner = held // 2, w_gate.shape[2]
     core = lax.axis_index("section")
@@ -733,17 +729,25 @@
             ),
         )
 
-    def compute(block, sent):
-        picked = rows[block]
-        gate_block = gates[block].astype(jnp.float32)
+    length = grad.shape[0]
+
+    def compute(a, b, first, sent):
+        stacked[:length] = rows[a]
+        stacked[length:] = rows[b]
+        gate_block = jnp.concatenate([gates[a], gates[b]], axis=0).astype(jnp.float32)
         dots[...] = jnp.zeros(dots.shape, jnp.float32)
+        spans = ((a, slice(0, length)), (b, slice(length, 2 * length)))
+
+        def both(ref, e):
+            return jnp.concatenate([ref[e, a], ref[e, b]], axis=0).astype(jnp.float32)
 
         def one(e, place, j):
+            if first:
+                wait_weight(2, e)
             raw = lax.dot_general(
-                picked, w_down[e], turned_dims, preferred_element_type=jnp.float32
+                stacked[...], w_down[e], turned_dims, preferred_element_type=jnp.float32
             )
-            gate_pre = gate_keep[e, block].astype(jnp.float32)
-            up_pre = up_keep[e, block].astype(jnp.float32)
+            gate_pre, up_pre = both(gate_keep, e), both(up_keep, e)
             sigmoid = sigmoid_of(gate_pre)
             silu = gate_pre * sigmoid
             column = z * held + e
@@ -751,56 +755,60 @@
             here = lax.broadcasted_iota(jnp.int32, dots.shape, 1) == column
             dots[...] += jnp.where(here, dot, 0.0)
             active = column_of(gate_block, column) * raw
-            place[:, pl.ds(pl.multiple_of(j * inner, inner), inner)] = (
-                active * up_pre * sigmoid * (1.0 + gate_pre * (1.0 - sigmoid))
-            ).astype(jnp.bfloat16)
-            place[:, pl.ds(pl.multiple_of((half + j) * inner, inner), inner)] = (
-                active * silu
-            ).astype(jnp.bfloat16)
+            grads = (
+                (active * up_pre * sigmoid * (1.0 + gate_pre * (1.0 - sigmoid))).astype(
+                    jnp.bfloat16
+                ),
+                (active * silu).astype(jnp.bfloat16),
+            )
+            for kind, value in enumerate(grads):
+                mixed[kind, e] = value
+                at = pl.ds(pl.multiple_of((kind * half + j) * inner, inner), inner)
+                for block, span in spans:
+                    place(block)[:, at] = value[span]
 
         def own_half(j, carry):
-            one(core * half + j, pre_both.at[core, block], j)
+            one(core * half + j, lambda block: pre_both.at[core, block], j)
             return carry
 
         def other_half(j, carry):
-            one((1 - core) * half + j, away.at[block], j)
+            one((1 - core) * half + j, lambda block: away.at[block], j)
             return carry
 
         lax.fori_loop(0, half, other_half, 0)
-        for copy in block_copies(block):
-            copy.start()
+        for block in (a, b):
+            for copy in block_copies(block):
+                copy.start()
         lax.fori_loop(0, half, own_half, 0)
-        sum_gates[block] = dots[...].astype(jnp.bfloat16)
-
-        @pl.when(block == z)
-        def _():
-            out_gates[...] = dots[...]
-
-        sent(block, PARTS)
+        sum_gates[b] = dots[length:].astype(jnp.bfloat16)
+        sent(b, PARTS)
+        if first:
+            out_gates[...] = dots[:length]
+            for e in range(held):
+                wait_weight(0, e)
+                wait_weight(1, e)
+        else:
+            sum_gates[a] = dots[:length].astype(jnp.bfloat16)
+            sent(a, PARTS)
         width = out.shape[1] // PARTS
         for part in range(PARTS):
             at = pl.ds(part * width, width)
-            result = jnp.zeros((out.shape[0], width), jnp.float32)
-            for place, side in ((away.at[block], 1 - core), (pre_both.at[core, block], core)):
-                for kind, right in enumerate((w_gate, w_up)):
-                    for j in range(half):
-                        left = place[:, pl.ds((kind * half + j) * inner, inner)]
-                        result += lax.dot_general(
-                            left,
-                            right[side * half + j, at, :],
-                            turned_dims,
-                            preferred_element_type=jnp.float32,
-                        )
-
-            @pl.when(block == z)
-            def _():
-                out[:, at] = result
-
-            @pl.when(block != z)
-            def _():
-                sums[block, :, at] = result.astype(jnp.bfloat16)
-
-            sent(block, part)
+            result = jnp.zeros((2 * length, width), jnp.float32)
+            for kind, right in enumerate((w_gate, w_up)):
+                for e in range(held):
+                    result += lax.dot_general(
+                        mixed[kind, e],
+                        right[e, at, :],
+                        turned_dims,
+                        preferred_element_type=jnp.float32,
+                    )
+            sums[b, :, at] = result[length:].astype(jnp.bfloat16)
+            sent(b, part)
+            if first:
+                out[:, at] = result[:length]
+            else:
+                sums[a, :, at] = result[:length].astype(jnp.bfloat16)
+                sent(a, part)
 
     gate_piece = (lambda block: sum_gates.at[block], lambda way, block: returned_gates.at[way, block])
     start, run, collect, finish = move_rows(
@@ -814,11 +822,12 @@
         [{"section": 1 - core}],
     )
     start(0)
-    wait_weights = fetch_weights(layer, own, other, (w_gate, w_up, w_down), weight_sem)
+    wait_weight = fetch_weights(
+        layer, own, other, (w_gate, w_up, w_down), weight_sem, ((2,), (0, 1))
+    )
     for copy in whole_copies() + local_copies():
         copy.start()
     rows[z] = grad[...]
-    wait_weights()
     run()
     width = out.shape[1] // PARTS
 
@@ -885,7 +894,8 @@
     scratch = [
         pltpu.VMEM((n, length, width), low),
         pltpu.VMEM((2, n, length, width), low),
-        pltpu.VMEM((held, length, inner), low),
+        pltpu.VMEM((held, 2 * length, inner), low),
+        pltpu.VMEM((2 * length, width), low),
         pltpu.VMEM((length, width), full),
         pltpu.VMEM((n, 8, COLUMNS), full),
         pltpu.SemaphoreType.DMA((3 * held,)),
@@ -914,7 +924,9 @@
         pltpu.VMEM((2, n, length, width), low),
         pltpu.VMEM((2, n, length, COLUMNS), low),
         pltpu.VMEM((n, length, held * inner), low),
-        pltpu.VMEM((length, COLUMNS), full),
+        pltpu.VMEM((2 * length, COLUMNS), full),
+        pltpu.VMEM((2, held, 2 * length, inner), low),
+        pltpu.VMEM((2 * length, width), low),
         pltpu.SemaphoreType.DMA((3 * held,)),
         pltpu.SemaphoreType.DMA((2 + 2 * n,)),
         pltpu.SemaphoreType.DMA((2 + 2 * n,)),
@@ -1043,9 +1055,18 @@
         grad_gate_up = turned(
             rows_both.reshape(-1, D), pre_both.reshape(-1, held * inner)
         ).astype(jnp.bfloat16)
+        grad_down = turned(
+            gated_both.reshape(-1, held // 2 * inner), grad_both.reshape(-1, D)
+        ).astype(jnp.bfloat16)
         if s == 1:
-            grad_sum, grad_gate_up = lax.optimization_barrier((grad_sum, grad_gate_up))
+            dp = lax.axis_size("dp")
+            parts = grad_down.reshape(held // 2, dp, inner // dp, D)
+            parts = jnp.moveaxis(parts, 1, 0).reshape(-1, D)
+            grad_sum, grad_gate_up, parts = lax.optimization_barrier(
+                (grad_sum, grad_gate_up, parts)
+            )
             second_pre = lax.psum_scatter(grad_gate_up, "dp", scatter_dimension=0, tiled=True)
+            second_down = lax.psum_scatter(parts, "dp", scatter_dimension=0, tiled=True)
         else:
             grad_sum, second_pre = lax.optimization_barrier((grad_sum, second_pre))
         gates, grad_gates = gates[:, :experts], grad_gates[:, :experts]
@@ -1059,12 +1080,6 @@
         grad_inputs, grad_gain_attn, grad_qkv, grad_branch = attention_backward(
             grad_hidden, inputs, state, weights[s]
         )
-        if s == 1:
-            grad_inputs, gated_both = lax.optimization_barrier((grad_inputs, gated_both))
-        grad_down = turned(
-            gated_both.reshape(-1, held // 2 * inner), grad_both.reshape(-1, D)
-        ).astype(jnp.bfloat16)
-
         def halves(array):
             width = array.shape[1] // 2
             return (
@@ -1089,13 +1104,13 @@
         ).astype(jnp.bfloat16)
         small = jnp.pad(small, ((0, 0), (0, COLUMNS - small.shape[1])))
         if s == 1:
-            dp = lax.axis_size("dp")
-            parts = grad_down.reshape(held // 2, dp, inner // dp, D)
-            parts = jnp.moveaxis(parts, 1, 0).reshape(-1, D)
-            dense = jnp.concatenate([grad_w_qkv, grad_w_out, small], axis=1)
-            grad_inputs, parts, dense = lax.optimization_barrier((grad_inputs, parts, dense))
-            second_dense = lax.psum_scatter(dense, "dp", scatter_dimension=0, tiled=True)
-            second_down = lax.psum_scatter(parts, "dp", scatter_dimension=0, tiled=True)
+            grad_inputs, grad_w_qkv, grad_w_out = lax.optimization_barrier(
+                (grad_inputs, grad_w_qkv, grad_w_out)
+            )
+            second_qkv = lax.psum_scatter(grad_w_qkv, "dp", scatter_dimension=0, tiled=True)
+            second_out = lax.psum_scatter(grad_w_out, "dp", scatter_dimension=0, tiled=True)
+        else:
+            grad_w_qkv, second_down = lax.optimization_barrier((grad_w_qkv, second_down))
         grads[s] = (grad_gate_up, grad_down, grad_w_qkv, grad_w_out, small)
         input_grads[s] = grad_inputs
         grad_low = grad_inputs.astype(jnp.bfloat16)
@@ -1110,9 +1125,12 @@
     lanes += dense_lanes(len(arrays))
     for array in (grad_w_qkv, grad_w_out, small):
         arrays.append(array.reshape(dp, deep, array.shape[0] // (dp * deep), array.shape[1]))
-    lanes.append((len(arrays), None, [("expert", bits_of("expert"))]))
-    rows_each = second_dense.shape[0] // deep
-    arrays.append(second_dense.reshape(deep, rows_each, second_dense.shape[1]))
+    for array in (second_qkv, second_out):
+        lanes.append((len(arrays), None, [("expert", bits_of("expert"))]))
+        arrays.append(array.reshape(deep, array.shape[0] // deep, array.shape[1]))
+    lanes.append((len(arrays), None, dense_lanes(0)[2][2]))
+    small = grads[1][4]
+    arrays.append(small.reshape(dp, deep, small.shape[0] // (dp * deep), small.shape[1]))
     *sums, stats = sum_scatter(arrays, lanes, jnp.concatenate(stats, axis=0), 0)
     stats = lax.dynamic_index_in_dim(stats.reshape(2, 8, COLUMNS), core, 0)
     token_total = SEQ * lax.axis_size(("section", "dp", "expert"))
@@ -1129,12 +1147,7 @@
         jnp.stack(columns[half:]),
         second_down.reshape(half, inner // dp, D),
     )
-    qkv, out = grads[0][2].shape[1], grads[0][3].shape[1]
-    second_dense = sums[9]
-    second_dense = (
-        second_dense[:, :qkv], second_dense[:, qkv : qkv + out], second_dense[:, qkv + out :]
-    )
-    reduced = [(*first_experts, *sums[6:9]), (*second_experts, *second_dense)]
+    reduced = [(*first_experts, *sums[6:9]), (*second_experts, *sums[9:12])]
     final = []
     for a, b, dim in zip(reduced[0], reduced[1], (0, 0, 0, 1, 1, None)):
         keep = jnp.where(first, a, b)

time: 622 us -> 665 us (1.069)
  waiting for transfers between devices: 17.6 us -> 62.4 us
    reduce_scatter x1 -> x2, waiting for transfers between devices: 0.01 us -> 44 us  [the longest x1 44 us: body(): lax.psum_scatter(grad_w_qkv, 'dp', scatter_dimension=0, tiled=True)]
    pallas_call x4, Pallas kernels: 232 us -> 244 us  [expert_call(): pl.pallas_call(kernel, out_shape=shapes, in_specs=[vmem] * len(operands)...]
    unnamed x226 -> x256, local copies, waits for them, and re-layouts: 28.2 us -> 19.5 us
    pallas_call x1, Pallas kernels: 143 us -> 136 us  [sum_scatter(): pl.pallas_call(functools.partial(sum_scatter_kernel, (plans, len(arrays),...]
  transfers between devices with their start and end apart: 24 -> 25, of which waited for: 3 -> 4; matrix products, arithmetic and copies ran while one was open for 24% -> 21% of each run, Pallas kernels for 35% -> 10%
where the time goes in v7:
time: 665 us; the launch traced here: 654 us
  Pallas kernels  379 us (57%)
  matrix products  96.4 us (14%)
  waiting for transfers between devices  62.4 us (9%)
  other arithmetic  46.9 us (7%)
  local copies, waits for them, and re-layouts  45.7 us (7%)
  between operations  15.8 us (2%)
  starting transfers between devices  8.03 us (1%)
    pallas_call x4, Pallas kernels, expert_call(): pl.pallas_call(kernel, out_shape=shapes, in_specs=[vmem] * len(operands)...  244 us
    pallas_call x1, Pallas kernels, sum_scatter(): pl.pallas_call(functools.partial(sum_scatter_kernel, (plans, len(arrays),...  136 us
    reduce_scatter x1, waiting for transfers between devices, body(): lax.psum_scatter(grad_w_qkv, 'dp', scatter_dimension=0, tiled=True)  44 us
    dot_general x10, matrix products, turned(): jnp.einsum('tc,tq->cq', left, right, preferred_element_type=jnp.float32)  35.9 us
    dot_general x8, matrix products, matmul(): return jnp.dot(left_side, right_side, preferred_element_type=jnp.float32)  24.7 us
    unnamed x256, local copies, waits for them, and re-layouts  19.5 us
    ppermute x21, waiting for transfers between devices, swapped(): return lax.ppermute(array, 'section', [(0, 1), (1, 0)])  18.3 us
  transfers between devices with their start and end apart: 25, of which 4 were waited for; matrix products, arithmetic and copies ran while one was open for 21% of the time, Pallas kernels for 10%

profile of v7, /device:TPU:0, one launch (start us, length us, event | category | flops | bytes accessed | tf_op | source)
XLA Modules:
  0.0 654.4 jit_solution(16778718641616759817)
XLA Ops:
  11.1 1.4 dynamic-slice_bitcast_fusion
  13.7 1.8 collective-permute-done
  16.1 4.9 collective-permute-done.7
  32.7 2.2 fusion.22
  35.1 4.4 fusion.4
  39.6 1.6 fusion.120
  41.2 1.6 convolution_convert_fusion.9
  42.9 11.6 %collective-permute-done.4 = bf16[1536,1536]{1,0:T(8,128)(2,1)} collective-permute-done((bf16[1536,1536]{1,0:T(8,128)(2,1)}, bf16[1536,1536]{1,0:T(8,128)(2,1)}, u32[]{:S(2)}, u32[]{:S(2)}) %collective-permute-start.4) | collective-permute-done | bytes 4718624 | tf_op jit(solution)/shard_map/ppermute | solution.py:92
  54.5 3.6 multiply_reduce_fusion.7
  59.2 65.8 %shard_map.237 = (bf16[96,1536]{1,0:T(8,128)(2,1)S(1)}, bf16[4,96,1536]{2,1,0:T(8,128)(2,1)S(1)}, bf16[4,96,128]{2,1,0:T(8,128)(2,1)S(1)}, f32[96,128]{1,0:T(8,1...) custom-call(bf16[96,1536]{1,0:T(8,128)(2,1)S(1)} %multiply_convert_f, ...), custom_call_target="tpu_custom_call" | custom-call | flops 49999998976 | bytes 100000000 | tf_op jit(solution)/shard_map/pallas_call | solution.py:863
  127.6 2.7 fusion.25
  130.3 5.8 fusion.5
  137.9 5.1 multiply_reduce_fusion.6
  143.7 48.1 %shard_map.238 = (bf16[96,1536]{1,0:T(8,128)(2,1)S(1)}, bf16[4,96,1536]{2,1,0:T(8,128)(2,1)S(1)}, bf16[4,96,128]{2,1,0:T(8,128)(2,1)S(1)}, f32[96,128]{1,0:T(8,1...) custom-call(bf16[96,1536]{1,0:T(8,128)(2,1)S(1)} %multiply_convert_f, ...), custom_call_target="tpu_custom_call" | custom-call | flops 49999998976 | bytes 100000000 | tf_op jit(solution)/shard_map/pallas_call | solution.py:863
  191.8 62.8 %shard_map.239 = (f32[96,1536]{1,0:T(8,128)S(1)}, f32[96,128]{1,0:T(8,128)S(1)}, bf16[2,4,96,1536]{3,2,1,0:T(8,128)(2,1)}, bf16[2,4,96,1024]{3,2,1,0:T(8,128)(2,...) custom-call(bf16[96,1536]{1,0:T(8,128)(2,1)S(1)} %constant_dynamic-slice_fusion.9.grad, ...), custom_call_target="tpu_custom_call" | custom-call | flops 49999998976 | bytes 100000000 | tf_op jit(solution)/shard_map/pallas_call | solution.py:863
  254.7 4.6 bitcast_convert_fusion.3
  259.3 1.9 copy.110
  263.1 7.1 %bitcast_convert_fusion.1 = bf16[1536,2048]{1,0:T(8,128)(2,1)} fusion(bf16[2,4,96,1536]{3,2,1,0:T(8,128)(2,1)S(1)} %copy-done.125, bf16[2,4,96,2048]{3,2,1,0:T(8,128)(2,1)S(1)} %copy-done.123), kind=kOutput, calls=%fused_computation.3 | convolution fusion | flops 4834983936 | bytes 11796480 | tf_op jit(solution)/shard_map/tc,tq->cq/dot_general | solution.py:999
  274.1 6.5 convolution_convert_fusion.5
  281.6 3.0 multiply_reduce_fusion.1
  285.3 1.5 multiply_convert_fusion.1
  298.4 5.8 fusion.44
  310.8 2.2 convolution_convert_fusion.3
  313.1 3.1 convolution_convert_fusion.1
  318.0 66.8 %shard_map.240 = (f32[96,1536]{1,0:T(8,128)S(1)}, f32[96,128]{1,0:T(8,128)S(1)}, bf16[2,4,96,1536]{3,2,1,0:T(8,128)(2,1)}, bf16[2,4,96,1024]{3,2,1,0:T(8,128)(2,...) custom-call(bf16[96,1536]{1,0:T(8,128)(2,1)S(1)} %get-tuple-element.79.grad, ...), custom_call_target="tpu_custom_call" | custom-call | flops 49999998976 | bytes 100000000 | tf_op jit(solution)/shard_map/pallas_call | solution.py:863
  386.1 1.4 copy-done.7
  387.5 5.8 bitcast_convert_fusion.2
  393.4 7.2 %bitcast_convert_fusion = bf16[1536,2048]{1,0:T(8,128)(2,1)} fusion(bf16[2,4,96,1536]{3,2,1,0:T(8,128)(2,1)S(1)} %copy-done.124, bf16[2,4,96,2048]{3,2,1,0:T(8,128)(2,1)S(1)} %copy-done.122), kind=kOutput, calls=%fused_computation.2 | convolution fusion | flops 4834983936 | bytes 11796480 | tf_op jit(solution)/shard_map/tc,tq->cq/dot_general | solution.py:999
  401.5 4.2 convolution_convert_fusion.4
  411.5 1.7 fusion.20
  414.5 4.2 fusion.35
  420.0 2.2 collective-permute-start.13
  426.1 1.5 slice_bitcast_fusion.1
  430.8 3.2 convolution_convert_fusion
  434.9 2.2 convolution_convert_fusion.2
  437.1 44.0 %reduce-scatter.9.cloned.1.call-done = bf16[384,1280]{1,0:T(8,128)(2,1)} async-done(((bf16[1536,1280]{1,0:T(8,128)(2,1)}), bf16[384,1280]{1,0:T(8,128)(2,1)}) %reduce-scatter.9.cloned.1.call-update) | async-done | bytes 983056 | tf_op jit(solution)/shard_map/reduce_scatter | solution.py:1110
  481.2 135.6 %shard_map.241 = (bf16[384,512]{1,0:T(8,128)(2,1)}, bf16[384,512]{1,0:T(8,128)(2,1)}, bf16[384,512]{1,0:T(8,128)(2,1)}, bf16[384,512]{1,0:T(8,128)(2,1)}, bf16[1...) custom-call(bf16[4,384,2048]{2,1,0:T(8,128)(2,1)} %bitcast.335, ...), custom_call_target="tpu_custom_call" | custom-call | tf_op jit(solution)/shard_map/pallas_call | solution.py:347
  618.8 1.6 broadcast_select_fusion.35
  620.9 1.7 broadcast_select_fusion.33
  622.7 2.2 broadcast_select_fusion.16
  629.2 1.5 copy.131
  630.7 1.6 slice_reduce_fusion
  636.9 1.6 convert_select_fusion.3
  638.6 2.0 maximum_bitcast_fusion.1
  640.5 1.6 convert_select_fusion.1
  642.2 1.9 maximum_bitcast_fusion.2
  644.0 1.6 convert_select_fusion.5
  645.7 2.0 maximum_bitcast_fusion
  (422 shorter events, 80.5 us)
Async XLA Ops:
  7.2 8.6 %copy-start = (s32[2,96]{1,0:T(2,128)S(1)}, s32[2,96]{1,0:T(2,128)}, u32[]{:S(2)}) copy-start(s32[2,96]{1,0:T(2,128)} %param.16) | copy-start | bytes 2308
  7.2 393.4 %reduce-scatter.5.cloned.1.call-start = ((), (), s32[]{:S(2)}) async-start(), calls=%async_computation.4 | async-start | bytes 7864320 | tf_op jit(solution)/shard_map/reduce_scatter | solution.py:1068
  7.2 14.1 %collective-permute-start.1 = (bf16[1536,512]{1,0:T(8,128)(2,1)}, bf16[1536,512]{1,0:T(8,128)(2,1)S(1)}, u32[]{:S(2)}, u32[]{:S(2)}) collective-permute-start(bf16[1536,512]{1,0:T(8,128)(2,1)} %bitcast.336), channel_id=1, source_target_pairs={{0,16},{16,0},{1,17},{17,1},{2,18},{18,2},{3,19},{19,3},{4,20},{20... | collective-permute-start | bytes 4718600 | tf_op jit(solution)/shard_map/ppermute | solution.py:92
  7.8 16.2 %collective-permute-start.2 = (bf16[1536,512]{1,0:T(8,128)(2,1)}, bf16[1536,512]{1,0:T(8,128)(2,1)S(1)}, u32[]{:S(2)}, u32[]{:S(2)}) collective-permute-start(bf16[1536,512]{1,0:T(8,128)(2,1)} %bitcast.337), channel_id=1, source_target_pairs={{0,16},{16,0},{1,17},{17,1},{2,18},{18,2},{3,19},{19,3},{4,20},{20... | collective-permute-start | bytes 4718600 | tf_op jit(solution)/shard_map/ppermute | solution.py:92
  7.8 27.2 %collective-permute-start.3 = (bf16[1536,1536]{1,0:T(8,128)(2,1)}, bf16[1536,1536]{1,0:T(8,128)(2,1)}, u32[]{:S(2)}, u32[]{:S(2)}) collective-permute-start(bf16[1536,1536]{1,0:T(8,128)(2,1)} %bitcast.419), channel_id=1, source_target_pairs={{0,16},{16,0},{1,17},{17,1},{2,18},{18,2},{3,19},{19,3},{4,20},{20... | collective-permute-start | bytes 14155784 | tf_op jit(solution)/shard_map/ppermute | solution.py:92
  9.0 4.5 collective-permute-start.5
  9.9 17.0 %copy-start.109 = (bf16[1536]{0:T(1024)(128)(2,1)}, bf16[1536]{0:T(1024)(128)(2,1)S(1)}, u32[]{:S(2)}) copy-start(bf16[1536]{0:T(1024)(128)(2,1)S(1)} %reduce) | copy-start | bytes 9220
  9.9 5.6 collective-permute-start
  13.5 15.1 %copy-start.40 = (bf16[1,1536,16]{2,1,0:T(8,128)(2,1)}, bf16[1,1536,16]{2,1,0:T(8,128)(2,1)S(1)}, u32[]{:S(2)}) copy-start(bf16[1,1536,16]{2,1,0:T(8,128)(2,1)S(1)} %copy.105) | copy-start | bytes 147460
  13.5 13.3 %copy-start.114 = (bf16[1536]{0:T(1024)(128)(2,1)}, bf16[1536]{0:T(1024)(128)(2,1)S(1)}, u32[]{:S(2)}) copy-start(bf16[1536]{0:T(1024)(128)(2,1)S(1)} %collective-permute-done.5) | copy-start | bytes 9220
  13.5 2.3 collective-permute-start.6
  15.4 5.5 collective-permute-start.7
  15.8 42.9 %collective-permute-start.8 = (bf16[4,1536,512]{2,1,0:T(8,128)(2,1)}, bf16[4,1536,512]{2,1,0:T(8,128)(2,1)}, u32[]{:S(2)}, u32[]{:S(2)}) collective-permute-start(bf16[4,1536,512]{2,1,0:T(8,128)(2,1)} %bitcast.404), channel_id=1, source_target_pairs={{0,16},{16,0},{1,17},{17,1},{2,18},{18,2},{3,19},{19,3},{4,20},{20... | collective-permute-start | bytes 18874376 | tf_op jit(solution)/shard_map/ppermute | solution.py:92
  20.9 37.8 %collective-permute-start.9 = (bf16[4,1536,512]{2,1,0:T(8,128)(2,1)}, bf16[4,1536,512]{2,1,0:T(8,128)(2,1)}, u32[]{:S(2)}, u32[]{:S(2)}) collective-permute-start(bf16[4,1536,512]{2,1,0:T(8,128)(2,1)} %bitcast.409), channel_id=1, source_target_pairs={{0,16},{16,0},{1,17},{17,1},{2,18},{18,2},{3,19},{19,3},{4,20},{20... | collective-permute-start | bytes 18874376 | tf_op jit(solution)/shard_map/ppermute | solution.py:92
  21.7 37.1 %collective-permute-start.10 = (bf16[4,512,1536]{2,1,0:T(8,128)(2,1)}, bf16[4,512,1536]{2,1,0:T(8,128)(2,1)}, u32[]{:S(2)}, u32[]{:S(2)}) collective-permute-start(bf16[4,512,1536]{2,1,0:T(8,128)(2,1)} %bitcast.414), channel_id=1, source_target_pairs={{0,16},{16,0},{1,17},{17,1},{2,18},{18,2},{3,19},{19,3},{4,20},{20... | collective-permute-start | bytes 18874376 | tf_op jit(solution)/shard_map/ppermute | solution.py:92
  23.9 30.5 %collective-permute-start.4 = (bf16[1536,1536]{1,0:T(8,128)(2,1)}, bf16[1536,1536]{1,0:T(8,128)(2,1)}, u32[]{:S(2)}, u32[]{:S(2)}) collective-permute-start(bf16[1536,1536]{1,0:T(8,128)(2,1)} %bitcast.333), channel_id=1, source_target_pairs={{0,16},{16,0},{1,17},{17,1},{2,18},{18,2},{3,19},{19,3},{4,20},{20... | collective-permute-start | bytes 14155784 | tf_op jit(solution)/shard_map/ppermute | solution.py:92
  27.9 30.7 %copy-start.91 = (f32[1536]{0:T(1024)}, f32[1536]{0:T(1024)S(1)}, u32[]{:S(2)}) copy-start(f32[1536]{0:T(1024)S(1)} %get-tuple-element.224) | copy-start | bytes 18436
  28.6 98.2 %copy-start.101 = (f32[1536]{0:T(1024)}, f32[1536]{0:T(1024)S(1)}, u32[]{:S(2)}) copy-start(f32[1536]{0:T(1024)S(1)} %get-tuple-element.225) | copy-start | bytes 18436
  32.7 8.5 %copy-start.93 = (bf16[96,512]{0,1:T(8,128)(2,1)}, bf16[96,512]{0,1:T(8,128)(2,1)S(1)}, u32[]{:S(2)}) copy-start(bf16[96,512]{0,1:T(8,128)(2,1)S(1)} %copy.100) | copy-start | bytes 294916
  41.2 13.3 %copy-start.27 = (bf16[192,1536]{1,0:T(8,128)(2,1)S(1)}, bf16[192,1536]{1,0:T(8,128)(2,1)}, u32[]{:S(2)}) copy-start(bf16[192,1536]{1,0:T(8,128)(2,1)} %param.14) | copy-start | bytes 1769476
  42.9 15.2 %copy-start.29 = (bf16[8,64,3,96]{3,1,2,0:T(8,128)(2,1)}, bf16[8,64,3,96]{3,1,2,0:T(8,128)(2,1)S(1)}, u32[]{:S(2)}) copy-start(bf16[8,64,3,96]{3,1,2,0:T(8,128)(2,1)S(1)} %convolution_convert_fusion.9) | copy-start | bytes 884740
  58.0 67.0 %copy-start.2 = (f32[96,1536]{1,0:T(8,128)}, f32[96,1536]{1,0:T(8,128)S(1)}, u32[]{:S(2)}) copy-start(f32[96,1536]{1,0:T(8,128)S(1)} %get-tuple-element.240.hidden) | copy-start | bytes 1769476
  58.7 66.3 %copy-start.4 = (bf16[96,1536]{1,0:T(8,128)(2,1)}, bf16[96,1536]{1,0:T(8,128)(2,1)S(1)}, u32[]{:S(2)}) copy-start(bf16[96,1536]{1,0:T(8,128)(2,1)S(1)} %multiply_convert_fusion.3.x) | copy-start | bytes 884740
  59.1 67.8 %copy-start.17 = (bf16[1536,512]{1,0:T(8,128)(2,1)S(1)}, bf16[1536,512]{1,0:T(8,128)(2,1)}, u32[]{:S(2)}) copy-start(bf16[1536,512]{1,0:T(8,128)(2,1)} %copy-done.15) | copy-start | bytes 4718596
  127.5 9.5 %copy-start.95 = (bf16[96,512]{0,1:T(8,128)(2,1)}, bf16[96,512]{0,1:T(8,128)(2,1)S(1)}, u32[]{:S(2)}) copy-start(bf16[96,512]{0,1:T(8,128)(2,1)S(1)} %copy.106) | copy-start | bytes 294916
  130.3 6.0 copy-start.83
  143.6 128.6 %copy-start.113 = (f32[96]{0:T(128)}, f32[96]{0:T(128)S(1)}, u32[]{:S(2)}) copy-start(f32[96]{0:T(128)S(1)} %get-tuple-element.234) | copy-start | bytes 1156
  270.2 163.8 %reduce-scatter.7.cloned.1.call-start = ((), (), s32[]{:S(2)}) async-start(), calls=%async_computation.5 | async-start | bytes 3932160 | tf_op jit(solution)/shard_map/reduce_scatter | solution.py:1069
  274.1 6.6 %copy-start.47 = (bf16[96,1536]{1,0:T(8,128)(2,1)}, bf16[96,1536]{1,0:T(8,128)(2,1)S(1)}, u32[]{:S(2)}) copy-start(bf16[96,1536]{1,0:T(8,128)(2,1)S(1)} %get-tuple-element.166) | copy-start | bytes 884740
  274.1 7.5 %copy-start.57 = (f32[8,3,96,96]{2,3,1,0:T(8,128)S(1)}, f32[8,3,96,96]{2,3,1,0:T(8,128)}, u32[]{:S(2)}) copy-start(f32[8,3,96,96]{2,3,1,0:T(8,128)} %copy-done.56) | copy-start | bytes 2654212
  274.1 7.5 %copy-start.96 = (bf16[96,512]{0,1:T(8,128)(2,1)S(1)}, bf16[96,512]{0,1:T(8,128)(2,1)}, u32[]{:S(2)}) copy-start(bf16[96,512]{0,1:T(8,128)(2,1)} %copy-done.95) | copy-start | bytes 294916
  274.1 7.5 %copy-start.106 = (f32[8,3,96]{2,1,0:T(4,128)S(1)}, f32[8,3,96]{2,1,0:T(4,128)}, u32[]{:S(2)}) copy-start(f32[8,3,96]{2,1,0:T(4,128)} %copy-done.105) | copy-start | bytes 27652
  284.6 152.5 %reduce-scatter.11.cloned.1.call-start = ((), (), s32[]{:S(2)}) async-start(), calls=%async_computation.7 | async-start | bytes 2949120 | tf_op jit(solution)/shard_map/reduce_scatter | solution.py:1111
  295.4 12.4 %collective-permute-start.12 = (bf16[96,5120]{1,0:T(8,128)(2,1)}, bf16[96,5120]{1,0:T(8,128)(2,1)}, u32[]{:S(2)}, u32[]{:S(2)}) collective-permute-start(bf16[96,5120]{1,0:T(8,128)(2,1)} %pad_maximum_fusion), channel_id=1, source_target_pairs={{0,16},{16,0},{1,17},{17,1},{2,18},{18,2},{3,19},{19,3},{4,20},{20... | collective-permute-start | bytes 2949128 | tf_op jit(solution)/shard_map/ppermute | solution.py:92
  304.8 2.1 collective-permute-start.11
  316.2 164.9 %reduce-scatter.9.cloned.1.call-start = ((), (), s32[]{:S(2)}) async-start(), calls=%async_computation.6 | async-start | bytes 4915200 | tf_op jit(solution)/shard_map/reduce_scatter | solution.py:1110
  393.3 7.3 %copy-start.3 = (f32[96,1536]{1,0:T(8,128)S(1)}, f32[96,1536]{1,0:T(8,128)}, u32[]{:S(2)}) copy-start(f32[96,1536]{1,0:T(8,128)} %copy-done.2) | copy-start | bytes 1769476
  393.4 7.3 %copy-start.23 = (bf16[1536,16]{1,0:T(8,128)(2,1)S(1)}, bf16[1536,16]{1,0:T(8,128)(2,1)}, u32[]{:S(2)}) copy-start(bf16[1536,16]{1,0:T(8,128)(2,1)} %copy-done.22) | copy-start | bytes 147460
  393.4 7.3 %copy-start.92 = (f32[1536]{0:T(1024)S(1)}, f32[1536]{0:T(1024)}, u32[]{:S(2)}) copy-start(f32[1536]{0:T(1024)} %copy-done.91) | copy-start | bytes 18436
  393.4 7.3 %copy-start.112 = (f32[96]{0:T(128)S(1)}, f32[96]{0:T(128)}, u32[]{:S(2)}) copy-start(f32[96]{0:T(128)} %copy-done.111) | copy-start | bytes 1156
  420.0 7.6 %collective-permute-start.13 = (f32[96,1536]{1,0:T(8,128)}, f32[96,1536]{1,0:T(8,128)S(1)}, u32[]{:S(2)}, u32[]{:S(2)}) collective-permute-start(f32[96,1536]{1,0:T(8,128)} %get-tuple-element.175), channel_id=1, source_target_pairs={{0,16},{16,0},{1,17},{17,1},{2,18},{18,2},{3,19},{19,3},{4,20},{20... | collective-permute-start | bytes 1769480 | tf_op jit(solution)/shard_map/ppermute | solution.py:92
  424.7 4.0 collective-permute-start.14
  618.8 8.6 %collective-permute-start.15 = (bf16[96,128]{1,0:T(8,128)(2,1)S(1)}, bf16[96,128]{1,0:T(8,128)(2,1)S(1)}, u32[]{:S(2)}, u32[]{:S(2)}) collective-permute-start(bf16[96,128]{1,0:T(8,128)(2,1)S(1)} %broadcast_select_fusion.37), channel_id=1, source_target_pairs={{0,16},{16,0},{1,17},{17,1},{2,18},{18,2},{3,19},{19,3},{4,20},{20... | collective-permute-start | bytes 73736 | tf_op jit(solution)/shard_map/ppermute | solution.py:92
  620.4 11.8 %collective-permute-start.17 = (bf16[96,768]{1,0:T(8,128)(2,1)}, bf16[96,768]{1,0:T(8,128)(2,1)}, u32[]{:S(2)}, u32[]{:S(2)}) collective-permute-start(bf16[96,768]{1,0:T(8,128)(2,1)} %broadcast_select_fusion.35), channel_id=1, source_target_pairs={{0,16},{16,0},{1,17},{17,1},{2,18},{18,2},{3,19},{19,3},{4,20},{20... | collective-permute-start | bytes 442376 | tf_op jit(solution)/shard_map/ppermute | solution.py:92
  622.6 11.6 %collective-permute-start.16 = (bf16[96,1280]{1,0:T(8,128)(2,1)}, bf16[96,1280]{1,0:T(8,128)(2,1)}, u32[]{:S(2)}, u32[]{:S(2)}) collective-permute-start(bf16[96,1280]{1,0:T(8,128)(2,1)} %broadcast_select_fusion.33), channel_id=1, source_target_pairs={{0,16},{16,0},{1,17},{17,1},{2,18},{18,2},{3,19},{19,3},{4,20},{20... | collective-permute-start | bytes 737288 | tf_op jit(solution)/shard_map/ppermute | solution.py:92
  624.9 15.7 %collective-permute-start.20 = (bf16[2,128,1536]{2,1,0:T(8,128)(2,1)}, bf16[2,128,1536]{2,1,0:T(8,128)(2,1)}, u32[]{:S(2)}, u32[]{:S(2)}) collective-permute-start(bf16[2,128,1536]{2,1,0:T(8,128)(2,1)} %broadcast_select_fusion.16), channel_id=1, source_target_pairs={{0,16},{16,0},{1,17},{17,1},{2,18},{18,2},{3,19},{19,3},{4,20},{20... | collective-permute-start | bytes 2359304 | tf_op jit(solution)/shard_map/ppermute | solution.py:92
  626.3 10.6 %collective-permute-start.19 = (bf16[2,384,512]{2,1,0:T(8,128)(2,1)}, bf16[2,384,512]{2,1,0:T(8,128)(2,1)}, u32[]{:S(2)}, u32[]{:S(2)}) collective-permute-start(bf16[2,384,512]{2,1,0:T(8,128)(2,1)} %broadcast_select_fusion.18), channel_id=1, source_target_pairs={{0,16},{16,0},{1,17},{17,1},{2,18},{18,2},{3,19},{19,3},{4,20},{20... | collective-permute-start | bytes 2359304 | tf_op jit(solution)/shard_map/ppermute | solution.py:92
  627.4 16.6 %collective-permute-start.18 = (bf16[2,384,512]{2,1,0:T(8,128)(2,1)}, bf16[2,384,512]{2,1,0:T(8,128)(2,1)}, u32[]{:S(2)}, u32[]{:S(2)}) collective-permute-start(bf16[2,384,512]{2,1,0:T(8,128)(2,1)} %broadcast_select_fusion.20), channel_id=1, source_target_pairs={{0,16},{16,0},{1,17},{17,1},{2,18},{18,2},{3,19},{19,3},{4,20},{20... | collective-permute-start | bytes 2359304 | tf_op jit(solution)/shard_map/ppermute | solution.py:92
  (103 other events, 240.7 us)
Sparse Core Ops, SparseCore 0:
  270.3 68.7 reduce-scatter.4
  342.7 43.9 reduce-scatter.6
  390.3 37.3 reduce-scatter.10
  430.6 50.5 reduce-scatter.8

commit v8 on v6

--- a/solution.py
+++ b/solution.py
@@ -109,11 +109,16 @@
 def sum_scatter_kernel(plan, *refs):
     lanes, ins, copies = plan
     sources = refs[:ins]
-    stats_in = refs[ins]
-    outs = refs[ins + 1 : ins + 1 + len(lanes)]
-    stats = refs[ins + 1 + len(lanes)]
-    scratch = list(refs[ins + 2 + len(lanes) :])
-    send_sem, recv_sem, local_sem, stats_got, stats_send, stats_recv = scratch[-6:]
+    second_pre, stats_in = refs[ins : ins + 2]
+    gate_out, up_out, down_out, query_out, key_out, value_out, out_out, small_out, stats = refs[
+        ins + 2 : ins + 11
+    ]
+    scratch = list(refs[ins + 11 :])
+    stage = dict(zip(("pre", "down", "qkv", "out", "small"), scratch[-13:-8]))
+    send_sem, recv_sem, local_sem, stats_got, stats_send, stats_recv, core_send, core_recv = (
+        scratch[-8:]
+    )
+    core = lax.axis_index("section")
     partners = []
     for lane in lanes:
         for axis, bits in lane["phases"]:
@@ -185,6 +190,30 @@
 
     summing = sum_stats()
     next(summing)
+
+    def to_stage(number, source, kind, *at):
+        spot = stage[kind].at[(core, *at)]
+        return spot, pltpu.make_async_remote_copy(
+            src_ref=source,
+            dst_ref=spot,
+            send_sem=core_send.at[number],
+            recv_sem=core_recv.at[number],
+            device_id={"section": 1 - core},
+            device_id_type=pl.DeviceIdType.MESH,
+        )
+
+    spot, whole = to_stage(len(lanes), second_pre, "pre")
+    whole_here = pltpu.make_async_copy(second_pre, spot, core_send.at[len(lanes)])
+
+    @pl.when(core == 1)
+    def _():
+        whole_here.start()
+
+    @pl.when(core == 0)
+    def _():
+        whole.start()
+
+    moved = []
     started = []
     states = []
     for number, lane in enumerate(lanes):
@@ -285,7 +314,16 @@
             if final is not None and step >= sizes[0]:
                 state["final"] = final
                 if step == sum(sizes):
-                    outs[number][...] = final[...]
+                    spot, copy = to_stage(number, final, *lane["target"])
+                    moved.append((lane["layer"], copy))
+
+                    @pl.when(core == lane["layer"])
+                    def _(spot=spot, final=final):
+                        spot[...] = final[...]
+
+                    @pl.when(core != lane["layer"])
+                    def _(copy=copy):
+                        copy.start()
                 elif step < sum(sizes):
                     axis, bits = lane["phases"][1]
                     done = step - sizes[0]
@@ -306,13 +344,72 @@
             state["pending"] = state["pending_next"]
     for _ in summing:
         pass
+
+    @pl.when(core == 1)
+    def _():
+        whole.wait_recv()
+        whole_here.wait()
+
+    @pl.when(core == 0)
+    def _():
+        whole.wait_send()
+
+    for layer, copy in moved:
+        @pl.when(core == layer)
+        def _(copy=copy):
+            copy.wait_recv()
+
+        @pl.when(core != layer)
+        def _(copy=copy):
+            copy.wait_send()
+
+    pre, inner = stage["pre"], gate_out.shape[2]
+    half = gate_out.shape[0] // 2
+    rows = gate_out.shape[1]
+    line = 16 if rows % 16 == 0 else rows
+
+    def write(i, carry):
+        at = pl.ds(pl.multiple_of(i * line, line), line)
+        for c in range(2):
+            for j in range(half):
+                for kind, target in enumerate((gate_out, up_out)):
+                    columns = pl.ds((kind * half + j) * inner, inner)
+                    target[c * half + j, at] = pre[c, at, columns].astype(jnp.float32)
+        return carry
+
+    lax.fori_loop(0, rows // line, write, 0)
+    rows = down_out.shape[1]
+    line = 16 if rows % 16 == 0 else rows
+
+    def write_down(i, carry):
+        at = pl.ds(pl.multiple_of(i * line, line), line)
+        for c in range(2):
+            for j in range(half):
+                down_out[c * half + j, at] = stage["down"][c, j, at].astype(jnp.float32)
+        return carry
+
+    lax.fori_loop(0, rows // line, write_down, 0)
+    column = 0
+    width = stage["qkv"].shape[2]
+    for target in (query_out, key_out, value_out):
+        done = 0
+        while done < target.shape[1]:
+            c, at = divmod(column, width)
+            size = min(width - at, target.shape[1] - done)
+            target[:, done : done + size] = stage["qkv"][c, :, at : at + size].astype(jnp.float32)
+            done, column = done + size, column + size
+    width = stage["out"].shape[2]
+    for c in range(2):
+        out_out[:, c * width : (c + 1) * width] = stage["out"][c].astype(jnp.float32)
+    small_out[...] = stage["small"][0].astype(jnp.float32) + stage["small"][1].astype(jnp.float32)
     for copy in started:
         copy.wait_send()
 
 
-def sum_scatter(arrays, lanes, stats, collective):
+def sum_scatter(arrays, lanes, second_pre, stats, inner, collective):
     plans, scratch, shapes, copies, locals_ = [], [], [], 0, 0
-    for source, prefix, phases in lanes:
+    sizes = {}
+    for source, prefix, phases, layer, target in lanes:
         shape = arrays[source].shape
         if isinstance(prefix, int):
             shape = shape[1:]
@@ -329,9 +426,45 @@
             for step in range(1, len(phases[1][1]) + 1):
                 buffers.append((shape[1] >> step, *shape[2:]))
                 copies += shape[1] >> step
-        plans.append({"source": source, "prefix": prefix, "phases": phases, "buffers": buffers})
+        plans.append(
+            {
+                "source": source,
+                "prefix": prefix,
+                "phases": phases,
+                "buffers": buffers,
+                "layer": layer,
+                "target": target,
+            }
+        )
+        sizes.setdefault(target[0], shape[-2:])
         scratch += [pltpu.VMEM(buffer, jnp.bfloat16) for buffer in buffers]
-        shapes.append(jax.ShapeDtypeStruct(shape[-2:], jnp.bfloat16))
+    half = second_pre.shape[1] // (2 * inner)
+    heads, kv = H * HD, KVH * HD
+    shard = sizes["qkv"][0]
+    shapes = [
+        jax.ShapeDtypeStruct(shape, jnp.float32)
+        for shape in (
+            (2 * half, second_pre.shape[0], inner),
+            (2 * half, second_pre.shape[0], inner),
+            (2 * half, *sizes["down"]),
+            (shard, heads),
+            (shard, kv),
+            (shard, kv),
+            (shard, 2 * sizes["out"][1]),
+            (shard, COLUMNS),
+            stats.shape,
+        )
+    ]
+    scratch += [
+        pltpu.VMEM((2, *shape), jnp.bfloat16)
+        for shape in (
+            second_pre.shape,
+            (half, *sizes["down"]),
+            sizes["qkv"],
+            sizes["out"],
+            sizes["small"],
+        )
+    ]
     scratch += [
         pltpu.SemaphoreType.DMA((copies,)),
         pltpu.SemaphoreType.DMA((copies,)),
@@ -342,44 +475,49 @@
         pltpu.VMEM((hops, *stats.shape), jnp.float32),
         pltpu.SemaphoreType.DMA((hops,)),
         pltpu.SemaphoreType.DMA((hops,)),
+        pltpu.SemaphoreType.DMA((len(lanes) + 1,)),
+        pltpu.SemaphoreType.DMA((len(lanes) + 1,)),
     ]
-    shapes.append(jax.ShapeDtypeStruct(stats.shape, jnp.float32))
     return pl.pallas_call(
         functools.partial(sum_scatter_kernel, (plans, len(arrays), copies)),
         out_shape=shapes,
-        in_specs=[pl.BlockSpec(memory_space=pl.ANY)] * len(arrays)
+        in_specs=[pl.BlockSpec(memory_space=pl.ANY)] * (len(arrays) + 1)
         + [pl.BlockSpec(memory_space=pltpu.VMEM)],
-        out_specs=[pl.BlockSpec(memory_space=pltpu.VMEM)] * (len(lanes) + 1),
+        out_specs=[pl.BlockSpec(memory_space=pltpu.VMEM)] * len(shapes),
         scratch_shapes=scratch,
         compiler_params=pltpu.CompilerParams(
             collective_id=collective, has_side_effects=True, vmem_limit_bytes=60 * 2**20
         ),
-    )(*arrays, stats)
+    )(*arrays, second_pre, stats)
 
 
 def bits_of(axis):
     return list(range(lax.axis_size(axis).bit_length() - 1))
 
 
+def slice_of(start, size):
+    return (slice(None), pl.ds(start, size))
+
+
 def expert_lanes(first, inner):
-    up, down = bits_of("dp"), bits_of("dp")[::-1]
-    one, two = [("dp", up)], [("dp", down)]
+    up, down = [("dp", bits_of("dp"))], [("dp", bits_of("dp")[::-1])]
     return [
-        (first, (0, inner), one),
-        (first, (2 * inner, inner), two),
-        (first, (inner, inner), one),
-        (first, (3 * inner, inner), two),
-        (first + 1, 0, one),
-        (first + 1, 1, two),
+        (first, (at * inner, inner), phases, 0, ("pre", *slice_of(at * inner, inner)))
+        for at, phases in ((0, up), (2, down), (1, up), (3, down))
     ]
+
+
+def down_lanes(first, layer):
+    up, down = [("dp", bits_of("dp"))], [("dp", bits_of("dp")[::-1])]
+    return [(first, 0, up, layer, ("down", 0)), (first, 1, down, layer, ("down", 1))]
 
 
 def dense_lanes(first):
     up, down, deep = bits_of("dp"), bits_of("dp")[::-1], bits_of("expert")
     return [
-        (first, "inner", [("expert", deep), ("dp", up)]),
-        (first + 1, None, [("dp", down), ("expert", deep)]),
-        (first + 2, None, [("dp", up), ("expert", deep)]),
+        (first, "inner", [("expert", deep), ("dp", up)], 0, ("qkv",)),
+        (first + 1, None, [("dp", down), ("expert", deep)], 0, ("out",)),
+        (first + 2, None, [("dp", up), ("expert", deep)], 0, ("small",)),
     ]
 
 
@@ -603,7 +741,9 @@
     layer, experts, x, mask, hidden, router, *refs
 ):
     own, other, refs = refs[:3], refs[3:6], refs[6:]
+    own_dense, other_dense, refs = refs[:4], refs[4:8], refs[8:]
     out, rows, gates_all, gates, gate_keep, up_keep, gated, stats = refs[:8]
+    placed, place_sem, refs = refs[8:12], refs[-1], refs[:8] + refs[12:-1]
     w_gate, w_up, w_down, sums, returned, mixed, total, stats_all = refs[8:16]
     weight_sem, *sems = refs[16:]
     n, held = rows.shape[0], w_gate.shape[0]
@@ -656,6 +796,20 @@
     )
     start(0)
     wait_weights = fetch_weights(layer, own, other, (w_gate, w_up, w_down), weight_sem)
+    here = lax.axis_index("section") == 1 - layer
+
+    def place_copy(group, i):
+        return pltpu.make_async_copy(group[i], placed[i], place_sem.at[i])
+
+    for i in range(4):
+        @pl.when(here)
+        def _():
+            place_copy(own_dense, i).start()
+
+        @pl.when(jnp.logical_not(here))
+        def _():
+            place_copy(other_dense, i).start()
+
     logits = jnp.dot(x[...], router[...], preferred_element_type=jnp.float32)
     chosen = mask[...] > 0
     highest = jnp.max(jnp.where(chosen, logits, MASKED), axis=1, keepdims=True)
@@ -686,6 +840,8 @@
     collect(add)
     out[...] = total[...].astype(jnp.bfloat16)
     finish()
+    for i in range(4):
+        place_copy(own_dense, i).wait()
 
 
 def experts_backward_kernel(layer, grad, gates, gate_keep, up_keep, *refs):
@@ -848,14 +1004,14 @@
     ]
 
 
-def expert_call(kernel, operands, own, other, extra, shapes, scratch, collective):
+def expert_call(kernel, operands, own, other, extra, shapes, scratch, collective, loose=0):
     vmem, free = pl.BlockSpec(memory_space=pltpu.VMEM), pl.BlockSpec(memory_space=pl.ANY)
     weights = [pltpu.VMEM(array.shape, jnp.bfloat16) for array in own]
     return pl.pallas_call(
         kernel,
         out_shape=shapes,
         in_specs=[vmem] * len(operands) + [free] * (6 + len(extra)),
-        out_specs=[vmem] * len(shapes),
+        out_specs=[vmem] * (len(shapes) - loose) + [free] * loose,
         scratch_shapes=weights + scratch,
         compiler_params=pltpu.CompilerParams(
             collective_id=collective, has_side_effects=True, vmem_limit_bytes=50 * 2**20
@@ -866,7 +1022,9 @@
     )(*operands, *own, *other, *extra)
 
 
-def experts_forward(layer, normed_two, mask, hidden, router, own, other, experts):
+def experts_forward(
+    layer, normed_two, mask, hidden, router, own, other, own_dense, other_dense, experts
+):
     n, held = lax.axis_size("expert"), own[0].shape[0]
     length, width = normed_two.shape
     inner = own[0].shape[2]
@@ -881,7 +1039,7 @@
         kept,
         jax.ShapeDtypeStruct((n, length, held * inner), low),
         jax.ShapeDtypeStruct((8, COLUMNS), full),
-    ]
+    ] + [jax.ShapeDtypeStruct(array.shape, low) for array in own_dense]
     scratch = [
         pltpu.VMEM((n, length, width), low),
         pltpu.VMEM((2, n, length, width), low),
@@ -890,9 +1048,18 @@
         pltpu.VMEM((n, 8, COLUMNS), full),
         pltpu.SemaphoreType.DMA((3 * held,)),
     ] + exchange_scratch(n, 3, PARTS)
+    scratch.append(pltpu.SemaphoreType.DMA((4,)))
     kernel = functools.partial(experts_forward_kernel, layer, experts)
     return expert_call(
-        kernel, (normed_two, mask, hidden, router), own, other, (), shapes, scratch, 1 + layer
+        kernel,
+        (normed_two, mask, hidden, router),
+        own,
+        other,
+        (*own_dense, *other_dense),
+        shapes,
+        scratch,
+        1 + layer,
+        4,
     )
 
 
@@ -1014,9 +1181,19 @@
         state = attention_forward(inputs, weights[s], segment_row)
         hidden, normed_two = state[7], state[9]
         router = jnp.pad(weights[s][6], ((0, 0), (0, COLUMNS - experts)))
-        inputs_low, *expert_state, stat = experts_forward(
-            s, normed_two, masks[s], hidden, router, own_experts, other_experts, experts
-        )
+        inputs_low, *expert_state, stat, query, key, value, out = experts_forward(
+            s,
+            normed_two,
+            masks[s],
+            hidden,
+            router,
+            own_experts,
+            other_experts,
+            own[1:5],
+            other[1:5],
+            experts,
+        )
+        weights[1 - s][1:5] = [query, key, value, out]
         outs.append(inputs_low)
         stats.append(stat)
         saved.append((inputs, state, expert_state))
@@ -1089,67 +1266,39 @@
         ).astype(jnp.bfloat16)
         small = jnp.pad(small, ((0, 0), (0, COLUMNS - small.shape[1])))
         if s == 1:
-            dp = lax.axis_size("dp")
-            parts = grad_down.reshape(held // 2, dp, inner // dp, D)
-            parts = jnp.moveaxis(parts, 1, 0).reshape(-1, D)
-            dense = jnp.concatenate([grad_w_qkv, grad_w_out, small], axis=1)
-            grad_inputs, parts, dense = lax.optimization_barrier((grad_inputs, parts, dense))
-            second_dense = lax.psum_scatter(dense, "dp", scatter_dimension=0, tiled=True)
-            second_down = lax.psum_scatter(parts, "dp", scatter_dimension=0, tiled=True)
+            grad_inputs, grad_down, grad_w_qkv, grad_w_out = lax.optimization_barrier(
+                (grad_inputs, grad_down, grad_w_qkv, grad_w_out)
+            )
+            second_out = lax.psum_scatter(grad_w_out, "dp", scatter_dimension=0, tiled=True)
+            second_qkv = lax.psum_scatter(grad_w_qkv, "dp", scatter_dimension=0, tiled=True)
         grads[s] = (grad_gate_up, grad_down, grad_w_qkv, grad_w_out, small)
         input_grads[s] = grad_inputs
         grad_low = grad_inputs.astype(jnp.bfloat16)
 
     dp, deep = lax.axis_size("dp"), lax.axis_size("expert")
     half, inner = held // 2, w_gate.shape[3]
-    arrays, lanes = [], []
     grad_gate_up, grad_down, grad_w_qkv, grad_w_out, small = grads[0]
-    lanes += expert_lanes(len(arrays), inner)
-    arrays.append(grad_gate_up.reshape(dp, D // dp, held * inner))
-    arrays.append(grad_down.reshape(half, dp, inner // dp, D))
-    lanes += dense_lanes(len(arrays))
+    arrays = [
+        grad_gate_up.reshape(dp, D // dp, held * inner),
+        grad_down.reshape(half, dp, inner // dp, D),
+    ]
+    lanes = expert_lanes(0, inner) + down_lanes(1, 0) + down_lanes(2, 1) + dense_lanes(3)
+    arrays.append(grads[1][1].reshape(half, dp, inner // dp, D))
     for array in (grad_w_qkv, grad_w_out, small):
         arrays.append(array.reshape(dp, deep, array.shape[0] // (dp * deep), array.shape[1]))
-    lanes.append((len(arrays), None, [("expert", bits_of("expert"))]))
-    rows_each = second_dense.shape[0] // deep
-    arrays.append(second_dense.reshape(deep, rows_each, second_dense.shape[1]))
-    *sums, stats = sum_scatter(arrays, lanes, jnp.concatenate(stats, axis=0), 0)
+    for array, kind in ((second_qkv, "qkv"), (second_out, "out")):
+        lanes.append((len(arrays), None, [("expert", bits_of("expert"))], 1, (kind,)))
+        arrays.append(array.reshape(deep, array.shape[0] // deep, array.shape[1]))
+    lanes.append((len(arrays), None, dense_lanes(0)[2][2], 1, ("small",)))
+    small = grads[1][4]
+    arrays.append(small.reshape(dp, deep, small.shape[0] // (dp * deep), small.shape[1]))
+    w_gate_grad, w_up_grad, w_down_grad, query, key, value, grad_w_out, small, stats = sum_scatter(
+        arrays, lanes, second_pre, jnp.concatenate(stats, axis=0), inner, 0
+    )
     stats = lax.dynamic_index_in_dim(stats.reshape(2, 8, COLUMNS), core, 0)
     token_total = SEQ * lax.axis_size(("section", "dp", "expert"))
     counts, chances = stats[:, 1, :experts], stats[:, 0, :experts]
     balance = experts * (counts / (token_total * TOPK) * chances / token_total)
-    first_experts = (
-        jnp.stack([sums[0], sums[2]]),
-        jnp.stack([sums[1], sums[3]]),
-        jnp.stack([sums[4], sums[5]]),
-    )
-    columns = [second_pre[:, i * inner : (i + 1) * inner] for i in range(2 * half)]
-    second_experts = (
-        jnp.stack(columns[:half]),
-        jnp.stack(columns[half:]),
-        second_down.reshape(half, inner // dp, D),
-    )
-    qkv, out = grads[0][2].shape[1], grads[0][3].shape[1]
-    second_dense = sums[9]
-    second_dense = (
-        second_dense[:, :qkv], second_dense[:, qkv : qkv + out], second_dense[:, qkv + out :]
-    )
-    reduced = [(*first_experts, *sums[6:9]), (*second_experts, *second_dense)]
-    final = []
-    for a, b, dim in zip(reduced[0], reduced[1], (0, 0, 0, 1, 1, None)):
-        keep = jnp.where(first, a, b)
-        got = swapped(jnp.where(first, b, a))
-        keep, got = keep.astype(jnp.float32), got.astype(jnp.float32)
-        if dim is None:
-            final.append(keep + got)
-        else:
-            final.append(
-                jnp.concatenate(
-                    [jnp.where(first, keep, got), jnp.where(first, got, keep)], axis=dim
-                )
-            )
-    w_gate_grad, w_up_grad, w_down_grad, grad_w_qkv, grad_w_out, small = final
-    heads, kv = H * HD, KVH * HD
     out_keep = jnp.where(first, outs[0], outs[1])
     out_got = swapped(jnp.where(first, outs[1], outs[0]))
     layer_out = jnp.where(
@@ -1165,9 +1314,9 @@
         layer_out,
         input_grad,
         small[:, 0],
-        grad_w_qkv[:, :heads],
-        grad_w_qkv[:, heads : heads + kv],
-        grad_w_qkv[:, heads + kv :],
+        query,
+        key,
+        value,
         grad_w_out,
         small[:, 1],
         small[:, 2 : 2 + experts],

time: 622 us -> 1290 us (2.07)
  Pallas kernels: 376 us -> 1070 us
  other arithmetic: 50.8 us -> 19.8 us
  waiting for transfers between devices: 17.6 us -> 36.3 us
    pallas_call x4, Pallas kernels: 232 us -> 907 us  [expert_call(): pl.pallas_call(kernel, out_shape=shapes, in_specs=[vmem] * len(operands)...]
    pallas_call x1, Pallas kernels: 143 us -> 160 us  [sum_scatter(): pl.pallas_call(functools.partial(sum_scatter_kernel, (plans, len(arrays),...]
    select_n x11 -> x0, other arithmetic: 15.3 us -> none  [the longest x6 8.39 us: body(): got = swapped(jnp.where(first, b, a))]
    unnamed x226 -> x195, local copies, waits for them, and re-layouts: 28.2 us -> 27.8 us
  transfers between devices with their start and end apart: 24 -> 18, of which waited for: 3 -> 5; matrix products, arithmetic and copies ran while one was open for 24% -> 8% of each run, Pallas kernels for 35% -> 5%
where the time goes in v8:
time: 1290 us; the launch traced here: 1280 us
  Pallas kernels  1070 us (83%)
  matrix products  91.9 us (7%)
  local copies, waits for them, and re-layouts  49.6 us (4%)
  waiting for transfers between devices  36.3 us (3%)
  other arithmetic  19.8 us (2%)
  between operations  15.5 us (1%)
    pallas_call x4, Pallas kernels, expert_call(): pl.pallas_call(kernel, out_shape=shapes, in_specs=[vmem] * len(operands)...  907 us
    pallas_call x1, Pallas kernels, sum_scatter(): pl.pallas_call(functools.partial(sum_scatter_kernel, (plans, len(arrays),...  160 us
    dot_general x10, matrix products, turned(): jnp.einsum('tc,tq->cq', left, right, preferred_element_type=jnp.float32)  37.9 us
    unnamed x195, local copies, waits for them, and re-layouts  27.8 us
  transfers between devices with their start and end apart: 18, of which 5 were waited for; matrix products, arithmetic and copies ran while one was open for 8% of the time, Pallas kernels for 5%

profile of v8, /device:TPU:0, one launch (start us, length us, event | category | flops | bytes accessed | tf_op | source)
XLA Modules:
  0.0 1283.4 jit_solution(17134988091958594725)
XLA Ops:
  13.5 6.4 collective-permute-done.6
  25.6 1.2 broadcast_select_fusion
  28.2 2.2 fusion.13
  30.6 4.3 fusion.4
  35.1 1.6 fusion.117
  36.6 1.6 convolution_convert_fusion.9
  38.2 16.8 %collective-permute-done.4.refs_13_ = bf16[1536,1536]{1,0:T(8,128)(2,1)} collective-permute-done((bf16[1536,1536]{1,0:T(8,128)(2,1)}, bf16[1536,1536]{1,0:T(8,128)(2,1)}, u32[]{:S(2)}, u32[]{:S(2)}) %collective-permute-start.4) | collective-permute-done | bytes 4718624 | tf_op jit(solution)/shard_map/ppermute | solution.py:92
  55.1 3.6 multiply_reduce_fusion.7
  59.8 390.3 %shard_map.237 = (bf16[96,1536]{1,0:T(8,128)(2,1)S(1)}, bf16[4,96,1536]{2,1,0:T(8,128)(2,1)S(1)}, bf16[4,96,128]{2,1,0:T(8,128)(2,1)S(1)}, f32[96,128]{1,0:T(8,1...) custom-call(bf16[96,1536]{1,0:T(8,128)(2,1)S(1)} %multiply_convert_f, ...), custom_call_target="tpu_custom_call" | custom-call | flops 49999998976 | bytes 100000000 | tf_op jit(solution)/shard_map/pallas_call | solution.py:1010
  451.1 2.1 fusion.119
  453.4 4.4 fusion.120
  460.1 3.5 multiply_reduce_fusion.6
  464.7 385.9 %shard_map.238 = (bf16[96,1536]{1,0:T(8,128)(2,1)S(1)}, bf16[4,96,1536]{2,1,0:T(8,128)(2,1)S(1)}, bf16[4,96,128]{2,1,0:T(8,128)(2,1)S(1)}, f32[96,128]{1,0:T(8,1...) custom-call(bf16[96,1536]{1,0:T(8,128)(2,1)S(1)} %multiply_convert_f, ...), custom_call_target="tpu_custom_call" | custom-call | flops 49999998976 | bytes 100000000 | tf_op jit(solution)/shard_map/pallas_call | solution.py:1010
  850.6 66.2 %shard_map.239 = (f32[96,1536]{1,0:T(8,128)S(1)}, f32[96,128]{1,0:T(8,128)S(1)}, bf16[2,4,96,1536]{3,2,1,0:T(8,128)(2,1)}, bf16[2,4,96,1024]{3,2,1,0:T(8,128)(2,...) custom-call(bf16[96,1536]{1,0:T(8,128)(2,1)S(1)} %constant_dynamic-slice_fusion.9.grad, ...), custom_call_target="tpu_custom_call" | custom-call | flops 49999998976 | bytes 100000000 | tf_op jit(solution)/shard_map/pallas_call | solution.py:1010
  916.9 1.1 copy-done.6
  918.0 9.2 bitcast_convert_fusion.1
  927.3 1.9 copy.124
  929.3 1.9 copy.115
  933.4 4.1 convolution_convert_fusion.5
  938.4 1.5 multiply_reduce_fusion.1
  942.7 1.8 fusion.31
  950.3 4.3 fusion.54
  956.1 4.1 bitcast_convert_fusion.3
  966.0 2.2 convolution_convert_fusion.3
  968.3 3.1 convolution_convert_fusion.1
  971.7 1.3 copy-done.11
  972.9 64.0 %shard_map.240 = (f32[96,1536]{1,0:T(8,128)S(1)}, f32[96,128]{1,0:T(8,128)S(1)}, bf16[2,4,96,1536]{3,2,1,0:T(8,128)(2,1)}, bf16[2,4,96,1024]{3,2,1,0:T(8,128)(2,...) custom-call(bf16[96,1536]{1,0:T(8,128)(2,1)S(1)} %get-tuple-element.89.grad, ...), custom_call_target="tpu_custom_call" | custom-call | flops 49999998976 | bytes 100000000 | tf_op jit(solution)/shard_map/pallas_call | solution.py:1010
  1037.0 1.1 copy-done.8
  1038.3 9.2 bitcast_convert_fusion
  1049.3 3.9 convolution_convert_fusion.4
  1053.5 2.1 multiply_reduce_fusion
  1058.6 1.8 fusion.32
  1064.8 4.6 fusion.45
  1069.4 1.2 fusion.36
  1071.0 4.3 bitcast_convert_fusion.2
  1080.7 2.2 convolution_convert_fusion.2
  1083.0 3.2 convolution_convert_fusion
  1086.2 12.2 reduce-scatter.6.cloned.1.call-done
  1098.4 159.8 %shard_map.241 = (f32[4,384,512]{2,1,0:T(8,128)}, f32[4,384,512]{2,1,0:T(8,128)}, f32[4,128,1536]{2,1,0:T(8,128)}, f32[96,1536]{1,0:T(8,128)}, f32[96,512]{1,0:T...) custom-call(bf16[4,384,2048]{2,1,0:T(8,128)(2,1)} %bitcast.266, ...), custom_call_target="tpu_custom_call" | custom-call | tf_op jit(solution)/shard_map/pallas_call | solution.py:481
  1259.2 1.6 slice_reduce_fusion
  1262.6 2.1 copy.162
  1264.7 1.6 copy.163
  1267.0 1.9 copy.165
  1268.9 1.7 copy.166
  1270.6 1.4 copy-done.22
  1272.0 1.7 copy.167
  1273.6 1.4 copy-done.21
  1275.0 1.7 copy.168
  (326 shorter events, 56.8 us)
Async XLA Ops:
  7.2 6.3 copy-start
  7.2 18.2 %copy-start.15 = (bf16[192,1536]{1,0:T(8,128)(2,1)S(1)}, bf16[192,1536]{1,0:T(8,128)(2,1)}, u32[]{:S(2)}) copy-start(bf16[192,1536]{1,0:T(8,128)(2,1)} %param.14) | copy-start | bytes 1769476
  7.2 1040.3 %reduce-scatter.4.cloned.1.call-start = ((), (), s32[]{:S(2)}) async-start(), calls=%async_computation.3 | async-start | bytes 7864320 | tf_op jit(solution)/shard_map/reduce_scatter | solution.py:1225
  7.3 13.5 %collective-permute-start.2 = (bf16[1536,512]{1,0:T(8,128)(2,1)}, bf16[1536,512]{1,0:T(8,128)(2,1)}, u32[]{:S(2)}, u32[]{:S(2)}) collective-permute-start(bf16[1536,512]{1,0:T(8,128)(2,1)} %bitcast.350), channel_id=1, source_target_pairs={{0,16},{16,0},{1,17},{17,1},{2,18},{18,2},{3,19},{19,3},{4,20},{20... | collective-permute-start | bytes 4718600 | tf_op jit(solution)/shard_map/ppermute | solution.py:92
  7.8 14.4 %collective-permute-start.1 = (bf16[1536,512]{1,0:T(8,128)(2,1)}, bf16[1536,512]{1,0:T(8,128)(2,1)}, u32[]{:S(2)}, u32[]{:S(2)}) collective-permute-start(bf16[1536,512]{1,0:T(8,128)(2,1)} %bitcast.347), channel_id=1, source_target_pairs={{0,16},{16,0},{1,17},{17,1},{2,18},{18,2},{3,19},{19,3},{4,20},{20... | collective-permute-start | bytes 4718600 | tf_op jit(solution)/shard_map/ppermute | solution.py:92
  7.9 22.7 %collective-permute-start.3 = (bf16[1536,1536]{1,0:T(8,128)(2,1)}, bf16[1536,1536]{1,0:T(8,128)(2,1)}, u32[]{:S(2)}, u32[]{:S(2)}) collective-permute-start(bf16[1536,1536]{1,0:T(8,128)(2,1)} %bitcast.344), channel_id=1, source_target_pairs={{0,16},{16,0},{1,17},{17,1},{2,18},{18,2},{3,19},{19,3},{4,20},{20... | collective-permute-start | bytes 14155784 | tf_op jit(solution)/shard_map/ppermute | solution.py:92
  9.0 3.3 collective-permute-start
  9.9 3.2 collective-permute-start.5
  12.3 7.5 collective-permute-start.6
  13.1 7.3 collective-permute-start.7
  19.8 39.5 %collective-permute-start.10 = (bf16[4,512,1536]{2,1,0:T(8,128)(2,1)}, bf16[4,512,1536]{2,1,0:T(8,128)(2,1)}, u32[]{:S(2)}, u32[]{:S(2)}) collective-permute-start(bf16[4,512,1536]{2,1,0:T(8,128)(2,1)} %bitcast.339), channel_id=1, source_target_pairs={{0,16},{16,0},{1,17},{17,1},{2,18},{18,2},{3,19},{19,3},{4,20},{20... | collective-permute-start | bytes 18874376 | tf_op jit(solution)/shard_map/ppermute | solution.py:92
  20.4 5.0 copy-start.45
  20.4 39.0 %collective-permute-start.8 = (bf16[4,1536,512]{2,1,0:T(8,128)(2,1)}, bf16[4,1536,512]{2,1,0:T(8,128)(2,1)}, u32[]{:S(2)}, u32[]{:S(2)}) collective-permute-start(bf16[4,1536,512]{2,1,0:T(8,128)(2,1)} %bitcast.329), channel_id=1, source_target_pairs={{0,16},{16,0},{1,17},{17,1},{2,18},{18,2},{3,19},{19,3},{4,20},{20... | collective-permute-start | bytes 18874376 | tf_op jit(solution)/shard_map/ppermute | solution.py:92
  20.8 38.6 %collective-permute-start.9 = (bf16[4,1536,512]{2,1,0:T(8,128)(2,1)}, bf16[4,1536,512]{2,1,0:T(8,128)(2,1)}, u32[]{:S(2)}, u32[]{:S(2)}) collective-permute-start(bf16[4,1536,512]{2,1,0:T(8,128)(2,1)} %bitcast.334), channel_id=1, source_target_pairs={{0,16},{16,0},{1,17},{17,1},{2,18},{18,2},{3,19},{19,3},{4,20},{20... | collective-permute-start | bytes 18874376 | tf_op jit(solution)/shard_map/ppermute | solution.py:92
  22.1 32.9 %collective-permute-start.4 = (bf16[1536,1536]{1,0:T(8,128)(2,1)}, bf16[1536,1536]{1,0:T(8,128)(2,1)}, u32[]{:S(2)}, u32[]{:S(2)}) collective-permute-start(bf16[1536,1536]{1,0:T(8,128)(2,1)} %bitcast.267), channel_id=1, source_target_pairs={{0,16},{16,0},{1,17},{17,1},{2,18},{18,2},{3,19},{19,3},{4,20},{20... | collective-permute-start | bytes 14155784 | tf_op jit(solution)/shard_map/ppermute | solution.py:92
  25.3 425.7 %copy-start.69 = (f32[1536]{0:T(1024)}, f32[1536]{0:T(1024)S(1)}, u32[]{:S(2)}) copy-start(f32[1536]{0:T(1024)S(1)} %get-tuple-element.217) | copy-start | bytes 18436
  25.3 33.9 %copy-start.58 = (f32[1536]{0:T(1024)}, f32[1536]{0:T(1024)S(1)}, u32[]{:S(2)}) copy-start(f32[1536]{0:T(1024)S(1)} %get-tuple-element.216) | copy-start | bytes 18436
  25.4 438.8 %copy-start.60 = (f32[1536]{0:T(1024)}, f32[1536]{0:T(1024)S(1)}, u32[]{:S(2)}) copy-start(f32[1536]{0:T(1024)S(1)} %get-tuple-element.215) | copy-start | bytes 18436
  25.5 5.0 copy-start.29
  28.2 8.4 copy-start.63
  30.5 4.5 copy-start.47
  30.5 4.5 copy-start.49
  38.2 20.4 %copy-start.25 = (bf16[8,64,3,96]{3,1,2,0:T(8,128)(2,1)}, bf16[8,64,3,96]{3,1,2,0:T(8,128)(2,1)S(1)}, u32[]{:S(2)}) copy-start(bf16[8,64,3,96]{3,1,2,0:T(8,128)(2,1)S(1)} %convolution_convert_fusion.9) | copy-start | bytes 884740
  58.6 391.5 %copy-start.2 = (f32[96,1536]{1,0:T(8,128)}, f32[96,1536]{1,0:T(8,128)S(1)}, u32[]{:S(2)}) copy-start(f32[96,1536]{1,0:T(8,128)S(1)} %get-tuple-element.232.hidden) | copy-start | bytes 1769476
  59.4 390.8 %copy-start.4 = (bf16[96,1536]{1,0:T(8,128)(2,1)}, bf16[96,1536]{1,0:T(8,128)(2,1)S(1)}, u32[]{:S(2)}) copy-start(bf16[96,1536]{1,0:T(8,128)(2,1)S(1)} %multiply_convert_fusion.3.x) | copy-start | bytes 884740
  453.4 5.1 copy-start.51
  453.4 5.1 copy-start.53
  453.4 4.6 copy-start.13
  927.3 4.1 copy-start.20
  927.3 158.9 %reduce-scatter.8.cloned.1.call-start = ((), (), s32[]{:S(2)}) async-start(), calls=%async_computation.5 | async-start | bytes 2949120 | tf_op jit(solution)/shard_map/reduce_scatter | solution.py:1272
  933.4 5.0 copy-start.33
  933.4 5.0 copy-start.66
  933.4 5.0 copy-start.74
  948.1 14.9 %collective-permute-start.12 = (bf16[96,5120]{1,0:T(8,128)(2,1)}, bf16[96,5120]{1,0:T(8,128)(2,1)}, u32[]{:S(2)}, u32[]{:S(2)}) collective-permute-start(bf16[96,5120]{1,0:T(8,128)(2,1)} %pad_maximum_fusion), channel_id=1, source_target_pairs={{0,16},{16,0},{1,17},{17,1},{2,18},{18,2},{3,19},{19,3},{4,20},{20... | collective-permute-start | bytes 2949128 | tf_op jit(solution)/shard_map/ppermute | solution.py:92
  950.3 4.3 copy-start.24
  950.3 4.3 copy-start.86
  950.3 5.5 copy-start.90
  955.7 6.5 collective-permute-start.11
  971.4 127.0 %reduce-scatter.6.cloned.1.call-start = ((), (), s32[]{:S(2)}) async-start(), calls=%async_computation.4 | async-start | bytes 4915200 | tf_op jit(solution)/shard_map/reduce_scatter | solution.py:1273
  1049.3 4.2 copy-start.64
  1049.3 4.2 copy-start.72
  1062.5 15.2 %collective-permute-start.14 = (bf16[96,5120]{1,0:T(8,128)(2,1)}, bf16[96,5120]{1,0:T(8,128)(2,1)}, u32[]{:S(2)}, u32[]{:S(2)}) collective-permute-start(bf16[96,5120]{1,0:T(8,128)(2,1)} %pad_maximum_fusion.1), channel_id=1, source_target_pairs={{0,16},{16,0},{1,17},{17,1},{2,18},{18,2},{3,19},{19,3},{4,20},{20... | collective-permute-start | bytes 2949128 | tf_op jit(solution)/shard_map/ppermute | solution.py:92
  1064.7 4.6 copy-start.88
  1064.8 5.8 copy-start.91
  1070.5 6.1 collective-permute-start.13
  1071.0 4.3 copy-start.5
  1258.3 8.1 copy-start.56
  1262.6 6.3 copy-start.23
  (62 other events, 106.2 us)
Sparse Core Ops, SparseCore 0:
  927.4 69.3 reduce-scatter.3
  999.8 37.3 reduce-scatter.7
  1047.6 50.7 reduce-scatter.5

commit v9 on v8

--- a/solution.py
+++ b/solution.py
@@ -1,5 +1,6 @@
 import functools
 import itertools
+from types import SimpleNamespace
 
 import jax
 import jax.numpy as jnp
@@ -19,6 +20,10 @@
 EPSILON = 1e-05
 THETA = 10000.0
 MASKED = -1e30
+COLUMNS = 128
+GATE, UP, DOWN, QKV, OUT, SMALL = range(6)
+CORE, GROUP, LINE = "section", "dp", "expert"
+INNER = "inner"
 
 
 def matmul(left_side, right_side):
@@ -89,7 +94,7 @@
 
 
 def swapped(array):
-    return lax.ppermute(array, "section", [(0, 1), (1, 0)])
+    return lax.ppermute(array, CORE, [(0, 1), (1, 0)])
 
 
 def add_slab(total, arrived):
@@ -110,27 +115,24 @@
     lanes, ins, copies = plan
     sources = refs[:ins]
     second_pre, stats_in = refs[ins : ins + 2]
-    gate_out, up_out, down_out, query_out, key_out, value_out, out_out, small_out, stats = refs[
-        ins + 2 : ins + 11
-    ]
-    scratch = list(refs[ins + 11 :])
-    stage = dict(zip(("pre", "down", "qkv", "out", "small"), scratch[-13:-8]))
+    stage, stats = refs[ins + 2 : ins + 8], refs[ins + 8]
+    scratch = list(refs[ins + 9 :])
     send_sem, recv_sem, local_sem, stats_got, stats_send, stats_recv, core_send, core_recv = (
         scratch[-8:]
     )
-    core = lax.axis_index("section")
+    core = lax.axis_index(CORE)
     partners = []
     for lane in lanes:
-        for axis, bits in lane["phases"]:
+        for axis, bits in lane.phases:
             partners += [(axis, bit) for bit in bits if (axis, bit) not in partners]
-    partners.append(("section", 0))
+    partners.append((CORE, 0))
     index = {axis: lax.axis_index(axis) for axis, _ in partners}
     mine = {(axis, bit): (index[axis] >> bit) & 1 for axis, bit in partners}
     far = {key: index[key[0]] + (1 - 2 * mine[key]) * (1 << key[1]) for key in partners}
     barrier = pltpu.get_barrier_semaphore()
-    peers = [{axis: far[axis, bit]} for axis, bit in partners if axis != "dp"]
-    groups = lax.axis_size("dp")
-    peers += [{"dp": lax.rem(lax.axis_index("dp") + k, groups)} for k in range(1, groups)]
+    peers = [{axis: far[axis, bit]} for axis, bit in partners if axis != GROUP]
+    groups = lax.axis_size(GROUP)
+    peers += [{GROUP: lax.rem(lax.axis_index(GROUP) + k, groups)} for k in range(1, groups)]
     for peer in peers:
         pl.semaphore_signal(
             barrier, inc=1, device_id=peer, device_id_type=pl.DeviceIdType.MESH
@@ -159,8 +161,8 @@
         return total
 
     def sum_stats():
-        count = lax.axis_size("dp")
-        me = lax.axis_index("dp")
+        count = lax.axis_size(GROUP)
+        me = lax.axis_index(GROUP)
 
         def copy(at, source, slot, target):
             return pltpu.make_async_remote_copy(
@@ -173,20 +175,20 @@
             )
 
         for k in range(1, count):
-            copy(k, stats_in, me, {"dp": lax.rem(me + k, count)}).start()
+            copy(k, stats_in, me, {GROUP: lax.rem(me + k, count)}).start()
         yield
         stats[...] = stats_in[...]
         for k in range(1, count):
             peer = lax.rem(me + k, count)
-            copy(k, stats_in, peer, {"dp": peer}).wait_recv()
+            copy(k, stats_in, peer, {GROUP: peer}).wait_recv()
             stats[...] += stats_got[peer]
-        both = copy(0, stats, count, {"section": far["section", 0]})
+        both = copy(0, stats, count, {CORE: far[CORE, 0]})
         both.start()
         yield
         both.wait()
         stats[...] += stats_got[count]
         for k in range(1, count):
-            copy(k, stats_in, me, {"dp": lax.rem(me + k, count)}).wait_send()
+            copy(k, stats_in, me, {GROUP: lax.rem(me + k, count)}).wait_send()
 
     summing = sum_stats()
     next(summing)
@@ -198,40 +200,45 @@
             dst_ref=spot,
             send_sem=core_send.at[number],
             recv_sem=core_recv.at[number],
-            device_id={"section": 1 - core},
+            device_id={CORE: 1 - core},
             device_id_type=pl.DeviceIdType.MESH,
         )
 
-    spot, whole = to_stage(len(lanes), second_pre, "pre")
-    whole_here = pltpu.make_async_copy(second_pre, spot, core_send.at[len(lanes)])
-
-    @pl.when(core == 1)
-    def _():
-        whole_here.start()
-
-    @pl.when(core == 0)
-    def _():
-        whole.start()
+    inner = stage[GATE].shape[3]
+    wholes = []
+    for number in range(second_pre.shape[1] // inner):
+        kind, j = divmod(number, stage[GATE].shape[1])
+        source = second_pre.at[:, pl.ds(number * inner, inner)]
+        spot, copy = to_stage(len(lanes) + number, source, kind, j)
+        wholes.append((copy, pltpu.make_async_copy(source, spot, core_send.at[len(lanes) + number])))
+    for copy, here in wholes:
+        @pl.when(core == 1)
+        def _(here=here):
+            here.start()
+
+        @pl.when(core == 0)
+        def _(copy=copy):
+            copy.start()
 
     moved = []
     started = []
     states = []
     for number, lane in enumerate(lanes):
-        count = len(lane["buffers"])
+        count = len(lane.buffers)
         buffers, scratch = scratch[:count], scratch[count:]
-        source = sources[lane["source"]]
-        prefix = lane["prefix"]
+        source = sources[lane.source]
+        prefix = lane.prefix
         if isinstance(prefix, int):
             source = source.at[prefix]
 
         def part(at, source=source, prefix=prefix):
             if isinstance(prefix, tuple):
                 return source.at[at, :, pl.ds(*prefix)]
-            if prefix == "inner":
+            if prefix == INNER:
                 return source.at[:, at]
             return source.at[at]
 
-        axis, bits = lane["phases"][0]
+        axis, bits = lane.phases[0]
         total, arrived = buffers[0], buffers[1:]
         rest = [bit for bit in bits[1:]]
         pending = []
@@ -244,24 +251,24 @@
             pending.append((copy, slot))
             started.append(copy)
             states.append((number, part(here_at), slot, total))
-        lane_state = {"total": total, "arrived": arrived, "pending": pending, "rest": rest}
-        lane["state"] = lane_state
+        lane_state = SimpleNamespace(total=total, arrived=arrived, pending=pending)
+        lane.state = lane_state
     locals_ = {}
     for at, (number, here, slot, total) in enumerate(states):
         copy = pltpu.make_async_copy(here, total.at[slot], local_sem.at[at])
         copy.start()
         locals_[number, slot] = copy
-    longest = max(sum(len(bits) for _, bits in lane["phases"]) for lane in lanes)
+    longest = max(sum(len(bits) for _, bits in lane.phases) for lane in lanes)
     for step in range(1, longest + 1):
         if step == 2:
             next(summing)
         for number, lane in enumerate(lanes):
-            state = lane["state"]
-            sizes = [len(bits) for _, bits in lane["phases"]]
+            state = lane.state
+            sizes = [len(bits) for _, bits in lane.phases]
             if step > sum(sizes):
                 continue
             if step <= sizes[0]:
-                axis, bits = lane["phases"][0]
+                axis, bits = lane.phases[0]
                 resolved, rest = bits[:step], bits[step:]
 
                 def slot_of(values):
@@ -270,16 +277,16 @@
                         found = found + values.get(bit, mine[axis, bit]) * (1 << i)
                     return found
 
-                for copy, slot in state["pending"]:
+                for copy, slot in state.pending:
                     copy.wait_recv()
                     if step == 1:
                         locals_[number, slot].wait()
-                state["pending_next"] = []
+                state.pending_next = []
                 for choice in itertools.product((0, 1), repeat=len(rest)):
                     values = dict(zip(rest, choice))
                     got = sum(value << i for i, value in enumerate(choice))
                     add_slab(
-                        state["total"].at[slot_of(values)], state["arrived"][step - 1].at[got]
+                        state.total.at[slot_of(values)], state.arrived[step - 1].at[got]
                     )
                 if rest:
                     following = rest[1:]
@@ -288,44 +295,44 @@
                         got = sum(value << i for i, value in enumerate(choice))
                         values[rest[0]] = 1 - mine[axis, rest[0]]
                         copy = send(
-                            state["total"].at[slot_of(values)],
-                            state["arrived"][step].at[got],
+                            state.total.at[slot_of(values)],
+                            state.arrived[step].at[got],
                             (axis, rest[0]),
                         )
-                        state["pending_next"].append((copy, got))
+                        state.pending_next.append((copy, got))
                         started.append(copy)
-                final = state["total"].at[slot_of({})] if not rest else None
+                final = state.total.at[slot_of({})] if not rest else None
             else:
-                axis, bits = lane["phases"][1]
+                axis, bits = lane.phases[1]
                 done = step - sizes[0]
                 rest = bits[done:]
-                final = state["final"]
-                for copy, _ in state["pending"]:
+                final = state.final
+                for copy, _ in state.pending:
                     copy.wait_recv()
-                state["pending_next"] = []
+                state.pending_next = []
                 for choice in itertools.product((0, 1), repeat=len(rest)):
                     values = dict(zip(rest, choice))
                     got = sum(value << i for i, value in enumerate(choice))
                     at = place(axis, {bit: values.get(bit, mine[axis, bit]) for bit in bits})
-                    add_slab(final.at[at], state["arrived"][step - 1].at[got])
+                    add_slab(final.at[at], state.arrived[step - 1].at[got])
                 if not rest:
                     at = place(axis, {bit: mine[axis, bit] for bit in bits})
                     final = final.at[at]
             if final is not None and step >= sizes[0]:
-                state["final"] = final
+                state.final = final
                 if step == sum(sizes):
-                    spot, copy = to_stage(number, final, *lane["target"])
-                    moved.append((lane["layer"], copy))
-
-                    @pl.when(core == lane["layer"])
+                    spot, copy = to_stage(number, final, *lane.target)
+                    moved.append((lane.layer, copy))
+
+                    @pl.when(core == lane.layer)
                     def _(spot=spot, final=final):
                         spot[...] = final[...]
 
-                    @pl.when(core != lane["layer"])
+                    @pl.when(core != lane.layer)
                     def _(copy=copy):
                         copy.start()
                 elif step < sum(sizes):
-                    axis, bits = lane["phases"][1]
+                    axis, bits = lane.phases[1]
                     done = step - sizes[0]
                     bit, following = bits[done], bits[done + 1 :]
                     for choice in itertools.product((0, 1), repeat=len(following)):
@@ -338,21 +345,22 @@
                                 for b in bits
                             },
                         )
-                        copy = send(final.at[at], state["arrived"][step].at[got], (axis, bit))
-                        state["pending_next"].append((copy, got))
+                        copy = send(final.at[at], state.arrived[step].at[got], (axis, bit))
+                        state.pending_next.append((copy, got))
                         started.append(copy)
-            state["pending"] = state["pending_next"]
+            state.pending = state.pending_next
     for _ in summing:
         pass
 
-    @pl.when(core == 1)
-    def _():
-        whole.wait_recv()
-        whole_here.wait()
-
-    @pl.when(core == 0)
-    def _():
-        whole.wait_send()
+    for copy, here in wholes:
+        @pl.when(core == 1)
+        def _(copy=copy, here=here):
+            copy.wait_recv()
+            here.wait()
+
+        @pl.when(core == 0)
+        def _(copy=copy):
+            copy.wait_send()
 
     for layer, copy in moved:
         @pl.when(core == layer)
@@ -363,45 +371,6 @@
         def _(copy=copy):
             copy.wait_send()
 
-    pre, inner = stage["pre"], gate_out.shape[2]
-    half = gate_out.shape[0] // 2
-    rows = gate_out.shape[1]
-    line = 16 if rows % 16 == 0 else rows
-
-    def write(i, carry):
-        at = pl.ds(pl.multiple_of(i * line, line), line)
-        for c in range(2):
-            for j in range(half):
-                for kind, target in enumerate((gate_out, up_out)):
-                    columns = pl.ds((kind * half + j) * inner, inner)
-                    target[c * half + j, at] = pre[c, at, columns].astype(jnp.float32)
-        return carry
-
-    lax.fori_loop(0, rows // line, write, 0)
-    rows = down_out.shape[1]
-    line = 16 if rows % 16 == 0 else rows
-
-    def write_down(i, carry):
-        at = pl.ds(pl.multiple_of(i * line, line), line)
-        for c in range(2):
-            for j in range(half):
-                down_out[c * half + j, at] = stage["down"][c, j, at].astype(jnp.float32)
-        return carry
-
-    lax.fori_loop(0, rows // line, write_down, 0)
-    column = 0
-    width = stage["qkv"].shape[2]
-    for target in (query_out, key_out, value_out):
-        done = 0
-        while done < target.shape[1]:
-            c, at = divmod(column, width)
-            size = min(width - at, target.shape[1] - done)
-            target[:, done : done + size] = stage["qkv"][c, :, at : at + size].astype(jnp.float32)
-            done, column = done + size, column + size
-    width = stage["out"].shape[2]
-    for c in range(2):
-        out_out[:, c * width : (c + 1) * width] = stage["out"][c].astype(jnp.float32)
-    small_out[...] = stage["small"][0].astype(jnp.float32) + stage["small"][1].astype(jnp.float32)
     for copy in started:
         copy.wait_send()
 
@@ -413,7 +382,7 @@
         shape = arrays[source].shape
         if isinstance(prefix, int):
             shape = shape[1:]
-        elif prefix == "inner":
+        elif prefix == INNER:
             shape = (shape[1], shape[0], *shape[2:])
         elif prefix is not None:
             shape = (*shape[:-1], prefix[1])
@@ -427,56 +396,42 @@
                 buffers.append((shape[1] >> step, *shape[2:]))
                 copies += shape[1] >> step
         plans.append(
-            {
-                "source": source,
-                "prefix": prefix,
-                "phases": phases,
-                "buffers": buffers,
-                "layer": layer,
-                "target": target,
-            }
+            SimpleNamespace(
+                source=source,
+                prefix=prefix,
+                phases=phases,
+                buffers=buffers,
+                layer=layer,
+                target=target,
+            )
         )
         sizes.setdefault(target[0], shape[-2:])
         scratch += [pltpu.VMEM(buffer, jnp.bfloat16) for buffer in buffers]
     half = second_pre.shape[1] // (2 * inner)
-    heads, kv = H * HD, KVH * HD
-    shard = sizes["qkv"][0]
+    experts_shape = (2, half, second_pre.shape[0], inner)
     shapes = [
-        jax.ShapeDtypeStruct(shape, jnp.float32)
+        jax.ShapeDtypeStruct(shape, jnp.bfloat16)
         for shape in (
-            (2 * half, second_pre.shape[0], inner),
-            (2 * half, second_pre.shape[0], inner),
-            (2 * half, *sizes["down"]),
-            (shard, heads),
-            (shard, kv),
-            (shard, kv),
-            (shard, 2 * sizes["out"][1]),
-            (shard, COLUMNS),
-            stats.shape,
-        )
-    ]
-    scratch += [
-        pltpu.VMEM((2, *shape), jnp.bfloat16)
-        for shape in (
-            second_pre.shape,
-            (half, *sizes["down"]),
-            sizes["qkv"],
-            sizes["out"],
-            sizes["small"],
-        )
-    ]
+            experts_shape,
+            experts_shape,
+            (2, half, *sizes[DOWN]),
+            (2, *sizes[QKV]),
+            (2, *sizes[OUT]),
+            (2, *sizes[SMALL]),
+        )
+    ] + [jax.ShapeDtypeStruct(stats.shape, jnp.float32)]
     scratch += [
         pltpu.SemaphoreType.DMA((copies,)),
         pltpu.SemaphoreType.DMA((copies,)),
         pltpu.SemaphoreType.DMA((locals_,)),
     ]
-    hops = lax.axis_size("dp") + 1
+    hops = lax.axis_size(GROUP) + 1
     scratch += [
         pltpu.VMEM((hops, *stats.shape), jnp.float32),
         pltpu.SemaphoreType.DMA((hops,)),
         pltpu.SemaphoreType.DMA((hops,)),
-        pltpu.SemaphoreType.DMA((len(lanes) + 1,)),
-        pltpu.SemaphoreType.DMA((len(lanes) + 1,)),
+        pltpu.SemaphoreType.DMA((len(lanes) + 2 * half,)),
+        pltpu.SemaphoreType.DMA((len(lanes) + 2 * half,)),
     ]
     return pl.pallas_call(
         functools.partial(sum_scatter_kernel, (plans, len(arrays), copies)),
@@ -495,29 +450,26 @@
     return list(range(lax.axis_size(axis).bit_length() - 1))
 
 
-def slice_of(start, size):
-    return (slice(None), pl.ds(start, size))
-
-
 def expert_lanes(first, inner):
-    up, down = [("dp", bits_of("dp"))], [("dp", bits_of("dp")[::-1])]
+    up, down = [(GROUP, bits_of(GROUP))], [(GROUP, bits_of(GROUP)[::-1])]
     return [
-        (first, (at * inner, inner), phases, 0, ("pre", *slice_of(at * inner, inner)))
-        for at, phases in ((0, up), (2, down), (1, up), (3, down))
+        (first, ((2 * kind + j) * inner, inner), (up, down)[kind], 0, (kind, j))
+        for j in range(2)
+        for kind in (GATE, UP)
     ]
 
 
 def down_lanes(first, layer):
-    up, down = [("dp", bits_of("dp"))], [("dp", bits_of("dp")[::-1])]
-    return [(first, 0, up, layer, ("down", 0)), (first, 1, down, layer, ("down", 1))]
+    up, down = [(GROUP, bits_of(GROUP))], [(GROUP, bits_of(GROUP)[::-1])]
+    return [(first, 0, up, layer, (DOWN, 0)), (first, 1, down, layer, (DOWN, 1))]
 
 
 def dense_lanes(first):
-    up, down, deep = bits_of("dp"), bits_of("dp")[::-1], bits_of("expert")
+    up, down, deep = bits_of(GROUP), bits_of(GROUP)[::-1], bits_of(LINE)
     return [
-        (first, "inner", [("expert", deep), ("dp", up)], 0, ("qkv",)),
-        (first + 1, None, [("dp", down), ("expert", deep)], 0, ("out",)),
-        (first + 2, None, [("dp", up), ("expert", deep)], 0, ("small",)),
+        (first, INNER, [(LINE, deep), (GROUP, up)], 0, (QKV,)),
+        (first + 1, None, [(GROUP, down), (LINE, deep)], 0, (OUT,)),
+        (first + 2, None, [(GROUP, up), (LINE, deep)], 0, (SMALL,)),
     ]
 
 
@@ -551,7 +503,6 @@
 
 
 MESH = pl.DeviceIdType.MESH
-COLUMNS = 128
 PARTS = 3
 
 
@@ -560,7 +511,7 @@
     barrier = pltpu.get_barrier_semaphore()
     for k in range(1, n):
         peer = lax.rem(z + k, n)
-        pl.semaphore_signal(barrier, inc=1, device_id={"expert": peer}, device_id_type=MESH)
+        pl.semaphore_signal(barrier, inc=1, device_id={LINE: peer}, device_id_type=MESH)
     for peer in others:
         pl.semaphore_signal(barrier, inc=1, device_id=peer, device_id_type=MESH)
     pl.semaphore_wait(barrier, n - 1 + len(others))
@@ -574,7 +525,7 @@
             dst_ref=held[kind].at[block],
             send_sem=row_send.at[kind, way, hop],
             recv_sem=row_recv.at[kind, way, hop],
-            device_id={"expert": peer},
+            device_id={LINE: peer},
             device_id_type=MESH,
         )
 
@@ -604,9 +555,21 @@
                 def _():
                     row_copy(kind, way, hop + 1).start()
 
-    def behind(way):
-        peer = z - (1 - 2 * way)
-        return (peer >= 0) & (peer < n)
+    def waits(way, block):
+        peer, last = z - (1 - 2 * way), (n - 1) * (1 - way)
+        return (peer >= 0) & (peer < n) & ((block != last) | (peer != n - 1 - last))
+
+    def far_copy(p):
+        mine, arrived = pieces[p]
+        block, way = n - 1 - z, jnp.where(z == 0, 1, 0)
+        return pltpu.make_async_remote_copy(
+            src_ref=mine(block),
+            dst_ref=arrived(way, block),
+            send_sem=sum_send.at[block, p],
+            recv_sem=sum_recv.at[way, block, p],
+            device_id={LINE: block},
+            device_id_type=MESH,
+        )
 
     def sum_copy(way, block, p):
         mine, arrived = pieces[p]
@@ -615,14 +578,19 @@
             dst_ref=arrived(way, block),
             send_sem=sum_send.at[block, p],
             recv_sem=sum_recv.at[way, block, p],
-            device_id={"expert": jnp.clip(z + 1 - 2 * way, 0, n - 1)},
+            device_id={LINE: jnp.clip(z + 1 - 2 * way, 0, n - 1)},
             device_id_type=MESH,
         )
 
     def sent(block, p):
         way = jnp.where(block > z, 0, 1)
-
-        @pl.when((block != z) & jnp.logical_not(behind(way)))
+        far = ((z == 0) | (z == n - 1)) & (block == n - 1 - z)
+
+        @pl.when(far)
+        def _():
+            far_copy(p).start()
+
+        @pl.when((block != z) & jnp.logical_not(far) & jnp.logical_not(waits(way, block)))
         def _():
             sum_copy(way, block, p).start()
 
@@ -656,7 +624,7 @@
             for k in range(1, n):
                 block = z + (1 - 2 * way) * k
 
-                @pl.when(behind(way) & (block >= 0) & (block < n))
+                @pl.when(waits(way, block) & (block >= 0) & (block < n))
                 def _():
                     for p, (mine, arrived) in enumerate(pieces):
                         sum_copy(way, block, p).wait_recv()
@@ -668,11 +636,9 @@
 
     def collect(add):
         for way in range(2):
-            @pl.when(behind(way))
-            def _():
-                for p, (_, arrived) in enumerate(pieces):
-                    sum_copy(way, z, p).wait_recv()
-                    add(p, arrived(way, z)[...].astype(jnp.float32))
+            for p, (_, arrived) in enumerate(pieces):
+                sum_copy(way, z, p).wait_recv()
+                add(p, arrived(way, z)[...].astype(jnp.float32))
 
     def finish():
         for kind in range(len(held)):
@@ -703,7 +669,7 @@
 
 def fetch_weights(layer, own, other, places, sem):
     count = places[0].shape[0]
-    mine = lax.axis_index("section") == layer
+    mine = lax.axis_index(CORE) == layer
 
     def copy(group, kind, e):
         return pltpu.make_async_copy(
@@ -743,11 +709,12 @@
     own, other, refs = refs[:3], refs[3:6], refs[6:]
     own_dense, other_dense, refs = refs[:4], refs[4:8], refs[8:]
     out, rows, gates_all, gates, gate_keep, up_keep, gated, stats = refs[:8]
-    placed, place_sem, refs = refs[8:12], refs[-1], refs[:8] + refs[12:-1]
+    placed, place_sem = refs[8:12], refs[-1]
+    passing, refs = refs[-5:-1], refs[:8] + refs[12:-5]
     w_gate, w_up, w_down, sums, returned, mixed, total, stats_all = refs[8:16]
     weight_sem, *sems = refs[16:]
     n, held = rows.shape[0], w_gate.shape[0]
-    z = lax.axis_index("expert")
+    z = lax.axis_index(LINE)
 
     def compute(block, sent):
         picked = rows[block]
@@ -796,10 +763,13 @@
     )
     start(0)
     wait_weights = fetch_weights(layer, own, other, (w_gate, w_up, w_down), weight_sem)
-    here = lax.axis_index("section") == 1 - layer
+    here = lax.axis_index(CORE) == 1 - layer
 
     def place_copy(group, i):
-        return pltpu.make_async_copy(group[i], placed[i], place_sem.at[i])
+        return pltpu.make_async_copy(group[i], passing[i], place_sem.at[0, i])
+
+    def place_out(i):
+        return pltpu.make_async_copy(passing[i], placed[i], place_sem.at[1, i])
 
     for i in range(4):
         @pl.when(here)
@@ -831,6 +801,9 @@
     rows[z] = x[...]
     wait_weights()
     run()
+    for i in range(4):
+        place_copy(own_dense, i).wait()
+        place_out(i).start()
     stats[...] = jnp.sum(stats_all[...], axis=0)
     width = out.shape[1] // PARTS
 
@@ -841,7 +814,7 @@
     out[...] = total[...].astype(jnp.bfloat16)
     finish()
     for i in range(4):
-        place_copy(own_dense, i).wait()
+        place_out(i).wait()
 
 
 def experts_backward_kernel(layer, grad, gates, gate_keep, up_keep, *refs):
@@ -851,8 +824,8 @@
     weight_sem, core_send, core_recv, core_local, *sems = refs[15:]
     n, held = gates.shape[0], w_gate.shape[0]
     half, inner = held // 2, w_gate.shape[2]
-    core = lax.axis_index("section")
-    z = lax.axis_index("expert")
+    core = lax.axis_index(CORE)
+    z = lax.axis_index(LINE)
     turned_dims = (((1,), (1,)), ((), ()))
     rows = grad_both.at[core]
 
@@ -862,7 +835,7 @@
             dst_ref=target,
             send_sem=core_send.at[number],
             recv_sem=core_recv.at[number],
-            device_id={"section": 1 - core},
+            device_id={CORE: 1 - core},
             device_id_type=MESH,
         )
 
@@ -967,7 +940,7 @@
         compute,
         z,
         n,
-        [{"section": 1 - core}],
+        [{CORE: 1 - core}],
     )
     start(0)
     wait_weights = fetch_weights(layer, own, other, (w_gate, w_up, w_down), weight_sem)
@@ -1014,7 +987,7 @@
         out_specs=[vmem] * (len(shapes) - loose) + [free] * loose,
         scratch_shapes=weights + scratch,
         compiler_params=pltpu.CompilerParams(
-            collective_id=collective, has_side_effects=True, vmem_limit_bytes=50 * 2**20
+            collective_id=collective, has_side_effects=True, vmem_limit_bytes=46 * 2**20
         ),
         cost_estimate=pl.CostEstimate(
             flops=5 * 10**10, bytes_accessed=10**8, transcendentals=0
@@ -1025,7 +998,7 @@
 def experts_forward(
     layer, normed_two, mask, hidden, router, own, other, own_dense, other_dense, experts
 ):
-    n, held = lax.axis_size("expert"), own[0].shape[0]
+    n, held = lax.axis_size(LINE), own[0].shape[0]
     length, width = normed_two.shape
     inner = own[0].shape[2]
     low, full = jnp.bfloat16, jnp.float32
@@ -1048,7 +1021,8 @@
         pltpu.VMEM((n, 8, COLUMNS), full),
         pltpu.SemaphoreType.DMA((3 * held,)),
     ] + exchange_scratch(n, 3, PARTS)
-    scratch.append(pltpu.SemaphoreType.DMA((4,)))
+    scratch += [pltpu.VMEM(array.shape, low) for array in own_dense]
+    scratch.append(pltpu.SemaphoreType.DMA((2, 4)))
     kernel = functools.partial(experts_forward_kernel, layer, experts)
     return expert_call(
         kernel,
@@ -1155,7 +1129,7 @@
 
 
 def body(tokens, cotangent, segments, routes, *weight_arrays):
-    core = lax.axis_index("section")
+    core = lax.axis_index(CORE)
     first = core == 0
     experts = weight_arrays[6].shape[2]
     w_gate = weight_arrays[7]
@@ -1222,7 +1196,7 @@
         ).astype(jnp.bfloat16)
         if s == 1:
             grad_sum, grad_gate_up = lax.optimization_barrier((grad_sum, grad_gate_up))
-            second_pre = lax.psum_scatter(grad_gate_up, "dp", scatter_dimension=0, tiled=True)
+            second_pre = lax.psum_scatter(grad_gate_up, GROUP, scatter_dimension=0, tiled=True)
         else:
             grad_sum, second_pre = lax.optimization_barrier((grad_sum, second_pre))
         gates, grad_gates = gates[:, :experts], grad_gates[:, :experts]
@@ -1269,13 +1243,13 @@
             grad_inputs, grad_down, grad_w_qkv, grad_w_out = lax.optimization_barrier(
                 (grad_inputs, grad_down, grad_w_qkv, grad_w_out)
             )
-            second_out = lax.psum_scatter(grad_w_out, "dp", scatter_dimension=0, tiled=True)
-            second_qkv = lax.psum_scatter(grad_w_qkv, "dp", scatter_dimension=0, tiled=True)
+            dense = jnp.concatenate([grad_w_qkv, grad_w_out], axis=1)
+            second_dense = lax.psum_scatter(dense, GROUP, scatter_dimension=0, tiled=True)
         grads[s] = (grad_gate_up, grad_down, grad_w_qkv, grad_w_out, small)
         input_grads[s] = grad_inputs
         grad_low = grad_inputs.astype(jnp.bfloat16)
 
-    dp, deep = lax.axis_size("dp"), lax.axis_size("expert")
+    dp, deep = lax.axis_size(GROUP), lax.axis_size(LINE)
     half, inner = held // 2, w_gate.shape[3]
     grad_gate_up, grad_down, grad_w_qkv, grad_w_out, small = grads[0]
     arrays = [
@@ -1286,17 +1260,26 @@
     arrays.append(grads[1][1].reshape(half, dp, inner // dp, D))
     for array in (grad_w_qkv, grad_w_out, small):
         arrays.append(array.reshape(dp, deep, array.shape[0] // (dp * deep), array.shape[1]))
-    for array, kind in ((second_qkv, "qkv"), (second_out, "out")):
-        lanes.append((len(arrays), None, [("expert", bits_of("expert"))], 1, (kind,)))
+    width = grad_w_qkv.shape[1]
+    for array, kind in ((second_dense[:, :width], QKV), (second_dense[:, width:], OUT)):
+        lanes.append((len(arrays), None, [(LINE, bits_of(LINE))], 1, (kind,)))
         arrays.append(array.reshape(deep, array.shape[0] // deep, array.shape[1]))
-    lanes.append((len(arrays), None, dense_lanes(0)[2][2], 1, ("small",)))
+    lanes.append((len(arrays), None, dense_lanes(0)[2][2], 1, (SMALL,)))
     small = grads[1][4]
     arrays.append(small.reshape(dp, deep, small.shape[0] // (dp * deep), small.shape[1]))
-    w_gate_grad, w_up_grad, w_down_grad, query, key, value, grad_w_out, small, stats = sum_scatter(
+    *grads, qkv, out, small, stats = sum_scatter(
         arrays, lanes, second_pre, jnp.concatenate(stats, axis=0), inner, 0
     )
+    full = jnp.float32
+    w_gate_grad, w_up_grad, w_down_grad = (
+        grad.reshape(held, *grad.shape[2:]).astype(full) for grad in grads
+    )
+    qkv = jnp.concatenate([qkv[0], qkv[1]], axis=1).astype(full)
+    grad_w_out = jnp.concatenate([out[0], out[1]], axis=1).astype(full)
+    small = small[0].astype(full) + small[1].astype(full)
+    heads, kv = H * HD, KVH * HD
     stats = lax.dynamic_index_in_dim(stats.reshape(2, 8, COLUMNS), core, 0)
-    token_total = SEQ * lax.axis_size(("section", "dp", "expert"))
+    token_total = SEQ * lax.axis_size((CORE, GROUP, LINE))
     counts, chances = stats[:, 1, :experts], stats[:, 0, :experts]
     balance = experts * (counts / (token_total * TOPK) * chances / token_total)
     out_keep = jnp.where(first, outs[0], outs[1])
@@ -1314,9 +1297,9 @@
         layer_out,
         input_grad,
         small[:, 0],
-        query,
-        key,
-        value,
+        qkv[:, :heads],
+        qkv[:, heads : heads + kv],
+        qkv[:, heads + kv :],
         grad_w_out,
         small[:, 1],
         small[:, 2 : 2 + experts],
@@ -1332,35 +1315,35 @@
         body,
         mesh=mesh,
         in_specs=(
-            P(("dp", "expert"), None),
-            P(("dp", "expert"), None),
-            P(("dp", "expert"), None),
-            P("section", ("dp", "expert"), None),
-            P("section", None),
-            P("section", None, None),
-            P("section", None, None),
-            P("section", None, None),
-            P("section", None, None),
-            P("section", None),
-            P("section", None, None),
-            P("section", "expert", None, None),
-            P("section", "expert", None, None),
-            P("section", "expert", None, None),
+            P((GROUP, LINE), None),
+            P((GROUP, LINE), None),
+            P((GROUP, LINE), None),
+            P(CORE, (GROUP, LINE), None),
+            P(CORE, None),
+            P(CORE, None, None),
+            P(CORE, None, None),
+            P(CORE, None, None),
+            P(CORE, None, None),
+            P(CORE, None),
+            P(CORE, None, None),
+            P(CORE, LINE, None, None),
+            P(CORE, LINE, None, None),
+            P(CORE, LINE, None, None),
         ),
         out_specs=(
-            P("section", ("dp", "expert"), None),
-            P("section", ("dp", "expert"), None),
-            P("section", ("dp", "expert")),
-            P("section", ("dp", "expert"), None),
-            P("section", ("dp", "expert"), None),
-            P("section", ("dp", "expert"), None),
-            P("section", ("dp", "expert"), None),
-            P("section", ("dp", "expert")),
-            P("section", ("dp", "expert"), None),
-            P("section", "expert", "dp", None),
-            P("section", "expert", "dp", None),
-            P("section", "expert", "dp", None),
-            P("section", None),
+            P(CORE, (GROUP, LINE), None),
+            P(CORE, (GROUP, LINE), None),
+            P(CORE, (GROUP, LINE)),
+            P(CORE, (GROUP, LINE), None),
+            P(CORE, (GROUP, LINE), None),
+            P(CORE, (GROUP, LINE), None),
+            P(CORE, (GROUP, LINE), None),
+            P(CORE, (GROUP, LINE)),
+            P(CORE, (GROUP, LINE), None),
+            P(CORE, LINE, GROUP, None),
+            P(CORE, LINE, GROUP, None),
+            P(CORE, LINE, GROUP, None),
+            P(CORE, None),
         ),
         check_vma=False,
     )

time: 1290 us -> 601 us (0.47)
  Pallas kernels: 1070 us -> 384 us
    pallas_call x4, Pallas kernels: 907 us -> 222 us  [expert_call(): pl.pallas_call(kernel, out_shape=shapes, in_specs=[vmem] * len(operands)...]
    unnamed x195 -> x204, local copies, waits for them, and re-layouts: 27.8 us -> 19.2 us
  transfers between devices with their start and end apart: 18 -> 17, of which waited for: 5 -> 4; matrix products, arithmetic and copies ran while one was open for 8% -> 19% of each run, Pallas kernels for 5% -> 10%
where the time goes in v9:
time: 601 us; the launch traced here: 593 us
  Pallas kernels  384 us (64%)
  matrix products  89.8 us (15%)
  local copies, waits for them, and re-layouts  44.6 us (7%)
  other arithmetic  30.7 us (5%)
  waiting for transfers between devices  24 us (4%)
  between operations  16 us (3%)
    pallas_call x4, Pallas kernels, expert_call(): pl.pallas_call(kernel, out_shape=shapes, in_specs=[vmem] * len(operands)...  222 us
    pallas_call x1, Pallas kernels, sum_scatter(): pl.pallas_call(functools.partial(sum_scatter_kernel, (plans, len(arrays),...  162 us
    dot_general x10, matrix products, turned(): jnp.einsum('tc,tq->cq', left, right, preferred_element_type=jnp.float32)  35.2 us
    ppermute x15, waiting for transfers between devices, swapped(): return lax.ppermute(array, CORE, [(0, 1), (1, 0)])  24 us
    dot_general x8, matrix products, matmul(): return jnp.dot(left_side, right_side, preferred_element_type=jnp.float32)  21.2 us
    unnamed x204, local copies, waits for them, and re-layouts  19.2 us
  transfers between devices with their start and end apart: 17, of which 4 were waited for; matrix products, arithmetic and copies ran while one was open for 19% of the time, Pallas kernels for 10%

profile of v9, /device:TPU:0, one launch (start us, length us, event | category | flops | bytes accessed | tf_op | source)
XLA Modules:
  0.0 592.7 jit_solution(6538175373898913237)
XLA Ops:
  13.5 6.4 %collective-permute-done.6 = s32[96,8]{0,1:T(8,128)S(1)} collective-permute-done((s32[96,8]{0,1:T(8,128)S(1)}, s32[96,8]{0,1:T(8,128)S(1)}, u32[]{:S(2)}, u32[]{:S(2)}) %collective-permute-start.6) | collective-permute-done | bytes 3104 | tf_op jit(solution)/shard_map/ppermute | solution.py:97
  21.0 1.1 fusion.37
  25.6 1.2 broadcast_select_fusion
  28.3 2.2 fusion.13
  30.6 4.3 fusion.4
  35.1 1.6 fusion.118
  36.6 1.6 convolution_convert_fusion.9
  38.2 16.8 %collective-permute-done.4.refs_13_ = bf16[1536,1536]{1,0:T(8,128)(2,1)} collective-permute-done((bf16[1536,1536]{1,0:T(8,128)(2,1)}, bf16[1536,1536]{1,0:T(8,128)(2,1)}, u32[]{:S(2)}, u32[]{:S(2)}) %collective-permute-start.4) | collective-permute-done | bytes 4718624 | tf_op jit(solution)/shard_map/ppermute | solution.py:97
  55.1 3.6 multiply_reduce_fusion.7
  59.8 51.6 %shard_map.237 = (bf16[96,1536]{1,0:T(8,128)(2,1)S(1)}, bf16[4,96,1536]{2,1,0:T(8,128)(2,1)S(1)}, bf16[4,96,128]{2,1,0:T(8,128)(2,1)S(1)}, f32[96,128]{1,0:T(8,1...) custom-call(bf16[96,1536]{1,0:T(8,128)(2,1)S(1)} %multiply_convert_f, ...), custom_call_target="tpu_custom_call" | custom-call | flops 49999998976 | bytes 100000000 | tf_op jit(solution)/shard_map/pallas_call | solution.py:983
  111.5 1.2 copy-done.14
  114.7 2.2 fusion.120
  117.0 4.4 fusion.121
  123.8 3.5 multiply_reduce_fusion.6
  128.4 52.5 %shard_map.238 = (bf16[96,1536]{1,0:T(8,128)(2,1)S(1)}, bf16[4,96,1536]{2,1,0:T(8,128)(2,1)S(1)}, bf16[4,96,128]{2,1,0:T(8,128)(2,1)S(1)}, f32[96,128]{1,0:T(8,1...) custom-call(bf16[96,1536]{1,0:T(8,128)(2,1)S(1)} %multiply_convert_f, ...), custom_call_target="tpu_custom_call" | custom-call | flops 49999998976 | bytes 100000000 | tf_op jit(solution)/shard_map/pallas_call | solution.py:983
  180.9 1.1 copy-done.15
  182.0 58.2 %shard_map.239 = (f32[96,1536]{1,0:T(8,128)S(1)}, f32[96,128]{1,0:T(8,128)S(1)}, bf16[2,4,96,1536]{3,2,1,0:T(8,128)(2,1)}, bf16[2,4,96,1024]{3,2,1,0:T(8,128)(2,...) custom-call(bf16[96,1536]{1,0:T(8,128)(2,1)S(1)} %constant_dynamic-slice_fusion.9.grad, ...), custom_call_target="tpu_custom_call" | custom-call | flops 49999998976 | bytes 100000000 | tf_op jit(solution)/shard_map/pallas_call | solution.py:983
  240.2 1.1 copy-done.6
  241.4 9.2 %bitcast_convert_fusion.1 = bf16[1536,2048]{1,0:T(8,128)(2,1)} fusion(bf16[2,4,96,1536]{3,2,1,0:T(8,128)(2,1)} %get-tuple-element.78, bf16[2,4,96,2048]{3,2,1,0:T(8,128)(2,1)} %get-tuple-element.79), kind=kOutput, calls=%fused_computation.3 | convolution fusion | flops 4834983936 | bytes 11796480 | tf_op jit(solution)/shard_map/tc,tq->cq/dot_general | solution.py:1128
  250.6 1.9 copy.124
  252.5 1.9 copy.115
  256.7 4.5 convolution_convert_fusion.5
  262.2 1.5 multiply_reduce_fusion.1
  266.5 1.9 fusion.31
  274.1 4.7 fusion.54
  280.6 4.5 bitcast_convert_fusion.3
  291.9 1.2 convolution_convert_fusion.1
  293.2 3.5 pad_maximum_fusion
  296.7 1.4 copy-done.11
  298.1 1.4 copy-done.13
  299.6 1.3 copy-done.17
  300.8 59.7 %shard_map.240 = (f32[96,1536]{1,0:T(8,128)S(1)}, f32[96,128]{1,0:T(8,128)S(1)}, bf16[2,4,96,1536]{3,2,1,0:T(8,128)(2,1)}, bf16[2,4,96,1024]{3,2,1,0:T(8,128)(2,...) custom-call(bf16[96,1536]{1,0:T(8,128)(2,1)S(1)} %get-tuple-element.87.grad, ...), custom_call_target="tpu_custom_call" | custom-call | flops 49999998976 | bytes 100000000 | tf_op jit(solution)/shard_map/pallas_call | solution.py:983
  360.6 1.1 copy-done.8
  362.0 9.4 %bitcast_convert_fusion = bf16[1536,2048]{1,0:T(8,128)(2,1)} fusion(bf16[2,4,96,1536]{3,2,1,0:T(8,128)(2,1)} %get-tuple-element.102, bf16[2,4,96,2048]{3,2,1,0:T(8,128)(2,1)} %get-tuple-element.103), kind=kOutput, calls=%fused_computation.2 | convolution fusion | flops 4834983936 | bytes 11796480 | tf_op jit(solution)/shard_map/tc,tq->cq/dot_general | solution.py:1128
  372.3 3.9 convolution_convert_fusion.4
  376.5 1.8 multiply_reduce_fusion
  381.2 1.8 fusion.32
  387.1 4.3 fusion.45
  391.5 1.2 fusion.36
  393.1 4.2 bitcast_convert_fusion.2
  398.7 1.1 maximum_select_fusion
  402.8 2.2 convolution_convert_fusion.2
  405.0 3.2 convolution_convert_fusion
  408.3 2.2 slice.210
  410.5 1.9 slice.211
  412.4 161.8 %shard_map.241 = (bf16[2,2,384,512]{3,2,1,0:T(8,128)(2,1)}, bf16[2,2,384,512]{3,2,1,0:T(8,128)(2,1)}, bf16[2,2,128,1536]{3,2,1,0:T(8,128)(2,1)}, bf16[2,96,1280]...) custom-call(bf16[4,384,2048]{2,1,0:T(8,128)(2,1)} %bitcast.282, ...), custom_call_target="tpu_custom_call" | custom-call | tf_op jit(solution)/shard_map/pallas_call | solution.py:436
  577.1 2.1 bitcast_convert_fusion.4
  581.2 3.6 bitcast_convert_fusion.5
  (344 shorter events, 57.6 us)
Async XLA Ops:
  7.2 6.3 %copy-start = (s32[2,96]{1,0:T(2,128)S(1)}, s32[2,96]{1,0:T(2,128)}, u32[]{:S(2)}) copy-start(s32[2,96]{1,0:T(2,128)} %param.16) | copy-start | bytes 2308
  7.2 18.2 %copy-start.21 = (bf16[192,1536]{1,0:T(8,128)(2,1)S(1)}, bf16[192,1536]{1,0:T(8,128)(2,1)}, u32[]{:S(2)}) copy-start(bf16[192,1536]{1,0:T(8,128)(2,1)} %param.14) | copy-start | bytes 1769476
  7.2 364.2 %reduce-scatter.3.cloned.1.call-start = ((), (), s32[]{:S(2)}) async-start(), calls=%async_computation.2 | async-start | bytes 7864320 | tf_op jit(solution)/shard_map/reduce_scatter | solution.py:1199
  7.3 13.5 %collective-permute-start.2 = (bf16[1536,512]{1,0:T(8,128)(2,1)}, bf16[1536,512]{1,0:T(8,128)(2,1)}, u32[]{:S(2)}, u32[]{:S(2)}) collective-permute-start(bf16[1536,512]{1,0:T(8,128)(2,1)} %bitcast.362), channel_id=1, source_target_pairs={{0,16},{16,0},{1,17},{17,1},{2,18},{18,2},{3,19},{19,3},{4,20},{20... | collective-permute-start | bytes 4718600 | tf_op jit(solution)/shard_map/ppermute | solution.py:97
  7.8 14.4 %collective-permute-start.1 = (bf16[1536,512]{1,0:T(8,128)(2,1)}, bf16[1536,512]{1,0:T(8,128)(2,1)}, u32[]{:S(2)}, u32[]{:S(2)}) collective-permute-start(bf16[1536,512]{1,0:T(8,128)(2,1)} %bitcast.359), channel_id=1, source_target_pairs={{0,16},{16,0},{1,17},{17,1},{2,18},{18,2},{3,19},{19,3},{4,20},{20... | collective-permute-start | bytes 4718600 | tf_op jit(solution)/shard_map/ppermute | solution.py:97
  7.9 22.7 %collective-permute-start.3 = (bf16[1536,1536]{1,0:T(8,128)(2,1)}, bf16[1536,1536]{1,0:T(8,128)(2,1)}, u32[]{:S(2)}, u32[]{:S(2)}) collective-permute-start(bf16[1536,1536]{1,0:T(8,128)(2,1)} %bitcast.356), channel_id=1, source_target_pairs={{0,16},{16,0},{1,17},{17,1},{2,18},{18,2},{3,19},{19,3},{4,20},{20... | collective-permute-start | bytes 14155784 | tf_op jit(solution)/shard_map/ppermute | solution.py:97
  9.0 3.3 collective-permute-start
  9.9 3.2 collective-permute-start.5
  12.3 7.5 %collective-permute-start.6 = (s32[96,8]{0,1:T(8,128)S(1)}, s32[96,8]{0,1:T(8,128)S(1)}, u32[]{:S(2)}, u32[]{:S(2)}) collective-permute-start(s32[96,8]{0,1:T(8,128)S(1)} %dynamic-slice_bitcast_fusion), channel_id=1, source_target_pairs={{0,16},{16,0},{1,17},{17,1},{2,18},{18,2},{3,19},{19,3},{4,20},{20... | collective-permute-start | bytes 9224 | tf_op jit(solution)/shard_map/ppermute | solution.py:97
  13.1 7.3 %collective-permute-start.7 = (bf16[1536,16]{1,0:T(8,128)(2,1)S(1)}, bf16[1536,16]{1,0:T(8,128)(2,1)S(1)}, u32[]{:S(2)}, u32[]{:S(2)}) collective-permute-start(bf16[1536,16]{1,0:T(8,128)(2,1)S(1)} %bitcast.305), channel_id=1, source_target_pairs={{0,16},{16,0},{1,17},{17,1},{2,18},{18,2},{3,19},{19,3},{4,20},{20... | collective-permute-start | bytes 147464 | tf_op jit(solution)/shard_map/ppermute | solution.py:97
  19.8 39.5 %collective-permute-start.10 = (bf16[4,512,1536]{2,1,0:T(8,128)(2,1)}, bf16[4,512,1536]{2,1,0:T(8,128)(2,1)}, u32[]{:S(2)}, u32[]{:S(2)}) collective-permute-start(bf16[4,512,1536]{2,1,0:T(8,128)(2,1)} %bitcast.351), channel_id=1, source_target_pairs={{0,16},{16,0},{1,17},{17,1},{2,18},{18,2},{3,19},{19,3},{4,20},{20... | collective-permute-start | bytes 18874376 | tf_op jit(solution)/shard_map/ppermute | solution.py:97
  20.4 5.0 copy-start.51
  20.4 39.0 %collective-permute-start.8 = (bf16[4,1536,512]{2,1,0:T(8,128)(2,1)}, bf16[4,1536,512]{2,1,0:T(8,128)(2,1)}, u32[]{:S(2)}, u32[]{:S(2)}) collective-permute-start(bf16[4,1536,512]{2,1,0:T(8,128)(2,1)} %bitcast.341), channel_id=1, source_target_pairs={{0,16},{16,0},{1,17},{17,1},{2,18},{18,2},{3,19},{19,3},{4,20},{20... | collective-permute-start | bytes 18874376 | tf_op jit(solution)/shard_map/ppermute | solution.py:97
  20.8 38.6 %collective-permute-start.9 = (bf16[4,1536,512]{2,1,0:T(8,128)(2,1)}, bf16[4,1536,512]{2,1,0:T(8,128)(2,1)}, u32[]{:S(2)}, u32[]{:S(2)}) collective-permute-start(bf16[4,1536,512]{2,1,0:T(8,128)(2,1)} %bitcast.346), channel_id=1, source_target_pairs={{0,16},{16,0},{1,17},{17,1},{2,18},{18,2},{3,19},{19,3},{4,20},{20... | collective-permute-start | bytes 18874376 | tf_op jit(solution)/shard_map/ppermute | solution.py:97
  22.1 32.9 %collective-permute-start.4 = (bf16[1536,1536]{1,0:T(8,128)(2,1)}, bf16[1536,1536]{1,0:T(8,128)(2,1)}, u32[]{:S(2)}, u32[]{:S(2)}) collective-permute-start(bf16[1536,1536]{1,0:T(8,128)(2,1)} %bitcast.283), channel_id=1, source_target_pairs={{0,16},{16,0},{1,17},{17,1},{2,18},{18,2},{3,19},{19,3},{4,20},{20... | collective-permute-start | bytes 14155784 | tf_op jit(solution)/shard_map/ppermute | solution.py:97
  25.3 89.2 %copy-start.75 = (f32[1536]{0:T(1024)}, f32[1536]{0:T(1024)S(1)}, u32[]{:S(2)}) copy-start(f32[1536]{0:T(1024)S(1)} %get-tuple-element.219) | copy-start | bytes 18436
  25.3 33.9 %copy-start.64 = (f32[1536]{0:T(1024)}, f32[1536]{0:T(1024)S(1)}, u32[]{:S(2)}) copy-start(f32[1536]{0:T(1024)S(1)} %get-tuple-element.218) | copy-start | bytes 18436
  25.4 102.5 %copy-start.66 = (f32[1536]{0:T(1024)}, f32[1536]{0:T(1024)S(1)}, u32[]{:S(2)}) copy-start(f32[1536]{0:T(1024)S(1)} %get-tuple-element.217) | copy-start | bytes 18436
  25.5 5.0 copy-start.35
  28.2 8.4 %copy-start.69 = (bf16[96,512]{0,1:T(8,128)(2,1)}, bf16[96,512]{0,1:T(8,128)(2,1)S(1)}, u32[]{:S(2)}) copy-start(bf16[96,512]{0,1:T(8,128)(2,1)S(1)} %copy.98) | copy-start | bytes 294916
  30.5 4.5 copy-start.54
  30.5 4.5 copy-start.56
  38.2 20.4 %copy-start.28 = (bf16[8,64,3,96]{3,1,2,0:T(8,128)(2,1)}, bf16[8,64,3,96]{3,1,2,0:T(8,128)(2,1)S(1)}, u32[]{:S(2)}) copy-start(bf16[8,64,3,96]{3,1,2,0:T(8,128)(2,1)S(1)} %convolution_convert_fusion.9) | copy-start | bytes 884740
  58.6 52.8 %copy-start.2 = (f32[96,1536]{1,0:T(8,128)}, f32[96,1536]{1,0:T(8,128)S(1)}, u32[]{:S(2)}) copy-start(f32[96,1536]{1,0:T(8,128)S(1)} %get-tuple-element.234.hidden) | copy-start | bytes 1769476
  59.4 52.1 %copy-start.4 = (bf16[96,1536]{1,0:T(8,128)(2,1)}, bf16[96,1536]{1,0:T(8,128)(2,1)S(1)}, u32[]{:S(2)}) copy-start(bf16[96,1536]{1,0:T(8,128)(2,1)S(1)} %multiply_convert_fusion.3.x) | copy-start | bytes 884740
  117.0 5.1 copy-start.58
  117.0 5.1 copy-start.60
  117.0 4.6 copy-start.19
  250.6 157.7 %reduce-scatter.5.cloned.1.call-start = ((), (), s32[]{:S(2)}) async-start(), calls=%async_computation.3 | async-start | bytes 7864320 | tf_op jit(solution)/shard_map/reduce_scatter | solution.py:1247
  256.7 5.5 copy-start.39
  256.7 5.5 copy-start.72
  256.7 5.5 copy-start.81
  272.0 15.9 %collective-permute-start.12 = (bf16[96,5120]{1,0:T(8,128)(2,1)}, bf16[96,5120]{1,0:T(8,128)(2,1)}, u32[]{:S(2)}, u32[]{:S(2)}) collective-permute-start(bf16[96,5120]{1,0:T(8,128)(2,1)} %pad_maximum_fusion.1), channel_id=1, source_target_pairs={{0,16},{16,0},{1,17},{17,1},{2,18},{18,2},{3,19},{19,3},{4,20},{20... | collective-permute-start | bytes 2949128 | tf_op jit(solution)/shard_map/ppermute | solution.py:97
  274.1 4.7 copy-start.27
  274.1 4.7 copy-start.94
  274.1 5.8 copy-start.98
  280.0 7.1 %collective-permute-start.11 = (bf16[96,1536]{1,0:T(8,128)(2,1)}, bf16[96,1536]{1,0:T(8,128)(2,1)S(1)}, u32[]{:S(2)}, u32[]{:S(2)}) collective-permute-start(bf16[96,1536]{1,0:T(8,128)(2,1)} %get-tuple-element.189), channel_id=1, source_target_pairs={{0,16},{16,0},{1,17},{17,1},{2,18},{18,2},{3,19},{19,3},{4,20},{20... | collective-permute-start | bytes 884744 | tf_op jit(solution)/shard_map/ppermute | solution.py:97
  280.6 4.5 copy-start.82
  361.9 9.5 %copy-start.3 = (f32[96,1536]{1,0:T(8,128)S(1)}, f32[96,1536]{1,0:T(8,128)}, u32[]{:S(2)}) copy-start(f32[96,1536]{1,0:T(8,128)} %copy-done.2) | copy-start | bytes 1769476
  361.9 9.4 %copy-start.24 = (bf16[1536,16]{1,0:T(8,128)(2,1)S(1)}, bf16[1536,16]{1,0:T(8,128)(2,1)}, u32[]{:S(2)}) copy-start(bf16[1536,16]{1,0:T(8,128)(2,1)} %copy-done.23) | copy-start | bytes 147460
  361.9 9.4 %copy-start.65 = (f32[1536]{0:T(1024)S(1)}, f32[1536]{0:T(1024)}, u32[]{:S(2)}) copy-start(f32[1536]{0:T(1024)} %copy-done.64) | copy-start | bytes 18436
  362.0 9.4 %copy-start.88 = (f32[96]{0:T(128)S(1)}, f32[96]{0:T(128)}, u32[]{:S(2)}) copy-start(f32[96]{0:T(128)} %copy-done.87) | copy-start | bytes 1156
  385.0 14.8 %collective-permute-start.14 = (bf16[96,5120]{1,0:T(8,128)(2,1)}, bf16[96,5120]{1,0:T(8,128)(2,1)}, u32[]{:S(2)}, u32[]{:S(2)}) collective-permute-start(bf16[96,5120]{1,0:T(8,128)(2,1)} %pad_maximum_fusion.2), channel_id=1, source_target_pairs={{0,16},{16,0},{1,17},{17,1},{2,18},{18,2},{3,19},{19,3},{4,20},{20... | collective-permute-start | bytes 2949128 | tf_op jit(solution)/shard_map/ppermute | solution.py:97
  387.1 4.4 copy-start.96
  387.1 5.7 copy-start.99
  392.6 6.1 %collective-permute-start.13 = (f32[96,1536]{1,0:T(8,128)}, f32[96,1536]{1,0:T(8,128)S(1)}, u32[]{:S(2)}, u32[]{:S(2)}) collective-permute-start(f32[96,1536]{1,0:T(8,128)} %get-tuple-element.173), channel_id=1, source_target_pairs={{0,16},{16,0},{1,17},{17,1},{2,18},{18,2},{3,19},{19,3},{4,20},{20... | collective-permute-start | bytes 1769480 | tf_op jit(solution)/shard_map/ppermute | solution.py:97
  393.1 4.3 copy-start.5
  581.2 4.4 copy-start.1
  (69 other events, 125.6 us)
Sparse Core Ops, SparseCore 0:
  250.7 71.6 reduce-scatter.2
  325.4 70.2 reduce-scatter.4

commit v10 on v9

--- a/solution.py
+++ b/solution.py
@@ -114,9 +114,9 @@
 def sum_scatter_kernel(plan, *refs):
     lanes, ins, copies = plan
     sources = refs[:ins]
-    second_pre, stats_in = refs[ins : ins + 2]
-    stage, stats = refs[ins + 2 : ins + 8], refs[ins + 8]
-    scratch = list(refs[ins + 9 :])
+    second_pre, second_down, stats_in = refs[ins : ins + 3]
+    stage, stats = refs[ins + 3 : ins + 9], refs[ins + 9]
+    scratch = list(refs[ins + 10 :])
     send_sem, recv_sem, local_sem, stats_got, stats_send, stats_recv, core_send, core_recv = (
         scratch[-8:]
     )
@@ -206,9 +206,13 @@
 
     inner = stage[GATE].shape[3]
     wholes = []
-    for number in range(second_pre.shape[1] // inner):
-        kind, j = divmod(number, stage[GATE].shape[1])
-        source = second_pre.at[:, pl.ds(number * inner, inner)]
+    half = stage[GATE].shape[1]
+    for number in range(3 * half):
+        kind, j = divmod(number, half)
+        if kind == DOWN:
+            source = second_down.at[j]
+        else:
+            source = second_pre.at[:, pl.ds(number * inner, inner)]
         spot, copy = to_stage(len(lanes) + number, source, kind, j)
         wholes.append((copy, pltpu.make_async_copy(source, spot, core_send.at[len(lanes) + number])))
     for copy, here in wholes:
@@ -232,11 +236,13 @@
             source = source.at[prefix]
 
         def part(at, source=source, prefix=prefix):
-            if isinstance(prefix, tuple):
-                return source.at[at, :, pl.ds(*prefix)]
-            if prefix == INNER:
-                return source.at[:, at]
-            return source.at[at]
+            if isinstance(prefix, int):
+                return source.at[at]
+            inner, columns = prefix
+            where = (slice(None), at) if inner else (at,)
+            if columns is not None:
+                where += (slice(None),) * (len(source.shape) - len(where) - 1) + (pl.ds(*columns),)
+            return source.at[where]
 
         axis, bits = lane.phases[0]
         total, arrived = buffers[0], buffers[1:]
@@ -258,11 +264,16 @@
         copy = pltpu.make_async_copy(here, total.at[slot], local_sem.at[at])
         copy.start()
         locals_[number, slot] = copy
-    longest = max(sum(len(bits) for _, bits in lane.phases) for lane in lanes)
-    for step in range(1, longest + 1):
-        if step == 2:
+    short = [item for item in enumerate(lanes) if len(item[1].phases) == 1 and item[1].rows]
+    long = [item for item in enumerate(lanes) if item not in short]
+    turns = [(1, long), (1, short)]
+    count = max(sum(len(bits) for _, bits in lane.phases) for lane in lanes)
+    for step in range(2, count + 1):
+        turns += [(2 * step - 2, long), (2 * step - 1, long), (step, short)]
+    for at, (step, group) in enumerate(turns):
+        if at == 2:
             next(summing)
-        for number, lane in enumerate(lanes):
+        for number, lane in group:
             state = lane.state
             sizes = [len(bits) for _, bits in lane.phases]
             if step > sum(sizes):
@@ -375,17 +386,18 @@
         copy.wait_send()
 
 
-def sum_scatter(arrays, lanes, second_pre, stats, inner, collective):
+def sum_scatter(arrays, lanes, second_pre, second_down, stats, inner, collective):
     plans, scratch, shapes, copies, locals_ = [], [], [], 0, 0
     sizes = {}
     for source, prefix, phases, layer, target in lanes:
         shape = arrays[source].shape
         if isinstance(prefix, int):
             shape = shape[1:]
-        elif prefix == INNER:
-            shape = (shape[1], shape[0], *shape[2:])
-        elif prefix is not None:
-            shape = (*shape[:-1], prefix[1])
+        else:
+            if prefix[0]:
+                shape = (shape[1], shape[0], *shape[2:])
+            if prefix[1] is not None:
+                shape = (*shape[:-1], prefix[1][1])
         buffers = [(shape[0] // 2, *shape[1:])]
         for step in range(1, len(phases[0][1]) + 1):
             buffers.append((shape[0] >> step, *shape[1:]))
@@ -401,11 +413,14 @@
                 prefix=prefix,
                 phases=phases,
                 buffers=buffers,
+                rows=phases[0][0] == GROUP,
                 layer=layer,
                 target=target,
             )
         )
-        sizes.setdefault(target[0], shape[-2:])
+        width = sizes.get(target[0], (0, 0))[1] if len(target) > 2 else 0
+        if layer == 0:
+            sizes[target[0]] = (shape[-2], width + shape[-1])
         scratch += [pltpu.VMEM(buffer, jnp.bfloat16) for buffer in buffers]
     half = second_pre.shape[1] // (2 * inner)
     experts_shape = (2, half, second_pre.shape[0], inner)
@@ -430,20 +445,20 @@
         pltpu.VMEM((hops, *stats.shape), jnp.float32),
         pltpu.SemaphoreType.DMA((hops,)),
         pltpu.SemaphoreType.DMA((hops,)),
-        pltpu.SemaphoreType.DMA((len(lanes) + 2 * half,)),
-        pltpu.SemaphoreType.DMA((len(lanes) + 2 * half,)),
+        pltpu.SemaphoreType.DMA((len(lanes) + 3 * half,)),
+        pltpu.SemaphoreType.DMA((len(lanes) + 3 * half,)),
     ]
     return pl.pallas_call(
         functools.partial(sum_scatter_kernel, (plans, len(arrays), copies)),
         out_shape=shapes,
-        in_specs=[pl.BlockSpec(memory_space=pl.ANY)] * (len(arrays) + 1)
+        in_specs=[pl.BlockSpec(memory_space=pl.ANY)] * (len(arrays) + 2)
         + [pl.BlockSpec(memory_space=pltpu.VMEM)],
         out_specs=[pl.BlockSpec(memory_space=pltpu.VMEM)] * len(shapes),
         scratch_shapes=scratch,
         compiler_params=pltpu.CompilerParams(
             collective_id=collective, has_side_effects=True, vmem_limit_bytes=60 * 2**20
         ),
-    )(*arrays, second_pre, stats)
+    )(*arrays, second_pre, second_down, stats)
 
 
 def bits_of(axis):
@@ -453,7 +468,7 @@
 def expert_lanes(first, inner):
     up, down = [(GROUP, bits_of(GROUP))], [(GROUP, bits_of(GROUP)[::-1])]
     return [
-        (first, ((2 * kind + j) * inner, inner), (up, down)[kind], 0, (kind, j))
+        (first, (False, ((2 * kind + j) * inner, inner)), (up, down)[kind], 0, (kind, j))
         for j in range(2)
         for kind in (GATE, UP)
     ]
@@ -464,13 +479,33 @@
     return [(first, 0, up, layer, (DOWN, 0)), (first, 1, down, layer, (DOWN, 1))]
 
 
-def dense_lanes(first):
+def dense_lanes(first, width):
     up, down, deep = bits_of(GROUP), bits_of(GROUP)[::-1], bits_of(LINE)
+    near = width // 4 // COLUMNS * COLUMNS
+    away = width - near
     return [
-        (first, INNER, [(LINE, deep), (GROUP, up)], 0, (QKV,)),
-        (first + 1, None, [(GROUP, down), (LINE, deep)], 0, (OUT,)),
-        (first + 2, None, [(GROUP, up), (LINE, deep)], 0, (SMALL,)),
+        (
+            first,
+            (True, (0, away)),
+            [(LINE, deep), (GROUP, up)],
+            0,
+            (QKV, slice(None), pl.ds(0, away)),
+        ),
+        (
+            first,
+            (False, (away, near)),
+            [(GROUP, up), (LINE, deep)],
+            0,
+            (QKV, slice(None), pl.ds(away, near)),
+        ),
+        (first + 1, (False, None), [(GROUP, down), (LINE, deep)], 0, (OUT,)),
+        small_lane(first + 2, 0),
     ]
+
+
+def small_lane(first, layer):
+    phases = [(GROUP, bits_of(GROUP)), (LINE, bits_of(LINE))]
+    return (first, (False, None), phases, layer, (SMALL,))
 
 
 def attention_forward(inputs, weights, segment_row):
@@ -771,15 +806,6 @@
     def place_out(i):
         return pltpu.make_async_copy(passing[i], placed[i], place_sem.at[1, i])
 
-    for i in range(4):
-        @pl.when(here)
-        def _():
-            place_copy(own_dense, i).start()
-
-        @pl.when(jnp.logical_not(here))
-        def _():
-            place_copy(other_dense, i).start()
-
     logits = jnp.dot(x[...], router[...], preferred_element_type=jnp.float32)
     chosen = mask[...] > 0
     highest = jnp.max(jnp.where(chosen, logits, MASKED), axis=1, keepdims=True)
@@ -800,6 +826,15 @@
     start(2)
     rows[z] = x[...]
     wait_weights()
+    for i in range(4):
+        @pl.when(here)
+        def _():
+            place_copy(own_dense, i).start()
+
+        @pl.when(jnp.logical_not(here))
+        def _():
+            place_copy(other_dense, i).start()
+
     run()
     for i in range(4):
         place_copy(own_dense, i).wait()
@@ -819,6 +854,12 @@
 
 def experts_backward_kernel(layer, grad, gates, gate_keep, up_keep, *refs):
     own, other, saved_rows, saved_gated, refs = refs[:3], refs[3:6], refs[6], refs[7], refs[8:]
+    carried = layer == 0
+    if carried:
+        extra, refs = refs[0], refs[1:]
+        extra_sum, refs = refs[6], refs[:6] + refs[7:]
+        landed, extra_send, extra_recv = refs[-3:]
+        refs = refs[:-3]
     out, out_gates, rows_both, gated_both, grad_both, pre_both = refs[:6]
     w_gate, w_up, w_down, sums, sum_gates, returned, returned_gates, away, dots = refs[6:15]
     weight_sem, core_send, core_recv, core_local, *sems = refs[15:]
@@ -860,6 +901,19 @@
             pltpu.make_async_copy(
                 saved_gated.at[:, :, columns(core)], gated_both.at[core], core_local.at[1]
             ),
+        )
+
+    me, count = lax.axis_index(GROUP), lax.axis_size(GROUP)
+    peers = [lax.rem(me + k, count) for k in range(1, count)] if carried else []
+
+    def extra_copy(k, peer, slot):
+        return pltpu.make_async_remote_copy(
+            src_ref=extra.at[:, peer],
+            dst_ref=landed.at[slot],
+            send_sem=extra_send.at[k],
+            recv_sem=extra_recv.at[slot],
+            device_id={GROUP: peer},
+            device_id_type=MESH,
         )
 
     def compute(block, sent):
@@ -940,9 +994,14 @@
         compute,
         z,
         n,
-        [{CORE: 1 - core}],
+        [{CORE: 1 - core}] + [{GROUP: peer} for peer in peers],
     )
     start(0)
+    for k, peer in enumerate(peers):
+        extra_copy(k, peer, me).start()
+    if carried:
+        mine = pltpu.make_async_copy(extra.at[:, me], landed.at[me], extra_send.at[len(peers)])
+        mine.start()
     wait_weights = fetch_weights(layer, own, other, (w_gate, w_up, w_down), weight_sem)
     for copy in whole_copies() + local_copies():
         copy.start()
@@ -957,8 +1016,27 @@
         else:
             out[:, p * width : (p + 1) * width] += value
 
+    if carried:
+        mine.wait()
+        for k, peer in enumerate(peers):
+            extra_copy(k, peer, peer).wait_recv()
+        half, rows_each = extra_sum.shape[:2]
+        step = 16 if rows_each % 16 == 0 else rows_each
+
+        def add_up(i, carry):
+            at = pl.ds(pl.multiple_of(i * step, step), step)
+            for j in range(half):
+                value = landed[0, j, at].astype(jnp.float32)
+                for k in range(1, count):
+                    value += landed[k, j, at].astype(jnp.float32)
+                extra_sum[j, at] = value.astype(jnp.bfloat16)
+            return carry
+
+        lax.fori_loop(0, rows_each // step, add_up, 0)
     collect(add)
     finish()
+    for k, peer in enumerate(peers):
+        extra_copy(k, peer, me).wait_send()
     for copy in local_copies():
         copy.wait()
     for copy in whole_copies():
@@ -1037,7 +1115,7 @@
     )
 
 
-def experts_backward(layer, grad_low, gates, gate_keep, up_keep, rows, gated, own, other):
+def experts_backward(layer, grad_low, gates, gate_keep, up_keep, rows, gated, own, other, extra):
     held, n, length, inner = gate_keep.shape
     width = grad_low.shape[1]
     low, full = jnp.bfloat16, jnp.float32
@@ -1061,13 +1139,21 @@
         pltpu.SemaphoreType.DMA((2 + 2 * n,)),
         pltpu.SemaphoreType.DMA((2,)),
     ] + exchange_scratch(n, 1, PARTS + 1)
+    if layer == 0:
+        half, count, *block = extra.shape
+        shapes.append(jax.ShapeDtypeStruct((half, *block), low))
+        scratch += [
+            pltpu.VMEM((count, half, *block), low),
+            pltpu.SemaphoreType.DMA((count,)),
+            pltpu.SemaphoreType.DMA((count,)),
+        ]
     kernel = functools.partial(experts_backward_kernel, layer)
     return expert_call(
         kernel,
         (grad_low, gates, gate_keep, up_keep),
         own,
         other,
-        (rows, gated),
+        (rows, gated) if extra is None else (rows, gated, extra),
         shapes,
         scratch,
         3 + layer,
@@ -1154,6 +1240,7 @@
         inputs = inputs_low.astype(jnp.float32)
         state = attention_forward(inputs, weights[s], segment_row)
         hidden, normed_two = state[7], state[9]
+        both_cores = [jnp.concatenate([a, swapped(a)]) for a in (state[1], state[6])]
         router = jnp.pad(weights[s][6], ((0, 0), (0, COLUMNS - experts)))
         inputs_low, *expert_state, stat, query, key, value, out = experts_forward(
             s,
@@ -1170,16 +1257,17 @@
         weights[1 - s][1:5] = [query, key, value, out]
         outs.append(inputs_low)
         stats.append(stat)
-        saved.append((inputs, state, expert_state))
-
+        saved.append((inputs, state, expert_state, both_cores))
+
+    dp, deep = lax.axis_size(GROUP), lax.axis_size(LINE)
     grads = [None, None]
     input_grads = [None, None]
     for s in (1, 0):
-        inputs, state, expert_state = saved[s]
+        inputs, state, expert_state, both_cores = saved[s]
         (inverse_one, normed_one, _, _, _, _, attended, hidden, inverse_two, normed_two) = state
         rows_all, gates_all, gates, gate_keep, up_keep, gated = expert_state
         gain_moe, w_router = weights[s][5], weights[s][6]
-        grad_sum, grad_gates, rows_both, gated_both, grad_both, pre_both = experts_backward(
+        grad_sum, grad_gates, rows_both, gated_both, grad_both, pre_both, *sums = experts_backward(
             s,
             grad_low,
             gates_all,
@@ -1189,7 +1277,10 @@
             gated,
             own_experts,
             other_experts,
-        )
+            None if s == 1 else grads[1][1].reshape(held // 2, dp, -1, D),
+        )
+        if s == 0:
+            (second_down,) = sums
         inner = w_gate.shape[3]
         grad_gate_up = turned(
             rows_both.reshape(-1, D), pre_both.reshape(-1, held * inner)
@@ -1224,15 +1315,11 @@
             )
         qkv_keep, qkv_send = halves(grad_qkv)
         branch_keep, branch_send = halves(grad_branch)
-        packed = swapped(jnp.concatenate([normed_one, attended, qkv_send, branch_send], axis=1))
-        normed_got, attended_got = packed[:, :D], packed[:, D : 2 * D]
-        qkv_got = packed[:, 2 * D : 2 * D + qkv_send.shape[1]]
-        branch_got = packed[:, 2 * D + qkv_send.shape[1] :]
         grad_w_qkv = turned(
-            jnp.concatenate([normed_one, normed_got]), jnp.concatenate([qkv_keep, qkv_got])
+            both_cores[0], jnp.concatenate([qkv_keep, swapped(qkv_send)])
         ).astype(jnp.bfloat16)
         grad_w_out = turned(
-            jnp.concatenate([attended, attended_got]), jnp.concatenate([branch_keep, branch_got])
+            both_cores[1], jnp.concatenate([branch_keep, swapped(branch_send)])
         ).astype(jnp.bfloat16)
         grad_w_router = turned(normed_two, grad_logits)
         small = jnp.concatenate(
@@ -1256,19 +1343,22 @@
         grad_gate_up.reshape(dp, D // dp, held * inner),
         grad_down.reshape(half, dp, inner // dp, D),
     ]
-    lanes = expert_lanes(0, inner) + down_lanes(1, 0) + down_lanes(2, 1) + dense_lanes(3)
-    arrays.append(grads[1][1].reshape(half, dp, inner // dp, D))
+    lanes = dense_lanes(2, grad_w_qkv.shape[1])
     for array in (grad_w_qkv, grad_w_out, small):
         arrays.append(array.reshape(dp, deep, array.shape[0] // (dp * deep), array.shape[1]))
     width = grad_w_qkv.shape[1]
-    for array, kind in ((second_dense[:, :width], QKV), (second_dense[:, width:], OUT)):
-        lanes.append((len(arrays), None, [(LINE, bits_of(LINE))], 1, (kind,)))
-        arrays.append(array.reshape(deep, array.shape[0] // deep, array.shape[1]))
-    lanes.append((len(arrays), None, dense_lanes(0)[2][2], 1, (SMALL,)))
+    whole = second_dense.shape[1]
+    for columns, kind in (((0, width), QKV), ((width, whole - width), OUT)):
+        start, size = columns
+        target = (kind, slice(None), pl.ds(start - (start // width) * width, size))
+        lanes.append((len(arrays), (False, columns), [(LINE, bits_of(LINE))], 1, target))
+    arrays.append(second_dense.reshape(deep, second_dense.shape[0] // deep, whole))
+    lanes.append(small_lane(len(arrays), 1))
+    lanes += expert_lanes(0, inner) + down_lanes(1, 0)
     small = grads[1][4]
     arrays.append(small.reshape(dp, deep, small.shape[0] // (dp * deep), small.shape[1]))
     *grads, qkv, out, small, stats = sum_scatter(
-        arrays, lanes, second_pre, jnp.concatenate(stats, axis=0), inner, 0
+        arrays, lanes, second_pre, second_down, jnp.concatenate(stats, axis=0), inner, 0
     )
     full = jnp.float32
     w_gate_grad, w_up_grad, w_down_grad = (

time: 601 us -> 585 us (0.973)
  Pallas kernels: 384 us -> 358 us
  waiting for transfers between devices: 24 us -> 48.4 us
  local copies, waits for them, and re-layouts: 44.6 us -> 30.2 us
    reduce_scatter x1, waiting for transfers between devices: 0.01 us -> 27.1 us  [body(): lax.psum_scatter(dense, GROUP, scatter_dimension=0, tiled=True)]
    pallas_call x1, Pallas kernels: 162 us -> 136 us  [sum_scatter(): pl.pallas_call(functools.partial(sum_scatter_kernel, (plans, len(arrays),...]
    slice x8 -> x0, local copies, waits for them, and re-layouts: 10.1 us -> none  [the longest x1 2.21 us: body(): second_dense[:, :width]]
    ppermute x15 -> x21, waiting for transfers between devices: 24 us -> 21.3 us  [swapped(): return lax.ppermute(array, CORE, [(0, 1), (1, 0)])]
    unnamed x204 -> x194, local copies, waits for them, and re-layouts: 19.2 us -> 20.8 us
  transfers between devices with their start and end apart: 17 -> 23, of which waited for: 4 -> 5; matrix products, arithmetic and copies ran while one was open for 19% -> 18% of each run, Pallas kernels for 10% -> 34%
where the time goes in v10:
time: 585 us; the launch traced here: 577 us
  Pallas kernels  358 us (61%)
  matrix products  86.4 us (15%)
  waiting for transfers between devices  48.4 us (8%)
  other arithmetic  31.7 us (5%)
  local copies, waits for them, and re-layouts  30.2 us (5%)
  between operations  16 us (3%)
  starting transfers between devices  6.5 us (1%)
    pallas_call x4, Pallas kernels, expert_call(): pl.pallas_call(kernel, out_shape=shapes, in_specs=[vmem] * len(operands)...  221 us
    pallas_call x1, Pallas kernels, sum_scatter(): pl.pallas_call(functools.partial(sum_scatter_kernel, (plans, len(arrays),...  136 us
    dot_general x10, matrix products, turned(): jnp.einsum('tc,tq->cq', left, right, preferred_element_type=jnp.float32)  39.3 us
    reduce_scatter x1, waiting for transfers between devices, body(): lax.psum_scatter(dense, GROUP, scatter_dimension=0, tiled=True)  27.1 us
    dot_general x8, matrix products, matmul(): return jnp.dot(left_side, right_side, preferred_element_type=jnp.float32)  22.3 us
    ppermute x21, waiting for transfers between devices, swapped(): return lax.ppermute(array, CORE, [(0, 1), (1, 0)])  21.3 us
    unnamed x194, local copies, waits for them, and re-layouts  20.8 us
  transfers between devices with their start and end apart: 23, of which 5 were waited for; matrix products, arithmetic and copies ran while one was open for 18% of the time, Pallas kernels for 34%

profile of v10, /device:TPU:0, one launch (start us, length us, event | category | flops | bytes accessed | tf_op | source)
XLA Modules:
  0.0 576.9 jit_solution(2286311539137465096)
XLA Ops:
  13.5 6.4 %collective-permute-done.6 = s32[96,8]{0,1:T(8,128)S(1)} collective-permute-done((s32[96,8]{0,1:T(8,128)S(1)}, s32[96,8]{0,1:T(8,128)S(1)}, u32[]{:S(2)}, u32[]{:S(2)}) %collective-permute-start.6) | collective-permute-done | bytes 3104 | tf_op jit(solution)/shard_map/ppermute | solution.py:97
  21.6 1.1 fusion.49
  28.5 1.4 fusion.33
  30.7 2.3 fusion.13
  33.1 4.5 fusion.4
  37.7 1.9 fusion.116
  39.6 1.3 convolution_convert_fusion.9
  41.0 14.1 %collective-permute-done.4.refs_13_ = bf16[1536,1536]{1,0:T(8,128)(2,1)} collective-permute-done((bf16[1536,1536]{1,0:T(8,128)(2,1)}, bf16[1536,1536]{1,0:T(8,128)(2,1)}, u32[]{:S(2)}, u32[]{:S(2)}) %collective-permute-start.4) | collective-permute-done | bytes 4718624 | tf_op jit(solution)/shard_map/ppermute | solution.py:97
  55.1 3.6 multiply_reduce_fusion.7
  59.4 51.7 %shard_map.237 = (bf16[96,1536]{1,0:T(8,128)(2,1)S(1)}, bf16[4,96,1536]{2,1,0:T(8,128)(2,1)S(1)}, bf16[4,96,128]{2,1,0:T(8,128)(2,1)S(1)}, f32[96,128]{1,0:T(8,1...) custom-call(bf16[96,1536]{1,0:T(8,128)(2,1)S(1)} %multiply_convert_f, ...), custom_call_target="tpu_custom_call" | custom-call | flops 49999998976 | bytes 100000000 | tf_op jit(solution)/shard_map/pallas_call | solution.py:1061
  111.1 1.1 copy-done.13
  112.3 1.1 copy-done.15
  114.3 2.2 fusion.118
  116.6 4.4 fusion.119
  123.4 3.5 multiply_reduce_fusion.6
  128.0 49.3 %shard_map.238 = (bf16[96,1536]{1,0:T(8,128)(2,1)S(1)}, bf16[4,96,1536]{2,1,0:T(8,128)(2,1)S(1)}, bf16[4,96,128]{2,1,0:T(8,128)(2,1)S(1)}, f32[96,128]{1,0:T(8,1...) custom-call(bf16[96,1536]{1,0:T(8,128)(2,1)S(1)} %multiply_convert_f, ...), custom_call_target="tpu_custom_call" | custom-call | flops 49999998976 | bytes 100000000 | tf_op jit(solution)/shard_map/pallas_call | solution.py:1061
  177.3 1.1 copy-done.14
  178.5 58.6 %shard_map.239 = (f32[96,1536]{1,0:T(8,128)S(1)}, f32[96,128]{1,0:T(8,128)S(1)}, bf16[2,4,96,1536]{3,2,1,0:T(8,128)(2,1)}, bf16[2,4,96,1024]{3,2,1,0:T(8,128)(2,...) custom-call(bf16[96,1536]{1,0:T(8,128)(2,1)S(1)} %constant_dynamic-slice_fusion.9.grad, ...), custom_call_target="tpu_custom_call" | custom-call | flops 49999998976 | bytes 100000000 | tf_op jit(solution)/shard_map/pallas_call | solution.py:1061
  237.0 1.1 copy-done.7
  238.2 9.2 %bitcast_convert_fusion.1 = bf16[1536,2048]{1,0:T(8,128)(2,1)} fusion(bf16[2,4,96,1536]{3,2,1,0:T(8,128)(2,1)} %get-tuple-element.79, bf16[2,4,96,2048]{3,2,1,0:T(8,128)(2,1)} %get-tuple-element.80), kind=kOutput, calls=%fused_computation.3 | convolution fusion | flops 4834983936 | bytes 11796480 | tf_op jit(solution)/shard_map/tc,tq->cq/dot_general | solution.py:1214
  249.3 1.7 fusion.114
  251.0 4.0 convolution_convert_fusion.5
  255.9 1.5 multiply_reduce_fusion.1
  261.9 1.1 copy-done.19
  263.6 1.7 fusion.66
  267.8 1.1 select_bitcast_fusion
  270.0 4.3 bitcast_convert_fusion.3
  275.4 1.9 convolution_convert_fusion.3
  277.3 2.5 convolution_convert_fusion.1
  279.8 3.6 pad_maximum_fusion
  283.4 1.4 copy-done.10
  284.8 1.4 copy-done.12
  286.2 1.3 copy-done.16
  287.5 61.9 %shard_map.240 = (f32[96,1536]{1,0:T(8,128)S(1)}, f32[96,128]{1,0:T(8,128)S(1)}, bf16[2,4,96,1536]{3,2,1,0:T(8,128)(2,1)}, bf16[2,4,96,1024]{3,2,1,0:T(8,128)(2,...) custom-call(bf16[96,1536]{1,0:T(8,128)(2,1)S(1)} %get-tuple-element.88, ...), custom_call_target="tpu_custom_call" | custom-call | flops 49999998976 | bytes 100000000 | tf_op jit(solution)/shard_map/pallas_call | solution.py:1061
  350.7 5.8 %bitcast_convert_fusion.2 = bf16[1024,1536]{1,0:T(8,128)(2,1)} fusion(bf16[2,4,96,1024]{3,2,1,0:T(8,128)(2,1)S(1)} %get-tuple-element.106, bf16[2,4,96,1536]{3,2,1,0:T(8,128)(2,1)} %get-tuple-element.107), kind=kOutput, calls=%fused_computation.7 | convolution fusion | flops 2417491968 | bytes 7077888 | tf_op jit(solution)/shard_map/tc,tq->cq/dot_general | solution.py:1214
  356.6 7.3 %bitcast_convert_fusion = bf16[1536,2048]{1,0:T(8,128)(2,1)} fusion(bf16[2,4,96,1536]{3,2,1,0:T(8,128)(2,1)S(1)} %copy-done.90, bf16[2,4,96,2048]{3,2,1,0:T(8,128)(2,1)S(1)} %copy-done.89), kind=kOutput, calls=%fused_computation.2 | convolution fusion | flops 4834983936 | bytes 11796480 | tf_op jit(solution)/shard_map/tc,tq->cq/dot_general | solution.py:1214
  364.8 4.2 convolution_convert_fusion.4
  370.1 2.0 multiply_reduce_fusion
  378.3 1.7 fusion.57
  380.1 1.2 fusion.48
  382.9 3.3 convolution_convert_fusion.2
  386.2 4.6 convolution_convert_fusion
  390.9 27.1 %reduce-scatter.5.cloned.1.call-done = bf16[384,2048]{1,0:T(8,128)(2,1)} async-done(((bf16[1536,2048]{1,0:T(8,128)(2,1)}), bf16[384,2048]{1,0:T(8,128)(2,1)}) %reduce-scatter.5.cloned.1.call-update) | async-done | bytes 1572880 | tf_op jit(solution)/shard_map/reduce_scatter | solution.py:1334
  417.9 136.2 %shard_map.241 = (bf16[2,2,384,512]{3,2,1,0:T(8,128)(2,1)}, bf16[2,2,384,512]{3,2,1,0:T(8,128)(2,1)}, bf16[2,2,128,1536]{3,2,1,0:T(8,128)(2,1)}, bf16[2,96,1280]...) custom-call(bf16[4,384,2048]{2,1,0:T(8,128)(2,1)} %bitcast.285, ...), custom_call_target="tpu_custom_call" | custom-call | tf_op jit(solution)/shard_map/pallas_call | solution.py:451
  554.2 1.1 slice_bitcast_fusion.2
  559.1 5.1 bitcast_convert_fusion.5
  565.1 2.1 bitcast_convert_fusion.4
  567.1 2.4 maximum_select_fusion
  (330 shorter events, 47.5 us)
Async XLA Ops:
  7.2 6.3 %copy-start = (s32[2,96]{1,0:T(2,128)S(1)}, s32[2,96]{1,0:T(2,128)}, u32[]{:S(2)}) copy-start(s32[2,96]{1,0:T(2,128)} %param.16) | copy-start | bytes 2308
  7.2 18.8 %copy-start.20 = (bf16[192,1536]{1,0:T(8,128)(2,1)S(1)}, bf16[192,1536]{1,0:T(8,128)(2,1)}, u32[]{:S(2)}) copy-start(bf16[192,1536]{1,0:T(8,128)(2,1)} %param.14) | copy-start | bytes 1769476
  7.2 356.7 %reduce-scatter.3.cloned.1.call-start = ((), (), s32[]{:S(2)}) async-start(), calls=%async_computation.2 | async-start | bytes 7864320 | tf_op jit(solution)/shard_map/reduce_scatter | solution.py:1290
  7.3 13.5 %collective-permute-start.2 = (bf16[1536,512]{1,0:T(8,128)(2,1)}, bf16[1536,512]{1,0:T(8,128)(2,1)}, u32[]{:S(2)}, u32[]{:S(2)}) collective-permute-start(bf16[1536,512]{1,0:T(8,128)(2,1)} %bitcast.364), channel_id=1, source_target_pairs={{0,16},{16,0},{1,17},{17,1},{2,18},{18,2},{3,19},{19,3},{4,20},{20... | collective-permute-start | bytes 4718600 | tf_op jit(solution)/shard_map/ppermute | solution.py:97
  7.8 14.9 %collective-permute-start.1 = (bf16[1536,512]{1,0:T(8,128)(2,1)}, bf16[1536,512]{1,0:T(8,128)(2,1)}, u32[]{:S(2)}, u32[]{:S(2)}) collective-permute-start(bf16[1536,512]{1,0:T(8,128)(2,1)} %bitcast.361), channel_id=1, source_target_pairs={{0,16},{16,0},{1,17},{17,1},{2,18},{18,2},{3,19},{19,3},{4,20},{20... | collective-permute-start | bytes 4718600 | tf_op jit(solution)/shard_map/ppermute | solution.py:97
  7.9 25.2 %collective-permute-start.3 = (bf16[1536,1536]{1,0:T(8,128)(2,1)}, bf16[1536,1536]{1,0:T(8,128)(2,1)}, u32[]{:S(2)}, u32[]{:S(2)}) collective-permute-start(bf16[1536,1536]{1,0:T(8,128)(2,1)} %bitcast.358), channel_id=1, source_target_pairs={{0,16},{16,0},{1,17},{17,1},{2,18},{18,2},{3,19},{19,3},{4,20},{20... | collective-permute-start | bytes 14155784 | tf_op jit(solution)/shard_map/ppermute | solution.py:97
  9.0 3.3 collective-permute-start
  9.9 3.2 collective-permute-start.5
  12.3 7.5 %collective-permute-start.6 = (s32[96,8]{0,1:T(8,128)S(1)}, s32[96,8]{0,1:T(8,128)S(1)}, u32[]{:S(2)}, u32[]{:S(2)}) collective-permute-start(s32[96,8]{0,1:T(8,128)S(1)} %dynamic-slice_bitcast_fusion), channel_id=1, source_target_pairs={{0,16},{16,0},{1,17},{17,1},{2,18},{18,2},{3,19},{19,3},{4,20},{20... | collective-permute-start | bytes 9224 | tf_op jit(solution)/shard_map/ppermute | solution.py:97
  13.1 7.3 %collective-permute-start.7 = (bf16[1536,16]{1,0:T(8,128)(2,1)S(1)}, bf16[1536,16]{1,0:T(8,128)(2,1)S(1)}, u32[]{:S(2)}, u32[]{:S(2)}) collective-permute-start(bf16[1536,16]{1,0:T(8,128)(2,1)S(1)} %bitcast.305), channel_id=1, source_target_pairs={{0,16},{16,0},{1,17},{17,1},{2,18},{18,2},{3,19},{19,3},{4,20},{20... | collective-permute-start | bytes 147464 | tf_op jit(solution)/shard_map/ppermute | solution.py:97
  19.8 39.5 %collective-permute-start.10 = (bf16[4,512,1536]{2,1,0:T(8,128)(2,1)}, bf16[4,512,1536]{2,1,0:T(8,128)(2,1)}, u32[]{:S(2)}, u32[]{:S(2)}) collective-permute-start(bf16[4,512,1536]{2,1,0:T(8,128)(2,1)} %bitcast.353), channel_id=1, source_target_pairs={{0,16},{16,0},{1,17},{17,1},{2,18},{18,2},{3,19},{19,3},{4,20},{20... | collective-permute-start | bytes 18874376 | tf_op jit(solution)/shard_map/ppermute | solution.py:97
  20.4 39.0 %collective-permute-start.8 = (bf16[4,1536,512]{2,1,0:T(8,128)(2,1)}, bf16[4,1536,512]{2,1,0:T(8,128)(2,1)}, u32[]{:S(2)}, u32[]{:S(2)}) collective-permute-start(bf16[4,1536,512]{2,1,0:T(8,128)(2,1)} %bitcast.343), channel_id=1, source_target_pairs={{0,16},{16,0},{1,17},{17,1},{2,18},{18,2},{3,19},{19,3},{4,20},{20... | collective-permute-start | bytes 18874376 | tf_op jit(solution)/shard_map/ppermute | solution.py:97
  20.8 38.6 %collective-permute-start.9 = (bf16[4,1536,512]{2,1,0:T(8,128)(2,1)}, bf16[4,1536,512]{2,1,0:T(8,128)(2,1)}, u32[]{:S(2)}, u32[]{:S(2)}) collective-permute-start(bf16[4,1536,512]{2,1,0:T(8,128)(2,1)} %bitcast.348), channel_id=1, source_target_pairs={{0,16},{16,0},{1,17},{17,1},{2,18},{18,2},{3,19},{19,3},{4,20},{20... | collective-permute-start | bytes 18874376 | tf_op jit(solution)/shard_map/ppermute | solution.py:97
  22.7 32.4 %collective-permute-start.4 = (bf16[1536,1536]{1,0:T(8,128)(2,1)}, bf16[1536,1536]{1,0:T(8,128)(2,1)}, u32[]{:S(2)}, u32[]{:S(2)}) collective-permute-start(bf16[1536,1536]{1,0:T(8,128)(2,1)} %bitcast.286), channel_id=1, source_target_pairs={{0,16},{16,0},{1,17},{17,1},{2,18},{18,2},{3,19},{19,3},{4,20},{20... | collective-permute-start | bytes 14155784 | tf_op jit(solution)/shard_map/ppermute | solution.py:97
  25.9 88.2 %copy-start.67 = (f32[1536]{0:T(1024)}, f32[1536]{0:T(1024)S(1)}, u32[]{:S(2)}) copy-start(f32[1536]{0:T(1024)S(1)} %get-tuple-element.217) | copy-start | bytes 18436
  25.9 33.3 %copy-start.59 = (f32[1536]{0:T(1024)}, f32[1536]{0:T(1024)S(1)}, u32[]{:S(2)}) copy-start(f32[1536]{0:T(1024)S(1)} %get-tuple-element.216) | copy-start | bytes 18436
  25.9 101.5 %copy-start.61 = (f32[1536]{0:T(1024)}, f32[1536]{0:T(1024)S(1)}, u32[]{:S(2)}) copy-start(f32[1536]{0:T(1024)S(1)} %get-tuple-element.215) | copy-start | bytes 18436
  41.0 17.7 %copy-start.27 = (bf16[8,64,3,96]{3,1,2,0:T(8,128)(2,1)}, bf16[8,64,3,96]{3,1,2,0:T(8,128)(2,1)S(1)}, u32[]{:S(2)}) copy-start(bf16[8,64,3,96]{3,1,2,0:T(8,128)(2,1)S(1)} %convolution_convert_fusion.9) | copy-start | bytes 884740
  58.6 52.5 %copy-start.2 = (f32[96,1536]{1,0:T(8,128)}, f32[96,1536]{1,0:T(8,128)S(1)}, u32[]{:S(2)}) copy-start(f32[96,1536]{1,0:T(8,128)S(1)} %get-tuple-element.232.hidden) | copy-start | bytes 1769476
  59.2 51.9 %copy-start.79 = (f32[96]{0:T(128)}, f32[96]{0:T(128)S(1)}, u32[]{:S(2)}) copy-start(f32[96]{0:T(128)S(1)} %get-tuple-element.222) | copy-start | bytes 1156
  59.4 51.8 %copy-start.4 = (bf16[96,1536]{1,0:T(8,128)(2,1)}, bf16[96,1536]{1,0:T(8,128)(2,1)S(1)}, u32[]{:S(2)}) copy-start(bf16[96,1536]{1,0:T(8,128)(2,1)S(1)} %multiply_convert_fusion.3.x) | copy-start | bytes 884740
  116.6 5.1 copy-start.55
  116.6 5.1 copy-start.57
  247.4 170.6 %reduce-scatter.5.cloned.1.call-start = ((), (), s32[]{:S(2)}) async-start(), calls=%async_computation.3 | async-start | bytes 7864320 | tf_op jit(solution)/shard_map/reduce_scatter | solution.py:1334
  247.4 138.8 %collective-permute-start.17 = (bf16[96,1536]{1,0:T(8,128)(2,1)}, bf16[96,1536]{1,0:T(8,128)(2,1)}, u32[]{:S(2)}, u32[]{:S(2)}) collective-permute-start(bf16[96,1536]{1,0:T(8,128)(2,1)} %fusion.51), channel_id=1, source_target_pairs={{0,16},{16,0},{1,17},{17,1},{2,18},{18,2},{3,19},{19,3},{4,20},{20... | collective-permute-start | bytes 884744 | tf_op jit(solution)/shard_map/ppermute | solution.py:97
  247.5 27.3 %collective-permute-start.14 = (bf16[96,1536]{0,1:T(8,128)(2,1)}, bf16[96,1536]{0,1:T(8,128)(2,1)}, u32[]{:S(2)}, u32[]{:S(2)}) collective-permute-start(bf16[96,1536]{0,1:T(8,128)(2,1)} %bitcast.308), channel_id=1, source_target_pairs={{0,16},{16,0},{1,17},{17,1},{2,18},{18,2},{3,19},{19,3},{4,20},{20... | collective-permute-start | bytes 884744 | tf_op jit(solution)/shard_map/ppermute | solution.py:97
  248.0 29.2 %collective-permute-start.12 = (bf16[96,1536]{1,0:T(8,128)(2,1)S(1)}, bf16[96,1536]{1,0:T(8,128)(2,1)}, u32[]{:S(2)}, u32[]{:S(2)}) collective-permute-start(bf16[96,1536]{1,0:T(8,128)(2,1)S(1)} %fusion.60), channel_id=1, source_target_pairs={{0,16},{16,0},{1,17},{17,1},{2,18},{18,2},{3,19},{19,3},{4,20},{20... | collective-permute-start | bytes 884744 | tf_op jit(solution)/shard_map/ppermute | solution.py:97
  251.0 4.9 copy-start.38
  251.0 4.9 copy-start.72
  266.8 8.1 %collective-permute-start.15 = (bf16[96,768]{1,0:T(8,128)(2,1)S(1)}, bf16[96,768]{1,0:T(8,128)(2,1)S(1)}, u32[]{:S(2)}, u32[]{:S(2)}) collective-permute-start(bf16[96,768]{1,0:T(8,128)(2,1)S(1)} %get-tuple-element.203), channel_id=1, source_target_pairs={{0,16},{16,0},{1,17},{17,1},{2,18},{18,2},{3,19},{19,3},{4,20},{20... | collective-permute-start | bytes 442376 | tf_op jit(solution)/shard_map/ppermute | solution.py:97
  267.4 9.8 %collective-permute-start.13 = (bf16[96,1280]{0,1:T(8,128)(2,1)S(1)}, bf16[96,1280]{0,1:T(8,128)(2,1)S(1)}, u32[]{:S(2)}, u32[]{:S(2)}) collective-permute-start(bf16[96,1280]{0,1:T(8,128)(2,1)S(1)} %get-tuple-element.189), channel_id=1, source_target_pairs={{0,16},{16,0},{1,17},{17,1},{2,18},{18,2},{3,19},{19,3},{4,20},{20... | collective-permute-start | bytes 737288 | tf_op jit(solution)/shard_map/ppermute | solution.py:97
  270.0 5.4 copy-start.34
  274.9 108.0 %collective-permute-start.19 = (bf16[96,1536]{0,1:T(8,128)(2,1)S(1)}, bf16[96,1536]{0,1:T(8,128)(2,1)}, u32[]{:S(2)}, u32[]{:S(2)}) collective-permute-start(bf16[96,1536]{0,1:T(8,128)(2,1)S(1)} %bitcast.300), channel_id=1, source_target_pairs={{0,16},{16,0},{1,17},{17,1},{2,18},{18,2},{3,19},{19,3},{4,20},{20... | collective-permute-start | bytes 884744 | tf_op jit(solution)/shard_map/ppermute | solution.py:97
  274.9 74.9 %collective-permute-start.11 = (bf16[96,1536]{1,0:T(8,128)(2,1)}, bf16[96,1536]{1,0:T(8,128)(2,1)S(1)}, u32[]{:S(2)}, u32[]{:S(2)}) collective-permute-start(bf16[96,1536]{1,0:T(8,128)(2,1)} %get-tuple-element.191), channel_id=1, source_target_pairs={{0,16},{16,0},{1,17},{17,1},{2,18},{18,2},{3,19},{19,3},{4,20},{20... | collective-permute-start | bytes 884744 | tf_op jit(solution)/shard_map/ppermute | solution.py:97
  287.5 62.1 %copy-start.5 = (bf16[96,1536]{1,0:T(8,128)(2,1)S(1)}, bf16[96,1536]{1,0:T(8,128)(2,1)}, u32[]{:S(2)}) copy-start(bf16[96,1536]{1,0:T(8,128)(2,1)} %copy-done.4) | copy-start | bytes 884740
  349.4 7.2 %copy-start.6 = (bf16[2,128,1536]{2,1,0:T(8,128)(2,1)}, bf16[2,128,1536]{2,1,0:T(8,128)(2,1)S(1)}, u32[]{:S(2)}) copy-start(bf16[2,128,1536]{2,1,0:T(8,128)(2,1)S(1)} %get-tuple-element.111.refs_8_) | copy-start | bytes 2359300
  350.7 5.8 %copy-start.89 = (bf16[2,4,96,2048]{3,2,1,0:T(8,128)(2,1)S(1)}, bf16[2,4,96,2048]{3,2,1,0:T(8,128)(2,1)}, u32[]{:S(2)}) copy-start(bf16[2,4,96,2048]{3,2,1,0:T(8,128)(2,1)} %get-tuple-element.105) | copy-start | bytes 9437188
  350.7 5.8 %copy-start.90 = (bf16[2,4,96,1536]{3,2,1,0:T(8,128)(2,1)S(1)}, bf16[2,4,96,1536]{3,2,1,0:T(8,128)(2,1)}, u32[]{:S(2)}) copy-start(bf16[2,4,96,1536]{3,2,1,0:T(8,128)(2,1)} %get-tuple-element.104) | copy-start | bytes 7077892
  356.6 7.4 %copy-start.3 = (f32[96,1536]{1,0:T(8,128)S(1)}, f32[96,1536]{1,0:T(8,128)}, u32[]{:S(2)}) copy-start(f32[96,1536]{1,0:T(8,128)} %copy-done.2) | copy-start | bytes 1769476
  356.6 7.4 %copy-start.23 = (bf16[1536,16]{1,0:T(8,128)(2,1)S(1)}, bf16[1536,16]{1,0:T(8,128)(2,1)}, u32[]{:S(2)}) copy-start(bf16[1536,16]{1,0:T(8,128)(2,1)} %copy-done.22) | copy-start | bytes 147460
  356.6 7.4 %copy-start.60 = (f32[1536]{0:T(1024)S(1)}, f32[1536]{0:T(1024)}, u32[]{:S(2)}) copy-start(f32[1536]{0:T(1024)} %copy-done.59) | copy-start | bytes 18436
  356.6 7.4 %copy-start.80 = (f32[96]{0:T(128)S(1)}, f32[96]{0:T(128)}, u32[]{:S(2)}) copy-start(f32[96]{0:T(128)} %copy-done.79) | copy-start | bytes 1156
  364.8 5.3 copy-start.63
  364.8 5.3 copy-start.70
  370.1 12.8 %collective-permute-start.20 = (bf16[96,768]{1,0:T(8,128)(2,1)}, bf16[96,768]{1,0:T(8,128)(2,1)}, u32[]{:S(2)}, u32[]{:S(2)}) collective-permute-start(bf16[96,768]{1,0:T(8,128)(2,1)} %get-tuple-element.199), channel_id=1, source_target_pairs={{0,16},{16,0},{1,17},{17,1},{2,18},{18,2},{3,19},{19,3},{4,20},{20... | collective-permute-start | bytes 442376 | tf_op jit(solution)/shard_map/ppermute | solution.py:97
  375.4 10.8 %collective-permute-start.18 = (bf16[96,1280]{0,1:T(8,128)(2,1)S(1)}, bf16[96,1280]{0,1:T(8,128)(2,1)}, u32[]{:S(2)}, u32[]{:S(2)}) collective-permute-start(bf16[96,1280]{0,1:T(8,128)(2,1)S(1)} %get-tuple-element.187), channel_id=1, source_target_pairs={{0,16},{16,0},{1,17},{17,1},{2,18},{18,2},{3,19},{19,3},{4,20},{20... | collective-permute-start | bytes 737288 | tf_op jit(solution)/shard_map/ppermute | solution.py:97
  382.4 184.8 %collective-permute-start.16 = (f32[96,1536]{1,0:T(8,128)}, f32[96,1536]{1,0:T(8,128)}, u32[]{:S(2)}, u32[]{:S(2)}) collective-permute-start(f32[96,1536]{1,0:T(8,128)} %get-tuple-element.175), channel_id=1, source_target_pairs={{0,16},{16,0},{1,17},{17,1},{2,18},{18,2},{3,19},{19,3},{4,20},{20... | collective-permute-start | bytes 1769480 | tf_op jit(solution)/shard_map/ppermute | solution.py:97
  559.1 6.0 %copy-start.32 = (bf16[2,2,128,1536]{3,2,1,0:T(8,128)(2,1)S(1)}, bf16[2,2,128,1536]{3,2,1,0:T(8,128)(2,1)}, u32[]{:S(2)}) copy-start(bf16[2,2,128,1536]{3,2,1,0:T(8,128)(2,1)} %get-tuple-element.119) | copy-start | bytes 4718596
  (70 other events, 139.2 us)
Sparse Core Ops, SparseCore 0:
  247.5 98.7 reduce-scatter.2
  349.2 68.6 reduce-scatter.4

commit v11 on v10

--- a/solution.py
+++ b/solution.py
@@ -481,7 +481,7 @@
 
 def dense_lanes(first, width):
     up, down, deep = bits_of(GROUP), bits_of(GROUP)[::-1], bits_of(LINE)
-    near = width // 4 // COLUMNS * COLUMNS
+    near = width * 2 // 5 // COLUMNS * COLUMNS
     away = width - near
     return [
         (
@@ -1068,7 +1068,7 @@
             collective_id=collective, has_side_effects=True, vmem_limit_bytes=46 * 2**20
         ),
         cost_estimate=pl.CostEstimate(
-            flops=5 * 10**10, bytes_accessed=10**8, transcendentals=0
+            flops=10**10, bytes_accessed=10**7, transcendentals=0
         ),
     )(*operands, *own, *other, *extra)
 
@@ -1210,6 +1210,33 @@
     return grad_inputs, grad_gain_attn, grad_qkv, grad_branch
 
 
+class Halving:
+    def __init__(self, array, order):
+        self.order, self.left = list(order), sorted(order, reverse=True)
+        count = len(self.left)
+        self.array = array.reshape(*(2,) * count, array.shape[0] >> count, array.shape[1])
+
+    def split(self):
+        bit = self.order[0]
+        mine = (lax.axis_index(GROUP) >> bit) & 1
+        at = self.left.index(bit)
+        self.keep, self.away = (
+            lax.dynamic_index_in_dim(self.array, side, at, keepdims=False)
+            for side in (mine, 1 - mine)
+        )
+
+    def send(self):
+        bit = self.order.pop(0)
+        self.left.remove(bit)
+        count = lax.axis_size(GROUP)
+        pairs = [(i, i ^ (1 << bit)) for i in range(count)]
+        self.got = lax.ppermute(self.away, GROUP, pairs)
+
+    def add(self):
+        total = self.keep.astype(jnp.float32) + self.got.astype(jnp.float32)
+        self.array = total.astype(jnp.bfloat16)
+
+
 def turned(left, right):
     return jnp.einsum("tc,tq->cq", left, right, preferred_element_type=jnp.float32)
 
@@ -1281,6 +1308,20 @@
         )
         if s == 0:
             (second_down,) = sums
+            for part in second:
+                part.add()
+            while second[0].order:
+                for part in second:
+                    part.split()
+                grad_sum, *away = lax.optimization_barrier(
+                    (grad_sum, *(part.away for part in second))
+                )
+                for part, value in zip(second, away):
+                    part.away = value
+                    part.send()
+                if second[0].order:
+                    for part in second:
+                        part.add()
         inner = w_gate.shape[3]
         grad_gate_up = turned(
             rows_both.reshape(-1, D), pre_both.reshape(-1, held * inner)
@@ -1327,11 +1368,16 @@
         ).astype(jnp.bfloat16)
         small = jnp.pad(small, ((0, 0), (0, COLUMNS - small.shape[1])))
         if s == 1:
-            grad_inputs, grad_down, grad_w_qkv, grad_w_out = lax.optimization_barrier(
-                (grad_inputs, grad_down, grad_w_qkv, grad_w_out)
+            bits = bits_of(GROUP)
+            second = [Halving(grad_w_qkv, bits), Halving(grad_w_out, bits[::-1])]
+            for part in second:
+                part.split()
+            grad_inputs, grad_down, *away = lax.optimization_barrier(
+                (grad_inputs, grad_down, *(part.away for part in second))
             )
-            dense = jnp.concatenate([grad_w_qkv, grad_w_out], axis=1)
-            second_dense = lax.psum_scatter(dense, GROUP, scatter_dimension=0, tiled=True)
+            for part, value in zip(second, away):
+                part.away = value
+                part.send()
         grads[s] = (grad_gate_up, grad_down, grad_w_qkv, grad_w_out, small)
         input_grads[s] = grad_inputs
         grad_low = grad_inputs.astype(jnp.bfloat16)
@@ -1346,19 +1392,31 @@
     lanes = dense_lanes(2, grad_w_qkv.shape[1])
     for array in (grad_w_qkv, grad_w_out, small):
         arrays.append(array.reshape(dp, deep, array.shape[0] // (dp * deep), array.shape[1]))
-    width = grad_w_qkv.shape[1]
-    whole = second_dense.shape[1]
-    for columns, kind in (((0, width), QKV), ((width, whole - width), OUT)):
-        start, size = columns
-        target = (kind, slice(None), pl.ds(start - (start // width) * width, size))
-        lanes.append((len(arrays), (False, columns), [(LINE, bits_of(LINE))], 1, target))
-    arrays.append(second_dense.reshape(deep, second_dense.shape[0] // deep, whole))
+    for part, kind in zip(second, (QKV, OUT)):
+        grad_w_qkv, part.keep = lax.optimization_barrier((grad_w_qkv, part.keep))
+        part.add()
+        lanes.append((len(arrays), (False, None), [(LINE, bits_of(LINE))], 1, (kind,)))
+        rows, columns = part.array.shape
+        arrays.append(part.array.reshape(deep, rows // deep, columns))
     lanes.append(small_lane(len(arrays), 1))
     lanes += expert_lanes(0, inner) + down_lanes(1, 0)
     small = grads[1][4]
     arrays.append(small.reshape(dp, deep, small.shape[0] // (dp * deep), small.shape[1]))
+    out_keep = jnp.where(first, outs[0], outs[1])
+    out_got = swapped(jnp.where(first, outs[1], outs[0]))
+    layer_out = jnp.where(
+        first, jnp.concatenate([out_keep, out_got]), jnp.concatenate([out_got, out_keep])
+    )
+    low_one = input_grads[1].astype(jnp.bfloat16).astype(jnp.float32)
+    grad_keep = jnp.where(first, input_grads[0], low_one)
+    grad_got = swapped(jnp.where(first, low_one, input_grads[0]))
+    input_grad = jnp.where(
+        first, jnp.concatenate([grad_keep, grad_got]), jnp.concatenate([grad_got, grad_keep])
+    )
+    stats = jnp.concatenate(stats, axis=0)
+    stats, layer_out, input_grad = lax.optimization_barrier((stats, layer_out, input_grad))
     *grads, qkv, out, small, stats = sum_scatter(
-        arrays, lanes, second_pre, second_down, jnp.concatenate(stats, axis=0), inner, 0
+        arrays, lanes, second_pre, second_down, stats, inner, 0
     )
     full = jnp.float32
     w_gate_grad, w_up_grad, w_down_grad = (
@@ -1372,17 +1430,6 @@
     token_total = SEQ * lax.axis_size((CORE, GROUP, LINE))
     counts, chances = stats[:, 1, :experts], stats[:, 0, :experts]
     balance = experts * (counts / (token_total * TOPK) * chances / token_total)
-    out_keep = jnp.where(first, outs[0], outs[1])
-    out_got = swapped(jnp.where(first, outs[1], outs[0]))
-    layer_out = jnp.where(
-        first, jnp.concatenate([out_keep, out_got]), jnp.concatenate([out_got, out_keep])
-    )
-    low_one = input_grads[1].astype(jnp.bfloat16).astype(jnp.float32)
-    grad_keep = jnp.where(first, input_grads[0], low_one)
-    grad_got = swapped(jnp.where(first, low_one, input_grads[0]))
-    input_grad = jnp.where(
-        first, jnp.concatenate([grad_keep, grad_got]), jnp.concatenate([grad_got, grad_keep])
-    )
     results = (
         layer_out,
         input_grad,

time: 585 us -> 631 us (1.079)
  Pallas kernels: 358 us -> 409 us
  waiting for transfers between devices: 48.4 us -> 22.9 us
  other arithmetic: 31.7 us -> 40.3 us
  matrix products: 86.4 us -> 94.2 us
    pallas_call x4, Pallas kernels: 221 us -> 264 us  [expert_call(): pl.pallas_call(kernel, out_shape=shapes, in_specs=[vmem] * len(operands)...]
    reduce_scatter x1 -> x0, waiting for transfers between devices: 27.1 us -> none  [body(): lax.psum_scatter(dense, GROUP, scatter_dimension=0, tiled=True)]
    pallas_call x1, Pallas kernels: 136 us -> 146 us  [sum_scatter(): pl.pallas_call(functools.partial(sum_scatter_kernel, (plans, len(arrays),...]
    ppermute x0 -> x4, waiting for transfers between devices: none -> 8.35 us  [send(): self.got = lax.ppermute(self.away, GROUP, pairs)]
    unnamed x194 -> x192, local copies, waits for them, and re-layouts: 20.8 us -> 13.4 us
    convert_element_type x0 -> x4, other arithmetic: none -> 6.88 us  [add(): self.array = total.astype(jnp.bfloat16)]
    ppermute x21, waiting for transfers between devices: 21.3 us -> 14.6 us  [swapped(): return lax.ppermute(array, CORE, [(0, 1), (1, 0)])]
  transfers between devices with their start and end apart: 23 -> 26, of which waited for: 5 -> 4; matrix products, arithmetic and copies ran while one was open for 18% -> 22% of each run, Pallas kernels for 34% -> 42%
where the time goes in v11:
time: 631 us; the launch traced here: 623 us
  Pallas kernels  409 us (65%)
  matrix products  94.2 us (15%)
  other arithmetic  40.3 us (6%)
  local copies, waits for them, and re-layouts  28 us (4%)
  waiting for transfers between devices  22.9 us (4%)
  between operations  16 us (3%)
  starting transfers between devices  11.9 us (2%)
    pallas_call x4, Pallas kernels, expert_call(): pl.pallas_call(kernel, out_shape=shapes, in_specs=[vmem] * len(operands)...  264 us
    pallas_call x1, Pallas kernels, sum_scatter(): pl.pallas_call(functools.partial(sum_scatter_kernel, (plans, len(arrays),...  146 us
    dot_general x10, matrix products, turned(): jnp.einsum('tc,tq->cq', left, right, preferred_element_type=jnp.float32)  40.1 us
    dot_general x8, matrix products, matmul(): return jnp.dot(left_side, right_side, preferred_element_type=jnp.float32)  23.4 us
    ppermute x21, waiting for transfers between devices, swapped(): return lax.ppermute(array, CORE, [(0, 1), (1, 0)])  14.6 us
    unnamed x192, local copies, waits for them, and re-layouts  13.4 us
  transfers between devices with their start and end apart: 26, of which 4 were waited for; matrix products, arithmetic and copies ran while one was open for 22% of the time, Pallas kernels for 42%

profile of v11, /device:TPU:0, one launch (start us, length us, event | category | flops | bytes accessed | tf_op | source)
XLA Modules:
  0.0 622.5 jit_solution(3073438500734925690)
XLA Ops:
  11.1 1.4 fusion.90
  13.7 1.7 collective-permute-done.5
  16.1 4.9 collective-permute-done.7
  29.2 1.9 fusion.52
  34.8 2.3 fusion.15
  38.0 4.4 fusion.4
  42.6 1.6 fusion.117
  44.2 2.4 convolution_convert_fusion.9
  46.6 7.9 %collective-permute-done.4.refs_13_ = bf16[1536,1536]{1,0:T(8,128)(2,1)} collective-permute-done((bf16[1536,1536]{1,0:T(8,128)(2,1)}, bf16[1536,1536]{1,0:T(8,128)(2,1)}, u32[]{:S(2)}, u32[]{:S(2)}) %collective-permute-start.4) | collective-permute-done | bytes 4718624 | tf_op jit(solution)/shard_map/ppermute | solution.py:97
  54.8 3.7 multiply_reduce_fusion.7
  59.2 51.5 %shard_map.237 = (bf16[96,1536]{1,0:T(8,128)(2,1)S(1)}, bf16[4,96,1536]{2,1,0:T(8,128)(2,1)S(1)}, bf16[4,96,128]{2,1,0:T(8,128)(2,1)S(1)}, f32[96,128]{1,0:T(8,1...) custom-call(bf16[96,1536]{1,0:T(8,128)(2,1)S(1)} %multiply_convert_f, ...), custom_call_target="tpu_custom_call" | custom-call | flops 10000000000 | bytes 10000000 | tf_op jit(solution)/shard_map/pallas_call | solution.py:1061
  114.7 2.2 fusion.119
  117.0 4.5 fusion.120
  121.7 1.5 convolution_convert_fusion.10
  123.3 1.6 fusion.118
  124.9 2.3 convolution_convert_fusion.8
  127.7 3.5 multiply_reduce_fusion.6
  131.9 48.9 %shard_map.238 = (bf16[96,1536]{1,0:T(8,128)(2,1)S(1)}, bf16[4,96,1536]{2,1,0:T(8,128)(2,1)S(1)}, bf16[4,96,128]{2,1,0:T(8,128)(2,1)S(1)}, f32[96,128]{1,0:T(8,1...) custom-call(bf16[96,1536]{1,0:T(8,128)(2,1)S(1)} %multiply_convert_f, ...), custom_call_target="tpu_custom_call" | custom-call | flops 10000000000 | bytes 10000000 | tf_op jit(solution)/shard_map/pallas_call | solution.py:1061
  182.0 58.7 %shard_map.239 = (f32[96,1536]{1,0:T(8,128)S(1)}, f32[96,128]{1,0:T(8,128)S(1)}, bf16[2,4,96,1536]{3,2,1,0:T(8,128)(2,1)}, bf16[2,4,96,1024]{3,2,1,0:T(8,128)(2,...) custom-call(bf16[96,1536]{1,0:T(8,128)(2,1)S(1)} %constant_dynamic-slice_fusion.9.grad, ...), custom_call_target="tpu_custom_call" | custom-call | flops 10000000000 | bytes 10000000 | tf_op jit(solution)/shard_map/pallas_call | solution.py:1061
  242.1 9.2 %bitcast_convert_fusion.1 = bf16[1536,2048]{1,0:T(8,128)(2,1)} fusion(bf16[2,4,96,1536]{3,2,1,0:T(8,128)(2,1)} %get-tuple-element.88, bf16[2,4,96,2048]{3,2,1,0:T(8,128)(2,1)} %get-tuple-element.89), kind=kOutput, calls=%fused_computation.3 | convolution fusion | flops 4834983936 | bytes 11796480 | tf_op jit(solution)/shard_map/tc,tq->cq/dot_general | solution.py:1241
  251.2 2.7 multiply_reduce_fusion.2
  254.5 2.2 fusion.115
  256.7 3.9 convolution_convert_fusion.5
  260.9 1.8 multiply_reduce_fusion.1
  268.3 1.7 fusion.67
  270.8 2.0 broadcast_select_fusion.3
  274.3 4.3 bitcast_convert_fusion.3
  280.9 2.0 convolution_convert_fusion.3
  284.0 2.7 convolution_convert_fusion.1
  286.8 1.4 dynamic-slice_bitcast_fusion
  288.2 1.6 collective-permute-start.17
  289.8 1.7 collective-permute-start.16
  291.5 104.5 %shard_map.240 = (f32[96,1536]{1,0:T(8,128)S(1)}, f32[96,128]{1,0:T(8,128)S(1)}, bf16[2,4,96,1536]{3,2,1,0:T(8,128)(2,1)}, bf16[2,4,96,1024]{3,2,1,0:T(8,128)(2,...) custom-call(bf16[96,1536]{1,0:T(8,128)(2,1)S(1)} %get-tuple-element.97, ...), custom_call_target="tpu_custom_call" | custom-call | flops 10000000000 | bytes 10000000 | tf_op jit(solution)/shard_map/pallas_call | solution.py:1061
  397.3 9.2 %bitcast_convert_fusion = bf16[1536,2048]{1,0:T(8,128)(2,1)} fusion(bf16[2,4,96,1536]{3,2,1,0:T(8,128)(2,1)} %get-tuple-element.118, bf16[2,4,96,2048]{3,2,1,0:T(8,128)(2,1)} %get-tuple-element.119), kind=kOutput, calls=%fused_computation.2 | convolution fusion | flops 4834983936 | bytes 11796480 | tf_op jit(solution)/shard_map/tc,tq->cq/dot_general | solution.py:1241
  406.5 1.5 fusion.14
  408.1 2.0 fusion.8
  411.3 1.5 collective-permute-start.24
  412.7 4.3 bitcast_convert_fusion.2
  418.1 8.3 %collective-permute-done.24 = bf16[384,768]{1,0:T(8,128)(2,1)S(1)} collective-permute-done((bf16[384,768]{1,0:T(8,128)(2,1)S(1)}, bf16[384,768]{1,0:T(8,128)(2,1)S(1)}, u32[]{:S(2)}, u32[]{:S(2)}) %collective-permute-start.24) | collective-permute-done | bytes 589856 | tf_op jit(solution)/shard_map/ppermute | solution.py:1233
  429.3 3.9 convolution_convert_fusion.4
  433.5 1.8 multiply_reduce_fusion
  442.2 1.7 fusion.58
  446.5 3.4 convolution_convert_fusion.2
  449.9 4.7 convolution_convert_fusion
  454.6 2.4 add_convert_fusion
  458.1 145.7 %shard_map.241 = (bf16[2,2,384,512]{3,2,1,0:T(8,128)(2,1)}, bf16[2,2,384,512]{3,2,1,0:T(8,128)(2,1)}, bf16[2,2,128,1536]{3,2,1,0:T(8,128)(2,1)}, bf16[2,96,1280]...) custom-call(bf16[4,384,2048]{2,1,0:T(8,128)(2,1)} %bitcast.326, ...), custom_call_target="tpu_custom_call" | custom-call | tf_op jit(solution)/shard_map/pallas_call | solution.py:451
  606.7 2.1 bitcast_convert_fusion.4
  610.8 3.6 bitcast_convert_fusion.5
  (340 shorter events, 62.1 us)
Async XLA Ops:
  7.2 8.6 %copy-start = (s32[2,96]{1,0:T(2,128)S(1)}, s32[2,96]{1,0:T(2,128)}, u32[]{:S(2)}) copy-start(s32[2,96]{1,0:T(2,128)} %param.16) | copy-start | bytes 2308
  7.2 420.1 %reduce-scatter.2.cloned.1.call-start = ((), (), s32[]{:S(2)}) async-start(), calls=%async_computation.1 | async-start | bytes 7864320 | tf_op jit(solution)/shard_map/reduce_scatter | solution.py:1331
  7.2 14.1 %collective-permute-start.2 = (bf16[1536,512]{1,0:T(8,128)(2,1)}, bf16[1536,512]{1,0:T(8,128)(2,1)S(1)}, u32[]{:S(2)}, u32[]{:S(2)}) collective-permute-start(bf16[1536,512]{1,0:T(8,128)(2,1)} %bitcast.330), channel_id=1, source_target_pairs={{0,16},{16,0},{1,17},{17,1},{2,18},{18,2},{3,19},{19,3},{4,20},{20... | collective-permute-start | bytes 4718600 | tf_op jit(solution)/shard_map/ppermute | solution.py:97
  7.8 16.2 %collective-permute-start.1 = (bf16[1536,512]{1,0:T(8,128)(2,1)}, bf16[1536,512]{1,0:T(8,128)(2,1)S(1)}, u32[]{:S(2)}, u32[]{:S(2)}) collective-permute-start(bf16[1536,512]{1,0:T(8,128)(2,1)} %bitcast.327), channel_id=1, source_target_pairs={{0,16},{16,0},{1,17},{17,1},{2,18},{18,2},{3,19},{19,3},{4,20},{20... | collective-permute-start | bytes 4718600 | tf_op jit(solution)/shard_map/ppermute | solution.py:97
  7.8 29.3 %collective-permute-start.3 = (bf16[1536,1536]{1,0:T(8,128)(2,1)}, bf16[1536,1536]{1,0:T(8,128)(2,1)}, u32[]{:S(2)}, u32[]{:S(2)}) collective-permute-start(bf16[1536,1536]{1,0:T(8,128)(2,1)} %bitcast.318), channel_id=1, source_target_pairs={{0,16},{16,0},{1,17},{17,1},{2,18},{18,2},{3,19},{19,3},{4,20},{20... | collective-permute-start | bytes 14155784 | tf_op jit(solution)/shard_map/ppermute | solution.py:97
  9.0 4.6 collective-permute-start
  9.9 17.4 %copy-start.76 = (bf16[1536]{0:T(1024)(128)(2,1)}, bf16[1536]{0:T(1024)(128)(2,1)S(1)}, u32[]{:S(2)}) copy-start(bf16[1536]{0:T(1024)(128)(2,1)S(1)} %reduce.1) | copy-start | bytes 9220
  9.9 5.6 collective-permute-start.5
  13.6 2.3 collective-permute-start.6
  15.4 5.5 collective-permute-start.7
  15.8 5.8 copy-start.83
  15.8 43.3 %collective-permute-start.10 = (bf16[4,512,1536]{2,1,0:T(8,128)(2,1)}, bf16[4,512,1536]{2,1,0:T(8,128)(2,1)}, u32[]{:S(2)}, u32[]{:S(2)}) collective-permute-start(bf16[4,512,1536]{2,1,0:T(8,128)(2,1)} %bitcast.307), channel_id=1, source_target_pairs={{0,16},{16,0},{1,17},{17,1},{2,18},{18,2},{3,19},{19,3},{4,20},{20... | collective-permute-start | bytes 18874376 | tf_op jit(solution)/shard_map/ppermute | solution.py:97
  20.9 38.2 %collective-permute-start.8 = (bf16[4,1536,512]{2,1,0:T(8,128)(2,1)}, bf16[4,1536,512]{2,1,0:T(8,128)(2,1)}, u32[]{:S(2)}, u32[]{:S(2)}) collective-permute-start(bf16[4,1536,512]{2,1,0:T(8,128)(2,1)} %bitcast.297), channel_id=1, source_target_pairs={{0,16},{16,0},{1,17},{17,1},{2,18},{18,2},{3,19},{19,3},{4,20},{20... | collective-permute-start | bytes 18874376 | tf_op jit(solution)/shard_map/ppermute | solution.py:97
  21.7 7.5 %copy-start.17 = (bf16[1536,512]{1,0:T(8,128)(2,1)}, bf16[1536,512]{1,0:T(8,128)(2,1)S(1)}, u32[]{:S(2)}) copy-start(bf16[1536,512]{1,0:T(8,128)(2,1)S(1)} %collective-permute-done.2.refs_11_) | copy-start | bytes 4718596
  21.7 37.5 %collective-permute-start.9 = (bf16[4,1536,512]{2,1,0:T(8,128)(2,1)}, bf16[4,1536,512]{2,1,0:T(8,128)(2,1)}, u32[]{:S(2)}, u32[]{:S(2)}) collective-permute-start(bf16[4,1536,512]{2,1,0:T(8,128)(2,1)} %bitcast.302), channel_id=1, source_target_pairs={{0,16},{16,0},{1,17},{17,1},{2,18},{18,2},{3,19},{19,3},{4,20},{20... | collective-permute-start | bytes 18874376 | tf_op jit(solution)/shard_map/ppermute | solution.py:97
  23.9 30.5 %collective-permute-start.4 = (bf16[1536,1536]{1,0:T(8,128)(2,1)}, bf16[1536,1536]{1,0:T(8,128)(2,1)}, u32[]{:S(2)}, u32[]{:S(2)}) collective-permute-start(bf16[1536,1536]{1,0:T(8,128)(2,1)} %bitcast.312), channel_id=1, source_target_pairs={{0,16},{16,0},{1,17},{17,1},{2,18},{18,2},{3,19},{19,3},{4,20},{20... | collective-permute-start | bytes 14155784 | tf_op jit(solution)/shard_map/ppermute | solution.py:97
  25.0 7.3 %copy-start.79 = (f32[96]{0:T(128)}, f32[96]{0:T(128)S(1)}, u32[]{:S(2)}) copy-start(f32[96]{0:T(128)S(1)} %get-tuple-element.238) | copy-start | bytes 1156
  34.7 9.4 %copy-start.62 = (bf16[96,512]{0,1:T(8,128)(2,1)}, bf16[96,512]{0,1:T(8,128)(2,1)S(1)}, u32[]{:S(2)}) copy-start(bf16[96,512]{0,1:T(8,128)(2,1)S(1)} %copy.86) | copy-start | bytes 294916
  37.2 5.4 copy-start.55
  37.2 412.7 %collective-permute-start.19 = (bf16[96,1536]{1,0:T(8,128)(2,1)}, bf16[96,1536]{1,0:T(8,128)(2,1)}, u32[]{:S(2)}, u32[]{:S(2)}) collective-permute-start(bf16[96,1536]{1,0:T(8,128)(2,1)} %fusion.52), channel_id=1, source_target_pairs={{0,16},{16,0},{1,17},{17,1},{2,18},{18,2},{3,19},{19,3},{4,20},{20... | collective-permute-start | bytes 884744 | tf_op jit(solution)/shard_map/ppermute | solution.py:97
  44.2 10.7 %copy-start.20 = (bf16[192,1536]{1,0:T(8,128)(2,1)S(1)}, bf16[192,1536]{1,0:T(8,128)(2,1)}, u32[]{:S(2)}) copy-start(bf16[192,1536]{1,0:T(8,128)(2,1)} %param.14) | copy-start | bytes 1769476
  54.5 391.9 %collective-permute-start.21 = (bf16[96,1536]{0,1:T(8,128)(2,1)}, bf16[96,1536]{0,1:T(8,128)(2,1)}, u32[]{:S(2)}, u32[]{:S(2)}) collective-permute-start(bf16[96,1536]{0,1:T(8,128)(2,1)} %bitcast.15), channel_id=1, source_target_pairs={{0,16},{16,0},{1,17},{17,1},{2,18},{18,2},{3,19},{19,3},{4,20},{20... | collective-permute-start | bytes 884744 | tf_op jit(solution)/shard_map/ppermute | solution.py:97
  59.0 51.7 %copy-start.81 = (f32[96]{0:T(128)}, f32[96]{0:T(128)S(1)}, u32[]{:S(2)}) copy-start(f32[96]{0:T(128)S(1)} %get-tuple-element.240) | copy-start | bytes 1156
  59.2 54.5 %copy-start.68 = (f32[1536]{0:T(1024)S(1)}, f32[1536]{0:T(1024)}, u32[]{:S(2)}) copy-start(f32[1536]{0:T(1024)} %get-tuple-element.235) | copy-start | bytes 18436
  113.7 154.5 %copy-start.78 = (f32[96]{0:T(128)}, f32[96]{0:T(128)S(1)}, u32[]{:S(2)}) copy-start(f32[96]{0:T(128)S(1)} %get-tuple-element.242) | copy-start | bytes 1156
  114.6 169.4 %collective-permute-start.12 = (bf16[96,1536]{1,0:T(8,128)(2,1)}, bf16[96,1536]{1,0:T(8,128)(2,1)}, u32[]{:S(2)}, u32[]{:S(2)}) collective-permute-start(bf16[96,1536]{1,0:T(8,128)(2,1)} %fusion.61), channel_id=1, source_target_pairs={{0,16},{16,0},{1,17},{17,1},{2,18},{18,2},{3,19},{19,3},{4,20},{20... | collective-permute-start | bytes 884744 | tf_op jit(solution)/shard_map/ppermute | solution.py:97
  117.0 6.3 %copy-start.57 = (bf16[96,8,32]{0,2,1:T(8,128)(2,1)}, bf16[96,8,32]{0,2,1:T(8,128)(2,1)S(1)}, u32[]{:S(2)}) copy-start(bf16[96,8,32]{0,2,1:T(8,128)(2,1)S(1)} %get-tuple-element.225) | copy-start | bytes 147460
  117.0 6.3 %copy-start.59 = (bf16[96,8,32]{0,2,1:T(8,128)(2,1)}, bf16[96,8,32]{0,2,1:T(8,128)(2,1)S(1)}, u32[]{:S(2)}) copy-start(bf16[96,8,32]{0,2,1:T(8,128)(2,1)S(1)} %get-tuple-element.226) | copy-start | bytes 147460
  127.2 153.6 %collective-permute-start.14 = (bf16[96,1536]{0,1:T(8,128)(2,1)}, bf16[96,1536]{0,1:T(8,128)(2,1)}, u32[]{:S(2)}, u32[]{:S(2)}) collective-permute-start(bf16[96,1536]{0,1:T(8,128)(2,1)} %bitcast.37), channel_id=1, source_target_pairs={{0,16},{16,0},{1,17},{17,1},{2,18},{18,2},{3,19},{19,3},{4,20},{20... | collective-permute-start | bytes 884744 | tf_op jit(solution)/shard_map/ppermute | solution.py:97
  270.7 9.6 %collective-permute-start.15 = (bf16[96,768]{1,0:T(8,128)(2,1)}, bf16[96,768]{1,0:T(8,128)(2,1)}, u32[]{:S(2)}, u32[]{:S(2)}) collective-permute-start(bf16[96,768]{1,0:T(8,128)(2,1)} %get-tuple-element.221), channel_id=1, source_target_pairs={{0,16},{16,0},{1,17},{17,1},{2,18},{18,2},{3,19},{19,3},{4,20},{20... | collective-permute-start | bytes 442376 | tf_op jit(solution)/shard_map/ppermute | solution.py:97
  274.3 6.0 copy-start.52
  274.3 6.5 %copy-start.53 = (bf16[96,1536]{1,0:T(8,128)(2,1)S(1)}, bf16[96,1536]{1,0:T(8,128)(2,1)}, u32[]{:S(2)}) copy-start(bf16[96,1536]{1,0:T(8,128)(2,1)} %get-tuple-element.209) | copy-start | bytes 884740
  280.3 3.7 collective-permute-start.13
  280.8 115.4 %collective-permute-start.11 = (bf16[96,1536]{1,0:T(8,128)(2,1)S(1)}, bf16[96,1536]{1,0:T(8,128)(2,1)S(1)}, u32[]{:S(2)}, u32[]{:S(2)}) collective-permute-start(bf16[96,1536]{1,0:T(8,128)(2,1)S(1)} %copy-done.53), channel_id=1, source_target_pairs={{0,16},{16,0},{1,17},{17,1},{2,18},{18,2},{3,19},{19,3},{4,20},{20... | collective-permute-start | bytes 884744 | tf_op jit(solution)/shard_map/ppermute | solution.py:97
  284.0 7.5 %copy-start.9 = (bf16[4,96,1536]{2,1,0:T(8,128)(2,1)S(1)}, bf16[4,96,1536]{2,1,0:T(8,128)(2,1)}, u32[]{:S(2)}) copy-start(bf16[4,96,1536]{2,1,0:T(8,128)(2,1)} %copy-done.8) | copy-start | bytes 3538948
  288.2 118.3 %collective-permute-start.17 = (bf16[2,384,768]{2,1,0:T(8,128)(2,1)}, bf16[2,384,768]{2,1,0:T(8,128)(2,1)}, u32[]{:S(2)}, u32[]{:S(2)}) collective-permute-start(bf16[2,384,768]{2,1,0:T(8,128)(2,1)} %dynamic-slice_bitcast_fusion.1), channel_id=1, source_target_pairs={{0,8},{4,12},{8,0},{12,4},{1,9},{5,13},{9,1},{13,5},{2,10},{6,14},... | collective-permute-start | bytes 3538952 | tf_op jit(solution)/shard_map/ppermute | solution.py:1233
  289.8 118.4 %collective-permute-start.16 = (bf16[2,384,1280]{2,1,0:T(8,128)(2,1)}, bf16[2,384,1280]{2,1,0:T(8,128)(2,1)}, u32[]{:S(2)}, u32[]{:S(2)}) collective-permute-start(bf16[2,384,1280]{2,1,0:T(8,128)(2,1)} %dynamic-slice_bitcast_fusion), channel_id=1, source_target_pairs={{0,4},{4,0},{8,12},{12,8},{1,5},{5,1},{9,13},{13,9},{2,6},{6,2},{1... | collective-permute-start | bytes 5898248 | tf_op jit(solution)/shard_map/ppermute | solution.py:1233
  291.5 104.7 %copy-start.35 = (bf16[96,1536]{1,0:T(8,128)(2,1)S(1)}, bf16[96,1536]{1,0:T(8,128)(2,1)}, u32[]{:S(2)}) copy-start(bf16[96,1536]{1,0:T(8,128)(2,1)} %get-tuple-element.208) | copy-start | bytes 884740
  396.0 10.5 %copy-start.10 = (bf16[2,128,1536]{2,1,0:T(8,128)(2,1)}, bf16[2,128,1536]{2,1,0:T(8,128)(2,1)S(1)}, u32[]{:S(2)}) copy-start(bf16[2,128,1536]{2,1,0:T(8,128)(2,1)S(1)} %get-tuple-element.126.refs_9_) | copy-start | bytes 2359300
  411.3 15.1 %collective-permute-start.24 = (bf16[384,768]{1,0:T(8,128)(2,1)S(1)}, bf16[384,768]{1,0:T(8,128)(2,1)S(1)}, u32[]{:S(2)}, u32[]{:S(2)}) collective-permute-start(bf16[384,768]{1,0:T(8,128)(2,1)S(1)} %get-tuple-element.124), channel_id=1, source_target_pairs={{0,4},{4,0},{8,12},{12,8},{1,5},{5,1},{9,13},{13,9},{2,6},{6,2},{1... | collective-permute-start | bytes 1769480 | tf_op jit(solution)/shard_map/ppermute | solution.py:1233
  417.0 10.3 %copy-start.23 = (bf16[1536,16]{1,0:T(8,128)(2,1)S(1)}, bf16[1536,16]{1,0:T(8,128)(2,1)}, u32[]{:S(2)}) copy-start(bf16[1536,16]{1,0:T(8,128)(2,1)} %copy-done.22) | copy-start | bytes 147460
  417.0 10.3 %copy-start.82 = (f32[96]{0:T(128)S(1)}, f32[96]{0:T(128)}, u32[]{:S(2)}) copy-start(f32[96]{0:T(128)} %copy-done.81) | copy-start | bytes 1156
  417.0 11.2 %copy-start.85 = (f32[96]{0:T(128)S(1)}, f32[96]{0:T(128)}, u32[]{:S(2)}) copy-start(f32[96]{0:T(128)} %get-tuple-element.239) | copy-start | bytes 1156
  417.0 37.6 %collective-permute-start.23 = (bf16[384,1280]{1,0:T(8,128)(2,1)}, bf16[384,1280]{1,0:T(8,128)(2,1)}, u32[]{:S(2)}, u32[]{:S(2)}) collective-permute-start(bf16[384,1280]{1,0:T(8,128)(2,1)} %get-tuple-element.123), channel_id=1, source_target_pairs={{0,8},{4,12},{8,0},{12,4},{1,9},{5,13},{9,1},{13,5},{2,10},{6,14},... | collective-permute-start | bytes 2949128 | tf_op jit(solution)/shard_map/ppermute | solution.py:1233
  435.4 6.5 %slice-start.2 = ((s8[4718592]{0:T(1024)(128)(4,1)}), s8[4194304]{0:T(1024)(128)(4,1)S(1)}, s32[]{:S(2)}) async-start(s8[4718592]{0:T(1024)(128)(4,1)} %bitcast.333), calls=%async_computation.4 | async-start | bytes 8388608
  440.0 9.9 %collective-permute-start.20 = (bf16[96,1280]{0,1:T(8,128)(2,1)}, bf16[96,1280]{0,1:T(8,128)(2,1)}, u32[]{:S(2)}, u32[]{:S(2)}) collective-permute-start(bf16[96,1280]{0,1:T(8,128)(2,1)} %get-tuple-element.205), channel_id=1, source_target_pairs={{0,16},{16,0},{1,17},{17,1},{2,18},{18,2},{3,19},{19,3},{4,20},{20... | collective-permute-start | bytes 737288 | tf_op jit(solution)/shard_map/ppermute | solution.py:97
  441.8 4.7 collective-permute-start.22
  446.3 10.7 %collective-permute-start.18 = (f32[96,1536]{1,0:T(8,128)}, f32[96,1536]{1,0:T(8,128)S(1)}, u32[]{:S(2)}, u32[]{:S(2)}) collective-permute-start(f32[96,1536]{1,0:T(8,128)} %get-tuple-element.189), channel_id=1, source_target_pairs={{0,16},{16,0},{1,17},{17,1},{2,18},{18,2},{3,19},{19,3},{4,20},{20... | collective-permute-start | bytes 1769480 | tf_op jit(solution)/shard_map/ppermute | solution.py:97
  (72 other events, 177.0 us)
Sparse Core Ops, SparseCore 0:
  254.6 96.9 reduce-scatter.1

commit v12 on v10

--- a/solution.py
+++ b/solution.py
@@ -652,7 +652,16 @@
 
             return carry
 
-        lax.fori_loop(0, 2 * n - 1, turn, 0)
+        def far_first(k, carry):
+            block = z + (n - 1 - lax.div(k, 2)) * (1 - 2 * lax.rem(k, 2))
+
+            @pl.when((block >= 0) & (block < n))
+            def _():
+                compute(block, sent)
+
+            return carry
+
+        lax.fori_loop(0, 2 * n - 1, turn if held else far_first, 0)
 
         first = jnp.where(2 * z < n, 0, 1)
         for way in (first, 1 - first):
@@ -868,7 +877,8 @@
     core = lax.axis_index(CORE)
     z = lax.axis_index(LINE)
     turned_dims = (((1,), (1,)), ((), ()))
-    rows = grad_both.at[core]
+    gathered = layer == 1
+    rows = grad if gathered else grad_both.at[core]
 
     def to_core(number, source, target):
         return pltpu.make_async_remote_copy(
@@ -881,27 +891,31 @@
         )
 
     def block_copies(block):
-        return (
-            to_core(2 + block, rows.at[block], rows.at[block]),
-            to_core(2 + n + block, away.at[block], pre_both.at[core, block]),
-        )
+        away_copy = to_core(2 + n + block, away.at[block], pre_both.at[core, block])
+        if gathered:
+            return (away_copy,)
+        return (to_core(2 + block, rows.at[block], rows.at[block]), away_copy)
 
     def columns(at):
         return pl.ds(pl.multiple_of(at * half * inner, half * inner), half * inner)
 
     def whole_copies():
-        return (
+        copies = (
             to_core(0, saved_rows, rows_both.at[core]),
             to_core(1, saved_gated.at[:, :, columns(1 - core)], gated_both.at[core]),
         )
+        return copies + ((to_core(2, grad, grad_both.at[core]),) if gathered else ())
 
     def local_copies():
-        return (
+        copies = (
             pltpu.make_async_copy(saved_rows, rows_both.at[core], core_local.at[0]),
             pltpu.make_async_copy(
                 saved_gated.at[:, :, columns(core)], gated_both.at[core], core_local.at[1]
             ),
         )
+        if gathered:
+            copies += (pltpu.make_async_copy(grad, grad_both.at[core], core_local.at[2]),)
+        return copies
 
     me, count = lax.axis_index(GROUP), lax.axis_size(GROUP)
     peers = [lax.rem(me + k, count) for k in range(1, count)] if carried else []
@@ -987,8 +1001,8 @@
 
     gate_piece = (lambda block: sum_gates.at[block], lambda way, block: returned_gates.at[way, block])
     start, run, collect, finish = move_rows(
-        (grad,),
-        (rows,),
+        () if gathered else (grad,),
+        () if gathered else (rows,),
         row_pieces(sums, returned, PARTS) + [gate_piece],
         sems,
         compute,
@@ -996,7 +1010,8 @@
         n,
         [{CORE: 1 - core}] + [{GROUP: peer} for peer in peers],
     )
-    start(0)
+    if not gathered:
+        start(0)
     for k, peer in enumerate(peers):
         extra_copy(k, peer, me).start()
     if carried:
@@ -1005,7 +1020,8 @@
     wait_weights = fetch_weights(layer, own, other, (w_gate, w_up, w_down), weight_sem)
     for copy in whole_copies() + local_copies():
         copy.start()
-    rows[z] = grad[...]
+    if not gathered:
+        rows[z] = grad[...]
     wait_weights()
     run()
     width = out.shape[1] // PARTS
@@ -1117,7 +1133,7 @@
 
 def experts_backward(layer, grad_low, gates, gate_keep, up_keep, rows, gated, own, other, extra):
     held, n, length, inner = gate_keep.shape
-    width = grad_low.shape[1]
+    width = grad_low.shape[-1]
     low, full = jnp.bfloat16, jnp.float32
     shapes = [
         jax.ShapeDtypeStruct((length, width), full),
@@ -1137,7 +1153,7 @@
         pltpu.SemaphoreType.DMA((3 * held,)),
         pltpu.SemaphoreType.DMA((2 + 2 * n,)),
         pltpu.SemaphoreType.DMA((2 + 2 * n,)),
-        pltpu.SemaphoreType.DMA((2,)),
+        pltpu.SemaphoreType.DMA((3,)),
     ] + exchange_scratch(n, 1, PARTS + 1)
     if layer == 0:
         half, count, *block = extra.shape
@@ -1228,6 +1244,7 @@
     ]
     inputs_low = lax.dynamic_slice_in_dim(tokens, core * SEQ, SEQ, 0)
     grad_low = lax.dynamic_slice_in_dim(cotangent, core * SEQ, SEQ, 0)
+    cotangent_all = lax.all_gather(grad_low, LINE, axis=0)
     segment_row = lax.dynamic_index_in_dim(segments, core, 0, keepdims=False)
     mine = lax.dynamic_slice_in_dim(routes[0], core * SEQ, SEQ, 0)
     got = swapped(lax.dynamic_slice_in_dim(routes[0], (1 - core) * SEQ, SEQ, 0))
@@ -1269,7 +1286,7 @@
         gain_moe, w_router = weights[s][5], weights[s][6]
         grad_sum, grad_gates, rows_both, gated_both, grad_both, pre_both, *sums = experts_backward(
             s,
-            grad_low,
+            cotangent_all if s == 1 else grad_low,
             gates_all,
             gate_keep,
             up_keep,
@@ -1357,8 +1374,21 @@
     lanes += expert_lanes(0, inner) + down_lanes(1, 0)
     small = grads[1][4]
     arrays.append(small.reshape(dp, deep, small.shape[0] // (dp * deep), small.shape[1]))
+    out_keep = jnp.where(first, outs[0], outs[1])
+    out_got = swapped(jnp.where(first, outs[1], outs[0]))
+    layer_out = jnp.where(
+        first, jnp.concatenate([out_keep, out_got]), jnp.concatenate([out_got, out_keep])
+    )
+    low_one = input_grads[1].astype(jnp.bfloat16).astype(jnp.float32)
+    grad_keep = jnp.where(first, input_grads[0], low_one)
+    grad_got = swapped(jnp.where(first, low_one, input_grads[0]))
+    input_grad = jnp.where(
+        first, jnp.concatenate([grad_keep, grad_got]), jnp.concatenate([grad_got, grad_keep])
+    )
+    stats = jnp.concatenate(stats, axis=0)
+    stats, layer_out, input_grad = lax.optimization_barrier((stats, layer_out, input_grad))
     *grads, qkv, out, small, stats = sum_scatter(
-        arrays, lanes, second_pre, second_down, jnp.concatenate(stats, axis=0), inner, 0
+        arrays, lanes, second_pre, second_down, stats, inner, 0
     )
     full = jnp.float32
     w_gate_grad, w_up_grad, w_down_grad = (
@@ -1372,17 +1402,6 @@
     token_total = SEQ * lax.axis_size((CORE, GROUP, LINE))
     counts, chances = stats[:, 1, :experts], stats[:, 0, :experts]
     balance = experts * (counts / (token_total * TOPK) * chances / token_total)
-    out_keep = jnp.where(first, outs[0], outs[1])
-    out_got = swapped(jnp.where(first, outs[1], outs[0]))
-    layer_out = jnp.where(
-        first, jnp.concatenate([out_keep, out_got]), jnp.concatenate([out_got, out_keep])
-    )
-    low_one = input_grads[1].astype(jnp.bfloat16).astype(jnp.float32)
-    grad_keep = jnp.where(first, input_grads[0], low_one)
-    grad_got = swapped(jnp.where(first, low_one, input_grads[0]))
-    input_grad = jnp.where(
-        first, jnp.concatenate([grad_keep, grad_got]), jnp.concatenate([grad_got, grad_keep])
-    )
     results = (
         layer_out,
         input_grad,

time: 585 us -> 583 us (level)
  Pallas kernels: 358 us -> 347 us
  local copies, waits for them, and re-layouts: 30.2 us -> 40.1 us
    pallas_call x4, Pallas kernels: 221 us -> 210 us  [expert_call(): pl.pallas_call(kernel, out_shape=shapes, in_specs=[vmem] * len(operands)...]
    unnamed x194 -> x224, local copies, waits for them, and re-layouts: 20.8 us -> 30 us
  transfers between devices with their start and end apart: 23 -> 24, of which waited for: 5 -> 4; matrix products, arithmetic and copies ran while one was open for 18% -> 19% of each run, Pallas kernels for 34% -> 28%
where the time goes in v12:
time: 583 us; the launch traced here: 575 us
  Pallas kernels  347 us (60%)
  matrix products  89.1 us (15%)
  waiting for transfers between devices  50.4 us (9%)
  local copies, waits for them, and re-layouts  40.1 us (7%)
  other arithmetic  26.9 us (5%)
  between operations  15.9 us (3%)
    pallas_call x4, Pallas kernels, expert_call(): pl.pallas_call(kernel, out_shape=shapes, in_specs=[vmem] * len(operands)...  210 us
    pallas_call x1, Pallas kernels, sum_scatter(): pl.pallas_call(functools.partial(sum_scatter_kernel, (plans, len(arrays),...  136 us
    dot_general x10, matrix products, turned(): jnp.einsum('tc,tq->cq', left, right, preferred_element_type=jnp.float32)  39.4 us
    unnamed x224, local copies, waits for them, and re-layouts  30 us
    reduce_scatter x1, waiting for transfers between devices, body(): lax.psum_scatter(dense, GROUP, scatter_dimension=0, tiled=True)  26.1 us
    ppermute x21, waiting for transfers between devices, swapped(): return lax.ppermute(array, CORE, [(0, 1), (1, 0)])  24.2 us
    dot_general x8, matrix products, matmul(): return jnp.dot(left_side, right_side, preferred_element_type=jnp.float32)  21.2 us
  transfers between devices with their start and end apart: 24, of which 4 were waited for; matrix products, arithmetic and copies ran while one was open for 19% of the time, Pallas kernels for 28%

profile of v12, /device:TPU:0, one launch (start us, length us, event | category | flops | bytes accessed | tf_op | source)
XLA Modules:
  0.0 574.7 jit_solution(9229361144249029537)
XLA Ops:
  10.4 1.7 constant_dynamic-slice_fusion.9
  16.2 3.6 collective-permute-done.6
  25.9 2.2 fusion.13
  28.2 4.4 fusion.4
  34.8 20.3 %collective-permute-done.4.refs_13_ = bf16[1536,1536]{1,0:T(8,128)(2,1)} collective-permute-done((bf16[1536,1536]{1,0:T(8,128)(2,1)}, bf16[1536,1536]{1,0:T(8,128)(2,1)}, u32[]{:S(2)}, u32[]{:S(2)}) %collective-permute-start.4) | collective-permute-done | bytes 4718624 | tf_op jit(solution)/shard_map/ppermute | solution.py:97
  55.1 3.7 multiply_reduce_fusion.7
  59.5 51.7 %shard_map.237 = (bf16[96,1536]{1,0:T(8,128)(2,1)S(1)}, bf16[4,96,1536]{2,1,0:T(8,128)(2,1)S(1)}, bf16[4,96,128]{2,1,0:T(8,128)(2,1)S(1)}, f32[96,128]{1,0:T(8,1...) custom-call(bf16[96,1536]{1,0:T(8,128)(2,1)S(1)} %multiply_convert_f, ...), custom_call_target="tpu_custom_call" | custom-call | flops 49999998976 | bytes 100000000 | tf_op jit(solution)/shard_map/pallas_call | solution.py:1077
  111.2 1.2 copy-done.14
  113.4 2.3 fusion.117
  115.9 4.4 fusion.118
  121.0 1.6 fusion.116
  122.6 1.5 convolution_convert_fusion.8
  124.2 3.5 multiply_reduce_fusion.6
  128.8 49.3 %shard_map.238 = (bf16[96,1536]{1,0:T(8,128)(2,1)S(1)}, bf16[4,96,1536]{2,1,0:T(8,128)(2,1)S(1)}, bf16[4,96,128]{2,1,0:T(8,128)(2,1)S(1)}, f32[96,128]{1,0:T(8,1...) custom-call(bf16[96,1536]{1,0:T(8,128)(2,1)S(1)} %multiply_convert_f, ...), custom_call_target="tpu_custom_call" | custom-call | flops 49999998976 | bytes 100000000 | tf_op jit(solution)/shard_map/pallas_call | solution.py:1077
  178.1 1.1 copy-done.15
  179.3 1.1 copy-done.17
  180.4 1.1 copy-done.19
  183.2 1.3 copy-done.7
  184.5 1.4 copy-done.16
  185.9 1.4 copy-done.18
  187.3 1.3 copy-done.21
  189.4 50.1 %shard_map.239 = (f32[96,1536]{1,0:T(8,128)S(1)}, f32[96,128]{1,0:T(8,128)S(1)}, bf16[2,4,96,1536]{3,2,1,0:T(8,128)(2,1)}, bf16[2,4,96,1024]{3,2,1,0:T(8,128)(2,...) custom-call(bf16[4,96,1536]{2,1,0:T(8,128)(2,1)S(1)} %bitcast.278, ...), custom_call_target="tpu_custom_call" | custom-call | flops 49999998976 | bytes 100000000 | tf_op jit(solution)/shard_map/pallas_call | solution.py:1077
  239.5 1.1 copy-done.8
  240.6 9.1 %bitcast_convert_fusion.1 = bf16[1536,2048]{1,0:T(8,128)(2,1)} fusion(bf16[2,4,96,1536]{3,2,1,0:T(8,128)(2,1)} %get-tuple-element.84, bf16[2,4,96,2048]{3,2,1,0:T(8,128)(2,1)} %get-tuple-element.85), kind=kOutput, calls=%fused_computation.3 | convolution fusion | flops 4834983936 | bytes 11796480 | tf_op jit(solution)/shard_map/tc,tq->cq/dot_general | solution.py:1230
  250.7 1.9 multiply_reduce_fusion.2
  252.7 1.7 fusion.113
  255.1 4.9 convolution_convert_fusion.5
  260.3 1.8 multiply_reduce_fusion.1
  268.4 2.6 fusion.65
  272.6 1.4 pad_maximum_fusion.1
  276.1 4.3 bitcast_convert_fusion.3
  281.5 1.9 convolution_convert_fusion.3
  283.5 2.5 convolution_convert_fusion.1
  286.0 3.5 pad_maximum_fusion
  289.6 1.5 copy-done.11
  291.0 1.4 copy-done.13
  292.4 59.5 %shard_map.240 = (f32[96,1536]{1,0:T(8,128)S(1)}, f32[96,128]{1,0:T(8,128)S(1)}, bf16[2,4,96,1536]{3,2,1,0:T(8,128)(2,1)}, bf16[2,4,96,1024]{3,2,1,0:T(8,128)(2,...) custom-call(bf16[96,1536]{1,0:T(8,128)(2,1)S(1)} %get-tuple-element.93, ...), custom_call_target="tpu_custom_call" | custom-call | flops 49999998976 | bytes 100000000 | tf_op jit(solution)/shard_map/pallas_call | solution.py:1077
  353.2 5.8 %bitcast_convert_fusion.2 = bf16[1024,1536]{1,0:T(8,128)(2,1)} fusion(bf16[2,4,96,1024]{3,2,1,0:T(8,128)(2,1)S(1)} %get-tuple-element.113, bf16[2,4,96,1536]{3,2,1,0:T(8,128)(2,1)} %get-tuple-element.114), kind=kOutput, calls=%fused_computation.7 | convolution fusion | flops 2417491968 | bytes 7077888 | tf_op jit(solution)/shard_map/tc,tq->cq/dot_general | solution.py:1230
  359.1 7.3 %bitcast_convert_fusion = bf16[1536,2048]{1,0:T(8,128)(2,1)} fusion(bf16[2,4,96,1536]{3,2,1,0:T(8,128)(2,1)S(1)} %copy-done.105, bf16[2,4,96,2048]{3,2,1,0:T(8,128)(2,1)S(1)} %copy-done.104), kind=kOutput, calls=%fused_computation.2 | convolution fusion | flops 4834983936 | bytes 11796480 | tf_op jit(solution)/shard_map/tc,tq->cq/dot_general | solution.py:1230
  367.3 4.3 convolution_convert_fusion.4
  371.8 1.8 multiply_reduce_fusion
  379.4 1.7 fusion.56
  384.8 3.5 convolution_convert_fusion.2
  388.3 4.6 convolution_convert_fusion
  394.0 26.1 %reduce-scatter.5.cloned.1.call-done = bf16[384,2048]{1,0:T(8,128)(2,1)} async-done(((bf16[1536,2048]{1,0:T(8,128)(2,1)}), bf16[384,2048]{1,0:T(8,128)(2,1)}) %reduce-scatter.5.cloned.1.call-update) | async-done | bytes 1572880 | tf_op jit(solution)/shard_map/reduce_scatter | solution.py:1351
  420.2 136.1 %shard_map.241 = (bf16[2,2,384,512]{3,2,1,0:T(8,128)(2,1)}, bf16[2,2,384,512]{3,2,1,0:T(8,128)(2,1)}, bf16[2,2,128,1536]{3,2,1,0:T(8,128)(2,1)}, bf16[2,96,1280]...) custom-call(bf16[4,384,2048]{2,1,0:T(8,128)(2,1)} %bitcast.283, ...), custom_call_target="tpu_custom_call" | custom-call | tf_op jit(solution)/shard_map/pallas_call | solution.py:451
  559.1 2.1 bitcast_convert_fusion.4
  563.3 3.6 bitcast_convert_fusion.5
  (363 shorter events, 52.7 us)
Async XLA Ops:
  7.2 13.7 %copy-start = (s32[2,96]{1,0:T(2,128)S(1)}, s32[2,96]{1,0:T(2,128)}, u32[]{:S(2)}) copy-start(s32[2,96]{1,0:T(2,128)} %param.16) | copy-start | bytes 2308
  7.2 15.0 %copy-start.90 = (s32[1,192,8]{1,2,0:T(8,128)S(1)}, s32[1,192,8]{1,2,0:T(8,128)}, u32[]{:S(2)}) copy-start(s32[1,192,8]{1,2,0:T(8,128)} %param.17) | copy-start | bytes 18436
  7.2 15.6 %copy-start.29 = (bf16[192,1536]{1,0:T(8,128)(2,1)S(1)}, bf16[192,1536]{1,0:T(8,128)(2,1)}, u32[]{:S(2)}) copy-start(bf16[192,1536]{1,0:T(8,128)(2,1)} %param.14) | copy-start | bytes 1769476
  7.2 176.0 %all-gather.3.cloned.1.call-start = ((), (), s32[]{:S(2)}) async-start(), calls=%async_computation.4 | async-start | bytes 1474560 | tf_op jit(solution)/shard_map/all_gather | solution.py:1247
  7.3 13.5 %collective-permute-start.2 = (bf16[1536,512]{1,0:T(8,128)(2,1)}, bf16[1536,512]{1,0:T(8,128)(2,1)}, u32[]{:S(2)}, u32[]{:S(2)}) collective-permute-start(bf16[1536,512]{1,0:T(8,128)(2,1)} %bitcast.360), channel_id=1, source_target_pairs={{0,16},{16,0},{1,17},{17,1},{2,18},{18,2},{3,19},{19,3},{4,20},{20... | collective-permute-start | bytes 4718600 | tf_op jit(solution)/shard_map/ppermute | solution.py:97
  7.8 13.8 %collective-permute-start.1 = (bf16[1536,512]{1,0:T(8,128)(2,1)}, bf16[1536,512]{1,0:T(8,128)(2,1)}, u32[]{:S(2)}, u32[]{:S(2)}) collective-permute-start(bf16[1536,512]{1,0:T(8,128)(2,1)} %bitcast.357), channel_id=1, source_target_pairs={{0,16},{16,0},{1,17},{17,1},{2,18},{18,2},{3,19},{19,3},{4,20},{20... | collective-permute-start | bytes 4718600 | tf_op jit(solution)/shard_map/ppermute | solution.py:97
  7.9 20.3 %collective-permute-start.3 = (bf16[1536,1536]{1,0:T(8,128)(2,1)}, bf16[1536,1536]{1,0:T(8,128)(2,1)}, u32[]{:S(2)}, u32[]{:S(2)}) collective-permute-start(bf16[1536,1536]{1,0:T(8,128)(2,1)} %bitcast.354), channel_id=1, source_target_pairs={{0,16},{16,0},{1,17},{17,1},{2,18},{18,2},{3,19},{19,3},{4,20},{20... | collective-permute-start | bytes 14155784 | tf_op jit(solution)/shard_map/ppermute | solution.py:97
  9.0 6.1 %collective-permute-start = (bf16[1536]{0:T(1024)(128)(2,1)S(1)}, bf16[1536]{0:T(1024)(128)(2,1)S(1)}, u32[]{:S(2)}, u32[]{:S(2)}) collective-permute-start(bf16[1536]{0:T(1024)(128)(2,1)S(1)} %reduce), channel_id=1, source_target_pairs={{0,16},{16,0},{1,17},{17,1},{2,18},{18,2},{3,19},{19,3},{4,20},{20... | collective-permute-start | bytes 9224 | tf_op jit(solution)/shard_map/ppermute | solution.py:97
  9.9 5.4 collective-permute-start.5
  12.1 354.3 %reduce-scatter.3.cloned.1.call-start = ((), (), s32[]{:S(2)}) async-start(), calls=%async_computation.2 | async-start | bytes 7864320 | tf_op jit(solution)/shard_map/reduce_scatter | solution.py:1307
  15.1 4.7 collective-permute-start.6
  15.2 5.2 collective-permute-start.7
  16.2 6.6 %copy-start.93 = (f32[96]{0:T(128)}, f32[96]{0:T(128)S(1)}, u32[]{:S(2)}) copy-start(f32[96]{0:T(128)S(1)} %get-tuple-element.226) | copy-start | bytes 1156
  19.8 39.6 %collective-permute-start.10 = (bf16[4,512,1536]{2,1,0:T(8,128)(2,1)}, bf16[4,512,1536]{2,1,0:T(8,128)(2,1)}, u32[]{:S(2)}, u32[]{:S(2)}) collective-permute-start(bf16[4,512,1536]{2,1,0:T(8,128)(2,1)} %bitcast.349), channel_id=1, source_target_pairs={{0,16},{16,0},{1,17},{17,1},{2,18},{18,2},{3,19},{19,3},{4,20},{20... | collective-permute-start | bytes 18874376 | tf_op jit(solution)/shard_map/ppermute | solution.py:97
  20.4 39.1 %collective-permute-start.8 = (bf16[4,1536,512]{2,1,0:T(8,128)(2,1)}, bf16[4,1536,512]{2,1,0:T(8,128)(2,1)}, u32[]{:S(2)}, u32[]{:S(2)}) collective-permute-start(bf16[4,1536,512]{2,1,0:T(8,128)(2,1)} %bitcast.339), channel_id=1, source_target_pairs={{0,16},{16,0},{1,17},{17,1},{2,18},{18,2},{3,19},{19,3},{4,20},{20... | collective-permute-start | bytes 18874376 | tf_op jit(solution)/shard_map/ppermute | solution.py:97
  20.8 38.7 %collective-permute-start.9 = (bf16[4,1536,512]{2,1,0:T(8,128)(2,1)}, bf16[4,1536,512]{2,1,0:T(8,128)(2,1)}, u32[]{:S(2)}, u32[]{:S(2)}) collective-permute-start(bf16[4,1536,512]{2,1,0:T(8,128)(2,1)} %bitcast.344), channel_id=1, source_target_pairs={{0,16},{16,0},{1,17},{17,1},{2,18},{18,2},{3,19},{19,3},{4,20},{20... | collective-permute-start | bytes 18874376 | tf_op jit(solution)/shard_map/ppermute | solution.py:97
  21.6 33.5 %collective-permute-start.4 = (bf16[1536,1536]{1,0:T(8,128)(2,1)}, bf16[1536,1536]{1,0:T(8,128)(2,1)}, u32[]{:S(2)}, u32[]{:S(2)}) collective-permute-start(bf16[1536,1536]{1,0:T(8,128)(2,1)} %bitcast.284), channel_id=1, source_target_pairs={{0,16},{16,0},{1,17},{17,1},{2,18},{18,2},{3,19},{19,3},{4,20},{20... | collective-permute-start | bytes 14155784 | tf_op jit(solution)/shard_map/ppermute | solution.py:97
  22.7 90.6 %copy-start.80 = (f32[1536]{0:T(1024)}, f32[1536]{0:T(1024)S(1)}, u32[]{:S(2)}) copy-start(f32[1536]{0:T(1024)S(1)} %get-tuple-element.223) | copy-start | bytes 18436
  22.7 36.6 %copy-start.71 = (f32[1536]{0:T(1024)}, f32[1536]{0:T(1024)S(1)}, u32[]{:S(2)}) copy-start(f32[1536]{0:T(1024)S(1)} %get-tuple-element.222) | copy-start | bytes 18436
  22.7 105.5 %copy-start.73 = (f32[1536]{0:T(1024)}, f32[1536]{0:T(1024)S(1)}, u32[]{:S(2)}) copy-start(f32[1536]{0:T(1024)S(1)} %get-tuple-element.221) | copy-start | bytes 18436
  22.9 5.2 copy-start.48
  58.8 52.4 %copy-start.2 = (f32[96,1536]{1,0:T(8,128)}, f32[96,1536]{1,0:T(8,128)S(1)}, u32[]{:S(2)}) copy-start(f32[96,1536]{1,0:T(8,128)S(1)} %get-tuple-element.238.hidden) | copy-start | bytes 1769476
  59.3 51.9 %copy-start.95 = (f32[96]{0:T(128)}, f32[96]{0:T(128)S(1)}, u32[]{:S(2)}) copy-start(f32[96]{0:T(128)S(1)} %get-tuple-element.228) | copy-start | bytes 1156
  59.5 51.7 %copy-start.4 = (bf16[96,1536]{1,0:T(8,128)(2,1)}, bf16[96,1536]{1,0:T(8,128)(2,1)S(1)}, u32[]{:S(2)}) copy-start(bf16[96,1536]{1,0:T(8,128)(2,1)S(1)} %multiply_convert_fusion.3.x) | copy-start | bytes 884740
  113.4 7.0 %copy-start.24 = (bf16[96,1536]{1,0:T(8,128)(2,1)}, bf16[96,1536]{1,0:T(8,128)(2,1)S(1)}, u32[]{:S(2)}) copy-start(bf16[96,1536]{1,0:T(8,128)(2,1)S(1)} %fusion.59) | copy-start | bytes 884740
  115.8 5.2 copy-start.67
  249.8 170.3 %reduce-scatter.5.cloned.1.call-start = ((), (), s32[]{:S(2)}) async-start(), calls=%async_computation.3 | async-start | bytes 7864320 | tf_op jit(solution)/shard_map/reduce_scatter | solution.py:1351
  249.9 138.5 %collective-permute-start.17 = (bf16[96,1536]{1,0:T(8,128)(2,1)}, bf16[96,1536]{1,0:T(8,128)(2,1)}, u32[]{:S(2)}, u32[]{:S(2)}) collective-permute-start(bf16[96,1536]{1,0:T(8,128)(2,1)} %copy-done.48), channel_id=1, source_target_pairs={{0,16},{16,0},{1,17},{17,1},{2,18},{18,2},{3,19},{19,3},{4,20},{20... | collective-permute-start | bytes 884744 | tf_op jit(solution)/shard_map/ppermute | solution.py:97
  249.9 31.1 %collective-permute-start.14 = (bf16[96,1536]{0,1:T(8,128)(2,1)}, bf16[96,1536]{0,1:T(8,128)(2,1)}, u32[]{:S(2)}, u32[]{:S(2)}) collective-permute-start(bf16[96,1536]{0,1:T(8,128)(2,1)} %bitcast.303), channel_id=1, source_target_pairs={{0,16},{16,0},{1,17},{17,1},{2,18},{18,2},{3,19},{19,3},{4,20},{20... | collective-permute-start | bytes 884744 | tf_op jit(solution)/shard_map/ppermute | solution.py:97
  250.4 33.0 %collective-permute-start.12 = (bf16[96,1536]{1,0:T(8,128)(2,1)}, bf16[96,1536]{1,0:T(8,128)(2,1)}, u32[]{:S(2)}, u32[]{:S(2)}) collective-permute-start(bf16[96,1536]{1,0:T(8,128)(2,1)} %copy-done.24), channel_id=1, source_target_pairs={{0,16},{16,0},{1,17},{17,1},{2,18},{18,2},{3,19},{19,3},{4,20},{20... | collective-permute-start | bytes 884744 | tf_op jit(solution)/shard_map/ppermute | solution.py:97
  255.1 5.2 copy-start.77
  255.1 5.2 copy-start.86
  272.4 8.6 %collective-permute-start.15 = (bf16[96,768]{1,0:T(8,128)(2,1)S(1)}, bf16[96,768]{1,0:T(8,128)(2,1)S(1)}, u32[]{:S(2)}, u32[]{:S(2)}) collective-permute-start(bf16[96,768]{1,0:T(8,128)(2,1)S(1)} %get-tuple-element.209), channel_id=1, source_target_pairs={{0,16},{16,0},{1,17},{17,1},{2,18},{18,2},{3,19},{19,3},{4,20},{20... | collective-permute-start | bytes 442376 | tf_op jit(solution)/shard_map/ppermute | solution.py:97
  274.1 9.4 %collective-permute-start.13 = (bf16[96,1280]{0,1:T(8,128)(2,1)S(1)}, bf16[96,1280]{0,1:T(8,128)(2,1)S(1)}, u32[]{:S(2)}, u32[]{:S(2)}) collective-permute-start(bf16[96,1280]{0,1:T(8,128)(2,1)S(1)} %get-tuple-element.195), channel_id=1, source_target_pairs={{0,16},{16,0},{1,17},{17,1},{2,18},{18,2},{3,19},{19,3},{4,20},{20... | collective-permute-start | bytes 737288 | tf_op jit(solution)/shard_map/ppermute | solution.py:97
  276.1 5.4 copy-start.44
  281.0 103.8 %collective-permute-start.19 = (bf16[96,1536]{0,1:T(8,128)(2,1)}, bf16[96,1536]{0,1:T(8,128)(2,1)}, u32[]{:S(2)}, u32[]{:S(2)}) collective-permute-start(bf16[96,1536]{0,1:T(8,128)(2,1)} %bitcast.15), channel_id=1, source_target_pairs={{0,16},{16,0},{1,17},{17,1},{2,18},{18,2},{3,19},{19,3},{4,20},{20... | collective-permute-start | bytes 884744 | tf_op jit(solution)/shard_map/ppermute | solution.py:97
  281.1 71.2 %collective-permute-start.11 = (bf16[96,1536]{1,0:T(8,128)(2,1)S(1)}, bf16[96,1536]{1,0:T(8,128)(2,1)S(1)}, u32[]{:S(2)}, u32[]{:S(2)}) collective-permute-start(bf16[96,1536]{1,0:T(8,128)(2,1)S(1)} %get-tuple-element.197), channel_id=1, source_target_pairs={{0,16},{16,0},{1,17},{17,1},{2,18},{18,2},{3,19},{19,3},{4,20},{20... | collective-permute-start | bytes 884744 | tf_op jit(solution)/shard_map/ppermute | solution.py:97
  292.4 59.7 %copy-start.5 = (bf16[96,1536]{1,0:T(8,128)(2,1)S(1)}, bf16[96,1536]{1,0:T(8,128)(2,1)}, u32[]{:S(2)}) copy-start(bf16[96,1536]{1,0:T(8,128)(2,1)} %copy-done.4) | copy-start | bytes 884740
  351.9 7.2 %copy-start.6 = (bf16[2,128,1536]{2,1,0:T(8,128)(2,1)}, bf16[2,128,1536]{2,1,0:T(8,128)(2,1)S(1)}, u32[]{:S(2)}) copy-start(bf16[2,128,1536]{2,1,0:T(8,128)(2,1)S(1)} %get-tuple-element.118.refs_8_) | copy-start | bytes 2359300
  353.2 5.8 %copy-start.104 = (bf16[2,4,96,2048]{3,2,1,0:T(8,128)(2,1)S(1)}, bf16[2,4,96,2048]{3,2,1,0:T(8,128)(2,1)}, u32[]{:S(2)}) copy-start(bf16[2,4,96,2048]{3,2,1,0:T(8,128)(2,1)} %get-tuple-element.112) | copy-start | bytes 9437188
  353.2 5.8 %copy-start.105 = (bf16[2,4,96,1536]{3,2,1,0:T(8,128)(2,1)S(1)}, bf16[2,4,96,1536]{3,2,1,0:T(8,128)(2,1)}, u32[]{:S(2)}) copy-start(bf16[2,4,96,1536]{3,2,1,0:T(8,128)(2,1)} %get-tuple-element.111) | copy-start | bytes 7077892
  359.1 7.4 %copy-start.3 = (f32[96,1536]{1,0:T(8,128)S(1)}, f32[96,1536]{1,0:T(8,128)}, u32[]{:S(2)}) copy-start(f32[96,1536]{1,0:T(8,128)} %copy-done.2) | copy-start | bytes 1769476
  359.1 7.4 %copy-start.32 = (bf16[1536,16]{1,0:T(8,128)(2,1)S(1)}, bf16[1536,16]{1,0:T(8,128)(2,1)}, u32[]{:S(2)}) copy-start(bf16[1536,16]{1,0:T(8,128)(2,1)} %copy-done.31) | copy-start | bytes 147460
  359.1 7.4 %copy-start.72 = (f32[1536]{0:T(1024)S(1)}, f32[1536]{0:T(1024)}, u32[]{:S(2)}) copy-start(f32[1536]{0:T(1024)} %copy-done.71) | copy-start | bytes 18436
  359.1 7.4 %copy-start.96 = (f32[96]{0:T(128)S(1)}, f32[96]{0:T(128)}, u32[]{:S(2)}) copy-start(f32[96]{0:T(128)} %copy-done.95) | copy-start | bytes 1156
  381.8 3.0 collective-permute-start.20
  382.8 5.6 collective-permute-start.18
  383.6 9.3 %collective-permute-start.16 = (f32[96,1536]{1,0:T(8,128)S(1)}, f32[96,1536]{1,0:T(8,128)S(1)}, u32[]{:S(2)}, u32[]{:S(2)}) collective-permute-start(f32[96,1536]{1,0:T(8,128)S(1)} %get-tuple-element.181), channel_id=1, source_target_pairs={{0,16},{16,0},{1,17},{17,1},{2,18},{18,2},{3,19},{19,3},{4,20},{20... | collective-permute-start | bytes 1769480 | tf_op jit(solution)/shard_map/ppermute | solution.py:97
  (86 other events, 179.5 us)
Sparse Core Ops, SparseCore 0:
  12.2 32.8 all-gather.2
  249.9 98.8 reduce-scatter.2
  351.8 68.2 reduce-scatter.4

commit v13 on v12

--- a/solution.py
+++ b/solution.py
@@ -752,13 +752,25 @@
 ):
     own, other, refs = refs[:3], refs[3:6], refs[6:]
     own_dense, other_dense, refs = refs[:4], refs[4:8], refs[8:]
-    out, rows, gates_all, gates, gate_keep, up_keep, gated, stats = refs[:8]
-    placed, place_sem = refs[8:12], refs[-1]
-    passing, refs = refs[-5:-1], refs[:8] + refs[12:-5]
+    out, rows, gates_all, gates, stats, gate_out, up_out, gated_out = refs[:8]
+    placed, place_sem, keep_sem = refs[8:12], refs[-2], refs[-1]
+    passing, (gate_keep, up_keep, gated) = refs[-9:-5], refs[-5:-2]
+    refs = refs[:8] + refs[12:-9]
     w_gate, w_up, w_down, sums, returned, mixed, total, stats_all = refs[8:16]
     weight_sem, *sems = refs[16:]
     n, held = rows.shape[0], w_gate.shape[0]
     z = lax.axis_index(LINE)
+
+    def keep_copies(block):
+        pairs = (
+            (gate_keep.at[:, block], gate_out.at[:, block]),
+            (up_keep.at[:, block], up_out.at[:, block]),
+            (gated.at[block], gated_out.at[block]),
+        )
+        return [
+            pltpu.make_async_copy(source, target, keep_sem.at[i, block])
+            for i, (source, target) in enumerate(pairs)
+        ]
 
     def compute(block, sent):
         picked = rows[block]
@@ -777,6 +789,8 @@
             return carry
 
         lax.fori_loop(0, held, one, 0)
+        for copy in keep_copies(block):
+            copy.start()
         width = out.shape[1] // PARTS
         for part in range(PARTS):
             at = pl.ds(part * width, width)
@@ -859,10 +873,16 @@
     finish()
     for i in range(4):
         place_out(i).wait()
-
-
-def experts_backward_kernel(layer, grad, gates, gate_keep, up_keep, *refs):
+    for block in range(n):
+        for copy in keep_copies(block):
+            copy.wait()
+
+
+def experts_backward_kernel(layer, grad, gates, *refs):
     own, other, saved_rows, saved_gated, refs = refs[:3], refs[3:6], refs[6], refs[7], refs[8:]
+    kept, refs = refs[:2], refs[2:]
+    keep_places, keep_sem, refs = refs[-3:-1], refs[-1], refs[:-3]
+    gate_keep, up_keep = keep_places
     carried = layer == 0
     if carried:
         extra, refs = refs[0], refs[1:]
@@ -1018,10 +1038,17 @@
         mine = pltpu.make_async_copy(extra.at[:, me], landed.at[me], extra_send.at[len(peers)])
         mine.start()
     wait_weights = fetch_weights(layer, own, other, (w_gate, w_up, w_down), weight_sem)
+    keep_copies = [
+        pltpu.make_async_copy(kept[i], keep_places[i], keep_sem.at[i]) for i in range(2)
+    ]
+    for copy in keep_copies:
+        copy.start()
     for copy in whole_copies() + local_copies():
         copy.start()
     if not gathered:
         rows[z] = grad[...]
+    for copy in keep_copies:
+        copy.wait()
     wait_weights()
     run()
     width = out.shape[1] // PARTS
@@ -1102,10 +1129,10 @@
         jax.ShapeDtypeStruct((n, length, width), low),
         jax.ShapeDtypeStruct((n, length, COLUMNS), low),
         jax.ShapeDtypeStruct((length, COLUMNS), full),
+        jax.ShapeDtypeStruct((8, COLUMNS), full),
         kept,
         kept,
         jax.ShapeDtypeStruct((n, length, held * inner), low),
-        jax.ShapeDtypeStruct((8, COLUMNS), full),
     ] + [jax.ShapeDtypeStruct(array.shape, low) for array in own_dense]
     scratch = [
         pltpu.VMEM((n, length, width), low),
@@ -1116,7 +1143,9 @@
         pltpu.SemaphoreType.DMA((3 * held,)),
     ] + exchange_scratch(n, 3, PARTS)
     scratch += [pltpu.VMEM(array.shape, low) for array in own_dense]
+    scratch += [pltpu.VMEM(shape.shape, low) for shape in shapes[5:8]]
     scratch.append(pltpu.SemaphoreType.DMA((2, 4)))
+    scratch.append(pltpu.SemaphoreType.DMA((3, n)))
     kernel = functools.partial(experts_forward_kernel, layer, experts)
     return expert_call(
         kernel,
@@ -1127,7 +1156,7 @@
         shapes,
         scratch,
         1 + layer,
-        4,
+        7,
     )
 
 
@@ -1163,13 +1192,14 @@
             pltpu.SemaphoreType.DMA((count,)),
             pltpu.SemaphoreType.DMA((count,)),
         ]
+    scratch += [pltpu.VMEM(gate_keep.shape, low)] * 2 + [pltpu.SemaphoreType.DMA((2,))]
     kernel = functools.partial(experts_backward_kernel, layer)
     return expert_call(
         kernel,
-        (grad_low, gates, gate_keep, up_keep),
+        (grad_low, gates),
         own,
         other,
-        (rows, gated) if extra is None else (rows, gated, extra),
+        (rows, gated, gate_keep, up_keep) + (() if extra is None else (extra,)),
         shapes,
         scratch,
         3 + layer,
@@ -1257,9 +1287,11 @@
         inputs = inputs_low.astype(jnp.float32)
         state = attention_forward(inputs, weights[s], segment_row)
         hidden, normed_two = state[7], state[9]
+        if s == 0:
+            normed_two, cotangent_all = lax.optimization_barrier((normed_two, cotangent_all))
         both_cores = [jnp.concatenate([a, swapped(a)]) for a in (state[1], state[6])]
         router = jnp.pad(weights[s][6], ((0, 0), (0, COLUMNS - experts)))
-        inputs_low, *expert_state, stat, query, key, value, out = experts_forward(
+        inputs_low, rows, gates_all, gates, stat, *kept, query, key, value, out = experts_forward(
             s,
             normed_two,
             masks[s],
@@ -1274,6 +1306,7 @@
         weights[1 - s][1:5] = [query, key, value, out]
         outs.append(inputs_low)
         stats.append(stat)
+        expert_state = (rows, gates_all, gates, *kept)
         saved.append((inputs, state, expert_state, both_cores))
 
     dp, deep = lax.axis_size(GROUP), lax.axis_size(LINE)

time: 583 us -> 575 us (0.986)
    unnamed x224 -> x186, local copies, waits for them, and re-layouts: 30 us -> 22.5 us
  transfers between devices with their start and end apart: 24 -> 24, of which waited for: 4 -> 4; matrix products, arithmetic and copies ran while one was open for 19% -> 16% of each run, Pallas kernels for 28% -> 11%
where the time goes in v13:
time: 575 us; the launch traced here: 567 us
  Pallas kernels  351 us (61%)
  matrix products  83.4 us (15%)
  waiting for transfers between devices  50.6 us (9%)
  local copies, waits for them, and re-layouts  34.3 us (6%)
  other arithmetic  26 us (5%)
  between operations  15.7 us (3%)
  starting transfers between devices  6.07 us (1%)
    pallas_call x4, Pallas kernels, expert_call(): pl.pallas_call(kernel, out_shape=shapes, in_specs=[vmem] * len(operands)...  215 us
    pallas_call x1, Pallas kernels, sum_scatter(): pl.pallas_call(functools.partial(sum_scatter_kernel, (plans, len(arrays),...  136 us
    dot_general x10, matrix products, turned(): jnp.einsum('tc,tq->cq', left, right, preferred_element_type=jnp.float32)  39.3 us
    ppermute x21, waiting for transfers between devices, swapped(): return lax.ppermute(array, CORE, [(0, 1), (1, 0)])  25.7 us
    reduce_scatter x1, waiting for transfers between devices, body(): lax.psum_scatter(dense, GROUP, scatter_dimension=0, tiled=True)  24.9 us
    unnamed x186, local copies, waits for them, and re-layouts  22.5 us
    dot_general x8, matrix products, matmul(): return jnp.dot(left_side, right_side, preferred_element_type=jnp.float32)  21 us
  transfers between devices with their start and end apart: 24, of which 4 were waited for; matrix products, arithmetic and copies ran while one was open for 16% of the time, Pallas kernels for 11%

profile of v13, /device:TPU:0, one launch (start us, length us, event | category | flops | bytes accessed | tf_op | source)
XLA Modules:
  0.0 566.8 jit_solution(4150137074627498768)
XLA Ops:
  10.4 1.7 constant_dynamic-slice_fusion.9
  12.9 1.1 fusion.48
  16.2 3.6 collective-permute-done.6
  22.8 1.4 copy-done.82
  24.9 2.2 fusion.13
  27.2 4.4 fusion.4
  33.3 21.8 %collective-permute-done.4.refs_13_ = bf16[1536,1536]{1,0:T(8,128)(2,1)} collective-permute-done((bf16[1536,1536]{1,0:T(8,128)(2,1)}, bf16[1536,1536]{1,0:T(8,128)(2,1)}, u32[]{:S(2)}, u32[]{:S(2)}) %collective-permute-start.4) | collective-permute-done | bytes 4718624 | tf_op jit(solution)/shard_map/ppermute | solution.py:97
  55.1 3.6 multiply_reduce_fusion.7
  59.8 52.8 %shard_map.237 = (bf16[96,1536]{1,0:T(8,128)(2,1)S(1)}, bf16[4,96,1536]{2,1,0:T(8,128)(2,1)S(1)}, bf16[4,96,128]{2,1,0:T(8,128)(2,1)S(1)}, f32[96,128]{1,0:T(8,1...) custom-call(bf16[96,1536]{1,0:T(8,128)(2,1)S(1)} %multiply_convert_f, ...), custom_call_target="tpu_custom_call" | custom-call | flops 49999998976 | bytes 100000000 | tf_op jit(solution)/shard_map/pallas_call | solution.py:1104
  112.6 1.1 copy-done.13
  113.7 1.0 copy-done.16
  115.7 2.2 fusion.117
  118.1 4.4 fusion.118
  124.8 3.4 multiply_reduce_fusion.6
  128.9 50.6 %shard_map.238 = (bf16[96,1536]{1,0:T(8,128)(2,1)S(1)}, bf16[4,96,1536]{2,1,0:T(8,128)(2,1)S(1)}, bf16[4,96,128]{2,1,0:T(8,128)(2,1)S(1)}, f32[96,128]{1,0:T(8,1...) custom-call(bf16[96,1536]{1,0:T(8,128)(2,1)S(1)} %multiply_convert_f, ...), custom_call_target="tpu_custom_call" | custom-call | flops 49999998976 | bytes 100000000 | tf_op jit(solution)/shard_map/pallas_call | solution.py:1104
  179.5 1.1 copy-done.15
  180.6 50.6 %shard_map.239 = (f32[96,1536]{1,0:T(8,128)S(1)}, f32[96,128]{1,0:T(8,128)S(1)}, bf16[2,4,96,1536]{3,2,1,0:T(8,128)(2,1)}, bf16[2,4,96,1024]{3,2,1,0:T(8,128)(2,...) custom-call(bf16[4,96,1536]{2,1,0:T(8,128)(2,1)S(1)} %bitcast.278, ...), custom_call_target="tpu_custom_call" | custom-call | flops 49999998976 | bytes 100000000 | tf_op jit(solution)/shard_map/pallas_call | solution.py:1104
  231.2 1.1 copy-done.8
  232.4 9.1 %bitcast_convert_fusion.1 = bf16[1536,2048]{1,0:T(8,128)(2,1)} fusion(bf16[2,4,96,1536]{3,2,1,0:T(8,128)(2,1)} %get-tuple-element.88, bf16[2,4,96,2048]{3,2,1,0:T(8,128)(2,1)} %get-tuple-element.89), kind=kOutput, calls=%fused_computation.3 | convolution fusion | flops 4834983936 | bytes 11796480 | tf_op jit(solution)/shard_map/tc,tq->cq/dot_general | solution.py:1260
  242.5 1.1 multiply_reduce_fusion.2
  243.6 1.7 fusion.113
  245.3 4.7 convolution_convert_fusion.5
  250.0 1.9 copy.96
  251.9 1.4 multiply_reduce_fusion.1
  258.2 1.0 copy-done.20
  259.9 1.7 fusion.65
  264.1 1.1 broadcast_select_fusion.3
  266.2 4.3 bitcast_convert_fusion.3
  271.6 1.9 convolution_convert_fusion.3
  273.4 2.5 convolution_convert_fusion.1
  276.0 3.6 pad_maximum_fusion
  279.6 1.4 copy-done.11
  281.0 1.5 copy-done.14
  282.5 1.3 copy-done.17
  283.8 60.6 %shard_map.240 = (f32[96,1536]{1,0:T(8,128)S(1)}, f32[96,128]{1,0:T(8,128)S(1)}, bf16[2,4,96,1536]{3,2,1,0:T(8,128)(2,1)}, bf16[2,4,96,1024]{3,2,1,0:T(8,128)(2,...) custom-call(bf16[96,1536]{1,0:T(8,128)(2,1)S(1)} %get-tuple-element.97, ...), custom_call_target="tpu_custom_call" | custom-call | flops 49999998976 | bytes 100000000 | tf_op jit(solution)/shard_map/pallas_call | solution.py:1104
  345.7 5.9 %bitcast_convert_fusion.2 = bf16[1024,1536]{1,0:T(8,128)(2,1)} fusion(bf16[2,4,96,1024]{3,2,1,0:T(8,128)(2,1)S(1)} %get-tuple-element.117, bf16[2,4,96,1536]{3,2,1,0:T(8,128)(2,1)} %get-tuple-element.118), kind=kOutput, calls=%fused_computation.7 | convolution fusion | flops 2417491968 | bytes 7077888 | tf_op jit(solution)/shard_map/tc,tq->cq/dot_general | solution.py:1260
  351.6 7.3 %bitcast_convert_fusion = bf16[1536,2048]{1,0:T(8,128)(2,1)} fusion(bf16[2,4,96,1536]{3,2,1,0:T(8,128)(2,1)S(1)} %copy-done.86, bf16[2,4,96,2048]{3,2,1,0:T(8,128)(2,1)S(1)} %copy-done.85), kind=kOutput, calls=%fused_computation.2 | convolution fusion | flops 4834983936 | bytes 11796480 | tf_op jit(solution)/shard_map/tc,tq->cq/dot_general | solution.py:1260
  359.9 4.4 convolution_convert_fusion.4
  365.2 1.4 multiply_reduce_fusion
  372.8 1.7 fusion.56
  378.2 3.4 convolution_convert_fusion.2
  381.6 4.6 convolution_convert_fusion
  386.2 1.1 maximum_select_fusion
  387.4 24.9 %reduce-scatter.5.cloned.1.call-done = bf16[384,2048]{1,0:T(8,128)(2,1)} async-done(((bf16[1536,2048]{1,0:T(8,128)(2,1)}), bf16[384,2048]{1,0:T(8,128)(2,1)}) %reduce-scatter.5.cloned.1.call-update) | async-done | bytes 1572880 | tf_op jit(solution)/shard_map/reduce_scatter | solution.py:1384
  412.3 136.2 %shard_map.241 = (bf16[2,2,384,512]{3,2,1,0:T(8,128)(2,1)}, bf16[2,2,384,512]{3,2,1,0:T(8,128)(2,1)}, bf16[2,2,128,1536]{3,2,1,0:T(8,128)(2,1)}, bf16[2,96,1280]...) custom-call(bf16[4,384,2048]{2,1,0:T(8,128)(2,1)} %bitcast.283, ...), custom_call_target="tpu_custom_call" | custom-call | tf_op jit(solution)/shard_map/pallas_call | solution.py:451
  548.4 1.1 slice_bitcast_fusion.2
  551.3 2.1 bitcast_convert_fusion.4
  555.4 3.6 bitcast_convert_fusion.5
  (325 shorter events, 44.5 us)
Async XLA Ops:
  7.2 13.7 %copy-start = (s32[2,96]{1,0:T(2,128)S(1)}, s32[2,96]{1,0:T(2,128)}, u32[]{:S(2)}) copy-start(s32[2,96]{1,0:T(2,128)} %param.16) | copy-start | bytes 2308
  7.2 14.4 %copy-start.70 = (s32[1,192,8]{1,2,0:T(8,128)S(1)}, s32[1,192,8]{1,2,0:T(8,128)}, u32[]{:S(2)}) copy-start(s32[1,192,8]{1,2,0:T(8,128)} %param.17) | copy-start | bytes 18436
  7.2 15.0 %copy-start.21 = (bf16[192,1536]{1,0:T(8,128)(2,1)S(1)}, bf16[192,1536]{1,0:T(8,128)(2,1)}, u32[]{:S(2)}) copy-start(bf16[192,1536]{1,0:T(8,128)(2,1)} %param.14) | copy-start | bytes 1769476
  7.2 52.2 %all-gather.3.cloned.1.call-start = ((), (), s32[]{:S(2)}) async-start(), calls=%async_computation.4 | async-start | bytes 1474560 | tf_op jit(solution)/shard_map/all_gather | solution.py:1277
  7.3 13.5 %collective-permute-start.2 = (bf16[1536,512]{1,0:T(8,128)(2,1)}, bf16[1536,512]{1,0:T(8,128)(2,1)S(1)}, u32[]{:S(2)}, u32[]{:S(2)}) collective-permute-start(bf16[1536,512]{1,0:T(8,128)(2,1)} %bitcast.363), channel_id=1, source_target_pairs={{0,16},{16,0},{1,17},{17,1},{2,18},{18,2},{3,19},{19,3},{4,20},{20... | collective-permute-start | bytes 4718600 | tf_op jit(solution)/shard_map/ppermute | solution.py:97
  7.8 13.2 %collective-permute-start.1 = (bf16[1536,512]{1,0:T(8,128)(2,1)}, bf16[1536,512]{1,0:T(8,128)(2,1)}, u32[]{:S(2)}, u32[]{:S(2)}) collective-permute-start(bf16[1536,512]{1,0:T(8,128)(2,1)} %bitcast.360), channel_id=1, source_target_pairs={{0,16},{16,0},{1,17},{17,1},{2,18},{18,2},{3,19},{19,3},{4,20},{20... | collective-permute-start | bytes 4718600 | tf_op jit(solution)/shard_map/ppermute | solution.py:97
  7.9 19.3 %collective-permute-start.3 = (bf16[1536,1536]{1,0:T(8,128)(2,1)}, bf16[1536,1536]{1,0:T(8,128)(2,1)}, u32[]{:S(2)}, u32[]{:S(2)}) collective-permute-start(bf16[1536,1536]{1,0:T(8,128)(2,1)} %bitcast.357), channel_id=1, source_target_pairs={{0,16},{16,0},{1,17},{17,1},{2,18},{18,2},{3,19},{19,3},{4,20},{20... | collective-permute-start | bytes 14155784 | tf_op jit(solution)/shard_map/ppermute | solution.py:97
  9.0 6.1 %collective-permute-start = (bf16[1536]{0:T(1024)(128)(2,1)S(1)}, bf16[1536]{0:T(1024)(128)(2,1)S(1)}, u32[]{:S(2)}, u32[]{:S(2)}) collective-permute-start(bf16[1536]{0:T(1024)(128)(2,1)S(1)} %reduce), channel_id=1, source_target_pairs={{0,16},{16,0},{1,17},{17,1},{2,18},{18,2},{3,19},{19,3},{4,20},{20... | collective-permute-start | bytes 9224 | tf_op jit(solution)/shard_map/ppermute | solution.py:97
  9.9 5.4 collective-permute-start.5
  12.1 346.9 %reduce-scatter.3.cloned.1.call-start = ((), (), s32[]{:S(2)}) async-start(), calls=%async_computation.2 | async-start | bytes 7864320 | tf_op jit(solution)/shard_map/reduce_scatter | solution.py:1340
  15.1 4.7 collective-permute-start.6
  15.2 5.2 collective-permute-start.7
  16.2 6.4 %copy-start.73 = (f32[96]{0:T(128)}, f32[96]{0:T(128)S(1)}, u32[]{:S(2)}) copy-start(f32[96]{0:T(128)S(1)} %get-tuple-element.230) | copy-start | bytes 1156
  19.8 39.6 %collective-permute-start.10 = (bf16[4,512,1536]{2,1,0:T(8,128)(2,1)}, bf16[4,512,1536]{2,1,0:T(8,128)(2,1)}, u32[]{:S(2)}, u32[]{:S(2)}) collective-permute-start(bf16[4,512,1536]{2,1,0:T(8,128)(2,1)} %bitcast.352), channel_id=1, source_target_pairs={{0,16},{16,0},{1,17},{17,1},{2,18},{18,2},{3,19},{19,3},{4,20},{20... | collective-permute-start | bytes 18874376 | tf_op jit(solution)/shard_map/ppermute | solution.py:97
  20.4 39.0 %collective-permute-start.8 = (bf16[4,1536,512]{2,1,0:T(8,128)(2,1)}, bf16[4,1536,512]{2,1,0:T(8,128)(2,1)}, u32[]{:S(2)}, u32[]{:S(2)}) collective-permute-start(bf16[4,1536,512]{2,1,0:T(8,128)(2,1)} %bitcast.342), channel_id=1, source_target_pairs={{0,16},{16,0},{1,17},{17,1},{2,18},{18,2},{3,19},{19,3},{4,20},{20... | collective-permute-start | bytes 18874376 | tf_op jit(solution)/shard_map/ppermute | solution.py:97
  20.8 38.7 %collective-permute-start.9 = (bf16[4,1536,512]{2,1,0:T(8,128)(2,1)}, bf16[4,1536,512]{2,1,0:T(8,128)(2,1)}, u32[]{:S(2)}, u32[]{:S(2)}) collective-permute-start(bf16[4,1536,512]{2,1,0:T(8,128)(2,1)} %bitcast.347), channel_id=1, source_target_pairs={{0,16},{16,0},{1,17},{17,1},{2,18},{18,2},{3,19},{19,3},{4,20},{20... | collective-permute-start | bytes 18874376 | tf_op jit(solution)/shard_map/ppermute | solution.py:97
  21.0 34.1 %collective-permute-start.4 = (bf16[1536,1536]{1,0:T(8,128)(2,1)}, bf16[1536,1536]{1,0:T(8,128)(2,1)}, u32[]{:S(2)}, u32[]{:S(2)}) collective-permute-start(bf16[1536,1536]{1,0:T(8,128)(2,1)} %bitcast.284), channel_id=1, source_target_pairs={{0,16},{16,0},{1,17},{17,1},{2,18},{18,2},{3,19},{19,3},{4,20},{20... | collective-permute-start | bytes 14155784 | tf_op jit(solution)/shard_map/ppermute | solution.py:97
  22.2 37.1 %copy-start.60 = (f32[1536]{0:T(1024)}, f32[1536]{0:T(1024)S(1)}, u32[]{:S(2)}) copy-start(f32[1536]{0:T(1024)S(1)} %get-tuple-element.226) | copy-start | bytes 18436
  24.8 7.5 %copy-start.62 = (bf16[96,512]{0,1:T(8,128)(2,1)}, bf16[96,512]{0,1:T(8,128)(2,1)S(1)}, u32[]{:S(2)}) copy-start(bf16[96,512]{0,1:T(8,128)(2,1)S(1)} %copy.86) | copy-start | bytes 294916
  33.3 25.4 %copy-start.28 = (bf16[8,64,3,96]{3,1,2,0:T(8,128)(2,1)}, bf16[8,64,3,96]{3,1,2,0:T(8,128)(2,1)S(1)}, u32[]{:S(2)}) copy-start(bf16[8,64,3,96]{3,1,2,0:T(8,128)(2,1)S(1)} %convolution_convert_fusion.9) | copy-start | bytes 884740
  58.7 53.9 %copy-start.2 = (f32[96,1536]{1,0:T(8,128)}, f32[96,1536]{1,0:T(8,128)S(1)}, u32[]{:S(2)}) copy-start(f32[96,1536]{1,0:T(8,128)S(1)} %get-tuple-element.242.hidden) | copy-start | bytes 1769476
  59.4 53.2 %copy-start.4 = (bf16[96,1536]{1,0:T(8,128)(2,1)}, bf16[96,1536]{1,0:T(8,128)(2,1)S(1)}, u32[]{:S(2)}) copy-start(bf16[96,1536]{1,0:T(8,128)(2,1)S(1)} %multiply_convert_fusion.3.x) | copy-start | bytes 884740
  118.1 5.1 copy-start.58
  128.7 50.8 %copy-start.77 = (f32[96]{0:T(128)}, f32[96]{0:T(128)S(1)}, u32[]{:S(2)}) copy-start(f32[96]{0:T(128)S(1)} %get-tuple-element.236) | copy-start | bytes 1156
  128.8 51.8 %copy-start.7 = (bf16[384,1536]{1,0:T(8,128)(2,1)S(1)}, bf16[384,1536]{1,0:T(8,128)(2,1)}, u32[]{:S(2)}) copy-start(bf16[384,1536]{1,0:T(8,128)(2,1)} %all-gather.3.cloned.1.call-done) | copy-start | bytes 3538948
  241.5 170.7 %reduce-scatter.5.cloned.1.call-start = ((), (), s32[]{:S(2)}) async-start(), calls=%async_computation.3 | async-start | bytes 7864320 | tf_op jit(solution)/shard_map/reduce_scatter | solution.py:1384
  241.6 140.0 %collective-permute-start.17 = (bf16[96,1536]{1,0:T(8,128)(2,1)}, bf16[96,1536]{1,0:T(8,128)(2,1)}, u32[]{:S(2)}, u32[]{:S(2)}) collective-permute-start(bf16[96,1536]{1,0:T(8,128)(2,1)} %copy-done.40), channel_id=1, source_target_pairs={{0,16},{16,0},{1,17},{17,1},{2,18},{18,2},{3,19},{19,3},{4,20},{20... | collective-permute-start | bytes 884744 | tf_op jit(solution)/shard_map/ppermute | solution.py:97
  241.7 29.5 %collective-permute-start.14 = (bf16[96,1536]{0,1:T(8,128)(2,1)S(1)}, bf16[96,1536]{0,1:T(8,128)(2,1)}, u32[]{:S(2)}, u32[]{:S(2)}) collective-permute-start(bf16[96,1536]{0,1:T(8,128)(2,1)S(1)} %bitcast.306), channel_id=1, source_target_pairs={{0,16},{16,0},{1,17},{17,1},{2,18},{18,2},{3,19},{19,3},{4,20},{20... | collective-permute-start | bytes 884744 | tf_op jit(solution)/shard_map/ppermute | solution.py:97
  242.2 31.2 %collective-permute-start.12 = (bf16[96,1536]{1,0:T(8,128)(2,1)S(1)}, bf16[96,1536]{1,0:T(8,128)(2,1)}, u32[]{:S(2)}, u32[]{:S(2)}) collective-permute-start(bf16[96,1536]{1,0:T(8,128)(2,1)S(1)} %fusion.59), channel_id=1, source_target_pairs={{0,16},{16,0},{1,17},{17,1},{2,18},{18,2},{3,19},{19,3},{4,20},{20... | collective-permute-start | bytes 884744 | tf_op jit(solution)/shard_map/ppermute | solution.py:97
  245.3 6.6 %copy-start.38 = (f32[8,3,96,96]{2,3,1,0:T(8,128)S(1)}, f32[8,3,96,96]{2,3,1,0:T(8,128)}, u32[]{:S(2)}) copy-start(f32[8,3,96,96]{2,3,1,0:T(8,128)} %copy-done.37) | copy-start | bytes 2654212
  263.0 8.0 %collective-permute-start.15 = (bf16[96,768]{1,0:T(8,128)(2,1)S(1)}, bf16[96,768]{1,0:T(8,128)(2,1)S(1)}, u32[]{:S(2)}, u32[]{:S(2)}) collective-permute-start(bf16[96,768]{1,0:T(8,128)(2,1)S(1)} %get-tuple-element.213), channel_id=1, source_target_pairs={{0,16},{16,0},{1,17},{17,1},{2,18},{18,2},{3,19},{19,3},{4,20},{20... | collective-permute-start | bytes 442376 | tf_op jit(solution)/shard_map/ppermute | solution.py:97
  263.6 9.8 %collective-permute-start.13 = (bf16[96,1280]{0,1:T(8,128)(2,1)S(1)}, bf16[96,1280]{0,1:T(8,128)(2,1)S(1)}, u32[]{:S(2)}, u32[]{:S(2)}) collective-permute-start(bf16[96,1280]{0,1:T(8,128)(2,1)S(1)} %get-tuple-element.199), channel_id=1, source_target_pairs={{0,16},{16,0},{1,17},{17,1},{2,18},{18,2},{3,19},{19,3},{4,20},{20... | collective-permute-start | bytes 737288 | tf_op jit(solution)/shard_map/ppermute | solution.py:97
  271.0 107.2 %collective-permute-start.19 = (bf16[96,1536]{0,1:T(8,128)(2,1)S(1)}, bf16[96,1536]{0,1:T(8,128)(2,1)}, u32[]{:S(2)}, u32[]{:S(2)}) collective-permute-start(bf16[96,1536]{0,1:T(8,128)(2,1)S(1)} %bitcast.298), channel_id=1, source_target_pairs={{0,16},{16,0},{1,17},{17,1},{2,18},{18,2},{3,19},{19,3},{4,20},{20... | collective-permute-start | bytes 884744 | tf_op jit(solution)/shard_map/ppermute | solution.py:97
  271.2 73.6 %collective-permute-start.11 = (bf16[96,1536]{1,0:T(8,128)(2,1)}, bf16[96,1536]{1,0:T(8,128)(2,1)S(1)}, u32[]{:S(2)}, u32[]{:S(2)}) collective-permute-start(bf16[96,1536]{1,0:T(8,128)(2,1)} %get-tuple-element.201), channel_id=1, source_target_pairs={{0,16},{16,0},{1,17},{17,1},{2,18},{18,2},{3,19},{19,3},{4,20},{20... | collective-permute-start | bytes 884744 | tf_op jit(solution)/shard_map/ppermute | solution.py:97
  283.8 60.8 %copy-start.5 = (bf16[96,1536]{1,0:T(8,128)(2,1)S(1)}, bf16[96,1536]{1,0:T(8,128)(2,1)}, u32[]{:S(2)}) copy-start(bf16[96,1536]{1,0:T(8,128)(2,1)} %copy-done.4) | copy-start | bytes 884740
  344.4 7.2 %copy-start.6 = (bf16[2,128,1536]{2,1,0:T(8,128)(2,1)}, bf16[2,128,1536]{2,1,0:T(8,128)(2,1)S(1)}, u32[]{:S(2)}) copy-start(bf16[2,128,1536]{2,1,0:T(8,128)(2,1)S(1)} %get-tuple-element.122.refs_8_) | copy-start | bytes 2359300
  345.7 5.9 %copy-start.85 = (bf16[2,4,96,2048]{3,2,1,0:T(8,128)(2,1)S(1)}, bf16[2,4,96,2048]{3,2,1,0:T(8,128)(2,1)}, u32[]{:S(2)}) copy-start(bf16[2,4,96,2048]{3,2,1,0:T(8,128)(2,1)} %get-tuple-element.116) | copy-start | bytes 9437188
  345.7 5.9 %copy-start.86 = (bf16[2,4,96,1536]{3,2,1,0:T(8,128)(2,1)S(1)}, bf16[2,4,96,1536]{3,2,1,0:T(8,128)(2,1)}, u32[]{:S(2)}) copy-start(bf16[2,4,96,1536]{3,2,1,0:T(8,128)(2,1)} %get-tuple-element.115) | copy-start | bytes 7077892
  351.6 7.4 %copy-start.3 = (f32[96,1536]{1,0:T(8,128)S(1)}, f32[96,1536]{1,0:T(8,128)}, u32[]{:S(2)}) copy-start(f32[96,1536]{1,0:T(8,128)} %copy-done.2) | copy-start | bytes 1769476
  351.6 7.4 %copy-start.24 = (bf16[1536,16]{1,0:T(8,128)(2,1)S(1)}, bf16[1536,16]{1,0:T(8,128)(2,1)}, u32[]{:S(2)}) copy-start(bf16[1536,16]{1,0:T(8,128)(2,1)} %copy-done.23) | copy-start | bytes 147460
  351.6 7.4 %copy-start.61 = (f32[1536]{0:T(1024)S(1)}, f32[1536]{0:T(1024)}, u32[]{:S(2)}) copy-start(f32[1536]{0:T(1024)} %copy-done.60) | copy-start | bytes 18436
  351.6 7.4 %copy-start.76 = (f32[96]{0:T(128)S(1)}, f32[96]{0:T(128)}, u32[]{:S(2)}) copy-start(f32[96]{0:T(128)} %copy-done.75) | copy-start | bytes 1156
  359.8 5.3 copy-start.36
  359.9 5.3 copy-start.63
  359.9 5.3 copy-start.69
  375.2 3.0 collective-permute-start.20
  376.2 5.4 collective-permute-start.18
  377.0 9.2 %collective-permute-start.16 = (f32[96,1536]{1,0:T(8,128)S(1)}, f32[96,1536]{1,0:T(8,128)S(1)}, u32[]{:S(2)}, u32[]{:S(2)}) collective-permute-start(f32[96,1536]{1,0:T(8,128)S(1)} %get-tuple-element.185), channel_id=1, source_target_pairs={{0,16},{16,0},{1,17},{17,1},{2,18},{18,2},{3,19},{19,3},{4,20},{20... | collective-permute-start | bytes 1769480 | tf_op jit(solution)/shard_map/ppermute | solution.py:97
  (67 other events, 134.6 us)
Sparse Core Ops, SparseCore 0:
  12.2 32.8 all-gather.2
  241.7 99.2 reduce-scatter.2
  344.0 68.2 reduce-scatter.4

commit v14 on v13

--- a/solution.py
+++ b/solution.py
@@ -629,6 +629,12 @@
         def _():
             sum_copy(way, block, p).start()
 
+    def between(block):
+        if held:
+            @pl.when(block == z)
+            def _():
+                take(0)
+
     def run():
         def both(hop):
             return (hop >= 0) & (z - 1 - hop >= 0) & (z + 1 + hop < n)
@@ -638,7 +644,7 @@
             block = z + (1 + hop) * (1 - 2 * lax.rem(k, 2))
             odd = lax.rem(k, 2) == 1
 
-            @pl.when(odd & jnp.logical_not(both(hop - 1)))
+            @pl.when(odd & (hop > 0) & jnp.logical_not(both(hop - 1)))
             def _():
                 take(hop)
 
@@ -648,7 +654,7 @@
 
             @pl.when((block >= 0) & (block < n))
             def _():
-                compute(block, sent)
+                compute(block, sent, between)
 
             return carry
 
@@ -657,11 +663,14 @@
 
             @pl.when((block >= 0) & (block < n))
             def _():
-                compute(block, sent)
+                compute(block, sent, between)
 
             return carry
 
-        lax.fori_loop(0, 2 * n - 1, turn if held else far_first, 0)
+        if held:
+            lax.fori_loop(0, 2 * n - 1, turn, 0)
+        else:
+            lax.fori_loop(0, 2 * n - 2, far_first, 0)
 
         first = jnp.where(2 * z < n, 0, 1)
         for way in (first, 1 - first):
@@ -677,6 +686,9 @@
                             own[...].astype(jnp.float32) + other[...].astype(jnp.float32)
                         ).astype(jnp.bfloat16)
                         sum_copy(way, block, p).start()
+
+        if not held:
+            compute(z, sent, between)
 
     def collect(add):
         for way in range(2):
@@ -772,7 +784,7 @@
             for i, (source, target) in enumerate(pairs)
         ]
 
-    def compute(block, sent):
+    def compute(block, sent, between):
         picked = rows[block]
         gate_block = gates_all[block].astype(jnp.float32)
 
@@ -789,6 +801,7 @@
             return carry
 
         lax.fori_loop(0, held, one, 0)
+        between(block)
         for copy in keep_copies(block):
             copy.start()
         width = out.shape[1] // PARTS
@@ -950,7 +963,7 @@
             device_id_type=MESH,
         )
 
-    def compute(block, sent):
+    def compute(block, sent, between):
         picked = rows[block]
         gate_block = gates[block].astype(jnp.float32)
         dots[...] = jnp.zeros(dots.shape, jnp.float32)
@@ -987,6 +1000,7 @@
         for copy in block_copies(block):
             copy.start()
         lax.fori_loop(0, half, own_half, 0)
+        between(block)
         sum_gates[block] = dots[...].astype(jnp.bfloat16)
 
         @pl.when(block == z)

time: 575 us -> 564 us (0.981)
  Pallas kernels: 351 us -> 340 us
    pallas_call x4, Pallas kernels: 215 us -> 204 us  [expert_call(): pl.pallas_call(kernel, out_shape=shapes, in_specs=[vmem] * len(operands)...]
where the time goes in v14:
time: 564 us; the launch traced here: 556 us
  Pallas kernels  340 us (60%)
  matrix products  83.3 us (15%)
  waiting for transfers between devices  50.9 us (9%)
  local copies, waits for them, and re-layouts  34.2 us (6%)
  other arithmetic  26 us (5%)
  between operations  15.5 us (3%)
  starting transfers between devices  6.07 us (1%)
    pallas_call x4, Pallas kernels, expert_call(): pl.pallas_call(kernel, out_shape=shapes, in_specs=[vmem] * len(operands)...  204 us
    pallas_call x1, Pallas kernels, sum_scatter(): pl.pallas_call(functools.partial(sum_scatter_kernel, (plans, len(arrays),...  136 us
    dot_general x10, matrix products, turned(): jnp.einsum('tc,tq->cq', left, right, preferred_element_type=jnp.float32)  39.3 us
    ppermute x21, waiting for transfers between devices, swapped(): return lax.ppermute(array, CORE, [(0, 1), (1, 0)])  25.7 us
    reduce_scatter x1, waiting for transfers between devices, body(): lax.psum_scatter(dense, GROUP, scatter_dimension=0, tiled=True)  25.1 us
    unnamed x186, local copies, waits for them, and re-layouts  22.4 us
    dot_general x8, matrix products, matmul(): return jnp.dot(left_side, right_side, preferred_element_type=jnp.float32)  21 us
  transfers between devices with their start and end apart: 24, of which 4 were waited for; matrix products, arithmetic and copies ran while one was open for 16% of the time, Pallas kernels for 11%

profile of v14, /device:TPU:0, one launch (start us, length us, event | category | flops | bytes accessed | tf_op | source)
XLA Modules:
  0.0 555.9 jit_solution(12849726035232353992)
XLA Ops:
  10.4 1.7 constant_dynamic-slice_fusion.9
  12.9 1.1 fusion.48
  16.2 3.6 collective-permute-done.6
  22.8 1.4 copy-done.82
  24.8 2.2 fusion.13
  27.2 4.4 fusion.4
  33.3 21.8 %collective-permute-done.4.refs_13_ = bf16[1536,1536]{1,0:T(8,128)(2,1)} collective-permute-done((bf16[1536,1536]{1,0:T(8,128)(2,1)}, bf16[1536,1536]{1,0:T(8,128)(2,1)}, u32[]{:S(2)}, u32[]{:S(2)}) %collective-permute-start.4) | collective-permute-done | bytes 4718624 | tf_op jit(solution)/shard_map/ppermute | solution.py:97
  55.1 3.6 multiply_reduce_fusion.7
  59.8 51.0 %shard_map.237 = (bf16[96,1536]{1,0:T(8,128)(2,1)S(1)}, bf16[4,96,1536]{2,1,0:T(8,128)(2,1)S(1)}, bf16[4,96,128]{2,1,0:T(8,128)(2,1)S(1)}, f32[96,128]{1,0:T(8,1...) custom-call(bf16[96,1536]{1,0:T(8,128)(2,1)S(1)} %multiply_convert_f, ...), custom_call_target="tpu_custom_call" | custom-call | flops 49999998976 | bytes 100000000 | tf_op jit(solution)/shard_map/pallas_call | solution.py:1118
  110.8 1.1 copy-done.13
  111.9 1.0 copy-done.16
  113.9 2.2 fusion.117
  116.3 4.4 fusion.118
  123.0 3.4 multiply_reduce_fusion.6
  127.1 48.8 %shard_map.238 = (bf16[96,1536]{1,0:T(8,128)(2,1)S(1)}, bf16[4,96,1536]{2,1,0:T(8,128)(2,1)S(1)}, bf16[4,96,128]{2,1,0:T(8,128)(2,1)S(1)}, f32[96,128]{1,0:T(8,1...) custom-call(bf16[96,1536]{1,0:T(8,128)(2,1)S(1)} %multiply_convert_f, ...), custom_call_target="tpu_custom_call" | custom-call | flops 49999998976 | bytes 100000000 | tf_op jit(solution)/shard_map/pallas_call | solution.py:1118
  175.9 1.1 copy-done.15
  177.1 43.7 %shard_map.239 = (f32[96,1536]{1,0:T(8,128)S(1)}, f32[96,128]{1,0:T(8,128)S(1)}, bf16[2,4,96,1536]{3,2,1,0:T(8,128)(2,1)}, bf16[2,4,96,1024]{3,2,1,0:T(8,128)(2,...) custom-call(bf16[4,96,1536]{2,1,0:T(8,128)(2,1)S(1)} %bitcast.278, ...), custom_call_target="tpu_custom_call" | custom-call | flops 49999998976 | bytes 100000000 | tf_op jit(solution)/shard_map/pallas_call | solution.py:1118
  220.8 1.1 copy-done.8
  221.9 9.1 %bitcast_convert_fusion.1 = bf16[1536,2048]{1,0:T(8,128)(2,1)} fusion(bf16[2,4,96,1536]{3,2,1,0:T(8,128)(2,1)} %get-tuple-element.88, bf16[2,4,96,2048]{3,2,1,0:T(8,128)(2,1)} %get-tuple-element.89), kind=kOutput, calls=%fused_computation.3 | convolution fusion | flops 4834983936 | bytes 11796480 | tf_op jit(solution)/shard_map/tc,tq->cq/dot_general | solution.py:1274
  232.1 1.1 multiply_reduce_fusion.2
  233.2 1.7 fusion.113
  234.9 4.7 convolution_convert_fusion.5
  239.6 1.9 copy.96
  241.5 1.5 multiply_reduce_fusion.1
  247.7 1.2 copy-done.20
  249.5 1.7 fusion.65
  253.7 1.1 broadcast_select_fusion.3
  255.6 4.2 bitcast_convert_fusion.3
  261.0 1.9 convolution_convert_fusion.3
  262.9 2.5 convolution_convert_fusion.1
  265.4 3.6 pad_maximum_fusion
  269.0 1.4 copy-done.11
  270.4 1.5 copy-done.14
  271.9 1.3 copy-done.17
  273.2 60.2 %shard_map.240 = (f32[96,1536]{1,0:T(8,128)S(1)}, f32[96,128]{1,0:T(8,128)S(1)}, bf16[2,4,96,1536]{3,2,1,0:T(8,128)(2,1)}, bf16[2,4,96,1024]{3,2,1,0:T(8,128)(2,...) custom-call(bf16[96,1536]{1,0:T(8,128)(2,1)S(1)} %get-tuple-element.97, ...), custom_call_target="tpu_custom_call" | custom-call | flops 49999998976 | bytes 100000000 | tf_op jit(solution)/shard_map/pallas_call | solution.py:1118
  334.8 5.9 %bitcast_convert_fusion.2 = bf16[1024,1536]{1,0:T(8,128)(2,1)} fusion(bf16[2,4,96,1024]{3,2,1,0:T(8,128)(2,1)S(1)} %get-tuple-element.117, bf16[2,4,96,1536]{3,2,1,0:T(8,128)(2,1)} %get-tuple-element.118), kind=kOutput, calls=%fused_computation.7 | convolution fusion | flops 2417491968 | bytes 7077888 | tf_op jit(solution)/shard_map/tc,tq->cq/dot_general | solution.py:1274
  340.7 7.3 %bitcast_convert_fusion = bf16[1536,2048]{1,0:T(8,128)(2,1)} fusion(bf16[2,4,96,1536]{3,2,1,0:T(8,128)(2,1)S(1)} %copy-done.86, bf16[2,4,96,2048]{3,2,1,0:T(8,128)(2,1)S(1)} %copy-done.85), kind=kOutput, calls=%fused_computation.2 | convolution fusion | flops 4834983936 | bytes 11796480 | tf_op jit(solution)/shard_map/tc,tq->cq/dot_general | solution.py:1274
  348.9 4.4 convolution_convert_fusion.4
  354.2 1.5 multiply_reduce_fusion
  361.8 1.7 fusion.56
  367.2 3.4 convolution_convert_fusion.2
  370.6 4.6 convolution_convert_fusion
  375.2 1.1 maximum_select_fusion
  376.4 25.1 %reduce-scatter.5.cloned.1.call-done = bf16[384,2048]{1,0:T(8,128)(2,1)} async-done(((bf16[1536,2048]{1,0:T(8,128)(2,1)}), bf16[384,2048]{1,0:T(8,128)(2,1)}) %reduce-scatter.5.cloned.1.call-update) | async-done | bytes 1572880 | tf_op jit(solution)/shard_map/reduce_scatter | solution.py:1398
  401.5 136.1 %shard_map.241 = (bf16[2,2,384,512]{3,2,1,0:T(8,128)(2,1)}, bf16[2,2,384,512]{3,2,1,0:T(8,128)(2,1)}, bf16[2,2,128,1536]{3,2,1,0:T(8,128)(2,1)}, bf16[2,96,1280]...) custom-call(bf16[4,384,2048]{2,1,0:T(8,128)(2,1)} %bitcast.283, ...), custom_call_target="tpu_custom_call" | custom-call | tf_op jit(solution)/shard_map/pallas_call | solution.py:451
  537.7 1.1 slice_bitcast_fusion.2
  540.5 2.1 bitcast_convert_fusion.4
  544.7 3.6 bitcast_convert_fusion.5
  (325 shorter events, 44.3 us)
Async XLA Ops:
  7.2 13.7 %copy-start = (s32[2,96]{1,0:T(2,128)S(1)}, s32[2,96]{1,0:T(2,128)}, u32[]{:S(2)}) copy-start(s32[2,96]{1,0:T(2,128)} %param.16) | copy-start | bytes 2308
  7.2 14.4 %copy-start.70 = (s32[1,192,8]{1,2,0:T(8,128)S(1)}, s32[1,192,8]{1,2,0:T(8,128)}, u32[]{:S(2)}) copy-start(s32[1,192,8]{1,2,0:T(8,128)} %param.17) | copy-start | bytes 18436
  7.2 15.0 %copy-start.21 = (bf16[192,1536]{1,0:T(8,128)(2,1)S(1)}, bf16[192,1536]{1,0:T(8,128)(2,1)}, u32[]{:S(2)}) copy-start(bf16[192,1536]{1,0:T(8,128)(2,1)} %param.14) | copy-start | bytes 1769476
  7.2 52.2 %all-gather.3.cloned.1.call-start = ((), (), s32[]{:S(2)}) async-start(), calls=%async_computation.4 | async-start | bytes 1474560 | tf_op jit(solution)/shard_map/all_gather | solution.py:1291
  7.3 13.5 %collective-permute-start.2 = (bf16[1536,512]{1,0:T(8,128)(2,1)}, bf16[1536,512]{1,0:T(8,128)(2,1)S(1)}, u32[]{:S(2)}, u32[]{:S(2)}) collective-permute-start(bf16[1536,512]{1,0:T(8,128)(2,1)} %bitcast.363), channel_id=1, source_target_pairs={{0,16},{16,0},{1,17},{17,1},{2,18},{18,2},{3,19},{19,3},{4,20},{20... | collective-permute-start | bytes 4718600 | tf_op jit(solution)/shard_map/ppermute | solution.py:97
  7.8 13.2 %collective-permute-start.1 = (bf16[1536,512]{1,0:T(8,128)(2,1)}, bf16[1536,512]{1,0:T(8,128)(2,1)}, u32[]{:S(2)}, u32[]{:S(2)}) collective-permute-start(bf16[1536,512]{1,0:T(8,128)(2,1)} %bitcast.360), channel_id=1, source_target_pairs={{0,16},{16,0},{1,17},{17,1},{2,18},{18,2},{3,19},{19,3},{4,20},{20... | collective-permute-start | bytes 4718600 | tf_op jit(solution)/shard_map/ppermute | solution.py:97
  7.9 19.3 %collective-permute-start.3 = (bf16[1536,1536]{1,0:T(8,128)(2,1)}, bf16[1536,1536]{1,0:T(8,128)(2,1)}, u32[]{:S(2)}, u32[]{:S(2)}) collective-permute-start(bf16[1536,1536]{1,0:T(8,128)(2,1)} %bitcast.357), channel_id=1, source_target_pairs={{0,16},{16,0},{1,17},{17,1},{2,18},{18,2},{3,19},{19,3},{4,20},{20... | collective-permute-start | bytes 14155784 | tf_op jit(solution)/shard_map/ppermute | solution.py:97
  9.0 6.1 %collective-permute-start = (bf16[1536]{0:T(1024)(128)(2,1)S(1)}, bf16[1536]{0:T(1024)(128)(2,1)S(1)}, u32[]{:S(2)}, u32[]{:S(2)}) collective-permute-start(bf16[1536]{0:T(1024)(128)(2,1)S(1)} %reduce), channel_id=1, source_target_pairs={{0,16},{16,0},{1,17},{17,1},{2,18},{18,2},{3,19},{19,3},{4,20},{20... | collective-permute-start | bytes 9224 | tf_op jit(solution)/shard_map/ppermute | solution.py:97
  9.9 5.4 collective-permute-start.5
  12.1 335.9 %reduce-scatter.3.cloned.1.call-start = ((), (), s32[]{:S(2)}) async-start(), calls=%async_computation.2 | async-start | bytes 7864320 | tf_op jit(solution)/shard_map/reduce_scatter | solution.py:1354
  15.1 4.7 collective-permute-start.6
  15.2 5.2 collective-permute-start.7
  16.2 6.4 %copy-start.73 = (f32[96]{0:T(128)}, f32[96]{0:T(128)S(1)}, u32[]{:S(2)}) copy-start(f32[96]{0:T(128)S(1)} %get-tuple-element.230) | copy-start | bytes 1156
  19.8 39.6 %collective-permute-start.10 = (bf16[4,512,1536]{2,1,0:T(8,128)(2,1)}, bf16[4,512,1536]{2,1,0:T(8,128)(2,1)}, u32[]{:S(2)}, u32[]{:S(2)}) collective-permute-start(bf16[4,512,1536]{2,1,0:T(8,128)(2,1)} %bitcast.352), channel_id=1, source_target_pairs={{0,16},{16,0},{1,17},{17,1},{2,18},{18,2},{3,19},{19,3},{4,20},{20... | collective-permute-start | bytes 18874376 | tf_op jit(solution)/shard_map/ppermute | solution.py:97
  20.4 39.0 %collective-permute-start.8 = (bf16[4,1536,512]{2,1,0:T(8,128)(2,1)}, bf16[4,1536,512]{2,1,0:T(8,128)(2,1)}, u32[]{:S(2)}, u32[]{:S(2)}) collective-permute-start(bf16[4,1536,512]{2,1,0:T(8,128)(2,1)} %bitcast.342), channel_id=1, source_target_pairs={{0,16},{16,0},{1,17},{17,1},{2,18},{18,2},{3,19},{19,3},{4,20},{20... | collective-permute-start | bytes 18874376 | tf_op jit(solution)/shard_map/ppermute | solution.py:97
  20.8 38.7 %collective-permute-start.9 = (bf16[4,1536,512]{2,1,0:T(8,128)(2,1)}, bf16[4,1536,512]{2,1,0:T(8,128)(2,1)}, u32[]{:S(2)}, u32[]{:S(2)}) collective-permute-start(bf16[4,1536,512]{2,1,0:T(8,128)(2,1)} %bitcast.347), channel_id=1, source_target_pairs={{0,16},{16,0},{1,17},{17,1},{2,18},{18,2},{3,19},{19,3},{4,20},{20... | collective-permute-start | bytes 18874376 | tf_op jit(solution)/shard_map/ppermute | solution.py:97
  21.0 34.1 %collective-permute-start.4 = (bf16[1536,1536]{1,0:T(8,128)(2,1)}, bf16[1536,1536]{1,0:T(8,128)(2,1)}, u32[]{:S(2)}, u32[]{:S(2)}) collective-permute-start(bf16[1536,1536]{1,0:T(8,128)(2,1)} %bitcast.284), channel_id=1, source_target_pairs={{0,16},{16,0},{1,17},{17,1},{2,18},{18,2},{3,19},{19,3},{4,20},{20... | collective-permute-start | bytes 14155784 | tf_op jit(solution)/shard_map/ppermute | solution.py:97
  22.2 37.1 %copy-start.60 = (f32[1536]{0:T(1024)}, f32[1536]{0:T(1024)S(1)}, u32[]{:S(2)}) copy-start(f32[1536]{0:T(1024)S(1)} %get-tuple-element.226) | copy-start | bytes 18436
  24.8 7.5 %copy-start.62 = (bf16[96,512]{0,1:T(8,128)(2,1)}, bf16[96,512]{0,1:T(8,128)(2,1)S(1)}, u32[]{:S(2)}) copy-start(bf16[96,512]{0,1:T(8,128)(2,1)S(1)} %copy.86) | copy-start | bytes 294916
  33.3 25.4 %copy-start.28 = (bf16[8,64,3,96]{3,1,2,0:T(8,128)(2,1)}, bf16[8,64,3,96]{3,1,2,0:T(8,128)(2,1)S(1)}, u32[]{:S(2)}) copy-start(bf16[8,64,3,96]{3,1,2,0:T(8,128)(2,1)S(1)} %convolution_convert_fusion.9) | copy-start | bytes 884740
  58.7 52.1 %copy-start.2 = (f32[96,1536]{1,0:T(8,128)}, f32[96,1536]{1,0:T(8,128)S(1)}, u32[]{:S(2)}) copy-start(f32[96,1536]{1,0:T(8,128)S(1)} %get-tuple-element.242.hidden) | copy-start | bytes 1769476
  59.4 51.4 %copy-start.4 = (bf16[96,1536]{1,0:T(8,128)(2,1)}, bf16[96,1536]{1,0:T(8,128)(2,1)S(1)}, u32[]{:S(2)}) copy-start(bf16[96,1536]{1,0:T(8,128)(2,1)S(1)} %multiply_convert_fusion.3.x) | copy-start | bytes 884740
  116.3 5.1 copy-start.58
  126.9 49.0 %copy-start.77 = (f32[96]{0:T(128)}, f32[96]{0:T(128)S(1)}, u32[]{:S(2)}) copy-start(f32[96]{0:T(128)S(1)} %get-tuple-element.236) | copy-start | bytes 1156
  127.1 50.0 %copy-start.7 = (bf16[384,1536]{1,0:T(8,128)(2,1)S(1)}, bf16[384,1536]{1,0:T(8,128)(2,1)}, u32[]{:S(2)}) copy-start(bf16[384,1536]{1,0:T(8,128)(2,1)} %all-gather.3.cloned.1.call-done) | copy-start | bytes 3538948
  231.1 170.4 %reduce-scatter.5.cloned.1.call-start = ((), (), s32[]{:S(2)}) async-start(), calls=%async_computation.3 | async-start | bytes 7864320 | tf_op jit(solution)/shard_map/reduce_scatter | solution.py:1398
  231.2 139.4 %collective-permute-start.17 = (bf16[96,1536]{1,0:T(8,128)(2,1)}, bf16[96,1536]{1,0:T(8,128)(2,1)}, u32[]{:S(2)}, u32[]{:S(2)}) collective-permute-start(bf16[96,1536]{1,0:T(8,128)(2,1)} %copy-done.40), channel_id=1, source_target_pairs={{0,16},{16,0},{1,17},{17,1},{2,18},{18,2},{3,19},{19,3},{4,20},{20... | collective-permute-start | bytes 884744 | tf_op jit(solution)/shard_map/ppermute | solution.py:97
  231.2 29.5 %collective-permute-start.14 = (bf16[96,1536]{0,1:T(8,128)(2,1)S(1)}, bf16[96,1536]{0,1:T(8,128)(2,1)}, u32[]{:S(2)}, u32[]{:S(2)}) collective-permute-start(bf16[96,1536]{0,1:T(8,128)(2,1)S(1)} %bitcast.306), channel_id=1, source_target_pairs={{0,16},{16,0},{1,17},{17,1},{2,18},{18,2},{3,19},{19,3},{4,20},{20... | collective-permute-start | bytes 884744 | tf_op jit(solution)/shard_map/ppermute | solution.py:97
  231.7 31.1 %collective-permute-start.12 = (bf16[96,1536]{1,0:T(8,128)(2,1)S(1)}, bf16[96,1536]{1,0:T(8,128)(2,1)}, u32[]{:S(2)}, u32[]{:S(2)}) collective-permute-start(bf16[96,1536]{1,0:T(8,128)(2,1)S(1)} %fusion.59), channel_id=1, source_target_pairs={{0,16},{16,0},{1,17},{17,1},{2,18},{18,2},{3,19},{19,3},{4,20},{20... | collective-permute-start | bytes 884744 | tf_op jit(solution)/shard_map/ppermute | solution.py:97
  234.9 6.6 %copy-start.38 = (f32[8,3,96,96]{2,3,1,0:T(8,128)S(1)}, f32[8,3,96,96]{2,3,1,0:T(8,128)}, u32[]{:S(2)}) copy-start(f32[8,3,96,96]{2,3,1,0:T(8,128)} %copy-done.37) | copy-start | bytes 2654212
  252.7 7.8 %collective-permute-start.15 = (bf16[96,768]{1,0:T(8,128)(2,1)S(1)}, bf16[96,768]{1,0:T(8,128)(2,1)S(1)}, u32[]{:S(2)}, u32[]{:S(2)}) collective-permute-start(bf16[96,768]{1,0:T(8,128)(2,1)S(1)} %get-tuple-element.213), channel_id=1, source_target_pairs={{0,16},{16,0},{1,17},{17,1},{2,18},{18,2},{3,19},{19,3},{4,20},{20... | collective-permute-start | bytes 442376 | tf_op jit(solution)/shard_map/ppermute | solution.py:97
  253.1 9.8 %collective-permute-start.13 = (bf16[96,1280]{0,1:T(8,128)(2,1)S(1)}, bf16[96,1280]{0,1:T(8,128)(2,1)S(1)}, u32[]{:S(2)}, u32[]{:S(2)}) collective-permute-start(bf16[96,1280]{0,1:T(8,128)(2,1)S(1)} %get-tuple-element.199), channel_id=1, source_target_pairs={{0,16},{16,0},{1,17},{17,1},{2,18},{18,2},{3,19},{19,3},{4,20},{20... | collective-permute-start | bytes 737288 | tf_op jit(solution)/shard_map/ppermute | solution.py:97
  260.5 106.7 %collective-permute-start.19 = (bf16[96,1536]{0,1:T(8,128)(2,1)S(1)}, bf16[96,1536]{0,1:T(8,128)(2,1)}, u32[]{:S(2)}, u32[]{:S(2)}) collective-permute-start(bf16[96,1536]{0,1:T(8,128)(2,1)S(1)} %bitcast.298), channel_id=1, source_target_pairs={{0,16},{16,0},{1,17},{17,1},{2,18},{18,2},{3,19},{19,3},{4,20},{20... | collective-permute-start | bytes 884744 | tf_op jit(solution)/shard_map/ppermute | solution.py:97
  260.7 73.1 %collective-permute-start.11 = (bf16[96,1536]{1,0:T(8,128)(2,1)}, bf16[96,1536]{1,0:T(8,128)(2,1)S(1)}, u32[]{:S(2)}, u32[]{:S(2)}) collective-permute-start(bf16[96,1536]{1,0:T(8,128)(2,1)} %get-tuple-element.201), channel_id=1, source_target_pairs={{0,16},{16,0},{1,17},{17,1},{2,18},{18,2},{3,19},{19,3},{4,20},{20... | collective-permute-start | bytes 884744 | tf_op jit(solution)/shard_map/ppermute | solution.py:97
  273.2 60.4 %copy-start.5 = (bf16[96,1536]{1,0:T(8,128)(2,1)S(1)}, bf16[96,1536]{1,0:T(8,128)(2,1)}, u32[]{:S(2)}) copy-start(bf16[96,1536]{1,0:T(8,128)(2,1)} %copy-done.4) | copy-start | bytes 884740
  333.4 7.2 %copy-start.6 = (bf16[2,128,1536]{2,1,0:T(8,128)(2,1)}, bf16[2,128,1536]{2,1,0:T(8,128)(2,1)S(1)}, u32[]{:S(2)}) copy-start(bf16[2,128,1536]{2,1,0:T(8,128)(2,1)S(1)} %get-tuple-element.122.refs_8_) | copy-start | bytes 2359300
  334.8 5.9 %copy-start.85 = (bf16[2,4,96,2048]{3,2,1,0:T(8,128)(2,1)S(1)}, bf16[2,4,96,2048]{3,2,1,0:T(8,128)(2,1)}, u32[]{:S(2)}) copy-start(bf16[2,4,96,2048]{3,2,1,0:T(8,128)(2,1)} %get-tuple-element.116) | copy-start | bytes 9437188
  334.8 5.9 %copy-start.86 = (bf16[2,4,96,1536]{3,2,1,0:T(8,128)(2,1)S(1)}, bf16[2,4,96,1536]{3,2,1,0:T(8,128)(2,1)}, u32[]{:S(2)}) copy-start(bf16[2,4,96,1536]{3,2,1,0:T(8,128)(2,1)} %get-tuple-element.115) | copy-start | bytes 7077892
  340.6 7.4 %copy-start.3 = (f32[96,1536]{1,0:T(8,128)S(1)}, f32[96,1536]{1,0:T(8,128)}, u32[]{:S(2)}) copy-start(f32[96,1536]{1,0:T(8,128)} %copy-done.2) | copy-start | bytes 1769476
  340.6 7.4 %copy-start.24 = (bf16[1536,16]{1,0:T(8,128)(2,1)S(1)}, bf16[1536,16]{1,0:T(8,128)(2,1)}, u32[]{:S(2)}) copy-start(bf16[1536,16]{1,0:T(8,128)(2,1)} %copy-done.23) | copy-start | bytes 147460
  340.7 7.4 %copy-start.61 = (f32[1536]{0:T(1024)S(1)}, f32[1536]{0:T(1024)}, u32[]{:S(2)}) copy-start(f32[1536]{0:T(1024)} %copy-done.60) | copy-start | bytes 18436
  340.7 7.4 %copy-start.76 = (f32[96]{0:T(128)S(1)}, f32[96]{0:T(128)}, u32[]{:S(2)}) copy-start(f32[96]{0:T(128)} %copy-done.75) | copy-start | bytes 1156
  348.8 5.3 copy-start.36
  348.8 5.3 copy-start.63
  348.9 5.3 copy-start.69
  364.3 3.0 collective-permute-start.20
  365.2 5.4 collective-permute-start.18
  366.0 9.2 %collective-permute-start.16 = (f32[96,1536]{1,0:T(8,128)S(1)}, f32[96,1536]{1,0:T(8,128)S(1)}, u32[]{:S(2)}, u32[]{:S(2)}) collective-permute-start(f32[96,1536]{1,0:T(8,128)S(1)} %get-tuple-element.185), channel_id=1, source_target_pairs={{0,16},{16,0},{1,17},{17,1},{2,18},{18,2},{3,19},{19,3},{4,20},{20... | collective-permute-start | bytes 1769480 | tf_op jit(solution)/shard_map/ppermute | solution.py:97
  (67 other events, 135.1 us)
Sparse Core Ops, SparseCore 0:
  12.2 32.8 all-gather.2
  231.2 98.9 reduce-scatter.2
  333.2 68.2 reduce-scatter.4

commit v15 on v14

--- a/solution.py
+++ b/solution.py
@@ -114,9 +114,9 @@
 def sum_scatter_kernel(plan, *refs):
     lanes, ins, copies = plan
     sources = refs[:ins]
-    second_pre, second_down, stats_in = refs[ins : ins + 3]
-    stage, stats = refs[ins + 3 : ins + 9], refs[ins + 9]
-    scratch = list(refs[ins + 10 :])
+    second_pre, stats_in = refs[ins : ins + 2]
+    stage, stats = refs[ins + 2 : ins + 8], refs[ins + 8]
+    scratch = list(refs[ins + 9 :])
     send_sem, recv_sem, local_sem, stats_got, stats_send, stats_recv, core_send, core_recv = (
         scratch[-8:]
     )
@@ -207,12 +207,9 @@
     inner = stage[GATE].shape[3]
     wholes = []
     half = stage[GATE].shape[1]
-    for number in range(3 * half):
+    for number in range(2 * half):
         kind, j = divmod(number, half)
-        if kind == DOWN:
-            source = second_down.at[j]
-        else:
-            source = second_pre.at[:, pl.ds(number * inner, inner)]
+        source = second_pre.at[:, pl.ds(number * inner, inner)]
         spot, copy = to_stage(len(lanes) + number, source, kind, j)
         wholes.append((copy, pltpu.make_async_copy(source, spot, core_send.at[len(lanes) + number])))
     for copy, here in wholes:
@@ -386,7 +383,7 @@
         copy.wait_send()
 
 
-def sum_scatter(arrays, lanes, second_pre, second_down, stats, inner, collective):
+def sum_scatter(arrays, lanes, second_pre, stats, inner, collective):
     plans, scratch, shapes, copies, locals_ = [], [], [], 0, 0
     sizes = {}
     for source, prefix, phases, layer, target in lanes:
@@ -445,20 +442,20 @@
         pltpu.VMEM((hops, *stats.shape), jnp.float32),
         pltpu.SemaphoreType.DMA((hops,)),
         pltpu.SemaphoreType.DMA((hops,)),
-        pltpu.SemaphoreType.DMA((len(lanes) + 3 * half,)),
-        pltpu.SemaphoreType.DMA((len(lanes) + 3 * half,)),
+        pltpu.SemaphoreType.DMA((len(lanes) + 2 * half,)),
+        pltpu.SemaphoreType.DMA((len(lanes) + 2 * half,)),
     ]
     return pl.pallas_call(
         functools.partial(sum_scatter_kernel, (plans, len(arrays), copies)),
         out_shape=shapes,
-        in_specs=[pl.BlockSpec(memory_space=pl.ANY)] * (len(arrays) + 2)
+        in_specs=[pl.BlockSpec(memory_space=pl.ANY)] * (len(arrays) + 1)
         + [pl.BlockSpec(memory_space=pltpu.VMEM)],
         out_specs=[pl.BlockSpec(memory_space=pltpu.VMEM)] * len(shapes),
         scratch_shapes=scratch,
         compiler_params=pltpu.CompilerParams(
             collective_id=collective, has_side_effects=True, vmem_limit_bytes=60 * 2**20
         ),
-    )(*arrays, second_pre, second_down, stats)
+    )(*arrays, second_pre, stats)
 
 
 def bits_of(axis):
@@ -481,7 +478,7 @@
 
 def dense_lanes(first, width):
     up, down, deep = bits_of(GROUP), bits_of(GROUP)[::-1], bits_of(LINE)
-    near = width // 4 // COLUMNS * COLUMNS
+    near = width // 8 // COLUMNS * COLUMNS
     away = width - near
     return [
         (
@@ -896,12 +893,6 @@
     kept, refs = refs[:2], refs[2:]
     keep_places, keep_sem, refs = refs[-3:-1], refs[-1], refs[:-3]
     gate_keep, up_keep = keep_places
-    carried = layer == 0
-    if carried:
-        extra, refs = refs[0], refs[1:]
-        extra_sum, refs = refs[6], refs[:6] + refs[7:]
-        landed, extra_send, extra_recv = refs[-3:]
-        refs = refs[:-3]
     out, out_gates, rows_both, gated_both, grad_both, pre_both = refs[:6]
     w_gate, w_up, w_down, sums, sum_gates, returned, returned_gates, away, dots = refs[6:15]
     weight_sem, core_send, core_recv, core_local, *sems = refs[15:]
@@ -949,19 +940,6 @@
         if gathered:
             copies += (pltpu.make_async_copy(grad, grad_both.at[core], core_local.at[2]),)
         return copies
-
-    me, count = lax.axis_index(GROUP), lax.axis_size(GROUP)
-    peers = [lax.rem(me + k, count) for k in range(1, count)] if carried else []
-
-    def extra_copy(k, peer, slot):
-        return pltpu.make_async_remote_copy(
-            src_ref=extra.at[:, peer],
-            dst_ref=landed.at[slot],
-            send_sem=extra_send.at[k],
-            recv_sem=extra_recv.at[slot],
-            device_id={GROUP: peer},
-            device_id_type=MESH,
-        )
 
     def compute(block, sent, between):
         picked = rows[block]
@@ -1042,15 +1020,10 @@
         compute,
         z,
         n,
-        [{CORE: 1 - core}] + [{GROUP: peer} for peer in peers],
+        [{CORE: 1 - core}],
     )
     if not gathered:
         start(0)
-    for k, peer in enumerate(peers):
-        extra_copy(k, peer, me).start()
-    if carried:
-        mine = pltpu.make_async_copy(extra.at[:, me], landed.at[me], extra_send.at[len(peers)])
-        mine.start()
     wait_weights = fetch_weights(layer, own, other, (w_gate, w_up, w_down), weight_sem)
     keep_copies = [
         pltpu.make_async_copy(kept[i], keep_places[i], keep_sem.at[i]) for i in range(2)
@@ -1073,27 +1046,8 @@
         else:
             out[:, p * width : (p + 1) * width] += value
 
-    if carried:
-        mine.wait()
-        for k, peer in enumerate(peers):
-            extra_copy(k, peer, peer).wait_recv()
-        half, rows_each = extra_sum.shape[:2]
-        step = 16 if rows_each % 16 == 0 else rows_each
-
-        def add_up(i, carry):
-            at = pl.ds(pl.multiple_of(i * step, step), step)
-            for j in range(half):
-                value = landed[0, j, at].astype(jnp.float32)
-                for k in range(1, count):
-                    value += landed[k, j, at].astype(jnp.float32)
-                extra_sum[j, at] = value.astype(jnp.bfloat16)
-            return carry
-
-        lax.fori_loop(0, rows_each // step, add_up, 0)
     collect(add)
     finish()
-    for k, peer in enumerate(peers):
-        extra_copy(k, peer, me).wait_send()
     for copy in local_copies():
         copy.wait()
     for copy in whole_copies():
@@ -1174,7 +1128,7 @@
     )
 
 
-def experts_backward(layer, grad_low, gates, gate_keep, up_keep, rows, gated, own, other, extra):
+def experts_backward(layer, grad_low, gates, gate_keep, up_keep, rows, gated, own, other):
     held, n, length, inner = gate_keep.shape
     width = grad_low.shape[-1]
     low, full = jnp.bfloat16, jnp.float32
@@ -1198,14 +1152,6 @@
         pltpu.SemaphoreType.DMA((2 + 2 * n,)),
         pltpu.SemaphoreType.DMA((3,)),
     ] + exchange_scratch(n, 1, PARTS + 1)
-    if layer == 0:
-        half, count, *block = extra.shape
-        shapes.append(jax.ShapeDtypeStruct((half, *block), low))
-        scratch += [
-            pltpu.VMEM((count, half, *block), low),
-            pltpu.SemaphoreType.DMA((count,)),
-            pltpu.SemaphoreType.DMA((count,)),
-        ]
     scratch += [pltpu.VMEM(gate_keep.shape, low)] * 2 + [pltpu.SemaphoreType.DMA((2,))]
     kernel = functools.partial(experts_backward_kernel, layer)
     return expert_call(
@@ -1213,7 +1159,7 @@
         (grad_low, gates),
         own,
         other,
-        (rows, gated, gate_keep, up_keep) + (() if extra is None else (extra,)),
+        (rows, gated, gate_keep, up_keep),
         shapes,
         scratch,
         3 + layer,
@@ -1331,7 +1277,7 @@
         (inverse_one, normed_one, _, _, _, _, attended, hidden, inverse_two, normed_two) = state
         rows_all, gates_all, gates, gate_keep, up_keep, gated = expert_state
         gain_moe, w_router = weights[s][5], weights[s][6]
-        grad_sum, grad_gates, rows_both, gated_both, grad_both, pre_both, *sums = experts_backward(
+        grad_sum, grad_gates, rows_both, gated_both, grad_both, pre_both = experts_backward(
             s,
             cotangent_all if s == 1 else grad_low,
             gates_all,
@@ -1341,10 +1287,7 @@
             gated,
             own_experts,
             other_experts,
-            None if s == 1 else grads[1][1].reshape(held // 2, dp, -1, D),
-        )
-        if s == 0:
-            (second_down,) = sums
+        )
         inner = w_gate.shape[3]
         grad_gate_up = turned(
             rows_both.reshape(-1, D), pre_both.reshape(-1, held * inner)
@@ -1418,9 +1361,10 @@
         lanes.append((len(arrays), (False, columns), [(LINE, bits_of(LINE))], 1, target))
     arrays.append(second_dense.reshape(deep, second_dense.shape[0] // deep, whole))
     lanes.append(small_lane(len(arrays), 1))
-    lanes += expert_lanes(0, inner) + down_lanes(1, 0)
+    lanes += expert_lanes(0, inner) + down_lanes(1, 0) + down_lanes(len(arrays) + 1, 1)
     small = grads[1][4]
     arrays.append(small.reshape(dp, deep, small.shape[0] // (dp * deep), small.shape[1]))
+    arrays.append(grads[1][1].reshape(half, dp, inner // dp, D))
     out_keep = jnp.where(first, outs[0], outs[1])
     out_got = swapped(jnp.where(first, outs[1], outs[0]))
     layer_out = jnp.where(
@@ -1435,7 +1379,7 @@
     stats = jnp.concatenate(stats, axis=0)
     stats, layer_out, input_grad = lax.optimization_barrier((stats, layer_out, input_grad))
     *grads, qkv, out, small, stats = sum_scatter(
-        arrays, lanes, second_pre, second_down, stats, inner, 0
+        arrays, lanes, second_pre, stats, inner, 0
     )
     full = jnp.float32
     w_gate_grad, w_up_grad, w_down_grad = (

time: 564 us -> 564 us (level)
  waiting for transfers between devices: 50.9 us -> 25.7 us
  Pallas kernels: 340 us -> 364 us
    pallas_call x1, Pallas kernels: 136 us -> 162 us  [sum_scatter(): pl.pallas_call(functools.partial(sum_scatter_kernel, (plans, len(arrays),...]
    reduce_scatter x1, waiting for transfers between devices: 25.1 us -> 0.01 us  [body(): lax.psum_scatter(dense, GROUP, scatter_dimension=0, tiled=True)]
    unnamed x186 -> x212, local copies, waits for them, and re-layouts: 22.4 us -> 21.9 us
  transfers between devices with their start and end apart: 24 -> 24, of which waited for: 4 -> 3; matrix products, arithmetic and copies ran while one was open for 16% -> 16% of each run, Pallas kernels for 11% -> 11%
where the time goes in v15:
time: 564 us; the launch traced here: 556 us
  Pallas kernels  364 us (65%)
  matrix products  83.8 us (15%)
  local copies, waits for them, and re-layouts  33.1 us (6%)
  other arithmetic  26.8 us (5%)
  waiting for transfers between devices  25.7 us (5%)
  between operations  15.6 us (3%)
  starting transfers between devices  6.44 us (1%)
    pallas_call x4, Pallas kernels, expert_call(): pl.pallas_call(kernel, out_shape=shapes, in_specs=[vmem] * len(operands)...  202 us
    pallas_call x1, Pallas kernels, sum_scatter(): pl.pallas_call(functools.partial(sum_scatter_kernel, (plans, len(arrays),...  162 us
    dot_general x10, matrix products, turned(): jnp.einsum('tc,tq->cq', left, right, preferred_element_type=jnp.float32)  39.9 us
    ppermute x21, waiting for transfers between devices, swapped(): return lax.ppermute(array, CORE, [(0, 1), (1, 0)])  25.6 us
    unnamed x212, local copies, waits for them, and re-layouts  21.9 us
    dot_general x8, matrix products, matmul(): return jnp.dot(left_side, right_side, preferred_element_type=jnp.float32)  21 us
  transfers between devices with their start and end apart: 24, of which 3 were waited for; matrix products, arithmetic and copies ran while one was open for 16% of the time, Pallas kernels for 11%

profile of v15, /device:TPU:0, one launch (start us, length us, event | category | flops | bytes accessed | tf_op | source)
XLA Modules:
  0.0 555.6 jit_solution(17717543892914819516)
XLA Ops:
  10.4 1.7 constant_dynamic-slice_fusion.9
  12.9 1.1 fusion.48
  16.2 3.6 collective-permute-done.6
  22.8 1.4 copy-done.95
  24.9 2.2 fusion.13
  27.2 4.4 fusion.4
  33.4 21.7 %collective-permute-done.4.refs_13_ = bf16[1536,1536]{1,0:T(8,128)(2,1)} collective-permute-done((bf16[1536,1536]{1,0:T(8,128)(2,1)}, bf16[1536,1536]{1,0:T(8,128)(2,1)}, u32[]{:S(2)}, u32[]{:S(2)}) %collective-permute-start.4) | collective-permute-done | bytes 4718624 | tf_op jit(solution)/shard_map/ppermute | solution.py:97
  55.1 3.6 multiply_reduce_fusion.7
  59.8 51.0 %shard_map.237 = (bf16[96,1536]{1,0:T(8,128)(2,1)S(1)}, bf16[4,96,1536]{2,1,0:T(8,128)(2,1)S(1)}, bf16[4,96,128]{2,1,0:T(8,128)(2,1)S(1)}, f32[96,128]{1,0:T(8,1...) custom-call(bf16[96,1536]{1,0:T(8,128)(2,1)S(1)} %multiply_convert_f, ...), custom_call_target="tpu_custom_call" | custom-call | flops 49999998976 | bytes 100000000 | tf_op jit(solution)/shard_map/pallas_call | solution.py:1072
  110.8 1.1 copy-done.12
  111.9 1.0 copy-done.15
  114.0 2.2 fusion.117
  116.3 4.4 fusion.118
  123.1 3.4 multiply_reduce_fusion.6
  126.6 48.9 %shard_map.238 = (bf16[96,1536]{1,0:T(8,128)(2,1)S(1)}, bf16[4,96,1536]{2,1,0:T(8,128)(2,1)S(1)}, bf16[4,96,128]{2,1,0:T(8,128)(2,1)S(1)}, f32[96,128]{1,0:T(8,1...) custom-call(bf16[96,1536]{1,0:T(8,128)(2,1)S(1)} %multiply_convert_f, ...), custom_call_target="tpu_custom_call" | custom-call | flops 49999998976 | bytes 100000000 | tf_op jit(solution)/shard_map/pallas_call | solution.py:1072
  175.5 1.1 copy-done.14
  176.6 43.7 %shard_map.239 = (f32[96,1536]{1,0:T(8,128)S(1)}, f32[96,128]{1,0:T(8,128)S(1)}, bf16[2,4,96,1536]{3,2,1,0:T(8,128)(2,1)}, bf16[2,4,96,1024]{3,2,1,0:T(8,128)(2,...) custom-call(bf16[4,96,1536]{2,1,0:T(8,128)(2,1)S(1)} %bitcast.278, ...), custom_call_target="tpu_custom_call" | custom-call | flops 49999998976 | bytes 100000000 | tf_op jit(solution)/shard_map/pallas_call | solution.py:1072
  220.3 1.1 copy-done.7
  221.4 9.1 %bitcast_convert_fusion.1 = bf16[1536,2048]{1,0:T(8,128)(2,1)} fusion(bf16[2,4,96,1536]{3,2,1,0:T(8,128)(2,1)} %get-tuple-element.87, bf16[2,4,96,2048]{3,2,1,0:T(8,128)(2,1)} %get-tuple-element.88), kind=kOutput, calls=%fused_computation.3 | convolution fusion | flops 4834983936 | bytes 11796480 | tf_op jit(solution)/shard_map/tc,tq->cq/dot_general | solution.py:1220
  232.5 1.1 fusion.113
  233.6 4.7 convolution_convert_fusion.5
  238.3 1.9 copy.96
  240.2 1.4 multiply_reduce_fusion.1
  246.1 1.4 copy-done.19
  248.2 2.3 fusion.65
  252.5 1.1 pad_maximum_fusion.1
  254.1 1.1 broadcast_select_fusion.3
  255.9 4.2 bitcast_convert_fusion.3
  261.2 1.9 convolution_convert_fusion.3
  263.2 2.5 convolution_convert_fusion.1
  265.7 3.5 pad_maximum_fusion
  269.3 1.4 copy-done.10
  270.7 1.4 copy-done.13
  272.1 1.3 copy-done.16
  273.4 58.9 %shard_map.240 = (f32[96,1536]{1,0:T(8,128)S(1)}, f32[96,128]{1,0:T(8,128)S(1)}, bf16[2,4,96,1536]{3,2,1,0:T(8,128)(2,1)}, bf16[2,4,96,1024]{3,2,1,0:T(8,128)(2,...) custom-call(bf16[96,1536]{1,0:T(8,128)(2,1)S(1)} %get-tuple-element.96.grad, ...), custom_call_target="tpu_custom_call" | custom-call | flops 49999998976 | bytes 100000000 | tf_op jit(solution)/shard_map/pallas_call | solution.py:1072
  333.3 2.0 maximum_select_fusion.1
  335.3 5.9 %bitcast_convert_fusion.2 = bf16[1024,1536]{1,0:T(8,128)(2,1)} fusion(bf16[2,4,96,1024]{3,2,1,0:T(8,128)(2,1)S(1)} %get-tuple-element.115, bf16[2,4,96,1536]{3,2,1,0:T(8,128)(2,1)} %get-tuple-element.116), kind=kOutput, calls=%fused_computation.7 | convolution fusion | flops 2417491968 | bytes 7077888 | tf_op jit(solution)/shard_map/tc,tq->cq/dot_general | solution.py:1220
  341.2 7.3 %bitcast_convert_fusion = bf16[1536,2048]{1,0:T(8,128)(2,1)} fusion(bf16[2,4,96,1536]{3,2,1,0:T(8,128)(2,1)S(1)} %copy-done.99, bf16[2,4,96,2048]{3,2,1,0:T(8,128)(2,1)S(1)} %copy-done.98), kind=kOutput, calls=%fused_computation.2 | convolution fusion | flops 4834983936 | bytes 11796480 | tf_op jit(solution)/shard_map/tc,tq->cq/dot_general | solution.py:1220
  349.4 4.0 convolution_convert_fusion.4
  354.4 1.4 multiply_reduce_fusion
  361.6 1.7 fusion.56
  366.4 3.4 convolution_convert_fusion.2
  369.8 4.6 convolution_convert_fusion
  374.4 1.1 maximum_select_fusion
  375.6 161.8 %shard_map.241 = (bf16[2,2,384,512]{3,2,1,0:T(8,128)(2,1)}, bf16[2,2,384,512]{3,2,1,0:T(8,128)(2,1)}, bf16[2,2,128,1536]{3,2,1,0:T(8,128)(2,1)}, bf16[2,96,1280]...) custom-call(bf16[4,384,2048]{2,1,0:T(8,128)(2,1)} %bitcast.283, ...), custom_call_target="tpu_custom_call" | custom-call | tf_op jit(solution)/shard_map/pallas_call | solution.py:448
  537.4 1.1 slice_bitcast_fusion.2
  540.2 2.1 bitcast_convert_fusion.4
  544.4 3.6 bitcast_convert_fusion.5
  (351 shorter events, 43.3 us)
Async XLA Ops:
  7.2 13.7 %copy-start = (s32[2,96]{1,0:T(2,128)S(1)}, s32[2,96]{1,0:T(2,128)}, u32[]{:S(2)}) copy-start(s32[2,96]{1,0:T(2,128)} %param.16) | copy-start | bytes 2308
  7.2 14.4 %copy-start.82 = (s32[1,192,8]{1,2,0:T(8,128)S(1)}, s32[1,192,8]{1,2,0:T(8,128)}, u32[]{:S(2)}) copy-start(s32[1,192,8]{1,2,0:T(8,128)} %param.17) | copy-start | bytes 18436
  7.2 15.0 %copy-start.20 = (bf16[192,1536]{1,0:T(8,128)(2,1)S(1)}, bf16[192,1536]{1,0:T(8,128)(2,1)}, u32[]{:S(2)}) copy-start(bf16[192,1536]{1,0:T(8,128)(2,1)} %param.14) | copy-start | bytes 1769476
  7.2 52.2 %all-gather.3.cloned.1.call-start = ((), (), s32[]{:S(2)}) async-start(), calls=%async_computation.4 | async-start | bytes 1474560 | tf_op jit(solution)/shard_map/all_gather | solution.py:1237
  7.3 13.5 %collective-permute-start.2 = (bf16[1536,512]{1,0:T(8,128)(2,1)}, bf16[1536,512]{1,0:T(8,128)(2,1)S(1)}, u32[]{:S(2)}, u32[]{:S(2)}) collective-permute-start(bf16[1536,512]{1,0:T(8,128)(2,1)} %bitcast.364), channel_id=1, source_target_pairs={{0,16},{16,0},{1,17},{17,1},{2,18},{18,2},{3,19},{19,3},{4,20},{20... | collective-permute-start | bytes 4718600 | tf_op jit(solution)/shard_map/ppermute | solution.py:97
  7.8 13.2 %collective-permute-start.1 = (bf16[1536,512]{1,0:T(8,128)(2,1)}, bf16[1536,512]{1,0:T(8,128)(2,1)}, u32[]{:S(2)}, u32[]{:S(2)}) collective-permute-start(bf16[1536,512]{1,0:T(8,128)(2,1)} %bitcast.361), channel_id=1, source_target_pairs={{0,16},{16,0},{1,17},{17,1},{2,18},{18,2},{3,19},{19,3},{4,20},{20... | collective-permute-start | bytes 4718600 | tf_op jit(solution)/shard_map/ppermute | solution.py:97
  7.9 19.3 %collective-permute-start.3 = (bf16[1536,1536]{1,0:T(8,128)(2,1)}, bf16[1536,1536]{1,0:T(8,128)(2,1)}, u32[]{:S(2)}, u32[]{:S(2)}) collective-permute-start(bf16[1536,1536]{1,0:T(8,128)(2,1)} %bitcast.358), channel_id=1, source_target_pairs={{0,16},{16,0},{1,17},{17,1},{2,18},{18,2},{3,19},{19,3},{4,20},{20... | collective-permute-start | bytes 14155784 | tf_op jit(solution)/shard_map/ppermute | solution.py:97
  9.0 6.1 %collective-permute-start = (bf16[1536]{0:T(1024)(128)(2,1)S(1)}, bf16[1536]{0:T(1024)(128)(2,1)S(1)}, u32[]{:S(2)}, u32[]{:S(2)}) collective-permute-start(bf16[1536]{0:T(1024)(128)(2,1)S(1)} %reduce), channel_id=1, source_target_pairs={{0,16},{16,0},{1,17},{17,1},{2,18},{18,2},{3,19},{19,3},{4,20},{20... | collective-permute-start | bytes 9224 | tf_op jit(solution)/shard_map/ppermute | solution.py:97
  9.9 5.4 collective-permute-start.5
  12.1 336.4 %reduce-scatter.3.cloned.1.call-start = ((), (), s32[]{:S(2)}) async-start(), calls=%async_computation.2 | async-start | bytes 7864320 | tf_op jit(solution)/shard_map/reduce_scatter | solution.py:1297
  15.1 4.7 collective-permute-start.6
  15.2 5.2 collective-permute-start.7
  16.2 6.5 %copy-start.86 = (f32[96]{0:T(128)}, f32[96]{0:T(128)S(1)}, u32[]{:S(2)}) copy-start(f32[96]{0:T(128)S(1)} %get-tuple-element.228) | copy-start | bytes 1156
  19.8 39.6 %collective-permute-start.10 = (bf16[4,512,1536]{2,1,0:T(8,128)(2,1)}, bf16[4,512,1536]{2,1,0:T(8,128)(2,1)}, u32[]{:S(2)}, u32[]{:S(2)}) collective-permute-start(bf16[4,512,1536]{2,1,0:T(8,128)(2,1)} %bitcast.353), channel_id=1, source_target_pairs={{0,16},{16,0},{1,17},{17,1},{2,18},{18,2},{3,19},{19,3},{4,20},{20... | collective-permute-start | bytes 18874376 | tf_op jit(solution)/shard_map/ppermute | solution.py:97
  20.4 39.0 %collective-permute-start.8 = (bf16[4,1536,512]{2,1,0:T(8,128)(2,1)}, bf16[4,1536,512]{2,1,0:T(8,128)(2,1)}, u32[]{:S(2)}, u32[]{:S(2)}) collective-permute-start(bf16[4,1536,512]{2,1,0:T(8,128)(2,1)} %bitcast.343), channel_id=1, source_target_pairs={{0,16},{16,0},{1,17},{17,1},{2,18},{18,2},{3,19},{19,3},{4,20},{20... | collective-permute-start | bytes 18874376 | tf_op jit(solution)/shard_map/ppermute | solution.py:97
  20.8 38.7 %collective-permute-start.9 = (bf16[4,1536,512]{2,1,0:T(8,128)(2,1)}, bf16[4,1536,512]{2,1,0:T(8,128)(2,1)}, u32[]{:S(2)}, u32[]{:S(2)}) collective-permute-start(bf16[4,1536,512]{2,1,0:T(8,128)(2,1)} %bitcast.348), channel_id=1, source_target_pairs={{0,16},{16,0},{1,17},{17,1},{2,18},{18,2},{3,19},{19,3},{4,20},{20... | collective-permute-start | bytes 18874376 | tf_op jit(solution)/shard_map/ppermute | solution.py:97
  21.0 34.1 %collective-permute-start.4 = (bf16[1536,1536]{1,0:T(8,128)(2,1)}, bf16[1536,1536]{1,0:T(8,128)(2,1)}, u32[]{:S(2)}, u32[]{:S(2)}) collective-permute-start(bf16[1536,1536]{1,0:T(8,128)(2,1)} %bitcast.284), channel_id=1, source_target_pairs={{0,16},{16,0},{1,17},{17,1},{2,18},{18,2},{3,19},{19,3},{4,20},{20... | collective-permute-start | bytes 14155784 | tf_op jit(solution)/shard_map/ppermute | solution.py:97
  22.2 91.6 %copy-start.74 = (f32[1536]{0:T(1024)}, f32[1536]{0:T(1024)S(1)}, u32[]{:S(2)}) copy-start(f32[1536]{0:T(1024)S(1)} %get-tuple-element.225) | copy-start | bytes 18436
  22.2 37.0 %copy-start.64 = (f32[1536]{0:T(1024)}, f32[1536]{0:T(1024)S(1)}, u32[]{:S(2)}) copy-start(f32[1536]{0:T(1024)S(1)} %get-tuple-element.224) | copy-start | bytes 18436
  22.2 104.2 %copy-start.66 = (f32[1536]{0:T(1024)}, f32[1536]{0:T(1024)S(1)}, u32[]{:S(2)}) copy-start(f32[1536]{0:T(1024)S(1)} %get-tuple-element.223) | copy-start | bytes 18436
  24.9 7.5 %copy-start.68 = (bf16[96,512]{0,1:T(8,128)(2,1)}, bf16[96,512]{0,1:T(8,128)(2,1)S(1)}, u32[]{:S(2)}) copy-start(bf16[96,512]{0,1:T(8,128)(2,1)S(1)} %copy.86) | copy-start | bytes 294916
  33.4 25.3 %copy-start.27 = (bf16[8,64,3,96]{3,1,2,0:T(8,128)(2,1)}, bf16[8,64,3,96]{3,1,2,0:T(8,128)(2,1)S(1)}, u32[]{:S(2)}) copy-start(bf16[8,64,3,96]{3,1,2,0:T(8,128)(2,1)S(1)} %convolution_convert_fusion.9) | copy-start | bytes 884740
  58.7 52.1 %copy-start.2 = (f32[96,1536]{1,0:T(8,128)}, f32[96,1536]{1,0:T(8,128)S(1)}, u32[]{:S(2)}) copy-start(f32[96,1536]{1,0:T(8,128)S(1)} %get-tuple-element.240.hidden) | copy-start | bytes 1769476
  59.4 51.4 %copy-start.4 = (bf16[96,1536]{1,0:T(8,128)(2,1)}, bf16[96,1536]{1,0:T(8,128)(2,1)S(1)}, u32[]{:S(2)}) copy-start(bf16[96,1536]{1,0:T(8,128)(2,1)S(1)} %multiply_convert_fusion.3.x) | copy-start | bytes 884740
  116.3 5.1 copy-start.59
  116.3 5.1 copy-start.61
  126.6 50.0 %copy-start.6 = (bf16[384,1536]{1,0:T(8,128)(2,1)S(1)}, bf16[384,1536]{1,0:T(8,128)(2,1)}, u32[]{:S(2)}) copy-start(bf16[384,1536]{1,0:T(8,128)(2,1)} %all-gather.3.cloned.1.call-done) | copy-start | bytes 3538948
  230.6 145.0 %reduce-scatter.5.cloned.1.call-start = ((), (), s32[]{:S(2)}) async-start(), calls=%async_computation.3 | async-start | bytes 7864320 | tf_op jit(solution)/shard_map/reduce_scatter | solution.py:1341
  230.7 139.2 %collective-permute-start.17 = (bf16[96,1536]{1,0:T(8,128)(2,1)}, bf16[96,1536]{1,0:T(8,128)(2,1)}, u32[]{:S(2)}, u32[]{:S(2)}) collective-permute-start(bf16[96,1536]{1,0:T(8,128)(2,1)} %copy-done.40), channel_id=1, source_target_pairs={{0,16},{16,0},{1,17},{17,1},{2,18},{18,2},{3,19},{19,3},{4,20},{20... | collective-permute-start | bytes 884744 | tf_op jit(solution)/shard_map/ppermute | solution.py:97
  230.7 30.2 %collective-permute-start.14 = (bf16[96,1536]{0,1:T(8,128)(2,1)S(1)}, bf16[96,1536]{0,1:T(8,128)(2,1)}, u32[]{:S(2)}, u32[]{:S(2)}) collective-permute-start(bf16[96,1536]{0,1:T(8,128)(2,1)S(1)} %bitcast.306), channel_id=1, source_target_pairs={{0,16},{16,0},{1,17},{17,1},{2,18},{18,2},{3,19},{19,3},{4,20},{20... | collective-permute-start | bytes 884744 | tf_op jit(solution)/shard_map/ppermute | solution.py:97
  231.2 31.9 %collective-permute-start.12 = (bf16[96,1536]{1,0:T(8,128)(2,1)S(1)}, bf16[96,1536]{1,0:T(8,128)(2,1)}, u32[]{:S(2)}, u32[]{:S(2)}) collective-permute-start(bf16[96,1536]{1,0:T(8,128)(2,1)S(1)} %fusion.59), channel_id=1, source_target_pairs={{0,16},{16,0},{1,17},{17,1},{2,18},{18,2},{3,19},{19,3},{4,20},{20... | collective-permute-start | bytes 884744 | tf_op jit(solution)/shard_map/ppermute | solution.py:97
  233.6 6.6 %copy-start.38 = (f32[8,3,96,96]{2,3,1,0:T(8,128)S(1)}, f32[8,3,96,96]{2,3,1,0:T(8,128)}, u32[]{:S(2)}) copy-start(f32[8,3,96,96]{2,3,1,0:T(8,128)} %copy-done.37) | copy-start | bytes 2654212
  233.6 6.6 %copy-start.71 = (bf16[96,512]{0,1:T(8,128)(2,1)S(1)}, bf16[96,512]{0,1:T(8,128)(2,1)}, u32[]{:S(2)}) copy-start(bf16[96,512]{0,1:T(8,128)(2,1)} %copy-done.70) | copy-start | bytes 294916
  233.6 6.6 %copy-start.80 = (f32[8,3,96]{2,1,0:T(4,128)S(1)}, f32[8,3,96]{2,1,0:T(4,128)}, u32[]{:S(2)}) copy-start(f32[8,3,96]{2,1,0:T(4,128)} %copy-done.79) | copy-start | bytes 27652
  251.9 8.8 %collective-permute-start.15 = (bf16[96,768]{1,0:T(8,128)(2,1)S(1)}, bf16[96,768]{1,0:T(8,128)(2,1)S(1)}, u32[]{:S(2)}, u32[]{:S(2)}) collective-permute-start(bf16[96,768]{1,0:T(8,128)(2,1)S(1)} %get-tuple-element.211), channel_id=1, source_target_pairs={{0,16},{16,0},{1,17},{17,1},{2,18},{18,2},{3,19},{19,3},{4,20},{20... | collective-permute-start | bytes 442376 | tf_op jit(solution)/shard_map/ppermute | solution.py:97
  253.7 9.5 %collective-permute-start.13 = (bf16[96,1280]{0,1:T(8,128)(2,1)S(1)}, bf16[96,1280]{0,1:T(8,128)(2,1)S(1)}, u32[]{:S(2)}, u32[]{:S(2)}) collective-permute-start(bf16[96,1280]{0,1:T(8,128)(2,1)S(1)} %get-tuple-element.197), channel_id=1, source_target_pairs={{0,16},{16,0},{1,17},{17,1},{2,18},{18,2},{3,19},{19,3},{4,20},{20... | collective-permute-start | bytes 737288 | tf_op jit(solution)/shard_map/ppermute | solution.py:97
  260.7 105.7 %collective-permute-start.19 = (bf16[96,1536]{0,1:T(8,128)(2,1)S(1)}, bf16[96,1536]{0,1:T(8,128)(2,1)}, u32[]{:S(2)}, u32[]{:S(2)}) collective-permute-start(bf16[96,1536]{0,1:T(8,128)(2,1)S(1)} %bitcast.299), channel_id=1, source_target_pairs={{0,16},{16,0},{1,17},{17,1},{2,18},{18,2},{3,19},{19,3},{4,20},{20... | collective-permute-start | bytes 884744 | tf_op jit(solution)/shard_map/ppermute | solution.py:97
  261.0 72.3 %collective-permute-start.11 = (bf16[96,1536]{1,0:T(8,128)(2,1)}, bf16[96,1536]{1,0:T(8,128)(2,1)}, u32[]{:S(2)}, u32[]{:S(2)}) collective-permute-start(bf16[96,1536]{1,0:T(8,128)(2,1)} %get-tuple-element.199), channel_id=1, source_target_pairs={{0,16},{16,0},{1,17},{17,1},{2,18},{18,2},{3,19},{19,3},{4,20},{20... | collective-permute-start | bytes 884744 | tf_op jit(solution)/shard_map/ppermute | solution.py:97
  273.4 59.1 %copy-start.5 = (bf16[96,1536]{1,0:T(8,128)(2,1)S(1)}, bf16[96,1536]{1,0:T(8,128)(2,1)}, u32[]{:S(2)}) copy-start(bf16[96,1536]{1,0:T(8,128)(2,1)} %copy-done.4) | copy-start | bytes 884740
  335.3 5.9 %copy-start.98 = (bf16[2,4,96,2048]{3,2,1,0:T(8,128)(2,1)S(1)}, bf16[2,4,96,2048]{3,2,1,0:T(8,128)(2,1)}, u32[]{:S(2)}) copy-start(bf16[2,4,96,2048]{3,2,1,0:T(8,128)(2,1)} %get-tuple-element.114) | copy-start | bytes 9437188
  335.3 5.9 %copy-start.99 = (bf16[2,4,96,1536]{3,2,1,0:T(8,128)(2,1)S(1)}, bf16[2,4,96,1536]{3,2,1,0:T(8,128)(2,1)}, u32[]{:S(2)}) copy-start(bf16[2,4,96,1536]{3,2,1,0:T(8,128)(2,1)} %get-tuple-element.113) | copy-start | bytes 7077892
  341.1 7.4 %copy-start.3 = (f32[96,1536]{1,0:T(8,128)S(1)}, f32[96,1536]{1,0:T(8,128)}, u32[]{:S(2)}) copy-start(f32[96,1536]{1,0:T(8,128)} %copy-done.2) | copy-start | bytes 1769476
  341.2 7.4 %copy-start.23 = (bf16[1536,16]{1,0:T(8,128)(2,1)S(1)}, bf16[1536,16]{1,0:T(8,128)(2,1)}, u32[]{:S(2)}) copy-start(bf16[1536,16]{1,0:T(8,128)(2,1)} %copy-done.22) | copy-start | bytes 147460
  341.2 7.4 %copy-start.65 = (f32[1536]{0:T(1024)S(1)}, f32[1536]{0:T(1024)}, u32[]{:S(2)}) copy-start(f32[1536]{0:T(1024)} %copy-done.64) | copy-start | bytes 18436
  341.2 7.4 %copy-start.89 = (f32[96]{0:T(128)S(1)}, f32[96]{0:T(128)}, u32[]{:S(2)}) copy-start(f32[96]{0:T(128)} %copy-done.88) | copy-start | bytes 1156
  363.4 3.1 collective-permute-start.20
  364.4 5.4 collective-permute-start.18
  365.2 9.2 %collective-permute-start.16 = (f32[96,1536]{1,0:T(8,128)S(1)}, f32[96,1536]{1,0:T(8,128)S(1)}, u32[]{:S(2)}, u32[]{:S(2)}) collective-permute-start(f32[96,1536]{1,0:T(8,128)S(1)} %get-tuple-element.183), channel_id=1, source_target_pairs={{0,16},{16,0},{1,17},{17,1},{2,18},{18,2},{3,19},{19,3},{4,20},{20... | collective-permute-start | bytes 1769480 | tf_op jit(solution)/shard_map/ppermute | solution.py:97
  (80 other events, 166.8 us)
Sparse Core Ops, SparseCore 0:
  12.2 32.8 all-gather.2
  230.7 69.9 reduce-scatter.2
  303.7 70.2 reduce-scatter.4

commit v16 on v15

--- a/solution.py
+++ b/solution.py
@@ -476,25 +476,10 @@
     return [(first, 0, up, layer, (DOWN, 0)), (first, 1, down, layer, (DOWN, 1))]
 
 
-def dense_lanes(first, width):
+def dense_lanes(first):
     up, down, deep = bits_of(GROUP), bits_of(GROUP)[::-1], bits_of(LINE)
-    near = width // 8 // COLUMNS * COLUMNS
-    away = width - near
     return [
-        (
-            first,
-            (True, (0, away)),
-            [(LINE, deep), (GROUP, up)],
-            0,
-            (QKV, slice(None), pl.ds(0, away)),
-        ),
-        (
-            first,
-            (False, (away, near)),
-            [(GROUP, up), (LINE, deep)],
-            0,
-            (QKV, slice(None), pl.ds(away, near)),
-        ),
+        (first, (True, None), [(LINE, deep), (GROUP, up)], 0, (QKV,)),
         (first + 1, (False, None), [(GROUP, down), (LINE, deep)], 0, (OUT,)),
         small_lane(first + 2, 0),
     ]
@@ -1350,7 +1335,7 @@
         grad_gate_up.reshape(dp, D // dp, held * inner),
         grad_down.reshape(half, dp, inner // dp, D),
     ]
-    lanes = dense_lanes(2, grad_w_qkv.shape[1])
+    lanes = dense_lanes(2)
     for array in (grad_w_qkv, grad_w_out, small):
         arrays.append(array.reshape(dp, deep, array.shape[0] // (dp * deep), array.shape[1]))
     width = grad_w_qkv.shape[1]

time: 564 us -> 560 us (level)
  no operation moved by 1% of the time
where the time goes in v16:
time: 560 us; the launch traced here: 551 us
  Pallas kernels  360 us (64%)
  matrix products  83.8 us (15%)
  local copies, waits for them, and re-layouts  33.1 us (6%)
  other arithmetic  26.8 us (5%)
  waiting for transfers between devices  25.7 us (5%)
  between operations  15.6 us (3%)
  starting transfers between devices  6.44 us (1%)
    pallas_call x4, Pallas kernels, expert_call(): pl.pallas_call(kernel, out_shape=shapes, in_specs=[vmem] * len(operands)...  202 us
    pallas_call x1, Pallas kernels, sum_scatter(): pl.pallas_call(functools.partial(sum_scatter_kernel, (plans, len(arrays),...  157 us
    dot_general x10, matrix products, turned(): jnp.einsum('tc,tq->cq', left, right, preferred_element_type=jnp.float32)  39.9 us
    ppermute x21, waiting for transfers between devices, swapped(): return lax.ppermute(array, CORE, [(0, 1), (1, 0)])  25.6 us
    unnamed x212, local copies, waits for them, and re-layouts  21.9 us
    dot_general x8, matrix products, matmul(): return jnp.dot(left_side, right_side, preferred_element_type=jnp.float32)  21 us
  transfers between devices with their start and end apart: 24, of which 3 were waited for; matrix products, arithmetic and copies ran while one was open for 16% of the time, Pallas kernels for 11%

profile of v16, /device:TPU:0, one launch (start us, length us, event | category | flops | bytes accessed | tf_op | source)
XLA Modules:
  0.0 551.2 jit_solution(8085999360795512007)
XLA Ops:
  10.4 1.7 constant_dynamic-slice_fusion.9
  12.9 1.1 fusion.48
  16.2 3.6 collective-permute-done.6
  22.8 1.4 copy-done.95
  24.9 2.2 fusion.13
  27.2 4.4 fusion.4
  33.4 21.7 %collective-permute-done.4.refs_13_ = bf16[1536,1536]{1,0:T(8,128)(2,1)} collective-permute-done((bf16[1536,1536]{1,0:T(8,128)(2,1)}, bf16[1536,1536]{1,0:T(8,128)(2,1)}, u32[]{:S(2)}, u32[]{:S(2)}) %collective-permute-start.4) | collective-permute-done | bytes 4718624 | tf_op jit(solution)/shard_map/ppermute | solution.py:97
  55.1 3.6 multiply_reduce_fusion.7
  59.8 51.0 %shard_map.237 = (bf16[96,1536]{1,0:T(8,128)(2,1)S(1)}, bf16[4,96,1536]{2,1,0:T(8,128)(2,1)S(1)}, bf16[4,96,128]{2,1,0:T(8,128)(2,1)S(1)}, f32[96,128]{1,0:T(8,1...) custom-call(bf16[96,1536]{1,0:T(8,128)(2,1)S(1)} %multiply_convert_f, ...), custom_call_target="tpu_custom_call" | custom-call | flops 49999998976 | bytes 100000000 | tf_op jit(solution)/shard_map/pallas_call | solution.py:1057
  110.8 1.1 copy-done.12
  111.9 1.0 copy-done.15
  114.0 2.2 fusion.117
  116.3 4.4 fusion.118
  123.1 3.4 multiply_reduce_fusion.6
  126.6 48.9 %shard_map.238 = (bf16[96,1536]{1,0:T(8,128)(2,1)S(1)}, bf16[4,96,1536]{2,1,0:T(8,128)(2,1)S(1)}, bf16[4,96,128]{2,1,0:T(8,128)(2,1)S(1)}, f32[96,128]{1,0:T(8,1...) custom-call(bf16[96,1536]{1,0:T(8,128)(2,1)S(1)} %multiply_convert_f, ...), custom_call_target="tpu_custom_call" | custom-call | flops 49999998976 | bytes 100000000 | tf_op jit(solution)/shard_map/pallas_call | solution.py:1057
  175.5 1.1 copy-done.14
  176.6 43.7 %shard_map.239 = (f32[96,1536]{1,0:T(8,128)S(1)}, f32[96,128]{1,0:T(8,128)S(1)}, bf16[2,4,96,1536]{3,2,1,0:T(8,128)(2,1)}, bf16[2,4,96,1024]{3,2,1,0:T(8,128)(2,...) custom-call(bf16[4,96,1536]{2,1,0:T(8,128)(2,1)S(1)} %bitcast.278, ...), custom_call_target="tpu_custom_call" | custom-call | flops 49999998976 | bytes 100000000 | tf_op jit(solution)/shard_map/pallas_call | solution.py:1057
  220.3 1.1 copy-done.7
  221.4 9.1 %bitcast_convert_fusion.1 = bf16[1536,2048]{1,0:T(8,128)(2,1)} fusion(bf16[2,4,96,1536]{3,2,1,0:T(8,128)(2,1)} %get-tuple-element.87, bf16[2,4,96,2048]{3,2,1,0:T(8,128)(2,1)} %get-tuple-element.88), kind=kOutput, calls=%fused_computation.3 | convolution fusion | flops 4834983936 | bytes 11796480 | tf_op jit(solution)/shard_map/tc,tq->cq/dot_general | solution.py:1205
  232.5 1.1 fusion.113
  233.6 4.7 convolution_convert_fusion.5
  238.3 1.9 copy.96
  240.2 1.4 multiply_reduce_fusion.1
  246.1 1.4 copy-done.19
  248.2 2.3 fusion.65
  252.5 1.1 pad_maximum_fusion.1
  254.1 1.1 broadcast_select_fusion.3
  255.9 4.2 bitcast_convert_fusion.3
  261.2 1.9 convolution_convert_fusion.3
  263.2 2.5 convolution_convert_fusion.1
  265.7 3.5 pad_maximum_fusion
  269.3 1.4 copy-done.10
  270.7 1.4 copy-done.13
  272.1 1.3 copy-done.16
  273.4 58.9 %shard_map.240 = (f32[96,1536]{1,0:T(8,128)S(1)}, f32[96,128]{1,0:T(8,128)S(1)}, bf16[2,4,96,1536]{3,2,1,0:T(8,128)(2,1)}, bf16[2,4,96,1024]{3,2,1,0:T(8,128)(2,...) custom-call(bf16[96,1536]{1,0:T(8,128)(2,1)S(1)} %get-tuple-element.96.grad, ...), custom_call_target="tpu_custom_call" | custom-call | flops 49999998976 | bytes 100000000 | tf_op jit(solution)/shard_map/pallas_call | solution.py:1057
  333.3 2.0 maximum_select_fusion.1
  335.3 5.9 %bitcast_convert_fusion.2 = bf16[1024,1536]{1,0:T(8,128)(2,1)} fusion(bf16[2,4,96,1024]{3,2,1,0:T(8,128)(2,1)S(1)} %get-tuple-element.115, bf16[2,4,96,1536]{3,2,1,0:T(8,128)(2,1)} %get-tuple-element.116), kind=kOutput, calls=%fused_computation.7 | convolution fusion | flops 2417491968 | bytes 7077888 | tf_op jit(solution)/shard_map/tc,tq->cq/dot_general | solution.py:1205
  341.2 7.3 %bitcast_convert_fusion = bf16[1536,2048]{1,0:T(8,128)(2,1)} fusion(bf16[2,4,96,1536]{3,2,1,0:T(8,128)(2,1)S(1)} %copy-done.99, bf16[2,4,96,2048]{3,2,1,0:T(8,128)(2,1)S(1)} %copy-done.98), kind=kOutput, calls=%fused_computation.2 | convolution fusion | flops 4834983936 | bytes 11796480 | tf_op jit(solution)/shard_map/tc,tq->cq/dot_general | solution.py:1205
  349.4 4.0 convolution_convert_fusion.4
  354.4 1.4 multiply_reduce_fusion
  361.6 1.7 fusion.56
  366.4 3.4 convolution_convert_fusion.2
  369.8 4.6 convolution_convert_fusion
  374.4 1.1 maximum_select_fusion
  375.6 157.5 %shard_map.241 = (bf16[2,2,384,512]{3,2,1,0:T(8,128)(2,1)}, bf16[2,2,384,512]{3,2,1,0:T(8,128)(2,1)}, bf16[2,2,128,1536]{3,2,1,0:T(8,128)(2,1)}, bf16[2,96,1280]...) custom-call(bf16[4,384,2048]{2,1,0:T(8,128)(2,1)} %bitcast.283, ...), custom_call_target="tpu_custom_call" | custom-call | tf_op jit(solution)/shard_map/pallas_call | solution.py:448
  533.0 1.1 slice_bitcast_fusion.2
  535.9 2.1 bitcast_convert_fusion.4
  540.0 3.6 bitcast_convert_fusion.5
  (351 shorter events, 43.3 us)
Async XLA Ops:
  7.2 13.7 %copy-start = (s32[2,96]{1,0:T(2,128)S(1)}, s32[2,96]{1,0:T(2,128)}, u32[]{:S(2)}) copy-start(s32[2,96]{1,0:T(2,128)} %param.16) | copy-start | bytes 2308
  7.2 14.4 %copy-start.82 = (s32[1,192,8]{1,2,0:T(8,128)S(1)}, s32[1,192,8]{1,2,0:T(8,128)}, u32[]{:S(2)}) copy-start(s32[1,192,8]{1,2,0:T(8,128)} %param.17) | copy-start | bytes 18436
  7.2 15.0 %copy-start.20 = (bf16[192,1536]{1,0:T(8,128)(2,1)S(1)}, bf16[192,1536]{1,0:T(8,128)(2,1)}, u32[]{:S(2)}) copy-start(bf16[192,1536]{1,0:T(8,128)(2,1)} %param.14) | copy-start | bytes 1769476
  7.2 52.2 %all-gather.3.cloned.1.call-start = ((), (), s32[]{:S(2)}) async-start(), calls=%async_computation.4 | async-start | bytes 1474560 | tf_op jit(solution)/shard_map/all_gather | solution.py:1222
  7.3 13.5 %collective-permute-start.2 = (bf16[1536,512]{1,0:T(8,128)(2,1)}, bf16[1536,512]{1,0:T(8,128)(2,1)S(1)}, u32[]{:S(2)}, u32[]{:S(2)}) collective-permute-start(bf16[1536,512]{1,0:T(8,128)(2,1)} %bitcast.364), channel_id=1, source_target_pairs={{0,16},{16,0},{1,17},{17,1},{2,18},{18,2},{3,19},{19,3},{4,20},{20... | collective-permute-start | bytes 4718600 | tf_op jit(solution)/shard_map/ppermute | solution.py:97
  7.8 13.2 %collective-permute-start.1 = (bf16[1536,512]{1,0:T(8,128)(2,1)}, bf16[1536,512]{1,0:T(8,128)(2,1)}, u32[]{:S(2)}, u32[]{:S(2)}) collective-permute-start(bf16[1536,512]{1,0:T(8,128)(2,1)} %bitcast.361), channel_id=1, source_target_pairs={{0,16},{16,0},{1,17},{17,1},{2,18},{18,2},{3,19},{19,3},{4,20},{20... | collective-permute-start | bytes 4718600 | tf_op jit(solution)/shard_map/ppermute | solution.py:97
  7.9 19.3 %collective-permute-start.3 = (bf16[1536,1536]{1,0:T(8,128)(2,1)}, bf16[1536,1536]{1,0:T(8,128)(2,1)}, u32[]{:S(2)}, u32[]{:S(2)}) collective-permute-start(bf16[1536,1536]{1,0:T(8,128)(2,1)} %bitcast.358), channel_id=1, source_target_pairs={{0,16},{16,0},{1,17},{17,1},{2,18},{18,2},{3,19},{19,3},{4,20},{20... | collective-permute-start | bytes 14155784 | tf_op jit(solution)/shard_map/ppermute | solution.py:97
  9.0 6.1 %collective-permute-start = (bf16[1536]{0:T(1024)(128)(2,1)S(1)}, bf16[1536]{0:T(1024)(128)(2,1)S(1)}, u32[]{:S(2)}, u32[]{:S(2)}) collective-permute-start(bf16[1536]{0:T(1024)(128)(2,1)S(1)} %reduce), channel_id=1, source_target_pairs={{0,16},{16,0},{1,17},{17,1},{2,18},{18,2},{3,19},{19,3},{4,20},{20... | collective-permute-start | bytes 9224 | tf_op jit(solution)/shard_map/ppermute | solution.py:97
  9.9 5.4 collective-permute-start.5
  12.1 336.4 %reduce-scatter.3.cloned.1.call-start = ((), (), s32[]{:S(2)}) async-start(), calls=%async_computation.2 | async-start | bytes 7864320 | tf_op jit(solution)/shard_map/reduce_scatter | solution.py:1282
  15.1 4.7 collective-permute-start.6
  15.2 5.2 collective-permute-start.7
  16.2 6.5 %copy-start.86 = (f32[96]{0:T(128)}, f32[96]{0:T(128)S(1)}, u32[]{:S(2)}) copy-start(f32[96]{0:T(128)S(1)} %get-tuple-element.228) | copy-start | bytes 1156
  19.8 39.6 %collective-permute-start.10 = (bf16[4,512,1536]{2,1,0:T(8,128)(2,1)}, bf16[4,512,1536]{2,1,0:T(8,128)(2,1)}, u32[]{:S(2)}, u32[]{:S(2)}) collective-permute-start(bf16[4,512,1536]{2,1,0:T(8,128)(2,1)} %bitcast.353), channel_id=1, source_target_pairs={{0,16},{16,0},{1,17},{17,1},{2,18},{18,2},{3,19},{19,3},{4,20},{20... | collective-permute-start | bytes 18874376 | tf_op jit(solution)/shard_map/ppermute | solution.py:97
  20.4 39.0 %collective-permute-start.8 = (bf16[4,1536,512]{2,1,0:T(8,128)(2,1)}, bf16[4,1536,512]{2,1,0:T(8,128)(2,1)}, u32[]{:S(2)}, u32[]{:S(2)}) collective-permute-start(bf16[4,1536,512]{2,1,0:T(8,128)(2,1)} %bitcast.343), channel_id=1, source_target_pairs={{0,16},{16,0},{1,17},{17,1},{2,18},{18,2},{3,19},{19,3},{4,20},{20... | collective-permute-start | bytes 18874376 | tf_op jit(solution)/shard_map/ppermute | solution.py:97
  20.8 38.7 %collective-permute-start.9 = (bf16[4,1536,512]{2,1,0:T(8,128)(2,1)}, bf16[4,1536,512]{2,1,0:T(8,128)(2,1)}, u32[]{:S(2)}, u32[]{:S(2)}) collective-permute-start(bf16[4,1536,512]{2,1,0:T(8,128)(2,1)} %bitcast.348), channel_id=1, source_target_pairs={{0,16},{16,0},{1,17},{17,1},{2,18},{18,2},{3,19},{19,3},{4,20},{20... | collective-permute-start | bytes 18874376 | tf_op jit(solution)/shard_map/ppermute | solution.py:97
  21.0 34.1 %collective-permute-start.4 = (bf16[1536,1536]{1,0:T(8,128)(2,1)}, bf16[1536,1536]{1,0:T(8,128)(2,1)}, u32[]{:S(2)}, u32[]{:S(2)}) collective-permute-start(bf16[1536,1536]{1,0:T(8,128)(2,1)} %bitcast.284), channel_id=1, source_target_pairs={{0,16},{16,0},{1,17},{17,1},{2,18},{18,2},{3,19},{19,3},{4,20},{20... | collective-permute-start | bytes 14155784 | tf_op jit(solution)/shard_map/ppermute | solution.py:97
  22.2 91.6 %copy-start.74 = (f32[1536]{0:T(1024)}, f32[1536]{0:T(1024)S(1)}, u32[]{:S(2)}) copy-start(f32[1536]{0:T(1024)S(1)} %get-tuple-element.225) | copy-start | bytes 18436
  22.2 37.0 %copy-start.64 = (f32[1536]{0:T(1024)}, f32[1536]{0:T(1024)S(1)}, u32[]{:S(2)}) copy-start(f32[1536]{0:T(1024)S(1)} %get-tuple-element.224) | copy-start | bytes 18436
  22.2 104.2 %copy-start.66 = (f32[1536]{0:T(1024)}, f32[1536]{0:T(1024)S(1)}, u32[]{:S(2)}) copy-start(f32[1536]{0:T(1024)S(1)} %get-tuple-element.223) | copy-start | bytes 18436
  24.9 7.5 %copy-start.68 = (bf16[96,512]{0,1:T(8,128)(2,1)}, bf16[96,512]{0,1:T(8,128)(2,1)S(1)}, u32[]{:S(2)}) copy-start(bf16[96,512]{0,1:T(8,128)(2,1)S(1)} %copy.86) | copy-start | bytes 294916
  33.4 25.3 %copy-start.27 = (bf16[8,64,3,96]{3,1,2,0:T(8,128)(2,1)}, bf16[8,64,3,96]{3,1,2,0:T(8,128)(2,1)S(1)}, u32[]{:S(2)}) copy-start(bf16[8,64,3,96]{3,1,2,0:T(8,128)(2,1)S(1)} %convolution_convert_fusion.9) | copy-start | bytes 884740
  58.7 52.1 %copy-start.2 = (f32[96,1536]{1,0:T(8,128)}, f32[96,1536]{1,0:T(8,128)S(1)}, u32[]{:S(2)}) copy-start(f32[96,1536]{1,0:T(8,128)S(1)} %get-tuple-element.240.hidden) | copy-start | bytes 1769476
  59.4 51.4 %copy-start.4 = (bf16[96,1536]{1,0:T(8,128)(2,1)}, bf16[96,1536]{1,0:T(8,128)(2,1)S(1)}, u32[]{:S(2)}) copy-start(bf16[96,1536]{1,0:T(8,128)(2,1)S(1)} %multiply_convert_fusion.3.x) | copy-start | bytes 884740
  116.3 5.1 copy-start.59
  116.3 5.1 copy-start.61
  126.6 50.0 %copy-start.6 = (bf16[384,1536]{1,0:T(8,128)(2,1)S(1)}, bf16[384,1536]{1,0:T(8,128)(2,1)}, u32[]{:S(2)}) copy-start(bf16[384,1536]{1,0:T(8,128)(2,1)} %all-gather.3.cloned.1.call-done) | copy-start | bytes 3538948
  230.6 145.0 %reduce-scatter.5.cloned.1.call-start = ((), (), s32[]{:S(2)}) async-start(), calls=%async_computation.3 | async-start | bytes 7864320 | tf_op jit(solution)/shard_map/reduce_scatter | solution.py:1326
  230.7 139.2 %collective-permute-start.17 = (bf16[96,1536]{1,0:T(8,128)(2,1)}, bf16[96,1536]{1,0:T(8,128)(2,1)}, u32[]{:S(2)}, u32[]{:S(2)}) collective-permute-start(bf16[96,1536]{1,0:T(8,128)(2,1)} %copy-done.40), channel_id=1, source_target_pairs={{0,16},{16,0},{1,17},{17,1},{2,18},{18,2},{3,19},{19,3},{4,20},{20... | collective-permute-start | bytes 884744 | tf_op jit(solution)/shard_map/ppermute | solution.py:97
  230.7 30.2 %collective-permute-start.14 = (bf16[96,1536]{0,1:T(8,128)(2,1)S(1)}, bf16[96,1536]{0,1:T(8,128)(2,1)}, u32[]{:S(2)}, u32[]{:S(2)}) collective-permute-start(bf16[96,1536]{0,1:T(8,128)(2,1)S(1)} %bitcast.306), channel_id=1, source_target_pairs={{0,16},{16,0},{1,17},{17,1},{2,18},{18,2},{3,19},{19,3},{4,20},{20... | collective-permute-start | bytes 884744 | tf_op jit(solution)/shard_map/ppermute | solution.py:97
  231.2 31.9 %collective-permute-start.12 = (bf16[96,1536]{1,0:T(8,128)(2,1)S(1)}, bf16[96,1536]{1,0:T(8,128)(2,1)}, u32[]{:S(2)}, u32[]{:S(2)}) collective-permute-start(bf16[96,1536]{1,0:T(8,128)(2,1)S(1)} %fusion.59), channel_id=1, source_target_pairs={{0,16},{16,0},{1,17},{17,1},{2,18},{18,2},{3,19},{19,3},{4,20},{20... | collective-permute-start | bytes 884744 | tf_op jit(solution)/shard_map/ppermute | solution.py:97
  233.6 6.6 %copy-start.38 = (f32[8,3,96,96]{2,3,1,0:T(8,128)S(1)}, f32[8,3,96,96]{2,3,1,0:T(8,128)}, u32[]{:S(2)}) copy-start(f32[8,3,96,96]{2,3,1,0:T(8,128)} %copy-done.37) | copy-start | bytes 2654212
  233.6 6.6 %copy-start.71 = (bf16[96,512]{0,1:T(8,128)(2,1)S(1)}, bf16[96,512]{0,1:T(8,128)(2,1)}, u32[]{:S(2)}) copy-start(bf16[96,512]{0,1:T(8,128)(2,1)} %copy-done.70) | copy-start | bytes 294916
  233.6 6.6 %copy-start.80 = (f32[8,3,96]{2,1,0:T(4,128)S(1)}, f32[8,3,96]{2,1,0:T(4,128)}, u32[]{:S(2)}) copy-start(f32[8,3,96]{2,1,0:T(4,128)} %copy-done.79) | copy-start | bytes 27652
  251.9 8.8 %collective-permute-start.15 = (bf16[96,768]{1,0:T(8,128)(2,1)S(1)}, bf16[96,768]{1,0:T(8,128)(2,1)S(1)}, u32[]{:S(2)}, u32[]{:S(2)}) collective-permute-start(bf16[96,768]{1,0:T(8,128)(2,1)S(1)} %get-tuple-element.211), channel_id=1, source_target_pairs={{0,16},{16,0},{1,17},{17,1},{2,18},{18,2},{3,19},{19,3},{4,20},{20... | collective-permute-start | bytes 442376 | tf_op jit(solution)/shard_map/ppermute | solution.py:97
  253.7 9.5 %collective-permute-start.13 = (bf16[96,1280]{0,1:T(8,128)(2,1)S(1)}, bf16[96,1280]{0,1:T(8,128)(2,1)S(1)}, u32[]{:S(2)}, u32[]{:S(2)}) collective-permute-start(bf16[96,1280]{0,1:T(8,128)(2,1)S(1)} %get-tuple-element.197), channel_id=1, source_target_pairs={{0,16},{16,0},{1,17},{17,1},{2,18},{18,2},{3,19},{19,3},{4,20},{20... | collective-permute-start | bytes 737288 | tf_op jit(solution)/shard_map/ppermute | solution.py:97
  260.7 105.7 %collective-permute-start.19 = (bf16[96,1536]{0,1:T(8,128)(2,1)S(1)}, bf16[96,1536]{0,1:T(8,128)(2,1)}, u32[]{:S(2)}, u32[]{:S(2)}) collective-permute-start(bf16[96,1536]{0,1:T(8,128)(2,1)S(1)} %bitcast.299), channel_id=1, source_target_pairs={{0,16},{16,0},{1,17},{17,1},{2,18},{18,2},{3,19},{19,3},{4,20},{20... | collective-permute-start | bytes 884744 | tf_op jit(solution)/shard_map/ppermute | solution.py:97
  261.0 72.3 %collective-permute-start.11 = (bf16[96,1536]{1,0:T(8,128)(2,1)}, bf16[96,1536]{1,0:T(8,128)(2,1)}, u32[]{:S(2)}, u32[]{:S(2)}) collective-permute-start(bf16[96,1536]{1,0:T(8,128)(2,1)} %get-tuple-element.199), channel_id=1, source_target_pairs={{0,16},{16,0},{1,17},{17,1},{2,18},{18,2},{3,19},{19,3},{4,20},{20... | collective-permute-start | bytes 884744 | tf_op jit(solution)/shard_map/ppermute | solution.py:97
  273.4 59.1 %copy-start.5 = (bf16[96,1536]{1,0:T(8,128)(2,1)S(1)}, bf16[96,1536]{1,0:T(8,128)(2,1)}, u32[]{:S(2)}) copy-start(bf16[96,1536]{1,0:T(8,128)(2,1)} %copy-done.4) | copy-start | bytes 884740
  335.3 5.9 %copy-start.98 = (bf16[2,4,96,2048]{3,2,1,0:T(8,128)(2,1)S(1)}, bf16[2,4,96,2048]{3,2,1,0:T(8,128)(2,1)}, u32[]{:S(2)}) copy-start(bf16[2,4,96,2048]{3,2,1,0:T(8,128)(2,1)} %get-tuple-element.114) | copy-start | bytes 9437188
  335.3 5.9 %copy-start.99 = (bf16[2,4,96,1536]{3,2,1,0:T(8,128)(2,1)S(1)}, bf16[2,4,96,1536]{3,2,1,0:T(8,128)(2,1)}, u32[]{:S(2)}) copy-start(bf16[2,4,96,1536]{3,2,1,0:T(8,128)(2,1)} %get-tuple-element.113) | copy-start | bytes 7077892
  341.1 7.4 %copy-start.3 = (f32[96,1536]{1,0:T(8,128)S(1)}, f32[96,1536]{1,0:T(8,128)}, u32[]{:S(2)}) copy-start(f32[96,1536]{1,0:T(8,128)} %copy-done.2) | copy-start | bytes 1769476
  341.2 7.4 %copy-start.23 = (bf16[1536,16]{1,0:T(8,128)(2,1)S(1)}, bf16[1536,16]{1,0:T(8,128)(2,1)}, u32[]{:S(2)}) copy-start(bf16[1536,16]{1,0:T(8,128)(2,1)} %copy-done.22) | copy-start | bytes 147460
  341.2 7.4 %copy-start.65 = (f32[1536]{0:T(1024)S(1)}, f32[1536]{0:T(1024)}, u32[]{:S(2)}) copy-start(f32[1536]{0:T(1024)} %copy-done.64) | copy-start | bytes 18436
  341.2 7.4 %copy-start.89 = (f32[96]{0:T(128)S(1)}, f32[96]{0:T(128)}, u32[]{:S(2)}) copy-start(f32[96]{0:T(128)} %copy-done.88) | copy-start | bytes 1156
  363.4 3.1 collective-permute-start.20
  364.4 5.4 collective-permute-start.18
  365.2 9.2 %collective-permute-start.16 = (f32[96,1536]{1,0:T(8,128)S(1)}, f32[96,1536]{1,0:T(8,128)S(1)}, u32[]{:S(2)}, u32[]{:S(2)}) collective-permute-start(f32[96,1536]{1,0:T(8,128)S(1)} %get-tuple-element.183), channel_id=1, source_target_pairs={{0,16},{16,0},{1,17},{17,1},{2,18},{18,2},{3,19},{19,3},{4,20},{20... | collective-permute-start | bytes 1769480 | tf_op jit(solution)/shard_map/ppermute | solution.py:97
  (80 other events, 166.8 us)
Sparse Core Ops, SparseCore 0:
  12.2 32.8 all-gather.2
  230.7 69.9 reduce-scatter.2
  303.7 70.2 reduce-scatter.4

commit v17 on v16

--- a/solution.py
+++ b/solution.py
@@ -476,11 +476,20 @@
     return [(first, 0, up, layer, (DOWN, 0)), (first, 1, down, layer, (DOWN, 1))]
 
 
-def dense_lanes(first):
+def dense_lanes(first, half):
     up, down, deep = bits_of(GROUP), bits_of(GROUP)[::-1], bits_of(LINE)
     return [
         (first, (True, None), [(LINE, deep), (GROUP, up)], 0, (QKV,)),
-        (first + 1, (False, None), [(GROUP, down), (LINE, deep)], 0, (OUT,)),
+        *(
+            (
+                first + 1,
+                (False, (at, half)),
+                [(GROUP, order), (LINE, deep)],
+                0,
+                (OUT, slice(None), pl.ds(at, half)),
+            )
+            for at, order in ((0, up), (half, down))
+        ),
         small_lane(first + 2, 0),
     ]
 
@@ -1335,7 +1344,7 @@
         grad_gate_up.reshape(dp, D // dp, held * inner),
         grad_down.reshape(half, dp, inner // dp, D),
     ]
-    lanes = dense_lanes(2)
+    lanes = dense_lanes(2, grad_w_out.shape[1] // 2)
     for array in (grad_w_qkv, grad_w_out, small):
         arrays.append(array.reshape(dp, deep, array.shape[0] // (dp * deep), array.shape[1]))
     width = grad_w_qkv.shape[1]

time: 560 us -> 566 us (1.011)
  Pallas kernels: 360 us -> 366 us
    pallas_call x1, Pallas kernels: 157 us -> 164 us  [sum_scatter(): pl.pallas_call(functools.partial(sum_scatter_kernel, (plans, len(arrays),...]
where the time goes in v17:
time: 566 us; the launch traced here: 558 us
  Pallas kernels  366 us (65%)
  matrix products  83.8 us (15%)
  local copies, waits for them, and re-layouts  33.1 us (6%)
  other arithmetic  26.8 us (5%)
  waiting for transfers between devices  25.7 us (5%)
  between operations  15.6 us (3%)
  starting transfers between devices  6.44 us (1%)
    pallas_call x4, Pallas kernels, expert_call(): pl.pallas_call(kernel, out_shape=shapes, in_specs=[vmem] * len(operands)...  202 us
    pallas_call x1, Pallas kernels, sum_scatter(): pl.pallas_call(functools.partial(sum_scatter_kernel, (plans, len(arrays),...  164 us
    dot_general x10, matrix products, turned(): jnp.einsum('tc,tq->cq', left, right, preferred_element_type=jnp.float32)  39.9 us
    ppermute x21, waiting for transfers between devices, swapped(): return lax.ppermute(array, CORE, [(0, 1), (1, 0)])  25.6 us
    unnamed x212, local copies, waits for them, and re-layouts  21.9 us
    dot_general x8, matrix products, matmul(): return jnp.dot(left_side, right_side, preferred_element_type=jnp.float32)  21 us
  transfers between devices with their start and end apart: 24, of which 3 were waited for; matrix products, arithmetic and copies ran while one was open for 16% of the time, Pallas kernels for 11%

profile of v17, /device:TPU:0, one launch (start us, length us, event | category | flops | bytes accessed | tf_op | source)
XLA Modules:
  0.0 557.7 jit_solution(15963318186007485413)
XLA Ops:
  10.4 1.7 constant_dynamic-slice_fusion.9
  12.9 1.1 fusion.48
  16.2 3.6 collective-permute-done.6
  22.8 1.4 copy-done.95
  24.9 2.2 fusion.13
  27.2 4.4 fusion.4
  33.4 21.7 %collective-permute-done.4.refs_13_ = bf16[1536,1536]{1,0:T(8,128)(2,1)} collective-permute-done((bf16[1536,1536]{1,0:T(8,128)(2,1)}, bf16[1536,1536]{1,0:T(8,128)(2,1)}, u32[]{:S(2)}, u32[]{:S(2)}) %collective-permute-start.4) | collective-permute-done | bytes 4718624 | tf_op jit(solution)/shard_map/ppermute | solution.py:97
  55.1 3.6 multiply_reduce_fusion.7
  59.8 51.0 %shard_map.237 = (bf16[96,1536]{1,0:T(8,128)(2,1)S(1)}, bf16[4,96,1536]{2,1,0:T(8,128)(2,1)S(1)}, bf16[4,96,128]{2,1,0:T(8,128)(2,1)S(1)}, f32[96,128]{1,0:T(8,1...) custom-call(bf16[96,1536]{1,0:T(8,128)(2,1)S(1)} %multiply_convert_f, ...), custom_call_target="tpu_custom_call" | custom-call | flops 49999998976 | bytes 100000000 | tf_op jit(solution)/shard_map/pallas_call | solution.py:1066
  110.8 1.1 copy-done.12
  111.9 1.0 copy-done.15
  114.0 2.2 fusion.117
  116.3 4.4 fusion.118
  123.1 3.4 multiply_reduce_fusion.6
  126.6 48.9 %shard_map.238 = (bf16[96,1536]{1,0:T(8,128)(2,1)S(1)}, bf16[4,96,1536]{2,1,0:T(8,128)(2,1)S(1)}, bf16[4,96,128]{2,1,0:T(8,128)(2,1)S(1)}, f32[96,128]{1,0:T(8,1...) custom-call(bf16[96,1536]{1,0:T(8,128)(2,1)S(1)} %multiply_convert_f, ...), custom_call_target="tpu_custom_call" | custom-call | flops 49999998976 | bytes 100000000 | tf_op jit(solution)/shard_map/pallas_call | solution.py:1066
  175.5 1.1 copy-done.14
  176.6 43.7 %shard_map.239 = (f32[96,1536]{1,0:T(8,128)S(1)}, f32[96,128]{1,0:T(8,128)S(1)}, bf16[2,4,96,1536]{3,2,1,0:T(8,128)(2,1)}, bf16[2,4,96,1024]{3,2,1,0:T(8,128)(2,...) custom-call(bf16[4,96,1536]{2,1,0:T(8,128)(2,1)S(1)} %bitcast.278, ...), custom_call_target="tpu_custom_call" | custom-call | flops 49999998976 | bytes 100000000 | tf_op jit(solution)/shard_map/pallas_call | solution.py:1066
  220.3 1.1 copy-done.7
  221.4 9.1 %bitcast_convert_fusion.1 = bf16[1536,2048]{1,0:T(8,128)(2,1)} fusion(bf16[2,4,96,1536]{3,2,1,0:T(8,128)(2,1)} %get-tuple-element.87, bf16[2,4,96,2048]{3,2,1,0:T(8,128)(2,1)} %get-tuple-element.88), kind=kOutput, calls=%fused_computation.3 | convolution fusion | flops 4834983936 | bytes 11796480 | tf_op jit(solution)/shard_map/tc,tq->cq/dot_general | solution.py:1214
  232.5 1.1 fusion.113
  233.6 4.7 convolution_convert_fusion.5
  238.3 1.9 copy.96
  240.2 1.4 multiply_reduce_fusion.1
  246.1 1.4 copy-done.19
  248.2 2.3 fusion.65
  252.5 1.1 pad_maximum_fusion.1
  254.1 1.1 broadcast_select_fusion.3
  255.9 4.2 bitcast_convert_fusion.3
  261.2 1.9 convolution_convert_fusion.3
  263.2 2.5 convolution_convert_fusion.1
  265.7 3.5 pad_maximum_fusion
  269.3 1.4 copy-done.10
  270.7 1.4 copy-done.13
  272.1 1.3 copy-done.16
  273.4 58.9 %shard_map.240 = (f32[96,1536]{1,0:T(8,128)S(1)}, f32[96,128]{1,0:T(8,128)S(1)}, bf16[2,4,96,1536]{3,2,1,0:T(8,128)(2,1)}, bf16[2,4,96,1024]{3,2,1,0:T(8,128)(2,...) custom-call(bf16[96,1536]{1,0:T(8,128)(2,1)S(1)} %get-tuple-element.96.grad, ...), custom_call_target="tpu_custom_call" | custom-call | flops 49999998976 | bytes 100000000 | tf_op jit(solution)/shard_map/pallas_call | solution.py:1066
  333.3 2.0 maximum_select_fusion.1
  335.3 5.9 %bitcast_convert_fusion.2 = bf16[1024,1536]{1,0:T(8,128)(2,1)} fusion(bf16[2,4,96,1024]{3,2,1,0:T(8,128)(2,1)S(1)} %get-tuple-element.115, bf16[2,4,96,1536]{3,2,1,0:T(8,128)(2,1)} %get-tuple-element.116), kind=kOutput, calls=%fused_computation.7 | convolution fusion | flops 2417491968 | bytes 7077888 | tf_op jit(solution)/shard_map/tc,tq->cq/dot_general | solution.py:1214
  341.2 7.3 %bitcast_convert_fusion = bf16[1536,2048]{1,0:T(8,128)(2,1)} fusion(bf16[2,4,96,1536]{3,2,1,0:T(8,128)(2,1)S(1)} %copy-done.99, bf16[2,4,96,2048]{3,2,1,0:T(8,128)(2,1)S(1)} %copy-done.98), kind=kOutput, calls=%fused_computation.2 | convolution fusion | flops 4834983936 | bytes 11796480 | tf_op jit(solution)/shard_map/tc,tq->cq/dot_general | solution.py:1214
  349.4 4.0 convolution_convert_fusion.4
  354.4 1.4 multiply_reduce_fusion
  361.6 1.7 fusion.56
  366.4 3.4 convolution_convert_fusion.2
  369.8 4.6 convolution_convert_fusion
  374.4 1.1 maximum_select_fusion
  375.6 163.9 %shard_map.241 = (bf16[2,2,384,512]{3,2,1,0:T(8,128)(2,1)}, bf16[2,2,384,512]{3,2,1,0:T(8,128)(2,1)}, bf16[2,2,128,1536]{3,2,1,0:T(8,128)(2,1)}, bf16[2,96,1280]...) custom-call(bf16[4,384,2048]{2,1,0:T(8,128)(2,1)} %bitcast.283, ...), custom_call_target="tpu_custom_call" | custom-call | tf_op jit(solution)/shard_map/pallas_call | solution.py:448
  539.5 1.1 slice_bitcast_fusion.2
  542.4 2.1 bitcast_convert_fusion.4
  546.5 3.6 bitcast_convert_fusion.5
  (351 shorter events, 43.3 us)
Async XLA Ops:
  7.2 13.7 %copy-start = (s32[2,96]{1,0:T(2,128)S(1)}, s32[2,96]{1,0:T(2,128)}, u32[]{:S(2)}) copy-start(s32[2,96]{1,0:T(2,128)} %param.16) | copy-start | bytes 2308
  7.2 14.4 %copy-start.82 = (s32[1,192,8]{1,2,0:T(8,128)S(1)}, s32[1,192,8]{1,2,0:T(8,128)}, u32[]{:S(2)}) copy-start(s32[1,192,8]{1,2,0:T(8,128)} %param.17) | copy-start | bytes 18436
  7.2 15.0 %copy-start.20 = (bf16[192,1536]{1,0:T(8,128)(2,1)S(1)}, bf16[192,1536]{1,0:T(8,128)(2,1)}, u32[]{:S(2)}) copy-start(bf16[192,1536]{1,0:T(8,128)(2,1)} %param.14) | copy-start | bytes 1769476
  7.2 52.2 %all-gather.3.cloned.1.call-start = ((), (), s32[]{:S(2)}) async-start(), calls=%async_computation.4 | async-start | bytes 1474560 | tf_op jit(solution)/shard_map/all_gather | solution.py:1231
  7.3 13.5 %collective-permute-start.2 = (bf16[1536,512]{1,0:T(8,128)(2,1)}, bf16[1536,512]{1,0:T(8,128)(2,1)S(1)}, u32[]{:S(2)}, u32[]{:S(2)}) collective-permute-start(bf16[1536,512]{1,0:T(8,128)(2,1)} %bitcast.364), channel_id=1, source_target_pairs={{0,16},{16,0},{1,17},{17,1},{2,18},{18,2},{3,19},{19,3},{4,20},{20... | collective-permute-start | bytes 4718600 | tf_op jit(solution)/shard_map/ppermute | solution.py:97
  7.8 13.2 %collective-permute-start.1 = (bf16[1536,512]{1,0:T(8,128)(2,1)}, bf16[1536,512]{1,0:T(8,128)(2,1)}, u32[]{:S(2)}, u32[]{:S(2)}) collective-permute-start(bf16[1536,512]{1,0:T(8,128)(2,1)} %bitcast.361), channel_id=1, source_target_pairs={{0,16},{16,0},{1,17},{17,1},{2,18},{18,2},{3,19},{19,3},{4,20},{20... | collective-permute-start | bytes 4718600 | tf_op jit(solution)/shard_map/ppermute | solution.py:97
  7.9 19.3 %collective-permute-start.3 = (bf16[1536,1536]{1,0:T(8,128)(2,1)}, bf16[1536,1536]{1,0:T(8,128)(2,1)}, u32[]{:S(2)}, u32[]{:S(2)}) collective-permute-start(bf16[1536,1536]{1,0:T(8,128)(2,1)} %bitcast.358), channel_id=1, source_target_pairs={{0,16},{16,0},{1,17},{17,1},{2,18},{18,2},{3,19},{19,3},{4,20},{20... | collective-permute-start | bytes 14155784 | tf_op jit(solution)/shard_map/ppermute | solution.py:97
  9.0 6.1 %collective-permute-start = (bf16[1536]{0:T(1024)(128)(2,1)S(1)}, bf16[1536]{0:T(1024)(128)(2,1)S(1)}, u32[]{:S(2)}, u32[]{:S(2)}) collective-permute-start(bf16[1536]{0:T(1024)(128)(2,1)S(1)} %reduce), channel_id=1, source_target_pairs={{0,16},{16,0},{1,17},{17,1},{2,18},{18,2},{3,19},{19,3},{4,20},{20... | collective-permute-start | bytes 9224 | tf_op jit(solution)/shard_map/ppermute | solution.py:97
  9.9 5.4 collective-permute-start.5
  12.1 336.4 %reduce-scatter.3.cloned.1.call-start = ((), (), s32[]{:S(2)}) async-start(), calls=%async_computation.2 | async-start | bytes 7864320 | tf_op jit(solution)/shard_map/reduce_scatter | solution.py:1291
  15.1 4.7 collective-permute-start.6
  15.2 5.2 collective-permute-start.7
  16.2 6.5 %copy-start.86 = (f32[96]{0:T(128)}, f32[96]{0:T(128)S(1)}, u32[]{:S(2)}) copy-start(f32[96]{0:T(128)S(1)} %get-tuple-element.228) | copy-start | bytes 1156
  19.8 39.6 %collective-permute-start.10 = (bf16[4,512,1536]{2,1,0:T(8,128)(2,1)}, bf16[4,512,1536]{2,1,0:T(8,128)(2,1)}, u32[]{:S(2)}, u32[]{:S(2)}) collective-permute-start(bf16[4,512,1536]{2,1,0:T(8,128)(2,1)} %bitcast.353), channel_id=1, source_target_pairs={{0,16},{16,0},{1,17},{17,1},{2,18},{18,2},{3,19},{19,3},{4,20},{20... | collective-permute-start | bytes 18874376 | tf_op jit(solution)/shard_map/ppermute | solution.py:97
  20.4 39.0 %collective-permute-start.8 = (bf16[4,1536,512]{2,1,0:T(8,128)(2,1)}, bf16[4,1536,512]{2,1,0:T(8,128)(2,1)}, u32[]{:S(2)}, u32[]{:S(2)}) collective-permute-start(bf16[4,1536,512]{2,1,0:T(8,128)(2,1)} %bitcast.343), channel_id=1, source_target_pairs={{0,16},{16,0},{1,17},{17,1},{2,18},{18,2},{3,19},{19,3},{4,20},{20... | collective-permute-start | bytes 18874376 | tf_op jit(solution)/shard_map/ppermute | solution.py:97
  20.8 38.7 %collective-permute-start.9 = (bf16[4,1536,512]{2,1,0:T(8,128)(2,1)}, bf16[4,1536,512]{2,1,0:T(8,128)(2,1)}, u32[]{:S(2)}, u32[]{:S(2)}) collective-permute-start(bf16[4,1536,512]{2,1,0:T(8,128)(2,1)} %bitcast.348), channel_id=1, source_target_pairs={{0,16},{16,0},{1,17},{17,1},{2,18},{18,2},{3,19},{19,3},{4,20},{20... | collective-permute-start | bytes 18874376 | tf_op jit(solution)/shard_map/ppermute | solution.py:97
  21.0 34.1 %collective-permute-start.4 = (bf16[1536,1536]{1,0:T(8,128)(2,1)}, bf16[1536,1536]{1,0:T(8,128)(2,1)}, u32[]{:S(2)}, u32[]{:S(2)}) collective-permute-start(bf16[1536,1536]{1,0:T(8,128)(2,1)} %bitcast.284), channel_id=1, source_target_pairs={{0,16},{16,0},{1,17},{17,1},{2,18},{18,2},{3,19},{19,3},{4,20},{20... | collective-permute-start | bytes 14155784 | tf_op jit(solution)/shard_map/ppermute | solution.py:97
  22.2 91.6 %copy-start.74 = (f32[1536]{0:T(1024)}, f32[1536]{0:T(1024)S(1)}, u32[]{:S(2)}) copy-start(f32[1536]{0:T(1024)S(1)} %get-tuple-element.225) | copy-start | bytes 18436
  22.2 37.0 %copy-start.64 = (f32[1536]{0:T(1024)}, f32[1536]{0:T(1024)S(1)}, u32[]{:S(2)}) copy-start(f32[1536]{0:T(1024)S(1)} %get-tuple-element.224) | copy-start | bytes 18436
  22.2 104.2 %copy-start.66 = (f32[1536]{0:T(1024)}, f32[1536]{0:T(1024)S(1)}, u32[]{:S(2)}) copy-start(f32[1536]{0:T(1024)S(1)} %get-tuple-element.223) | copy-start | bytes 18436
  24.9 7.5 %copy-start.68 = (bf16[96,512]{0,1:T(8,128)(2,1)}, bf16[96,512]{0,1:T(8,128)(2,1)S(1)}, u32[]{:S(2)}) copy-start(bf16[96,512]{0,1:T(8,128)(2,1)S(1)} %copy.86) | copy-start | bytes 294916
  33.4 25.3 %copy-start.27 = (bf16[8,64,3,96]{3,1,2,0:T(8,128)(2,1)}, bf16[8,64,3,96]{3,1,2,0:T(8,128)(2,1)S(1)}, u32[]{:S(2)}) copy-start(bf16[8,64,3,96]{3,1,2,0:T(8,128)(2,1)S(1)} %convolution_convert_fusion.9) | copy-start | bytes 884740
  58.7 52.1 %copy-start.2 = (f32[96,1536]{1,0:T(8,128)}, f32[96,1536]{1,0:T(8,128)S(1)}, u32[]{:S(2)}) copy-start(f32[96,1536]{1,0:T(8,128)S(1)} %get-tuple-element.240.hidden) | copy-start | bytes 1769476
  59.4 51.4 %copy-start.4 = (bf16[96,1536]{1,0:T(8,128)(2,1)}, bf16[96,1536]{1,0:T(8,128)(2,1)S(1)}, u32[]{:S(2)}) copy-start(bf16[96,1536]{1,0:T(8,128)(2,1)S(1)} %multiply_convert_fusion.3.x) | copy-start | bytes 884740
  116.3 5.1 copy-start.59
  116.3 5.1 copy-start.61
  126.6 50.0 %copy-start.6 = (bf16[384,1536]{1,0:T(8,128)(2,1)S(1)}, bf16[384,1536]{1,0:T(8,128)(2,1)}, u32[]{:S(2)}) copy-start(bf16[384,1536]{1,0:T(8,128)(2,1)} %all-gather.3.cloned.1.call-done) | copy-start | bytes 3538948
  230.6 145.0 %reduce-scatter.5.cloned.1.call-start = ((), (), s32[]{:S(2)}) async-start(), calls=%async_computation.3 | async-start | bytes 7864320 | tf_op jit(solution)/shard_map/reduce_scatter | solution.py:1335
  230.7 139.2 %collective-permute-start.17 = (bf16[96,1536]{1,0:T(8,128)(2,1)}, bf16[96,1536]{1,0:T(8,128)(2,1)}, u32[]{:S(2)}, u32[]{:S(2)}) collective-permute-start(bf16[96,1536]{1,0:T(8,128)(2,1)} %copy-done.40), channel_id=1, source_target_pairs={{0,16},{16,0},{1,17},{17,1},{2,18},{18,2},{3,19},{19,3},{4,20},{20... | collective-permute-start | bytes 884744 | tf_op jit(solution)/shard_map/ppermute | solution.py:97
  230.7 30.2 %collective-permute-start.14 = (bf16[96,1536]{0,1:T(8,128)(2,1)S(1)}, bf16[96,1536]{0,1:T(8,128)(2,1)}, u32[]{:S(2)}, u32[]{:S(2)}) collective-permute-start(bf16[96,1536]{0,1:T(8,128)(2,1)S(1)} %bitcast.306), channel_id=1, source_target_pairs={{0,16},{16,0},{1,17},{17,1},{2,18},{18,2},{3,19},{19,3},{4,20},{20... | collective-permute-start | bytes 884744 | tf_op jit(solution)/shard_map/ppermute | solution.py:97
  231.2 31.9 %collective-permute-start.12 = (bf16[96,1536]{1,0:T(8,128)(2,1)S(1)}, bf16[96,1536]{1,0:T(8,128)(2,1)}, u32[]{:S(2)}, u32[]{:S(2)}) collective-permute-start(bf16[96,1536]{1,0:T(8,128)(2,1)S(1)} %fusion.59), channel_id=1, source_target_pairs={{0,16},{16,0},{1,17},{17,1},{2,18},{18,2},{3,19},{19,3},{4,20},{20... | collective-permute-start | bytes 884744 | tf_op jit(solution)/shard_map/ppermute | solution.py:97
  233.6 6.6 %copy-start.38 = (f32[8,3,96,96]{2,3,1,0:T(8,128)S(1)}, f32[8,3,96,96]{2,3,1,0:T(8,128)}, u32[]{:S(2)}) copy-start(f32[8,3,96,96]{2,3,1,0:T(8,128)} %copy-done.37) | copy-start | bytes 2654212
  233.6 6.6 %copy-start.71 = (bf16[96,512]{0,1:T(8,128)(2,1)S(1)}, bf16[96,512]{0,1:T(8,128)(2,1)}, u32[]{:S(2)}) copy-start(bf16[96,512]{0,1:T(8,128)(2,1)} %copy-done.70) | copy-start | bytes 294916
  233.6 6.6 %copy-start.80 = (f32[8,3,96]{2,1,0:T(4,128)S(1)}, f32[8,3,96]{2,1,0:T(4,128)}, u32[]{:S(2)}) copy-start(f32[8,3,96]{2,1,0:T(4,128)} %copy-done.79) | copy-start | bytes 27652
  251.9 8.8 %collective-permute-start.15 = (bf16[96,768]{1,0:T(8,128)(2,1)S(1)}, bf16[96,768]{1,0:T(8,128)(2,1)S(1)}, u32[]{:S(2)}, u32[]{:S(2)}) collective-permute-start(bf16[96,768]{1,0:T(8,128)(2,1)S(1)} %get-tuple-element.211), channel_id=1, source_target_pairs={{0,16},{16,0},{1,17},{17,1},{2,18},{18,2},{3,19},{19,3},{4,20},{20... | collective-permute-start | bytes 442376 | tf_op jit(solution)/shard_map/ppermute | solution.py:97
  253.7 9.5 %collective-permute-start.13 = (bf16[96,1280]{0,1:T(8,128)(2,1)S(1)}, bf16[96,1280]{0,1:T(8,128)(2,1)S(1)}, u32[]{:S(2)}, u32[]{:S(2)}) collective-permute-start(bf16[96,1280]{0,1:T(8,128)(2,1)S(1)} %get-tuple-element.197), channel_id=1, source_target_pairs={{0,16},{16,0},{1,17},{17,1},{2,18},{18,2},{3,19},{19,3},{4,20},{20... | collective-permute-start | bytes 737288 | tf_op jit(solution)/shard_map/ppermute | solution.py:97
  260.7 105.7 %collective-permute-start.19 = (bf16[96,1536]{0,1:T(8,128)(2,1)S(1)}, bf16[96,1536]{0,1:T(8,128)(2,1)}, u32[]{:S(2)}, u32[]{:S(2)}) collective-permute-start(bf16[96,1536]{0,1:T(8,128)(2,1)S(1)} %bitcast.299), channel_id=1, source_target_pairs={{0,16},{16,0},{1,17},{17,1},{2,18},{18,2},{3,19},{19,3},{4,20},{20... | collective-permute-start | bytes 884744 | tf_op jit(solution)/shard_map/ppermute | solution.py:97
  261.0 72.3 %collective-permute-start.11 = (bf16[96,1536]{1,0:T(8,128)(2,1)}, bf16[96,1536]{1,0:T(8,128)(2,1)}, u32[]{:S(2)}, u32[]{:S(2)}) collective-permute-start(bf16[96,1536]{1,0:T(8,128)(2,1)} %get-tuple-element.199), channel_id=1, source_target_pairs={{0,16},{16,0},{1,17},{17,1},{2,18},{18,2},{3,19},{19,3},{4,20},{20... | collective-permute-start | bytes 884744 | tf_op jit(solution)/shard_map/ppermute | solution.py:97
  273.4 59.1 %copy-start.5 = (bf16[96,1536]{1,0:T(8,128)(2,1)S(1)}, bf16[96,1536]{1,0:T(8,128)(2,1)}, u32[]{:S(2)}) copy-start(bf16[96,1536]{1,0:T(8,128)(2,1)} %copy-done.4) | copy-start | bytes 884740
  335.3 5.9 %copy-start.98 = (bf16[2,4,96,2048]{3,2,1,0:T(8,128)(2,1)S(1)}, bf16[2,4,96,2048]{3,2,1,0:T(8,128)(2,1)}, u32[]{:S(2)}) copy-start(bf16[2,4,96,2048]{3,2,1,0:T(8,128)(2,1)} %get-tuple-element.114) | copy-start | bytes 9437188
  335.3 5.9 %copy-start.99 = (bf16[2,4,96,1536]{3,2,1,0:T(8,128)(2,1)S(1)}, bf16[2,4,96,1536]{3,2,1,0:T(8,128)(2,1)}, u32[]{:S(2)}) copy-start(bf16[2,4,96,1536]{3,2,1,0:T(8,128)(2,1)} %get-tuple-element.113) | copy-start | bytes 7077892
  341.1 7.4 %copy-start.3 = (f32[96,1536]{1,0:T(8,128)S(1)}, f32[96,1536]{1,0:T(8,128)}, u32[]{:S(2)}) copy-start(f32[96,1536]{1,0:T(8,128)} %copy-done.2) | copy-start | bytes 1769476
  341.2 7.4 %copy-start.23 = (bf16[1536,16]{1,0:T(8,128)(2,1)S(1)}, bf16[1536,16]{1,0:T(8,128)(2,1)}, u32[]{:S(2)}) copy-start(bf16[1536,16]{1,0:T(8,128)(2,1)} %copy-done.22) | copy-start | bytes 147460
  341.2 7.4 %copy-start.65 = (f32[1536]{0:T(1024)S(1)}, f32[1536]{0:T(1024)}, u32[]{:S(2)}) copy-start(f32[1536]{0:T(1024)} %copy-done.64) | copy-start | bytes 18436
  341.2 7.4 %copy-start.89 = (f32[96]{0:T(128)S(1)}, f32[96]{0:T(128)}, u32[]{:S(2)}) copy-start(f32[96]{0:T(128)} %copy-done.88) | copy-start | bytes 1156
  363.4 3.1 collective-permute-start.20
  364.4 5.4 collective-permute-start.18
  365.2 9.2 %collective-permute-start.16 = (f32[96,1536]{1,0:T(8,128)S(1)}, f32[96,1536]{1,0:T(8,128)S(1)}, u32[]{:S(2)}, u32[]{:S(2)}) collective-permute-start(f32[96,1536]{1,0:T(8,128)S(1)} %get-tuple-element.183), channel_id=1, source_target_pairs={{0,16},{16,0},{1,17},{17,1},{2,18},{18,2},{3,19},{19,3},{4,20},{20... | collective-permute-start | bytes 1769480 | tf_op jit(solution)/shard_map/ppermute | solution.py:97
  (80 other events, 166.8 us)
Sparse Core Ops, SparseCore 0:
  12.2 32.8 all-gather.2
  230.7 69.9 reduce-scatter.2
  303.7 70.2 reduce-scatter.4
